TPU v7x, 512 devices: a whole 4x8x8 slice. The times are simulated.
512 devices in a mesh: rep: 64 (over z, y_lo, core), fsdp: 8 (over x, y_hi).
Axes of the slice: x: 4, y: 8 (y_hi: 2, y_lo: 4; y = y_hi * 4 + y_lo), z: 8, core: 2. Of those that a mesh axis runs over, the one named last changes fastest.
Arguments:
- tokens: bfloat16 [65536, 4096], P(('rep', 'fsdp')), may hold values from -18 to 18
- targets: bfloat16 [65536, 1024], P(('rep', 'fsdp')), may hold values from -6 to 6
- local_weights: bfloat16 [64, 4096, 1024], P('rep', 'fsdp'), may hold values from -6 to 6
- pending_delta: bfloat16 [64, 4096, 256], P('rep', 'fsdp'), may hold values from -15 to 15
- frag_order: int32 [8], replicated, may hold values from 0 to 7, each once
- global_frag: bfloat16 [4096, 256], P('fsdp'), may hold values from -6 to 6
- outer_momentum: float32 [4096, 256], P('fsdp'), may hold values from -3 to 3
Outputs:
- new_weights: bfloat16 [64, 4096, 1024], P('rep', 'fsdp')
- new_global: bfloat16 [4096, 256], P('fsdp')
- new_momentum: float32 [4096, 256], P('fsdp')
Inputs may be any that keep to these rules, and one draw needn't show every extreme that they name: frag_order is a permutation of 0 to 7; the pending fragment is made of heads frag_order[0] and frag_order[1].
All inputs are finite; a program needn't handle non-finite values.
Results may differ from a plain program's by a relative error of at most 0.0031.
Values may be sent and summed in bfloat16 or wider, within the bound.
No kernel may reach another device: no remote copies, remote signals or barrier semaphores. Data moves between devices by JAX's collectives and lax.ppermute only.
A program may use at most 64 MiB of HBM per device.

v0:
```python
import math

import jax
import jax.numpy as jnp
from jax import lax
from jax.sharding import PartitionSpec as P

D = 4096
HEAD = 128
FRAG_HEADS = 2
KV = 1024


def normalize(activations):
    floated = activations.astype(jnp.float32)
    meansq = jnp.mean(floated * floated, axis=-1, keepdims=True)
    return (floated * lax.rsqrt(meansq + 1e-06)).astype(jnp.bfloat16)


def merge_fragment(stepped, new_global, frag_order):
    merged = stepped
    anchor = jnp.zeros((), jnp.int32)
    for head_slot in range(FRAG_HEADS):
        column = frag_order[head_slot] * HEAD
        current = lax.dynamic_slice(merged, (anchor, column), (merged.shape[0], HEAD))
        incoming = new_global[:, head_slot * HEAD : (head_slot + 1) * HEAD].astype(jnp.float32)
        blended = 0.5 * current + 0.5 * incoming
        merged = lax.dynamic_update_slice(merged, blended, (anchor, column))
    return merged.astype(jnp.bfloat16)


def body(tokens, targets, local_weights, pending_delta, frag_order, global_frag, outer_momentum):
    factor = 1.0 / math.sqrt(D)
    replicas = lax.axis_size("rep")
    weight = local_weights[0]
    normed = normalize(tokens)
    columns = lax.all_to_all(normed, "fsdp", split_axis=1, concat_axis=0, tiled=True)
    raw_keys = jnp.dot(
        normed,
        lax.all_gather(weight, "fsdp", axis=0, tiled=True),
        preferred_element_type=jnp.float32,
    )
    residual = (raw_keys * factor - targets.astype(jnp.float32)).astype(jnp.bfloat16)
    all_residual = lax.all_gather(residual, "fsdp", axis=0, tiled=True)
    gradient = (
        lax.dot_general(
            columns, all_residual, (((0,), (0,)), ((), ())), preferred_element_type=jnp.float32
        )
        * factor
    )
    squares = lax.psum(jnp.sum(gradient * gradient), "fsdp")
    grad_scale = jnp.sqrt(squares / (D * KV) + 1e-06)
    stepped = weight.astype(jnp.float32) - 0.25 * gradient / grad_scale
    summed = lax.psum(pending_delta[0].astype(jnp.float32), "rep")
    delta_mean = summed / replicas
    new_momentum = 0.9 * outer_momentum + delta_mean
    new_global = (global_frag.astype(jnp.float32) - 0.7 * (delta_mean + 0.9 * new_momentum)).astype(
        jnp.bfloat16
    )
    merged = merge_fragment(stepped, new_global, frag_order)
    return (merged[None], new_global, new_momentum)


def solution(mesh):
    placed = (
        P(("rep", "fsdp"), None),
        P(("rep", "fsdp"), None),
        P("rep", "fsdp", None),
        P("rep", "fsdp", None),
        P(),
        P("fsdp", None),
        P("fsdp", None),
    )
    return jax.shard_map(
        body,
        mesh=mesh,
        in_specs=placed,
        out_specs=(P("rep", "fsdp", None), P("fsdp", None), P("fsdp", None)),
        check_vma=False,
    )
```

profile of v0, /device:TPU:6, one launch (start us, length us, event | category | flops | bytes accessed | tf_op | source)
XLA Modules:
  0.0 737.5 jit_solution(17602497017707384011)
XLA Ops:
  8.0 0.0 copy-start.1
  8.0 0.0 all-gather.6.cloned.1.call-start
  8.1 0.7 all-gather.6.cloned.1.call-update
  8.7 0.0 all-reduce.2.cloned.1.call-start
  8.8 1.8 bitcast_convert_fusion
  10.6 0.0 all-reduce.2.cloned.1.call-update
  10.6 0.0 all-gather.4.cloned.1.call-start
  10.6 0.0 copy-done.1
  10.7 0.7 copy.10
  11.3 0.0 copy-start.4
  11.3 0.6 fusion.2
  11.9 1.2 fusion.3
  13.1 180.6 %all-gather.6.cloned.1.call-done = bf16[1,4096,1024]{2,1,0:T(8,128)(2,1)} async-done(((bf16[1,512,1024]{2,1,0:T(8,128)(2,1)}), bf16[1,4096,1024]{2,1,0:T(8,128)(2,1)}) %all-gather.6.cloned.1.call-update) | async-done | bytes 8388624 | tf_op jit(solution)/shard_map/all_gather | solution.py:40
  193.7 0.0 copy-done.4
  193.7 5.7 fusion.10
  199.4 0.0 copy-start.6
  199.4 0.0 copy-start.3
  199.4 0.0 copy-start.5
  199.4 0.0 all-gather.4.cloned.1.call-update
  199.4 4.7 all-to-all-start
  204.1 0.0 copy-done.6
  204.1 0.6 fusion.13
  206.0 486.1 %all-reduce.2.cloned.1.call-done = f32[512,256]{1,0:T(8,128)} async-done(((f32[512,256]{1,0:T(8,128)}), f32[512,256]{1,0:T(8,128)}) %all-reduce.2.cloned.1.call-update) | async-done | bytes 524304 | tf_op jit(solution)/shard_map/psum | solution.py:54
  692.1 0.0 copy-done.3
  692.1 0.0 copy-done.5
  692.1 2.0 subtract_convert_fusion
  694.1 0.0 copy-start.2
  694.1 0.0 all-to-all-done
  694.1 1.3 copy.11
  695.4 0.0 all-gather.4.cloned.1.call-done
  695.4 0.0 copy-start
  695.4 4.2 multiply_reduce_fusion
  699.6 28.1 %psum.14 = f32[]{:T(128)} all-reduce(f32[]{:T(128)} %get-tuple-element.7), channel_id=1, replica_groups=mesh['rep'=64,'fsdp'=8] {'fsdp'}, use_global_device_ids=true, to_apply=%region_2.0 | all-reduce | flops 1 | bytes 8 | tf_op jit(solution)/shard_map/psum | solution.py:51
  728.4 0.0 copy-done
  728.4 0.4 convert_subtract_fusion
  728.7 0.1 multiply_dynamic-update-slice_fusion.1
  728.8 0.0 copy-done.2
  728.8 0.1 multiply_dynamic-update-slice_fusion
  728.9 1.1 convert_bitcast_fusion
  (1 shorter events, 0.0 us)
Async XLA Ops:
  8.0 2.7 copy-start.1
  8.0 185.7 %all-gather.6.cloned.1.call-start = ((), (), s32[]{:S(2)}) async-start(), calls=%async_computation.3 | async-start | bytes 9437184 | tf_op jit(solution)/shard_map/all_gather | solution.py:40
  8.7 683.4 %all-reduce.2.cloned.1.call-start = ((), (), s32[]{:S(2)}) async-start(), calls=%async_computation.2 | async-start | bytes 1048576 | tf_op jit(solution)/shard_map/psum | solution.py:54
  10.6 684.8 %all-gather.4.cloned.1.call-start = ((), (), s32[]{:S(2)}) async-start(), calls=%async_computation.1 | async-start | bytes 2359296 | tf_op jit(solution)/shard_map/all_gather | solution.py:44
  11.3 182.4 %copy-start.4 = (bf16[128,1024]{1,0:T(8,128)(2,1)S(1)}, bf16[128,1024]{1,0:T(8,128)(2,1)}, u32[]{:S(2)}) copy-start(bf16[128,1024]{1,0:T(8,128)(2,1)} %param.8) | copy-start | bytes 786436
  199.4 4.7 copy-start.6
  199.4 492.7 %copy-start.3 = (f32[512,256]{1,0:T(8,128)S(1)}, f32[512,256]{1,0:T(8,128)}, u32[]{:S(2)}) copy-start(f32[512,256]{1,0:T(8,128)} %param.13) | copy-start | bytes 1572868
  199.4 492.7 %copy-start.5 = (bf16[512,256]{1,0:T(8,128)(2,1)S(1)}, bf16[512,256]{1,0:T(8,128)(2,1)}, u32[]{:S(2)}) copy-start(bf16[512,256]{1,0:T(8,128)(2,1)} %param.12) | copy-start | bytes 786436
  199.4 494.6 %all-to-all-start = ((bf16[128,8,512]{0,2,1:T(8,128)(2,1)}), bf16[128,8,512]{0,2,1:T(8,128)(2,1)S(1)}, u32[]{:S(2)}, u32[]{:S(2)}) async-start(bf16[128,8,512]{0,2,1:T(8,128)(2,1)} %bitcast.1), calls=%async_computation | async-start | bytes 2097152 | tf_op jit(solution)/shard_map/all_to_all | solution.py:37
  694.1 34.7 %copy-start.2 = (bf16[512,256]{1,0:T(8,128)(2,1)}, bf16[512,256]{1,0:T(8,128)(2,1)S(1)}, u32[]{:S(2)}) copy-start(bf16[512,256]{1,0:T(8,128)(2,1)S(1)} %get-tuple-element.3) | copy-start | bytes 786436
  695.4 33.0 %copy-start = (bf16[1,512,1024]{2,1,0:T(8,128)(2,1)S(1)}, bf16[1,512,1024]{2,1,0:T(8,128)(2,1)}, u32[]{:S(2)}) copy-start(bf16[1,512,1024]{2,1,0:T(8,128)(2,1)} %param.9) | copy-start | bytes 3145732
Sparse Core Ops, SparseCore 0:
  12.1 181.5 all-gather.5
  199.6 85.5 all-gather.3
Sparse Core Ops, SparseCore 1:
  12.7 679.4 all-reduce.1
where the time goes:
time: 739 us; the launch traced here: 737 us
  waiting for transfers between devices  667 us (90%)
  blocking collectives  28.1 us (4%)
  between operations  17.5 us (2%)
  matrix products  9.93 us (1%)
    psum x1, waiting for transfers between devices, body(): summed = lax.psum(pending_delta[0].astype(jnp.float32), 'rep')  486 us
    all_gather x1, waiting for transfers between devices, body(): lax.all_gather(weight, 'fsdp', axis=0, tiled=True)  181 us
    psum x1, blocking collectives, body(): squares = lax.psum(jnp.sum(gradient * gradient), 'fsdp')  28.1 us
  transfers between devices with their start and end apart: 4, of which 2 were waited for; matrix products, arithmetic and copies ran while one was open for 2% of the time, Pallas kernels for 0%

commit v1 on v0

v1 whole, which is shorter than its diff:
```python
import math

import jax
import jax.numpy as jnp
from jax import lax
from jax.sharding import PartitionSpec as P

D = 4096
HEAD = 128
FRAG_HEADS = 2
KV = 1024
NX = 4
COLS = KV // NX
F32 = jnp.float32
BF16 = jnp.bfloat16

X_GROUPS = [[x * 2 + h for x in range(NX)] for h in range(2)]
Z_GROUPS = [[z * 8 + l for z in range(8)] for l in range(8)]
L_GROUPS = [[z * 8 + l for l in range(8)] for z in range(8)]
SWAP = [(i, i ^ 1) for i in range(8)]


def exchange(blocks, axis, groups):
    return lax.all_to_all(blocks, axis, 0, 0, axis_index_groups=groups, tiled=True)


def share(block, axis, groups):
    count = len(groups[0]) if groups else 8
    return exchange(jnp.broadcast_to(block[None], (count, *block.shape)), axis, groups)


def swap(block):
    return lax.ppermute(block, "fsdp", SWAP)


def sum_over_rep(delta):
    by_z = exchange(delta.reshape(8, 64, 256), "rep", Z_GROUPS)
    part = jnp.sum(by_z.astype(F32), axis=0)
    by_l = exchange(part.reshape(8, 8, 256), "rep", L_GROUPS)
    total = jnp.sum(by_l, axis=0)
    rows = share(total, "rep", L_GROUPS).reshape(64, 256)
    return share(rows, "rep", Z_GROUPS).reshape(512, 256)


def body(tokens, targets, local_weights, pending_delta, frag_order, global_frag, outer_momentum):
    factor = 1.0 / math.sqrt(D)
    half = lax.axis_index("fsdp") % 2
    weight = local_weights[0]

    with jax.named_scope("weight_columns"):
        rows = jnp.concatenate([weight, targets], axis=0)
        blocks = rows.reshape(640, NX, COLS).transpose(1, 0, 2)
        columns = exchange(blocks, "fsdp", X_GROUPS)
        my_weight = columns[:, :512].reshape(2048, COLS)
        my_targets = columns[:, 512:].reshape(512, COLS)

    with jax.named_scope("normalize"):
        floated = tokens.astype(F32)
        scale = lax.rsqrt(jnp.mean(floated * floated, axis=-1, keepdims=True) + 1e-06)
        normed = (floated * scale).astype(BF16).reshape(128, NX, 2, 512)
        mine = lax.dynamic_index_in_dim(normed, half, 2, keepdims=False).reshape(128, 2048)
        other = lax.dynamic_index_in_dim(normed, 1 - half, 2, keepdims=False).reshape(128, 2048)

    with jax.named_scope("activations"):
        arrived = swap(other)
        near = share(mine, "fsdp", X_GROUPS).reshape(512, 2048)
        far = share(arrived, "fsdp", X_GROUPS).reshape(512, 2048)

    with jax.named_scope("keys"):
        near_keys = jnp.dot(near, my_weight, preferred_element_type=F32) * factor
        near_part = near_keys - my_targets.astype(F32)
        far_rest = swap(near_part.astype(BF16))
        far_keys = jnp.dot(far, my_weight, preferred_element_type=F32) * factor
        near_rest = swap(far_keys.astype(BF16))
        far_residual = (far_keys + far_rest.astype(F32)).astype(BF16)
        near_residual = (near_part + near_rest.astype(F32)).astype(BF16)

    with jax.named_scope("gradient"):
        dims = (((0,), (0,)), ((), ()))
        gradient = (
            lax.dot_general(far, far_residual, dims, preferred_element_type=F32)
            + lax.dot_general(near, near_residual, dims, preferred_element_type=F32)
        ) * factor
        squares = jnp.sum(gradient * gradient)
        everyone = share(jnp.full((8, 128), squares, F32), "fsdp", None)
        total = jnp.sum(everyone[:, 0, 0])
        grad_scale = jnp.sqrt(total / (D * KV) + 1e-06)
        by_rows = exchange(gradient.astype(BF16).reshape(NX, 512, COLS), "fsdp", X_GROUPS)

    with jax.named_scope("outer"):
        delta_mean = sum_over_rep(pending_delta[0]) / lax.axis_size("rep")
        new_momentum = 0.9 * outer_momentum + delta_mean
        new_global = (
            global_frag.astype(F32) - 0.7 * (delta_mean + 0.9 * new_momentum)
        ).astype(BF16)

    with jax.named_scope("step"):
        row_gradient = by_rows.transpose(1, 0, 2).reshape(512, KV).astype(F32)
        merged = weight.astype(F32) - row_gradient * (0.25 / grad_scale)
        for slot in range(FRAG_HEADS):
            column = frag_order[slot] * HEAD
            current = lax.dynamic_slice(merged, (0, column), (512, HEAD))
            incoming = new_global[:, slot * HEAD : (slot + 1) * HEAD].astype(F32)
            merged = lax.dynamic_update_slice(
                merged, 0.5 * current + 0.5 * incoming, (0, column)
            )
        merged = merged.astype(BF16)
    return (merged[None], new_global, new_momentum)


def solution(mesh):
    placed = (
        P(("rep", "fsdp"), None),
        P(("rep", "fsdp"), None),
        P("rep", "fsdp", None),
        P("rep", "fsdp", None),
        P(),
        P("fsdp", None),
        P("fsdp", None),
    )
    return jax.shard_map(
        body,
        mesh=mesh,
        in_specs=placed,
        out_specs=(P("rep", "fsdp", None), P("fsdp", None), P("fsdp", None)),
        check_vma=False,
    )
```

time: 739 us -> 201 us (0.27)
  waiting for transfers between devices: 667 us -> 86.2 us
  starting transfers between devices: 4.78 us -> 63.7 us
  between operations: 17.5 us -> 2.95 us
  blocking collectives: 28.1 us -> 17.9 us
  local copies, waits for them, and re-layouts: 2.58 us -> 10.5 us
    psum x1 -> x0, waiting for transfers between devices: 486 us -> none  [body(): summed = lax.psum(pending_delta[0].astype(jnp.float32), 'rep')]
    all_gather x2 -> x0, waiting for transfers between devices: 181 us -> none  [the longest x1 181 us: body(): lax.all_gather(weight, 'fsdp', axis=0, tiled=True)]
    all_to_all x1 -> x8, waiting for transfers between devices: 0.01 us -> 58.7 us  [exchange(): lax.all_to_all(blocks, axis, 0, 0, axis_index_groups=groups, tiled=True)]
    all_to_all x1 -> x8, starting transfers between devices: 4.65 us -> 43 us  [exchange(): lax.all_to_all(blocks, axis, 0, 0, axis_index_groups=groups, tiled=True)]
    psum x1 -> x0, blocking collectives: 28.1 us -> none  [body(): squares = lax.psum(jnp.sum(gradient * gradient), 'fsdp')]
    ppermute x0 -> x3, waiting for transfers between devices: none -> 27.5 us  [swap(): return lax.ppermute(block, 'fsdp', SWAP)]
    ppermute x0 -> x3, starting transfers between devices: none -> 20.8 us  [swap(): return lax.ppermute(block, 'fsdp', SWAP)]
    all_to_all x0 -> x1, blocking collectives: none -> 17.9 us  [exchange(): lax.all_to_all(blocks, axis, 0, 0, axis_index_groups=groups, tiled=True)]
  transfers between devices with their start and end apart: 4 -> 11, of which waited for: 2 -> 8; matrix products, arithmetic and copies ran while one was open for 2% -> 9% of each run, Pallas kernels for 0% -> 0%
where the time goes in v1:
time: 201 us; the launch traced here: 198 us
  waiting for transfers between devices  86.2 us (43%)
  starting transfers between devices  63.7 us (32%)
  blocking collectives  17.9 us (9%)
  local copies, waits for them, and re-layouts  10.5 us (5%)
  matrix products  10.2 us (5%)
  other arithmetic  7.04 us (4%)
  between operations  2.95 us (1%)
    all_to_all x8, waiting for transfers between devices, exchange(): lax.all_to_all(blocks, axis, 0, 0, axis_index_groups=groups, tiled=True)  58.7 us
    all_to_all x8, starting transfers between devices, exchange(): lax.all_to_all(blocks, axis, 0, 0, axis_index_groups=groups, tiled=True)  43 us
    ppermute x3, waiting for transfers between devices, swap(): return lax.ppermute(block, 'fsdp', SWAP)  27.5 us
    ppermute x3, starting transfers between devices, swap(): return lax.ppermute(block, 'fsdp', SWAP)  20.8 us
    all_to_all x1, blocking collectives, exchange(): lax.all_to_all(blocks, axis, 0, 0, axis_index_groups=groups, tiled=True)  17.9 us
    broadcast_in_dim x6, local copies, waits for them, and re-layouts, share(): jnp.broadcast_to(block[None], (count, *block.shape))  5.72 us
  transfers between devices with their start and end apart: 11, of which 8 were waited for; matrix products, arithmetic and copies ran while one was open for 9% of the time, Pallas kernels for 0%

profile of v1, /device:TPU:6, one launch (start us, length us, event | category | flops | bytes accessed | tf_op | source)
XLA Modules:
  0.0 198.5 jit_solution(8209242408496040284)
XLA Ops:
  0.7 10.5 %all-to-all-start.5 = ((bf16[8,64,256]{2,1,0:T(8,128)(2,1)}), bf16[8,64,256]{2,1,0:T(8,128)(2,1)}, u32[]{:S(2)}, u32[]{:S(2)}) async-start(bf16[8,64,256]{2,1,0:T(8,128)(2,1)} %bitcast.57), calls=%async_computation.5 | async-start | bytes 524288 | tf_op jit(solution)/shard_map/outer/all_to_all | solution.py:24
  11.1 1.6 copy.30
  12.8 0.8 concatenate.8
  13.6 0.1 copy.32
  13.7 0.6 fusion.1
  14.3 8.8 %all-to-all-done.5 = bf16[8,64,256]{2,1,0:T(8,128)(2,1)} async-done(((bf16[8,64,256]{2,1,0:T(8,128)(2,1)}), bf16[8,64,256]{2,1,0:T(8,128)(2,1)}, u32[]{:S(2)}, u32[]{:S(2)}) %all-to-all-start.5) | async-done | bytes 262176 | tf_op jit(solution)/shard_map/outer/all_to_all | solution.py:24
  23.1 1.6 convert_reduce_fusion
  24.7 4.9 %all-to-all-start.6 = ((f32[8,8,256]{2,1,0:T(8,128)}), f32[8,8,256]{2,1,0:T(8,128)S(1)}, u32[]{:S(2)}, u32[]{:S(2)}) async-start(f32[8,8,256]{2,1,0:T(8,128)} %bitcast.13), calls=%async_computation.6 | async-start | bytes 131072 | tf_op jit(solution)/shard_map/outer/all_to_all | solution.py:24
  29.6 5.9 %all-to-all-done.6 = f32[8,8,256]{2,1,0:T(8,128)S(1)} async-done(((f32[8,8,256]{2,1,0:T(8,128)}), f32[8,8,256]{2,1,0:T(8,128)S(1)}, u32[]{:S(2)}, u32[]{:S(2)}) %all-to-all-start.6) | async-done | bytes 65568 | tf_op jit(solution)/shard_map/outer/all_to_all | solution.py:24
  35.5 0.6 broadcast_in_dim.37
  36.2 3.4 %all-to-all-start.7 = ((f32[8,8,256]{2,1,0:T(8,128)}), f32[8,8,256]{2,1,0:T(8,128)S(1)}, u32[]{:S(2)}, u32[]{:S(2)}) async-start(f32[8,8,256]{2,1,0:T(8,128)} %broadcast_in_dim.37), calls=%async_computation.7 | async-start | bytes 131072 | tf_op jit(solution)/shard_map/outer/all_to_all | solution.py:24
  39.5 1.2 maximum_bitcast_fusion
  40.7 4.7 %all-to-all-done.7 = f32[8,8,256]{2,1,0:T(8,128)S(1)} async-done(((f32[8,8,256]{2,1,0:T(8,128)}), f32[8,8,256]{2,1,0:T(8,128)S(1)}, u32[]{:S(2)}, u32[]{:S(2)}) %all-to-all-start.7) | async-done | bytes 65568 | tf_op jit(solution)/shard_map/outer/all_to_all | solution.py:24
  45.4 4.8 %all-to-all-start.1 = ((bf16[4,640,256]{2,1,0:T(8,128)(2,1)}), bf16[4,640,256]{2,1,0:T(8,128)(2,1)S(1)}, u32[]{:S(2)}, u32[]{:S(2)}) async-start(bf16[4,640,256]{2,1,0:T(8,128)(2,1)} %maximum_bitcast_fusion), calls=%async_computation.1 | async-start | bytes 2621440 | tf_op jit(solution)/shard_map/weight_columns/all_to_all | solution.py:24
  50.1 0.2 fusion.2
  50.4 0.1 constant_dynamic-slice_fusion.1
  50.5 6.1 %collective-permute-start = (bf16[128,2048]{0,1:T(8,128)(2,1)S(1)}, bf16[128,2048]{0,1:T(8,128)(2,1)S(1)}, u32[]{:S(2)}, u32[]{:S(2)}) collective-permute-start(bf16[128,2048]{0,1:T(8,128)(2,1)S(1)} %bitcast.54), channel_id=1, source_target_pairs={{0,1},{1,0},{2,3},{3,2},{4,5},{5,4},{6,7},{7,6},{8,9},{9,8},{10,11... | collective-permute-start | bytes 1572872 | tf_op jit(solution)/shard_map/activations/ppermute | solution.py:33
  56.6 23.9 %collective-permute-done = bf16[128,2048]{0,1:T(8,128)(2,1)S(1)} collective-permute-done((bf16[128,2048]{0,1:T(8,128)(2,1)S(1)}, bf16[128,2048]{0,1:T(8,128)(2,1)S(1)}, u32[]{:S(2)}, u32[]{:S(2)}) %collective-permute-start) | collective-permute-done | bytes 524320 | tf_op jit(solution)/shard_map/activations/ppermute | solution.py:33
  80.6 0.2 copy.31
  80.8 1.7 broadcast_in_dim.16
  82.5 4.8 %all-to-all-start = ((bf16[4,128,2048]{2,1,0:T(8,128)(2,1)}), bf16[4,128,2048]{2,1,0:T(8,128)(2,1)}, u32[]{:S(2)}, u32[]{:S(2)}) async-start(bf16[4,128,2048]{2,1,0:T(8,128)(2,1)} %broadcast_in_dim.16), calls=%async_computation | async-start | bytes 4194304 | tf_op jit(solution)/shard_map/activations/all_to_all | solution.py:24
  87.3 0.2 copy.34
  87.5 22.9 %all-to-all-done = bf16[4,128,2048]{2,1,0:T(8,128)(2,1)} async-done(((bf16[4,128,2048]{2,1,0:T(8,128)(2,1)}), bf16[4,128,2048]{2,1,0:T(8,128)(2,1)}, u32[]{:S(2)}, u32[]{:S(2)}) %all-to-all-start) | async-done | bytes 2097184 | tf_op jit(solution)/shard_map/activations/all_to_all | solution.py:24
  110.4 1.6 broadcast_in_dim.35
  112.0 5.6 %all-to-all-start.2 = ((bf16[4,128,2048]{2,1,0:T(8,128)(2,1)}), bf16[4,128,2048]{2,1,0:T(8,128)(2,1)S(1)}, u32[]{:S(2)}, u32[]{:S(2)}) async-start(bf16[4,128,2048]{2,1,0:T(8,128)(2,1)} %broadcast_in_dim.35), calls=%async_computation.2 | async-start | bytes 4194304 | tf_op jit(solution)/shard_map/activations/all_to_all | solution.py:24
  117.8 3.5 %fusion.9 = (bf16[512,256]{1,0:T(8,128)(2,1)S(1)}, f32[512,256]{1,0:T(8,128)}) fusion(bf16[512,2048]{1,0:T(8,128)(2,1)} %bitcast.3, bf16[2048,256]{1,0:T(8,128)(2,1)S(1)} %bitcast.52), kind=kOutput, calls=%fused_computation.32 | convolution fusion | flops 537133056 | bytes 3932160 | tf_op jit(solution)/shard_map/keys/dot_general | solution.py:73
  121.3 6.7 %collective-permute-start.2 = (bf16[512,256]{1,0:T(8,128)(2,1)S(1)}, bf16[512,256]{1,0:T(8,128)(2,1)S(1)}, u32[]{:S(2)}, u32[]{:S(2)}) collective-permute-start(bf16[512,256]{1,0:T(8,128)(2,1)S(1)} %get-tuple-element.11), channel_id=1, source_target_pairs={{0,1},{1,0},{2,3},{3,2},{4,5},{5,4},{6,7},{7,6},{8,9},{9,8},{10,11... | collective-permute-start | bytes 786440 | tf_op jit(solution)/shard_map/keys/ppermute | solution.py:33
  128.0 11.8 %all-to-all-done.2 = bf16[4,128,2048]{2,1,0:T(8,128)(2,1)S(1)} async-done(((bf16[4,128,2048]{2,1,0:T(8,128)(2,1)}), bf16[4,128,2048]{2,1,0:T(8,128)(2,1)S(1)}, u32[]{:S(2)}, u32[]{:S(2)}) %all-to-all-start.2) | async-done | bytes 2097184 | tf_op jit(solution)/shard_map/activations/all_to_all | solution.py:24
  139.8 0.8 broadcast_in_dim.39
  140.6 3.5 %all-to-all-start.8 = ((f32[8,64,256]{2,1,0:T(8,128)}), f32[8,64,256]{2,1,0:T(8,128)S(1)}, u32[]{:S(2)}, u32[]{:S(2)}) async-start(f32[8,64,256]{2,1,0:T(8,128)} %broadcast_in_dim.39), calls=%async_computation.8 | async-start | bytes 1048576 | tf_op jit(solution)/shard_map/outer/all_to_all | solution.py:24
  144.1 1.9 fusion.10
  146.0 7.9 %collective-permute-start.1 = (bf16[512,256]{1,0:T(8,128)(2,1)S(1)}, bf16[512,256]{1,0:T(8,128)(2,1)S(1)}, u32[]{:S(2)}, u32[]{:S(2)}) collective-permute-start(bf16[512,256]{1,0:T(8,128)(2,1)S(1)} %get-tuple-element.13), channel_id=1, source_target_pairs={{0,1},{1,0},{2,3},{3,2},{4,5},{5,4},{6,7},{7,6},{8,9},{9,8},{10,11... | collective-permute-start | bytes 786440 | tf_op jit(solution)/shard_map/keys/ppermute | solution.py:33
  154.0 0.8 fusion.7
  154.8 3.6 %collective-permute-done.1 = bf16[512,256]{1,0:T(8,128)(2,1)S(1)} collective-permute-done((bf16[512,256]{1,0:T(8,128)(2,1)S(1)}, bf16[512,256]{1,0:T(8,128)(2,1)S(1)}, u32[]{:S(2)}, u32[]{:S(2)}) %collective-permute-start.1) | collective-permute-done | bytes 262176 | tf_op jit(solution)/shard_map/keys/ppermute | solution.py:33
  158.3 4.0 %multiply_reduce_fusion = (f32[]{:T(128)}, bf16[2048,256]{1,0:T(8,128)(2,1)}) fusion(f32[2048,256]{1,0:T(8,128)S(1)} %fusion.7, bf16[512,2048]{1,0:T(8,128)(2,1)} %bitcast.3, f32[512,256]{1,0:T(8,128)S(1)} %copy-done.9, bf16[512,256]{1,0:T(8,128)(2,1)S(1)} %collective-permute-done.1), kind=kOutput, calls=%fused_computation.8 | convolution fusion | flops 539885568 | bytes 6029316 | tf_op jit(solution)/shard_map/gradient/dot_general | solution.py:81
  162.3 0.7 broadcast_in_dim.36
  163.1 17.9 %all_to_all.45 = f32[8,8,128]{2,1,0:T(8,128)S(1)} all-to-all(f32[8,8,128]{2,1,0:T(8,128)S(1)} %broadcast_in_dim.36), channel_id=1, replica_groups=mesh['rep'=64,'fsdp'=8] {'fsdp'}, dimensions={0} | all-to-all | bytes 65536 | tf_op jit(solution)/shard_map/gradient/all_to_all | solution.py:24
  180.9 5.6 %all-to-all-start.3 = ((bf16[4,512,256]{2,1,0:T(8,128)(2,1)}), bf16[4,512,256]{2,1,0:T(8,128)(2,1)S(1)}, u32[]{:S(2)}, u32[]{:S(2)}) async-start(bf16[4,512,256]{2,1,0:T(8,128)(2,1)} %bitcast.9), calls=%async_computation.3 | async-start | bytes 2097152 | tf_op jit(solution)/shard_map/gradient/all_to_all | solution.py:24
  186.5 0.6 fusion.8
  188.5 0.9 fusion.6
  189.4 0.6 slice_reduce_fusion
  190.7 4.6 %all-to-all-done.3 = bf16[4,512,256]{2,1,0:T(8,128)(2,1)S(1)} async-done(((bf16[4,512,256]{2,1,0:T(8,128)(2,1)}), bf16[4,512,256]{2,1,0:T(8,128)(2,1)S(1)}, u32[]{:S(2)}, u32[]{:S(2)}) %all-to-all-start.3) | async-done | bytes 1048608 | tf_op jit(solution)/shard_map/gradient/all_to_all | solution.py:24
  195.3 0.2 multiply_bitcast_fusion
  195.5 0.2 copy.39
  195.8 1.0 copy-done.2
  196.7 0.4 convert_subtract_fusion
  197.2 0.1 multiply_dynamic-update-slice_fusion.1
  197.3 1.1 convert_bitcast_fusion
  (30 shorter events, 0.3 us)
Async XLA Ops:
  0.6 12.1 %copy-start.6 = (bf16[128,1024]{1,0:T(8,128)(2,1)S(1)}, bf16[128,1024]{1,0:T(8,128)(2,1)}, u32[]{:S(2)}) copy-start(bf16[128,1024]{1,0:T(8,128)(2,1)} %param.8) | copy-start | bytes 786436
  0.6 12.1 %copy-start.1 = (bf16[1,512,1024]{2,1,0:T(8,128)(2,1)S(1)}, bf16[1,512,1024]{2,1,0:T(8,128)(2,1)}, u32[]{:S(2)}) copy-start(bf16[1,512,1024]{2,1,0:T(8,128)(2,1)} %param.9) | copy-start | bytes 3145732
  0.7 22.4 %all-to-all-start.5 = ((bf16[8,64,256]{2,1,0:T(8,128)(2,1)}), bf16[8,64,256]{2,1,0:T(8,128)(2,1)}, u32[]{:S(2)}, u32[]{:S(2)}) async-start(bf16[8,64,256]{2,1,0:T(8,128)(2,1)} %bitcast.57), calls=%async_computation.5 | async-start | bytes 524288 | tf_op jit(solution)/shard_map/outer/all_to_all | solution.py:24
  24.7 10.8 %all-to-all-start.6 = ((f32[8,8,256]{2,1,0:T(8,128)}), f32[8,8,256]{2,1,0:T(8,128)S(1)}, u32[]{:S(2)}, u32[]{:S(2)}) async-start(f32[8,8,256]{2,1,0:T(8,128)} %bitcast.13), calls=%async_computation.6 | async-start | bytes 131072 | tf_op jit(solution)/shard_map/outer/all_to_all | solution.py:24
  36.2 9.2 %all-to-all-start.7 = ((f32[8,8,256]{2,1,0:T(8,128)}), f32[8,8,256]{2,1,0:T(8,128)S(1)}, u32[]{:S(2)}, u32[]{:S(2)}) async-start(f32[8,8,256]{2,1,0:T(8,128)} %broadcast_in_dim.37), calls=%async_computation.7 | async-start | bytes 131072 | tf_op jit(solution)/shard_map/outer/all_to_all | solution.py:24
  45.4 35.4 %all-to-all-start.1 = ((bf16[4,640,256]{2,1,0:T(8,128)(2,1)}), bf16[4,640,256]{2,1,0:T(8,128)(2,1)S(1)}, u32[]{:S(2)}, u32[]{:S(2)}) async-start(bf16[4,640,256]{2,1,0:T(8,128)(2,1)} %maximum_bitcast_fusion), calls=%async_computation.1 | async-start | bytes 2621440 | tf_op jit(solution)/shard_map/weight_columns/all_to_all | solution.py:24
  50.5 30.1 %collective-permute-start = (bf16[128,2048]{0,1:T(8,128)(2,1)S(1)}, bf16[128,2048]{0,1:T(8,128)(2,1)S(1)}, u32[]{:S(2)}, u32[]{:S(2)}) collective-permute-start(bf16[128,2048]{0,1:T(8,128)(2,1)S(1)} %bitcast.54), channel_id=1, source_target_pairs={{0,1},{1,0},{2,3},{3,2},{4,5},{5,4},{6,7},{7,6},{8,9},{9,8},{10,11... | collective-permute-start | bytes 1572872 | tf_op jit(solution)/shard_map/activations/ppermute | solution.py:33
  80.8 36.9 %copy-start = (bf16[4,640,256]{2,1,0:T(8,128)(2,1)}, bf16[4,640,256]{2,1,0:T(8,128)(2,1)S(1)}, u32[]{:S(2)}) copy-start(bf16[4,640,256]{2,1,0:T(8,128)(2,1)S(1)} %all-to-all-done.1) | copy-start | bytes 3932164
  82.5 27.9 %all-to-all-start = ((bf16[4,128,2048]{2,1,0:T(8,128)(2,1)}), bf16[4,128,2048]{2,1,0:T(8,128)(2,1)}, u32[]{:S(2)}, u32[]{:S(2)}) async-start(bf16[4,128,2048]{2,1,0:T(8,128)(2,1)} %broadcast_in_dim.16), calls=%async_computation | async-start | bytes 4194304 | tf_op jit(solution)/shard_map/activations/all_to_all | solution.py:24
  112.0 27.7 %all-to-all-start.2 = ((bf16[4,128,2048]{2,1,0:T(8,128)(2,1)}), bf16[4,128,2048]{2,1,0:T(8,128)(2,1)S(1)}, u32[]{:S(2)}, u32[]{:S(2)}) async-start(bf16[4,128,2048]{2,1,0:T(8,128)(2,1)} %broadcast_in_dim.35), calls=%async_computation.2 | async-start | bytes 4194304 | tf_op jit(solution)/shard_map/activations/all_to_all | solution.py:24
  117.7 3.5 %copy-start.3 = (bf16[4,512,256]{2,1,0:T(8,128)(2,1)}, bf16[4,512,256]{2,1,0:T(8,128)(2,1)S(1)}, u32[]{:S(2)}) copy-start(bf16[4,512,256]{2,1,0:T(8,128)(2,1)S(1)} %slice.28) | copy-start | bytes 3145732
  117.8 26.3 %slice-start = ((bf16[4,640,256]{2,1,0:T(8,128)(2,1)}), bf16[4,128,256]{2,1,0:T(8,128)(2,1)S(1)}, s32[]{:S(2)}) async-start(bf16[4,640,256]{2,1,0:T(8,128)(2,1)} %copy-done), calls=%async_computation.9 | async-start | bytes 524288 | tf_op jit(solution)/shard_map/weight_columns/slice | solution.py:55
  121.3 32.7 %collective-permute-start.2 = (bf16[512,256]{1,0:T(8,128)(2,1)S(1)}, bf16[512,256]{1,0:T(8,128)(2,1)S(1)}, u32[]{:S(2)}, u32[]{:S(2)}) collective-permute-start(bf16[512,256]{1,0:T(8,128)(2,1)S(1)} %get-tuple-element.11), channel_id=1, source_target_pairs={{0,1},{1,0},{2,3},{3,2},{4,5},{5,4},{6,7},{7,6},{8,9},{9,8},{10,11... | collective-permute-start | bytes 786440 | tf_op jit(solution)/shard_map/keys/ppermute | solution.py:33
  140.6 21.8 %all-to-all-start.8 = ((f32[8,64,256]{2,1,0:T(8,128)}), f32[8,64,256]{2,1,0:T(8,128)S(1)}, u32[]{:S(2)}, u32[]{:S(2)}) async-start(f32[8,64,256]{2,1,0:T(8,128)} %broadcast_in_dim.39), calls=%async_computation.8 | async-start | bytes 1048576 | tf_op jit(solution)/shard_map/outer/all_to_all | solution.py:24
  146.0 12.3 %collective-permute-start.1 = (bf16[512,256]{1,0:T(8,128)(2,1)S(1)}, bf16[512,256]{1,0:T(8,128)(2,1)S(1)}, u32[]{:S(2)}, u32[]{:S(2)}) collective-permute-start(bf16[512,256]{1,0:T(8,128)(2,1)S(1)} %get-tuple-element.13), channel_id=1, source_target_pairs={{0,1},{1,0},{2,3},{3,2},{4,5},{5,4},{6,7},{7,6},{8,9},{9,8},{10,11... | collective-permute-start | bytes 786440 | tf_op jit(solution)/shard_map/keys/ppermute | solution.py:33
  154.0 4.3 %copy-start.9 = (f32[512,256]{1,0:T(8,128)S(1)}, f32[512,256]{1,0:T(8,128)}, u32[]{:S(2)}) copy-start(f32[512,256]{1,0:T(8,128)} %get-tuple-element.12) | copy-start | bytes 1572868
  162.3 24.2 %copy-start.8 = (s32[8]{0:T(128)S(1)}, s32[8]{0:T(128)}, u32[]{:S(2)}) copy-start(s32[8]{0:T(128)} %param.11) | copy-start | bytes 100
  162.3 26.1 %copy-start.5 = (f32[512,256]{1,0:T(8,128)S(1)}, f32[512,256]{1,0:T(8,128)}, u32[]{:S(2)}) copy-start(f32[512,256]{1,0:T(8,128)} %param.13) | copy-start | bytes 1572868
  162.3 26.1 %copy-start.7 = (bf16[512,256]{1,0:T(8,128)(2,1)S(1)}, bf16[512,256]{1,0:T(8,128)(2,1)}, u32[]{:S(2)}) copy-start(bf16[512,256]{1,0:T(8,128)(2,1)} %param.12) | copy-start | bytes 786436
  180.9 14.4 %all-to-all-start.3 = ((bf16[4,512,256]{2,1,0:T(8,128)(2,1)}), bf16[4,512,256]{2,1,0:T(8,128)(2,1)S(1)}, u32[]{:S(2)}, u32[]{:S(2)}) async-start(bf16[4,512,256]{2,1,0:T(8,128)(2,1)} %bitcast.9), calls=%async_computation.3 | async-start | bytes 2097152 | tf_op jit(solution)/shard_map/gradient/all_to_all | solution.py:24
  189.4 7.9 %copy-start.4 = (bf16[512,256]{1,0:T(8,128)(2,1)}, bf16[512,256]{1,0:T(8,128)(2,1)S(1)}, u32[]{:S(2)}) copy-start(bf16[512,256]{1,0:T(8,128)(2,1)S(1)} %get-tuple-element.3) | copy-start | bytes 786436
  195.5 1.2 copy-start.2

commit v2 on v0

v2 whole, which is shorter than its diff:
```python
import functools
import math

import jax
import jax.numpy as jnp
from jax import lax
from jax.experimental import pallas as pl
from jax.experimental.pallas import tpu as pltpu
from jax.sharding import PartitionSpec as P

D = 4096
HEAD = 128
FRAG_HEADS = 2
KV = 1024
NX = 4
COLS = KV // NX
FACTOR = 1.0 / math.sqrt(D)
F32 = jnp.float32
BF16 = jnp.bfloat16
SDS = jax.ShapeDtypeStruct
SMEM = pl.BlockSpec(memory_space=pltpu.SMEM)
PARAMS = pltpu.CompilerParams(vmem_limit_bytes=40 * 1024 * 1024)

X_GROUPS = [[x * 2 + h for x in range(NX)] for h in range(2)]
Z_GROUPS = [[z * 8 + l for z in range(8)] for l in range(8)]
L_GROUPS = [[z * 8 + l for l in range(8)] for z in range(8)]


def exchange(blocks, axis, groups):
    return lax.all_to_all(blocks, axis, 0, 0, axis_index_groups=groups, tiled=True)


def share(block, groups):
    return exchange(jnp.broadcast_to(block[None], (8, *block.shape)), "rep", groups)


def flip(block, mask):
    return lax.ppermute(block, "fsdp", [(i, i ^ mask) for i in range(8)])


def rotate(blocks):
    moves = [[(x * 2 + h, (x + d) % NX * 2 + h) for x in range(NX) for h in range(2)] for d in range(NX)]
    return [blocks[0]] + [lax.ppermute(blocks[d], "fsdp", moves[d]) for d in (1, 2, 3)]


def gather(block):
    return rotate([block] * NX)


def after(value, earlier):
    return lax.optimization_barrier((value, earlier))[0]


def split_kernel(half_ref, tokens_ref, mine_ref, other_ref):
    half = half_ref[0]
    floated = tokens_ref[...].astype(F32)
    scale = lax.rsqrt(jnp.mean(floated * floated, axis=-1, keepdims=True) + 1e-06)
    for x in range(NX):
        for ref, side in ((mine_ref, half), (other_ref, 1 - half)):
            start = pl.multiple_of((2 * x + side) * 512, 512)
            piece = tokens_ref[:, pl.ds(start, 512)].astype(F32) * scale
            ref[:, x * 512 : (x + 1) * 512] = piece.astype(BF16)


def split(half, tokens):
    return pl.pallas_call(
        split_kernel,
        grid=(4,),
        in_specs=[SMEM, pl.BlockSpec((32, D), lambda i: (i, 0))],
        out_specs=[pl.BlockSpec((32, D // 2), lambda i: (i, 0))] * 2,
        out_shape=[SDS((128, D // 2), BF16)] * 2,
        compiler_params=PARAMS,
        name="split",
    )(half, tokens)


def pack_kernel(weight_ref, targets_ref, out_ref):
    for x in range(NX):
        columns = slice(x * COLS, (x + 1) * COLS)
        out_ref[x, :512] = weight_ref[0, :, columns]
        out_ref[x, 512:] = targets_ref[:, columns]


def raw_keys(blocks, columns_ref):
    lhs = jnp.concatenate([b[...] for b in blocks], axis=0)
    weight = columns_ref[:, :512, :].reshape(2048, COLS)
    return jnp.dot(lhs, weight, preferred_element_type=F32) * FACTOR


def near_kernel(x_ref, b0, b1, b2, b3, columns_ref, part_ref, sent_ref):
    keys = raw_keys((b0, b1, b2, b3), columns_ref)
    for d in range(NX):
        rows = slice(d * 128, (d + 1) * 128)
        source = lax.rem(x_ref[0] - d + NX, NX)
        part = keys[rows] - columns_ref[source, 512:, :].astype(F32)
        part_ref[rows] = part
        sent_ref[rows] = part.astype(BF16)


def far_kernel(b0, b1, b2, b3, columns_ref, rest_ref, sent_ref, residual_ref):
    keys = raw_keys((b0, b1, b2, b3), columns_ref)
    sent_ref[...] = keys.astype(BF16)
    residual_ref[...] = (keys + rest_ref[...].astype(F32)).astype(BF16)


def turn_kernel(b0, b1, b2, b3, out_ref):
    for d, b in enumerate((b0, b1, b2, b3)):
        out_ref[:, d * 128 : (d + 1) * 128] = b[...].T


def far_gradient_kernel(turned_ref, residual_ref, out_ref):
    out_ref[...] = jnp.dot(turned_ref[...], residual_ref[...], preferred_element_type=F32)


def near_gradient_kernel(turned_ref, part_ref, rest_ref, far_ref, out_ref, squares_ref):
    residual = (part_ref[...] + rest_ref[...].astype(F32)).astype(BF16)
    squares = jnp.zeros((8, COLS), F32)
    for x in range(NX):
        rows = slice(x * 512, (x + 1) * 512)
        near = jnp.dot(turned_ref[rows], residual, preferred_element_type=F32)
        gradient = (near + far_ref[rows]) * FACTOR
        out_ref[x] = gradient.astype(BF16)
        squares += jnp.sum((gradient * gradient).reshape(64, 8, COLS), axis=0)
    squares_ref[...] = squares[:, :128] + squares[:, 128:]


def step_kernel(order_ref, squares_ref, rows_ref, weight_ref, global_ref, out_ref, new_ref):
    total = jnp.sum(squares_ref[...], axis=(0, 1), keepdims=True)
    rate = 0.25 * lax.rsqrt(total / (D * KV) + 1e-06)
    for x in range(NX):
        columns = slice(x * COLS, (x + 1) * COLS)
        weight = weight_ref[0, :, columns].astype(F32)
        new_ref[:, columns] = weight - rows_ref[x].astype(F32) * rate
    for slot in range(FRAG_HEADS):
        at = pl.ds(pl.multiple_of(order_ref[slot] * HEAD, HEAD), HEAD)
        incoming = global_ref[:, slot * HEAD : (slot + 1) * HEAD].astype(F32)
        new_ref[:, at] = 0.5 * new_ref[:, at] + 0.5 * incoming
    out_ref[0] = new_ref[...].astype(BF16)


def step(order, squares, rows, weight, new_global):
    return pl.pallas_call(
        step_kernel,
        grid=(4,),
        in_specs=[
            SMEM,
            pl.BlockSpec((8, 128), lambda i: (0, 0)),
            pl.BlockSpec((NX, 128, COLS), lambda i: (0, i, 0)),
            pl.BlockSpec((1, 128, KV), lambda i: (0, i, 0)),
            pl.BlockSpec((128, COLS), lambda i: (i, 0)),
        ],
        out_specs=pl.BlockSpec((1, 128, KV), lambda i: (0, i, 0)),
        out_shape=SDS((1, 512, KV), BF16),
        scratch_shapes=[pltpu.VMEM((128, KV), F32)],
        compiler_params=PARAMS,
        name="step",
    )(order, squares, rows, weight, new_global)


def call(kernel, outs, *args, scalars=0, flops=0):
    return pl.pallas_call(
        kernel,
        in_specs=[SMEM] * scalars + [pl.BlockSpec(memory_space=pltpu.VMEM)] * (len(args) - scalars),
        out_specs=jax.tree.map(lambda _: pl.BlockSpec(memory_space=pltpu.VMEM), outs),
        out_shape=outs,
        compiler_params=PARAMS,
        cost_estimate=pl.CostEstimate(flops=flops, bytes_accessed=4 << 20, transcendentals=0),
        name=kernel.__name__.removesuffix("_kernel"),
    )(*args)


def body(tokens, targets, local_weights, pending_delta, frag_order, global_frag, outer_momentum):
    place = lax.axis_index("fsdp")
    half = lax.rem(place, 2).astype(jnp.int32).reshape(1)
    my_x = lax.div(place, 2).astype(jnp.int32).reshape(1)
    dot_flops = 2 * 512 * 2048 * COLS

    with jax.named_scope("activations"):
        mine, other = split(half, tokens)
        arrived = flip(other, 1)
        near = gather(mine)

    with jax.named_scope("weight_columns"):
        blocks = call(pack_kernel, SDS((NX, 640, COLS), BF16), local_weights, targets)
        columns = exchange(blocks, "fsdp", X_GROUPS)

    with jax.named_scope("far_activations"):
        far = gather(arrived)

    with jax.named_scope("keys"):
        tall = (512, COLS)
        near_part, near_sent = call(
            near_kernel, (SDS(tall, F32), SDS(tall, BF16)), my_x, *near, columns, scalars=1, flops=dot_flops
        )
        far_rest = flip(near_sent, 1)
        near_turned = call(turn_kernel, SDS((2048, 512), BF16), *near)
        far_turned = call(turn_kernel, SDS((2048, 512), BF16), *far)
        far_sent, far_residual = call(
            far_kernel, (SDS(tall, BF16), SDS(tall, BF16)), *far, columns, far_rest, flops=dot_flops
        )
        near_rest = flip(far_sent, 1)

    with jax.named_scope("outer_sum"):
        by_z = exchange(pending_delta[0].reshape(8, 64, 256), "rep", Z_GROUPS)
        part = jnp.sum(by_z.astype(F32), axis=0)
        by_l = share(part.astype(BF16), L_GROUPS)
        total = jnp.sum(by_l.astype(F32), axis=0)
        mean = share(total, Z_GROUPS).reshape(512, 256) / lax.axis_size("rep")
        new_momentum = 0.9 * outer_momentum + mean
        new_global = (global_frag.astype(F32) - 0.7 * (mean + 0.9 * new_momentum)).astype(BF16)

    with jax.named_scope("gradient"):
        far_gradient = call(
            far_gradient_kernel, SDS((2048, COLS), F32), far_turned, far_residual, flops=dot_flops
        )
        gradient, squares = call(
            near_gradient_kernel,
            (SDS((NX, 512, COLS), BF16), SDS((8, 128), F32)),
            near_turned, near_part, near_rest, far_gradient, flops=dot_flops,
        )
        by_rows = exchange(gradient, "fsdp", X_GROUPS)
        for mask in (2, 4, 1):
            squares = squares + flip(squares, mask)

    with jax.named_scope("step"):
        new_weights = step(frag_order, squares, by_rows, local_weights, new_global)
    return (new_weights, new_global, new_momentum)


def solution(mesh):
    placed = (
        P(("rep", "fsdp"), None),
        P(("rep", "fsdp"), None),
        P("rep", "fsdp", None),
        P("rep", "fsdp", None),
        P(),
        P("fsdp", None),
        P("fsdp", None),
    )
    return jax.shard_map(
        body,
        mesh=mesh,
        in_specs=placed,
        out_specs=(P("rep", "fsdp", None), P("fsdp", None), P("fsdp", None)),
        check_vma=False,
    )
```

time: 739 us -> 168 us (0.23)
  waiting for transfers between devices: 667 us -> 60.2 us
  starting transfers between devices: 4.78 us -> 60.8 us
  between operations: 17.5 us -> 0.87 us
  Pallas kernels: 0 us -> 16.3 us
  matrix products: 9.93 us -> 0 us
    psum x1 -> x0, waiting for transfers between devices: 486 us -> none  [body(): summed = lax.psum(pending_delta[0].astype(jnp.float32), 'rep')]
    all_gather x2 -> x0, waiting for transfers between devices: 181 us -> none  [the longest x1 181 us: body(): lax.all_gather(weight, 'fsdp', axis=0, tiled=True)]
    ppermute x0 -> x12, waiting for transfers between devices: none -> 52.5 us  [the longest x6 38.1 us: flip(): return lax.ppermute(block, 'fsdp', [(i, i ^ mask) for i in range(8)])]
    ppermute x0 -> x12, starting transfers between devices: none -> 42.4 us  [the longest x6 25.1 us: flip(): return lax.ppermute(block, 'fsdp', [(i, i ^ mask) for i in range(8)])]
    psum x1 -> x0, blocking collectives: 28.1 us -> none  [body(): squares = lax.psum(jnp.sum(gradient * gradient), 'fsdp')]
    all_to_all x0 -> x1, blocking collectives: none -> 22.3 us  [exchange(): lax.all_to_all(blocks, axis, 0, 0, axis_index_groups=groups, tiled=True)]
    pallas_call x0 -> x9, Pallas kernels: none -> 16.3 us  [the longest x7 11.6 us: call(): pl.pallas_call(kernel, in_specs=[SMEM] * scalars + [pl.BlockSpec(memory_s...]
    all_to_all x1 -> x4, starting transfers between devices: 4.65 us -> 18.4 us  [exchange(): lax.all_to_all(blocks, axis, 0, 0, axis_index_groups=groups, tiled=True)]
  transfers between devices with their start and end apart: 4 -> 16, of which waited for: 2 -> 9; matrix products, arithmetic and copies ran while one was open for 2% -> 2% of each run, Pallas kernels for 0% -> 8%
where the time goes in v2:
time: 168 us; the launch traced here: 167 us
  starting transfers between devices  60.8 us (36%)
  waiting for transfers between devices  60.2 us (36%)
  blocking collectives  22.3 us (13%)
  Pallas kernels  16.3 us (10%)
  local copies, waits for them, and re-layouts  3.24 us (2%)
  other arithmetic  3.08 us (2%)
    ppermute x6, waiting for transfers between devices, flip(): return lax.ppermute(block, 'fsdp', [(i, i ^ mask) for i in range(8)])  38.1 us
    ppermute x6, starting transfers between devices, flip(): return lax.ppermute(block, 'fsdp', [(i, i ^ mask) for i in range(8)])  25.1 us
    all_to_all x1, blocking collectives, exchange(): lax.all_to_all(blocks, axis, 0, 0, axis_index_groups=groups, tiled=True)  22.3 us
    all_to_all x4, starting transfers between devices, exchange(): lax.all_to_all(blocks, axis, 0, 0, axis_index_groups=groups, tiled=True)  18.4 us
    ppermute x6, starting transfers between devices, rotate(): lax.ppermute(blocks[d], 'fsdp', moves[d])  17.3 us
    ppermute x6, waiting for transfers between devices, rotate(): lax.ppermute(blocks[d], 'fsdp', moves[d])  14.4 us
    pallas_call x7, Pallas kernels, call(): pl.pallas_call(kernel, in_specs=[SMEM] * scalars + [pl.BlockSpec(memory_s...  11.6 us
    all_to_all x4, waiting for transfers between devices, exchange(): lax.all_to_all(blocks, axis, 0, 0, axis_index_groups=groups, tiled=True)  7.63 us
  transfers between devices with their start and end apart: 16, of which 9 were waited for; matrix products, arithmetic and copies ran while one was open for 2% of the time, Pallas kernels for 8%

profile of v2, /device:TPU:6, one launch (start us, length us, event | category | flops | bytes accessed | tf_op | source)
XLA Modules:
  0.0 166.8 jit_solution(7518789719293173548)
XLA Ops:
  0.6 22.3 %all_to_all.25 = bf16[8,64,256]{2,1,0:T(8,128)(2,1)S(1)} all-to-all(bf16[8,64,256]{2,1,0:T(8,128)(2,1)} %bitcast.13), channel_id=1, replica_groups={{0,64,128,192,256,320,384,448},{8,72,136,200,264,328,392,456},{16,80,14..., dimensions={0} | all-to-all | bytes 524288 | tf_op jit(solution)/shard_map/outer_sum/all_to_all | solution.py:30
  23.0 0.7 broadcast_in_dim.4
  23.7 4.9 %all-to-all-start.3 = ((bf16[8,64,256]{2,1,0:T(8,128)(2,1)}), bf16[8,64,256]{2,1,0:T(8,128)(2,1)S(1)}, u32[]{:S(2)}, u32[]{:S(2)}) async-start(bf16[8,64,256]{2,1,0:T(8,128)(2,1)} %broadcast_in_dim.4), calls=%async_computation.3 | async-start | bytes 524288 | tf_op jit(solution)/shard_map/outer_sum/all_to_all | solution.py:30
  28.6 0.0 copy-start.3
  28.6 0.9 copy-done.3
  29.6 1.2 pack.1
  30.7 7.6 %all-to-all-done.3 = bf16[8,64,256]{2,1,0:T(8,128)(2,1)S(1)} async-done(((bf16[8,64,256]{2,1,0:T(8,128)(2,1)}), bf16[8,64,256]{2,1,0:T(8,128)(2,1)S(1)}, u32[]{:S(2)}, u32[]{:S(2)}) %all-to-all-start.3) | async-done | bytes 262176 | tf_op jit(solution)/shard_map/outer_sum/all_to_all | solution.py:30
  38.4 0.7 copy-done.5
  39.1 4.8 %all-to-all-start = ((bf16[4,640,256]{2,1,0:T(8,128)(2,1)}), bf16[4,640,256]{2,1,0:T(8,128)(2,1)S(1)}, u32[]{:S(2)}, u32[]{:S(2)}) async-start(bf16[4,640,256]{2,1,0:T(8,128)(2,1)} %pack.1), calls=%async_computation | async-start | bytes 2621440 | tf_op jit(solution)/shard_map/weight_columns/all_to_all | solution.py:30
  43.8 1.9 %split.1 = (bf16[128,2048]{1,0:T(8,128)(2,1)}, bf16[128,2048]{1,0:T(8,128)(2,1)}) custom-call(s32[1]{0:T(128)} %bitcast.half_ref, bf16[128,4096]{1,0:T(8,128)(2,1)S(1)} %copy-done.1), custom_call_target="tpu_custom_call" | custom-call | tf_op jit(solution)/shard_map/activations/split/pallas_call | solution.py:66
  45.7 6.2 %collective-permute-start.3 = (bf16[128,2048]{1,0:T(8,128)(2,1)}, bf16[128,2048]{1,0:T(8,128)(2,1)S(1)}, u32[]{:S(2)}, u32[]{:S(2)}) collective-permute-start(bf16[128,2048]{1,0:T(8,128)(2,1)} %get-tuple-element.13), channel_id=1, source_target_pairs={{0,1},{1,0},{2,3},{3,2},{4,5},{5,4},{6,7},{7,6},{8,9},{9,8},{10,11... | collective-permute-start | bytes 1572872 | tf_op jit(solution)/shard_map/activations/ppermute | solution.py:38
  51.9 1.9 %collective-permute-start = (bf16[128,2048]{1,0:T(8,128)(2,1)}, bf16[128,2048]{1,0:T(8,128)(2,1)}, u32[]{:S(2)}, u32[]{:S(2)}) collective-permute-start(bf16[128,2048]{1,0:T(8,128)(2,1)} %get-tuple-element.11.b0), channel_id=1, source_target_pairs={{0,2},{1,3},{2,4},{3,5},{4,6},{5,7},{6,0},{7,1},{8,10},{9,11},{10,... | collective-permute-start | bytes 1572872 | tf_op jit(solution)/shard_map/activations/ppermute | solution.py:43
  53.8 4.8 %collective-permute-start.1 = (bf16[128,2048]{1,0:T(8,128)(2,1)}, bf16[128,2048]{1,0:T(8,128)(2,1)}, u32[]{:S(2)}, u32[]{:S(2)}) collective-permute-start(bf16[128,2048]{1,0:T(8,128)(2,1)} %get-tuple-element.11.b0), channel_id=1, source_target_pairs={{0,4},{1,5},{2,6},{3,7},{4,0},{5,1},{6,2},{7,3},{8,12},{9,13},{10,... | collective-permute-start | bytes 1572872 | tf_op jit(solution)/shard_map/activations/ppermute | solution.py:43
  58.7 1.9 %collective-permute-start.2 = (bf16[128,2048]{1,0:T(8,128)(2,1)}, bf16[128,2048]{1,0:T(8,128)(2,1)}, u32[]{:S(2)}, u32[]{:S(2)}) collective-permute-start(bf16[128,2048]{1,0:T(8,128)(2,1)} %get-tuple-element.11.b0), channel_id=1, source_target_pairs={{0,6},{1,7},{2,0},{3,1},{4,2},{5,3},{6,4},{7,5},{8,14},{9,15},{10,... | collective-permute-start | bytes 1572872 | tf_op jit(solution)/shard_map/activations/ppermute | solution.py:43
  60.6 1.0 convert_reduce_fusion
  61.6 0.0 all-to-all-done.columns_ref
  61.6 0.9 broadcast_in_dim.5
  62.5 4.1 %all-to-all-start.4 = ((f32[8,64,256]{2,1,0:T(8,128)}), f32[8,64,256]{2,1,0:T(8,128)}, u32[]{:S(2)}, u32[]{:S(2)}) async-start(f32[8,64,256]{2,1,0:T(8,128)} %broadcast_in_dim.5), calls=%async_computation.4 | async-start | bytes 1048576 | tf_op jit(solution)/shard_map/outer_sum/all_to_all | solution.py:30
  66.6 9.1 %collective-permute-done.3.b0 = bf16[128,2048]{1,0:T(8,128)(2,1)S(1)} collective-permute-done((bf16[128,2048]{1,0:T(8,128)(2,1)}, bf16[128,2048]{1,0:T(8,128)(2,1)S(1)}, u32[]{:S(2)}, u32[]{:S(2)}) %collective-permute-start.3) | collective-permute-done | bytes 524320 | tf_op jit(solution)/shard_map/activations/ppermute | solution.py:38
  75.7 2.2 %collective-permute-start.4 = (bf16[128,2048]{1,0:T(8,128)(2,1)S(1)}, bf16[128,2048]{1,0:T(8,128)(2,1)S(1)}, u32[]{:S(2)}, u32[]{:S(2)}) collective-permute-start(bf16[128,2048]{1,0:T(8,128)(2,1)S(1)} %collective-permute-done.3.b0), channel_id=1, source_target_pairs={{0,2},{1,3},{2,4},{3,5},{4,6},{5,7},{6,0},{7,1},{8,10},{9,11},{10,... | collective-permute-start | bytes 1572872 | tf_op jit(solution)/shard_map/far_activations/ppermute | solution.py:43
  77.9 4.6 %collective-permute-start.5 = (bf16[128,2048]{1,0:T(8,128)(2,1)S(1)}, bf16[128,2048]{1,0:T(8,128)(2,1)}, u32[]{:S(2)}, u32[]{:S(2)}) collective-permute-start(bf16[128,2048]{1,0:T(8,128)(2,1)S(1)} %collective-permute-done.3.b0), channel_id=1, source_target_pairs={{0,4},{1,5},{2,6},{3,7},{4,0},{5,1},{6,2},{7,3},{8,12},{9,13},{10,... | collective-permute-start | bytes 1572872 | tf_op jit(solution)/shard_map/far_activations/ppermute | solution.py:43
  82.4 0.0 collective-permute-done.b1
  82.5 1.9 %collective-permute-start.6 = (bf16[128,2048]{1,0:T(8,128)(2,1)S(1)}, bf16[128,2048]{1,0:T(8,128)(2,1)}, u32[]{:S(2)}, u32[]{:S(2)}) collective-permute-start(bf16[128,2048]{1,0:T(8,128)(2,1)S(1)} %collective-permute-done.3.b0), channel_id=1, source_target_pairs={{0,6},{1,7},{2,0},{3,1},{4,2},{5,3},{6,4},{7,5},{8,14},{9,15},{10,... | collective-permute-start | bytes 1572872 | tf_op jit(solution)/shard_map/far_activations/ppermute | solution.py:43
  84.4 0.0 collective-permute-done.2.b3
  84.4 2.2 %near.1 = (f32[512,256]{1,0:T(8,128)S(1)}, bf16[512,256]{1,0:T(8,128)(2,1)S(1)}) custom-call(s32[1]{0:T(128)} %bitcast.1.x_ref, bf16[128,2048]{1,0:T(8,128)(2,1)} %get-tuple-element.11.b0, bf16[128,2048]{1,0:T(8,128)(2,1)} %collective-permute-done.b1, bf16[128,2048]{1,0:T(8,128)(2,1)} %collective-permute-done.1.b2, ...), custom_call_target="tpu_custom_call" | custom-call | flops 536870912 | bytes 4194304 | tf_op jit(solution)/shard_map/keys/near/pallas_call | solution.py:161
  86.7 4.3 %collective-permute-start.7 = (bf16[512,256]{1,0:T(8,128)(2,1)S(1)}, bf16[512,256]{1,0:T(8,128)(2,1)S(1)}, u32[]{:S(2)}, u32[]{:S(2)}) collective-permute-start(bf16[512,256]{1,0:T(8,128)(2,1)S(1)} %get-tuple-element.14), channel_id=1, source_target_pairs={{0,1},{1,0},{2,3},{3,2},{4,5},{5,4},{6,7},{7,6},{8,9},{9,8},{10,11... | collective-permute-start | bytes 786440 | tf_op jit(solution)/shard_map/keys/ppermute | solution.py:38
  91.0 3.2 %collective-permute-done.4.b1 = bf16[128,2048]{1,0:T(8,128)(2,1)S(1)} collective-permute-done((bf16[128,2048]{1,0:T(8,128)(2,1)S(1)}, bf16[128,2048]{1,0:T(8,128)(2,1)S(1)}, u32[]{:S(2)}, u32[]{:S(2)}) %collective-permute-start.4) | collective-permute-done | bytes 524320 | tf_op jit(solution)/shard_map/far_activations/ppermute | solution.py:43
  94.2 2.1 %collective-permute-done.5.b2 = bf16[128,2048]{1,0:T(8,128)(2,1)} collective-permute-done((bf16[128,2048]{1,0:T(8,128)(2,1)S(1)}, bf16[128,2048]{1,0:T(8,128)(2,1)}, u32[]{:S(2)}, u32[]{:S(2)}) %collective-permute-start.5) | collective-permute-done | bytes 524320 | tf_op jit(solution)/shard_map/far_activations/ppermute | solution.py:43
  96.3 9.1 %collective-permute-done.6.b3 = bf16[128,2048]{1,0:T(8,128)(2,1)} collective-permute-done((bf16[128,2048]{1,0:T(8,128)(2,1)S(1)}, bf16[128,2048]{1,0:T(8,128)(2,1)}, u32[]{:S(2)}, u32[]{:S(2)}) %collective-permute-start.6) | collective-permute-done | bytes 524320 | tf_op jit(solution)/shard_map/far_activations/ppermute | solution.py:43
  105.4 0.0 collective-permute-done.7.rest_ref
  105.4 1.9 %far.1 = (bf16[512,256]{1,0:T(8,128)(2,1)S(1)}, bf16[512,256]{1,0:T(8,128)(2,1)S(1)}) custom-call(bf16[128,2048]{1,0:T(8,128)(2,1)S(1)} %collective-permute-done.3.b0, bf16[128,2048]{1,0:T(8,128)(2,1)S(1)} %collective-permute-done.4.b1, bf16[128,2048]{1,0:T(8,128)(2,1)} %collective-permute-done.5.b2, bf16[128,2048]{1,0:T(8,128)(2,1)} %collective-permute-done.6.b3, ...), custom_call_target="tpu_custom_call" | custom-call | flops 536870912 | bytes 4194304 | tf_op jit(solution)/shard_map/keys/far/pallas_call | solution.py:161
  107.4 5.2 %collective-permute-start.8 = (bf16[512,256]{1,0:T(8,128)(2,1)S(1)}, bf16[512,256]{1,0:T(8,128)(2,1)S(1)}, u32[]{:S(2)}, u32[]{:S(2)}) collective-permute-start(bf16[512,256]{1,0:T(8,128)(2,1)S(1)} %get-tuple-element.15), channel_id=1, source_target_pairs={{0,1},{1,0},{2,3},{3,2},{4,5},{5,4},{6,7},{7,6},{8,9},{9,8},{10,11... | collective-permute-start | bytes 786440 | tf_op jit(solution)/shard_map/keys/ppermute | solution.py:38
  112.5 2.1 %turn.2.turned_ref = bf16[2048,512]{1,0:T(8,128)(2,1)S(1)} custom-call(bf16[128,2048]{1,0:T(8,128)(2,1)} %get-tuple-element.11.b0, bf16[128,2048]{1,0:T(8,128)(2,1)} %collective-permute-done.b1, bf16[128,2048]{1,0:T(8,128)(2,1)} %collective-permute-done.1.b2, bf16[128,2048]{1,0:T(8,128)(2,1)} %collective-permute-done.2.b3), custom_call_target="tpu_custom_call" | custom-call | bytes 4194304 | tf_op jit(solution)/shard_map/keys/turn/pallas_call | solution.py:161
  114.6 1.8 %turn.3.turned_ref = bf16[2048,512]{1,0:T(8,128)(2,1)S(1)} custom-call(bf16[128,2048]{1,0:T(8,128)(2,1)S(1)} %collective-permute-done.3.b0, bf16[128,2048]{1,0:T(8,128)(2,1)S(1)} %collective-permute-done.4.b1, bf16[128,2048]{1,0:T(8,128)(2,1)} %collective-permute-done.5.b2, bf16[128,2048]{1,0:T(8,128)(2,1)} %collective-permute-done.6.b3), custom_call_target="tpu_custom_call" | custom-call | bytes 4194304 | tf_op jit(solution)/shard_map/keys/turn/pallas_call | solution.py:161
  116.4 0.7 far_gradient.1.far_ref
  117.1 9.4 %collective-permute-done.8.rest_ref = bf16[512,256]{1,0:T(8,128)(2,1)S(1)} collective-permute-done((bf16[512,256]{1,0:T(8,128)(2,1)S(1)}, bf16[512,256]{1,0:T(8,128)(2,1)S(1)}, u32[]{:S(2)}, u32[]{:S(2)}) %collective-permute-start.8) | collective-permute-done | bytes 262176 | tf_op jit(solution)/shard_map/keys/ppermute | solution.py:38
  126.5 1.7 %near_gradient.1 = (bf16[4,512,256]{2,1,0:T(8,128)(2,1)}, f32[8,128]{1,0:T(8,128)S(1)}) custom-call(bf16[2048,512]{1,0:T(8,128)(2,1)S(1)} %turn.2.turned_ref, f32[512,256]{1,0:T(8,128)S(1)} %get-tuple-element.12.part_ref, bf16[512,256]{1,0:T(8,128)(2,1)S(1)} %collective-permute-done.8.rest_ref, f32[2048,256]{1,0:T(8,128)S(1)} %far_gradient.1.far_ref), custom_call_target="tpu_custom_call" | custom-call | flops 536870912 | bytes 4194304 | tf_op jit(solution)/shard_map/gradient/near_gradient/pallas_call | solution.py:161
  128.2 0.0 all-to-all-done.4
  128.2 4.6 %all-to-all-start.1 = ((bf16[4,512,256]{2,1,0:T(8,128)(2,1)}), bf16[4,512,256]{2,1,0:T(8,128)(2,1)S(1)}, u32[]{:S(2)}, u32[]{:S(2)}) async-start(bf16[4,512,256]{2,1,0:T(8,128)(2,1)} %get-tuple-element.18), calls=%async_computation.1 | async-start | bytes 2097152 | tf_op jit(solution)/shard_map/gradient/all_to_all | solution.py:30
  132.9 2.9 %collective-permute-start.9 = (f32[8,128]{1,0:T(8,128)S(1)}, f32[8,128]{1,0:T(8,128)S(1)}, u32[]{:S(2)}, u32[]{:S(2)}) collective-permute-start(f32[8,128]{1,0:T(8,128)S(1)} %get-tuple-element.17), channel_id=1, source_target_pairs={{0,2},{1,3},{2,0},{3,1},{4,6},{5,7},{6,4},{7,5},{8,10},{9,11},{10,... | collective-permute-start | bytes 12296 | tf_op jit(solution)/shard_map/gradient/ppermute | solution.py:38
  135.8 9.8 %collective-permute-done.9 = f32[8,128]{1,0:T(8,128)S(1)} collective-permute-done((f32[8,128]{1,0:T(8,128)S(1)}, f32[8,128]{1,0:T(8,128)S(1)}, u32[]{:S(2)}, u32[]{:S(2)}) %collective-permute-start.9) | collective-permute-done | bytes 4128 | tf_op jit(solution)/shard_map/gradient/ppermute | solution.py:38
  145.6 2.8 %collective-permute-start.10 = (f32[8,128]{1,0:T(8,128)S(1)}, f32[8,128]{1,0:T(8,128)S(1)}, u32[]{:S(2)}, u32[]{:S(2)}) collective-permute-start(f32[8,128]{1,0:T(8,128)S(1)} %add.15), channel_id=1, source_target_pairs={{0,4},{1,5},{2,6},{3,7},{4,0},{5,1},{6,2},{7,3},{8,12},{9,13},{10,... | collective-permute-start | bytes 12296 | tf_op jit(solution)/shard_map/gradient/ppermute | solution.py:38
  148.4 4.2 %collective-permute-done.10 = f32[8,128]{1,0:T(8,128)S(1)} collective-permute-done((f32[8,128]{1,0:T(8,128)S(1)}, f32[8,128]{1,0:T(8,128)S(1)}, u32[]{:S(2)}, u32[]{:S(2)}) %collective-permute-start.10) | collective-permute-done | bytes 4128 | tf_op jit(solution)/shard_map/gradient/ppermute | solution.py:38
  152.6 3.7 %collective-permute-start.11 = (f32[8,128]{1,0:T(8,128)S(1)}, f32[8,128]{1,0:T(8,128)S(1)}, u32[]{:S(2)}, u32[]{:S(2)}) collective-permute-start(f32[8,128]{1,0:T(8,128)S(1)} %add.16), channel_id=1, source_target_pairs={{0,1},{1,0},{2,3},{3,2},{4,5},{5,4},{6,7},{7,6},{8,9},{9,8},{10,11... | collective-permute-start | bytes 12296 | tf_op jit(solution)/shard_map/gradient/ppermute | solution.py:38
  156.3 5.7 %collective-permute-done.11 = f32[8,128]{1,0:T(8,128)S(1)} collective-permute-done((f32[8,128]{1,0:T(8,128)S(1)}, f32[8,128]{1,0:T(8,128)S(1)}, u32[]{:S(2)}, u32[]{:S(2)}) %collective-permute-start.11) | collective-permute-done | bytes 4128 | tf_op jit(solution)/shard_map/gradient/ppermute | solution.py:38
  162.0 1.1 broadcast_multiply_fusion
  163.1 1.0 fusion.2
  164.0 2.8 %step.1 = bf16[1,512,1024]{2,1,0:T(8,128)(2,1)} custom-call(s32[8]{0:T(128)S(1)} %copy-done.4, f32[8,128]{1,0:T(8,128)S(1)} %add.17.squares_ref, bf16[4,512,256]{2,1,0:T(8,128)(2,1)S(1)} %all-to-all-done.1.rows_ref, bf16[1,512,1024]{2,1,0:T(8,128)(2,1)S(1)} %copy-done, bf16[512,256]{1,0:T(8,128)(2,1)S(1)} %get-tuple-element.19.global_ref), custom_call_target="tpu_custom_call" | custom-call | tf_op jit(solution)/shard_map/step/step/pallas_call | solution.py:142
  (19 shorter events, 0.1 us)
Async XLA Ops:
  0.6 28.0 %copy-start = (bf16[1,512,1024]{2,1,0:T(8,128)(2,1)S(1)}, bf16[1,512,1024]{2,1,0:T(8,128)(2,1)}, u32[]{:S(2)}) copy-start(bf16[1,512,1024]{2,1,0:T(8,128)(2,1)} %weight_ref.3) | copy-start | bytes 3145732
  23.7 14.6 %all-to-all-start.3 = ((bf16[8,64,256]{2,1,0:T(8,128)(2,1)}), bf16[8,64,256]{2,1,0:T(8,128)(2,1)S(1)}, u32[]{:S(2)}, u32[]{:S(2)}) async-start(bf16[8,64,256]{2,1,0:T(8,128)(2,1)} %broadcast_in_dim.4), calls=%async_computation.3 | async-start | bytes 524288 | tf_op jit(solution)/shard_map/outer_sum/all_to_all | solution.py:30
  28.6 1.0 copy-start.3
  29.6 14.3 %copy-start.1 = (bf16[128,4096]{1,0:T(8,128)(2,1)S(1)}, bf16[128,4096]{1,0:T(8,128)(2,1)}, u32[]{:S(2)}) copy-start(bf16[128,4096]{1,0:T(8,128)(2,1)} %tokens_ref.1) | copy-start | bytes 3145732
  38.4 0.7 copy-start.5
  39.1 22.5 %all-to-all-start = ((bf16[4,640,256]{2,1,0:T(8,128)(2,1)}), bf16[4,640,256]{2,1,0:T(8,128)(2,1)S(1)}, u32[]{:S(2)}, u32[]{:S(2)}) async-start(bf16[4,640,256]{2,1,0:T(8,128)(2,1)} %pack.1), calls=%async_computation | async-start | bytes 2621440 | tf_op jit(solution)/shard_map/weight_columns/all_to_all | solution.py:30
  45.7 30.0 %collective-permute-start.3 = (bf16[128,2048]{1,0:T(8,128)(2,1)}, bf16[128,2048]{1,0:T(8,128)(2,1)S(1)}, u32[]{:S(2)}, u32[]{:S(2)}) collective-permute-start(bf16[128,2048]{1,0:T(8,128)(2,1)} %get-tuple-element.13), channel_id=1, source_target_pairs={{0,1},{1,0},{2,3},{3,2},{4,5},{5,4},{6,7},{7,6},{8,9},{9,8},{10,11... | collective-permute-start | bytes 1572872 | tf_op jit(solution)/shard_map/activations/ppermute | solution.py:38
  51.9 30.5 %collective-permute-start = (bf16[128,2048]{1,0:T(8,128)(2,1)}, bf16[128,2048]{1,0:T(8,128)(2,1)}, u32[]{:S(2)}, u32[]{:S(2)}) collective-permute-start(bf16[128,2048]{1,0:T(8,128)(2,1)} %get-tuple-element.11.b0), channel_id=1, source_target_pairs={{0,2},{1,3},{2,4},{3,5},{4,6},{5,7},{6,0},{7,1},{8,10},{9,11},{10,... | collective-permute-start | bytes 1572872 | tf_op jit(solution)/shard_map/activations/ppermute | solution.py:43
  53.8 30.5 %collective-permute-start.1 = (bf16[128,2048]{1,0:T(8,128)(2,1)}, bf16[128,2048]{1,0:T(8,128)(2,1)}, u32[]{:S(2)}, u32[]{:S(2)}) collective-permute-start(bf16[128,2048]{1,0:T(8,128)(2,1)} %get-tuple-element.11.b0), channel_id=1, source_target_pairs={{0,4},{1,5},{2,6},{3,7},{4,0},{5,1},{6,2},{7,3},{8,12},{9,13},{10,... | collective-permute-start | bytes 1572872 | tf_op jit(solution)/shard_map/activations/ppermute | solution.py:43
  58.7 25.7 %collective-permute-start.2 = (bf16[128,2048]{1,0:T(8,128)(2,1)}, bf16[128,2048]{1,0:T(8,128)(2,1)}, u32[]{:S(2)}, u32[]{:S(2)}) collective-permute-start(bf16[128,2048]{1,0:T(8,128)(2,1)} %get-tuple-element.11.b0), channel_id=1, source_target_pairs={{0,6},{1,7},{2,0},{3,1},{4,2},{5,3},{6,4},{7,5},{8,14},{9,15},{10,... | collective-permute-start | bytes 1572872 | tf_op jit(solution)/shard_map/activations/ppermute | solution.py:43
  62.5 65.8 %all-to-all-start.4 = ((f32[8,64,256]{2,1,0:T(8,128)}), f32[8,64,256]{2,1,0:T(8,128)}, u32[]{:S(2)}, u32[]{:S(2)}) async-start(f32[8,64,256]{2,1,0:T(8,128)} %broadcast_in_dim.5), calls=%async_computation.4 | async-start | bytes 1048576 | tf_op jit(solution)/shard_map/outer_sum/all_to_all | solution.py:30
  75.7 18.5 %collective-permute-start.4 = (bf16[128,2048]{1,0:T(8,128)(2,1)S(1)}, bf16[128,2048]{1,0:T(8,128)(2,1)S(1)}, u32[]{:S(2)}, u32[]{:S(2)}) collective-permute-start(bf16[128,2048]{1,0:T(8,128)(2,1)S(1)} %collective-permute-done.3.b0), channel_id=1, source_target_pairs={{0,2},{1,3},{2,4},{3,5},{4,6},{5,7},{6,0},{7,1},{8,10},{9,11},{10,... | collective-permute-start | bytes 1572872 | tf_op jit(solution)/shard_map/far_activations/ppermute | solution.py:43
  77.9 18.4 %collective-permute-start.5 = (bf16[128,2048]{1,0:T(8,128)(2,1)S(1)}, bf16[128,2048]{1,0:T(8,128)(2,1)}, u32[]{:S(2)}, u32[]{:S(2)}) collective-permute-start(bf16[128,2048]{1,0:T(8,128)(2,1)S(1)} %collective-permute-done.3.b0), channel_id=1, source_target_pairs={{0,4},{1,5},{2,6},{3,7},{4,0},{5,1},{6,2},{7,3},{8,12},{9,13},{10,... | collective-permute-start | bytes 1572872 | tf_op jit(solution)/shard_map/far_activations/ppermute | solution.py:43
  82.5 23.0 %collective-permute-start.6 = (bf16[128,2048]{1,0:T(8,128)(2,1)S(1)}, bf16[128,2048]{1,0:T(8,128)(2,1)}, u32[]{:S(2)}, u32[]{:S(2)}) collective-permute-start(bf16[128,2048]{1,0:T(8,128)(2,1)S(1)} %collective-permute-done.3.b0), channel_id=1, source_target_pairs={{0,6},{1,7},{2,0},{3,1},{4,2},{5,3},{6,4},{7,5},{8,14},{9,15},{10,... | collective-permute-start | bytes 1572872 | tf_op jit(solution)/shard_map/far_activations/ppermute | solution.py:43
  86.7 18.8 %collective-permute-start.7 = (bf16[512,256]{1,0:T(8,128)(2,1)S(1)}, bf16[512,256]{1,0:T(8,128)(2,1)S(1)}, u32[]{:S(2)}, u32[]{:S(2)}) collective-permute-start(bf16[512,256]{1,0:T(8,128)(2,1)S(1)} %get-tuple-element.14), channel_id=1, source_target_pairs={{0,1},{1,0},{2,3},{3,2},{4,5},{5,4},{6,7},{7,6},{8,9},{9,8},{10,11... | collective-permute-start | bytes 786440 | tf_op jit(solution)/shard_map/keys/ppermute | solution.py:38
  107.4 19.2 %collective-permute-start.8 = (bf16[512,256]{1,0:T(8,128)(2,1)S(1)}, bf16[512,256]{1,0:T(8,128)(2,1)S(1)}, u32[]{:S(2)}, u32[]{:S(2)}) collective-permute-start(bf16[512,256]{1,0:T(8,128)(2,1)S(1)} %get-tuple-element.15), channel_id=1, source_target_pairs={{0,1},{1,0},{2,3},{3,2},{4,5},{5,4},{6,7},{7,6},{8,9},{9,8},{10,11... | collective-permute-start | bytes 786440 | tf_op jit(solution)/shard_map/keys/ppermute | solution.py:38
  128.2 34.8 %copy-start.6 = (f32[512,256]{1,0:T(8,128)S(1)}, f32[512,256]{1,0:T(8,128)}, u32[]{:S(2)}) copy-start(f32[512,256]{1,0:T(8,128)} %param.13) | copy-start | bytes 1572868
  128.2 34.8 %copy-start.7 = (bf16[512,256]{1,0:T(8,128)(2,1)S(1)}, bf16[512,256]{1,0:T(8,128)(2,1)}, u32[]{:S(2)}) copy-start(bf16[512,256]{1,0:T(8,128)(2,1)} %param.12) | copy-start | bytes 786436
  128.2 35.8 %all-to-all-start.1 = ((bf16[4,512,256]{2,1,0:T(8,128)(2,1)}), bf16[4,512,256]{2,1,0:T(8,128)(2,1)S(1)}, u32[]{:S(2)}, u32[]{:S(2)}) async-start(bf16[4,512,256]{2,1,0:T(8,128)(2,1)} %get-tuple-element.18), calls=%async_computation.1 | async-start | bytes 2097152 | tf_op jit(solution)/shard_map/gradient/all_to_all | solution.py:30
  132.9 31.2 %copy-start.4 = (s32[8]{0:T(128)S(1)}, s32[8]{0:T(128)}, u32[]{:S(2)}) copy-start(s32[8]{0:T(128)} %order_ref.1) | copy-start | bytes 100
  132.9 12.7 %collective-permute-start.9 = (f32[8,128]{1,0:T(8,128)S(1)}, f32[8,128]{1,0:T(8,128)S(1)}, u32[]{:S(2)}, u32[]{:S(2)}) collective-permute-start(f32[8,128]{1,0:T(8,128)S(1)} %get-tuple-element.17), channel_id=1, source_target_pairs={{0,2},{1,3},{2,0},{3,1},{4,6},{5,7},{6,4},{7,5},{8,10},{9,11},{10,... | collective-permute-start | bytes 12296 | tf_op jit(solution)/shard_map/gradient/ppermute | solution.py:38
  145.6 7.0 %collective-permute-start.10 = (f32[8,128]{1,0:T(8,128)S(1)}, f32[8,128]{1,0:T(8,128)S(1)}, u32[]{:S(2)}, u32[]{:S(2)}) collective-permute-start(f32[8,128]{1,0:T(8,128)S(1)} %add.15), channel_id=1, source_target_pairs={{0,4},{1,5},{2,6},{3,7},{4,0},{5,1},{6,2},{7,3},{8,12},{9,13},{10,... | collective-permute-start | bytes 12296 | tf_op jit(solution)/shard_map/gradient/ppermute | solution.py:38
  152.6 9.4 %collective-permute-start.11 = (f32[8,128]{1,0:T(8,128)S(1)}, f32[8,128]{1,0:T(8,128)S(1)}, u32[]{:S(2)}, u32[]{:S(2)}) collective-permute-start(f32[8,128]{1,0:T(8,128)S(1)} %add.16), channel_id=1, source_target_pairs={{0,1},{1,0},{2,3},{3,2},{4,5},{5,4},{6,7},{7,6},{8,9},{9,8},{10,11... | collective-permute-start | bytes 12296 | tf_op jit(solution)/shard_map/gradient/ppermute | solution.py:38
  164.0 2.8 %copy-start.2 = (bf16[512,256]{1,0:T(8,128)(2,1)}, bf16[512,256]{1,0:T(8,128)(2,1)S(1)}, u32[]{:S(2)}) copy-start(bf16[512,256]{1,0:T(8,128)(2,1)S(1)} %get-tuple-element.19.global_ref) | copy-start | bytes 786436

commit v3 on v2

--- a/solution.py
+++ b/solution.py
@@ -1,4 +1,3 @@
-import functools
 import math
 
 import jax
@@ -30,10 +29,6 @@
     return lax.all_to_all(blocks, axis, 0, 0, axis_index_groups=groups, tiled=True)
 
 
-def share(block, groups):
-    return exchange(jnp.broadcast_to(block[None], (8, *block.shape)), "rep", groups)
-
-
 def flip(block, mask):
     return lax.ppermute(block, "fsdp", [(i, i ^ mask) for i in range(8)])
 
@@ -45,10 +40,6 @@
 
 def gather(block):
     return rotate([block] * NX)
-
-
-def after(value, earlier):
-    return lax.optimization_barrier((value, earlier))[0]
 
 
 def split_kernel(half_ref, tokens_ref, mine_ref, other_ref):
@@ -201,11 +192,11 @@
         near_rest = flip(far_sent, 1)
 
     with jax.named_scope("outer_sum"):
-        by_z = exchange(pending_delta[0].reshape(8, 64, 256), "rep", Z_GROUPS)
-        part = jnp.sum(by_z.astype(F32), axis=0)
-        by_l = share(part.astype(BF16), L_GROUPS)
-        total = jnp.sum(by_l.astype(F32), axis=0)
-        mean = share(total, Z_GROUPS).reshape(512, 256) / lax.axis_size("rep")
+        by_z = lax.all_gather(pending_delta[0], "rep", axis_index_groups=Z_GROUPS)
+        by_z = lax.optimization_barrier((by_z, near_sent[:16, :128]))[0]
+        part = jnp.sum(by_z.astype(F32), axis=0).astype(BF16)
+        by_l = lax.all_gather(part, "rep", axis_index_groups=L_GROUPS)
+        mean = jnp.sum(by_l.astype(F32), axis=0) / lax.axis_size("rep")
         new_momentum = 0.9 * outer_momentum + mean
         new_global = (global_frag.astype(F32) - 0.7 * (mean + 0.9 * new_momentum)).astype(BF16)
 
@@ -219,8 +210,7 @@
             near_turned, near_part, near_rest, far_gradient, flops=dot_flops,
         )
         by_rows = exchange(gradient, "fsdp", X_GROUPS)
-        for mask in (2, 4, 1):
-            squares = squares + flip(squares, mask)
+        squares = sum(gather(squares + flip(squares, 1)))
 
     with jax.named_scope("step"):
         new_weights = step(frag_order, squares, by_rows, local_weights, new_global)

time: 168 us -> 199 us (1.18)
  the two profiles are of different devices: /device:TPU:6 before, /device:TPU:64 now
where the time goes in v3:
time: 199 us; the launch traced here: 198 us
  waiting for transfers between devices  84.3 us (42%)
  starting transfers between devices  76.1 us (38%)
  Pallas kernels  15.9 us (8%)
  between operations  14.3 us (7%)
  other arithmetic  5.54 us (3%)
    all_gather x1, waiting for transfers between devices, body(): by_z = lax.all_gather(pending_delta[0], 'rep', axis_index_groups=Z_GROUPS)  50 us
    ppermute x9, starting transfers between devices, rotate(): lax.ppermute(blocks[d], 'fsdp', moves[d])  34.4 us
    ppermute x4, starting transfers between devices, flip(): return lax.ppermute(block, 'fsdp', [(i, i ^ mask) for i in range(8)])  33.7 us
    ppermute x4, waiting for transfers between devices, flip(): return lax.ppermute(block, 'fsdp', [(i, i ^ mask) for i in range(8)])  29.7 us
    pallas_call x7, Pallas kernels, call(): pl.pallas_call(kernel, in_specs=[SMEM] * scalars + [pl.BlockSpec(memory_s...  11.3 us
    all_to_all x2, starting transfers between devices, exchange(): lax.all_to_all(blocks, axis, 0, 0, axis_index_groups=groups, tiled=True)  7.9 us
  transfers between devices with their start and end apart: 17, of which 7 were waited for; matrix products, arithmetic and copies ran while one was open for 1% of the time, Pallas kernels for 7%

profile of v3, /device:TPU:64, one launch (start us, length us, event | category | flops | bytes accessed | tf_op | source)
XLA Modules:
  0.0 198.1 jit_solution(17932760096801569333)
XLA Ops:
  7.2 0.0 all-gather.4.cloned.1.call-start
  7.2 0.7 all-gather.4.cloned.1.call-update
  7.9 0.0 all-gather.6.cloned.1.call-start
  8.0 50.0 %all-gather.4.cloned.1.call-done = bf16[8,512,256]{2,1,0:T(8,128)(2,1)} async-done(((bf16[1,512,256]{2,1,0:T(8,128)(2,1)}), bf16[8,512,256]{2,1,0:T(8,128)(2,1)}) %all-gather.4.cloned.1.call-update) | async-done | bytes 2097168 | tf_op jit(solution)/shard_map/outer_sum/all_gather | solution.py:195
  57.9 2.6 %reduce_sum.21 = bf16[512,256]{1,0:T(8,128)(2,1)} reduce(bf16[8,512,256]{2,1,0:T(8,128)(2,1)} %all-gather.4.cloned.1.call-done, bf16[]{:T(256)} %constant.17.clone.1), dimensions={0}, to_apply=%region_0.0 | reduce | flops 917504 | bytes 2359298 | tf_op jit(solution)/shard_map/outer_sum/reduce_sum | solution.py:197
  60.6 0.0 all-gather.6.cloned.1.call-update
  60.6 0.0 copy-start.3
  60.6 1.2 pack.1
  61.8 4.2 %all-to-all-start = ((bf16[4,640,256]{2,1,0:T(8,128)(2,1)}), bf16[4,640,256]{2,1,0:T(8,128)(2,1)S(1)}, u32[]{:S(2)}, u32[]{:S(2)}) async-start(bf16[4,640,256]{2,1,0:T(8,128)(2,1)} %pack.1), calls=%async_computation | async-start | bytes 2621440 | tf_op jit(solution)/shard_map/weight_columns/all_to_all | solution.py:29
  66.1 1.8 split.1
  67.9 7.4 %collective-permute-start.3 = (bf16[128,2048]{1,0:T(8,128)(2,1)S(1)}, bf16[128,2048]{1,0:T(8,128)(2,1)S(1)}, u32[]{:S(2)}, u32[]{:S(2)}) collective-permute-start(bf16[128,2048]{1,0:T(8,128)(2,1)S(1)} %get-tuple-element.13), channel_id=1, source_target_pairs={{0,1},{1,0},{2,3},{3,2},{4,5},{5,4},{6,7},{7,6},{8,9},{9,8},{10,11... | collective-permute-start | bytes 1572872 | tf_op jit(solution)/shard_map/activations/ppermute | solution.py:33
  75.2 3.9 %collective-permute-start = (bf16[128,2048]{1,0:T(8,128)(2,1)}, bf16[128,2048]{1,0:T(8,128)(2,1)S(1)}, u32[]{:S(2)}, u32[]{:S(2)}) collective-permute-start(bf16[128,2048]{1,0:T(8,128)(2,1)} %get-tuple-element.11.b0), channel_id=1, source_target_pairs={{0,2},{1,3},{2,4},{3,5},{4,6},{5,7},{6,0},{7,1},{8,10},{9,11},{10,... | collective-permute-start | bytes 1572872 | tf_op jit(solution)/shard_map/activations/ppermute | solution.py:38
  79.2 4.6 %collective-permute-start.1 = (bf16[128,2048]{1,0:T(8,128)(2,1)}, bf16[128,2048]{1,0:T(8,128)(2,1)}, u32[]{:S(2)}, u32[]{:S(2)}) collective-permute-start(bf16[128,2048]{1,0:T(8,128)(2,1)} %get-tuple-element.11.b0), channel_id=1, source_target_pairs={{0,4},{1,5},{2,6},{3,7},{4,0},{5,1},{6,2},{7,3},{8,12},{9,13},{10,... | collective-permute-start | bytes 1572872 | tf_op jit(solution)/shard_map/activations/ppermute | solution.py:38
  83.8 3.4 %collective-permute-start.2 = (bf16[128,2048]{1,0:T(8,128)(2,1)}, bf16[128,2048]{1,0:T(8,128)(2,1)}, u32[]{:S(2)}, u32[]{:S(2)}) collective-permute-start(bf16[128,2048]{1,0:T(8,128)(2,1)} %get-tuple-element.11.b0), channel_id=1, source_target_pairs={{0,6},{1,7},{2,0},{3,1},{4,2},{5,3},{6,4},{7,5},{8,14},{9,15},{10,... | collective-permute-start | bytes 1572872 | tf_op jit(solution)/shard_map/activations/ppermute | solution.py:38
  87.1 17.5 %collective-permute-done.3.b0 = bf16[128,2048]{1,0:T(8,128)(2,1)S(1)} collective-permute-done((bf16[128,2048]{1,0:T(8,128)(2,1)S(1)}, bf16[128,2048]{1,0:T(8,128)(2,1)S(1)}, u32[]{:S(2)}, u32[]{:S(2)}) %collective-permute-start.3) | collective-permute-done | bytes 524320 | tf_op jit(solution)/shard_map/activations/ppermute | solution.py:33
  104.6 4.0 %collective-permute-start.4 = (bf16[128,2048]{1,0:T(8,128)(2,1)S(1)}, bf16[128,2048]{1,0:T(8,128)(2,1)S(1)}, u32[]{:S(2)}, u32[]{:S(2)}) collective-permute-start(bf16[128,2048]{1,0:T(8,128)(2,1)S(1)} %collective-permute-done.3.b0), channel_id=1, source_target_pairs={{0,2},{1,3},{2,4},{3,5},{4,6},{5,7},{6,0},{7,1},{8,10},{9,11},{10,... | collective-permute-start | bytes 1572872 | tf_op jit(solution)/shard_map/far_activations/ppermute | solution.py:38
  108.6 4.6 %collective-permute-start.5 = (bf16[128,2048]{1,0:T(8,128)(2,1)S(1)}, bf16[128,2048]{1,0:T(8,128)(2,1)}, u32[]{:S(2)}, u32[]{:S(2)}) collective-permute-start(bf16[128,2048]{1,0:T(8,128)(2,1)S(1)} %collective-permute-done.3.b0), channel_id=1, source_target_pairs={{0,4},{1,5},{2,6},{3,7},{4,0},{5,1},{6,2},{7,3},{8,12},{9,13},{10,... | collective-permute-start | bytes 1572872 | tf_op jit(solution)/shard_map/far_activations/ppermute | solution.py:38
  113.2 0.0 collective-permute-done.b1
  113.2 0.0 copy-start.1
  113.2 0.8 copy-done.1
  114.0 3.4 %collective-permute-start.6 = (bf16[128,2048]{1,0:T(8,128)(2,1)S(1)}, bf16[128,2048]{1,0:T(8,128)(2,1)}, u32[]{:S(2)}, u32[]{:S(2)}) collective-permute-start(bf16[128,2048]{1,0:T(8,128)(2,1)S(1)} %collective-permute-done.3.b0), channel_id=1, source_target_pairs={{0,6},{1,7},{2,0},{3,1},{4,2},{5,3},{6,4},{7,5},{8,14},{9,15},{10,... | collective-permute-start | bytes 1572872 | tf_op jit(solution)/shard_map/far_activations/ppermute | solution.py:38
  117.4 0.0 collective-permute-done.1.b2
  117.4 0.0 collective-permute-done.2.b3
  117.4 0.0 copy-start.2
  117.4 1.0 copy-done.2
  118.4 2.1 %near.1 = (f32[512,256]{1,0:T(8,128)S(1)}, bf16[512,256]{1,0:T(8,128)(2,1)S(1)}) custom-call(s32[1]{0:T(128)} %bitcast.1.x_ref, bf16[128,2048]{1,0:T(8,128)(2,1)} %get-tuple-element.11.b0, bf16[128,2048]{1,0:T(8,128)(2,1)S(1)} %copy-done.2, bf16[128,2048]{1,0:T(8,128)(2,1)} %collective-permute-done.1.b2, bf16[128,2048]{1,0:T(8,128)(2,1)} %collective-permute-done.2.b3, ...), custom_call_target="tpu_custom_call" | custom-call | flops 536870912 | bytes 4194304 | tf_op jit(solution)/shard_map/keys/near/pallas_call | solution.py:152
  120.5 8.6 %collective-permute-start.7 = (bf16[512,256]{1,0:T(8,128)(2,1)S(1)}, bf16[512,256]{1,0:T(8,128)(2,1)S(1)}, u32[]{:S(2)}, u32[]{:S(2)}) collective-permute-start(bf16[512,256]{1,0:T(8,128)(2,1)S(1)} %get-tuple-element.14), channel_id=1, source_target_pairs={{0,1},{1,0},{2,3},{3,2},{4,5},{5,4},{6,7},{7,6},{8,9},{9,8},{10,11... | collective-permute-start | bytes 786440 | tf_op jit(solution)/shard_map/keys/ppermute | solution.py:33
  129.1 0.0 collective-permute-done.5.b2
  129.2 0.0 collective-permute-done.6.b3
  129.2 8.2 %collective-permute-done.7.rest_ref = bf16[512,256]{1,0:T(8,128)(2,1)S(1)} collective-permute-done((bf16[512,256]{1,0:T(8,128)(2,1)S(1)}, bf16[512,256]{1,0:T(8,128)(2,1)S(1)}, u32[]{:S(2)}, u32[]{:S(2)}) %collective-permute-start.7) | collective-permute-done | bytes 262176 | tf_op jit(solution)/shard_map/keys/ppermute | solution.py:33
  137.4 1.9 far.1
  139.3 10.9 %collective-permute-start.8 = (bf16[512,256]{1,0:T(8,128)(2,1)S(1)}, bf16[512,256]{1,0:T(8,128)(2,1)S(1)}, u32[]{:S(2)}, u32[]{:S(2)}) collective-permute-start(bf16[512,256]{1,0:T(8,128)(2,1)S(1)} %get-tuple-element.15), channel_id=1, source_target_pairs={{0,1},{1,0},{2,3},{3,2},{4,5},{5,4},{6,7},{7,6},{8,9},{9,8},{10,11... | collective-permute-start | bytes 786440 | tf_op jit(solution)/shard_map/keys/ppermute | solution.py:33
  150.2 2.0 turn.2.turned_ref
  152.2 1.8 turn.3.turned_ref
  154.0 0.7 far_gradient.1.far_ref
  154.7 1.5 collective-permute-done.8.rest_ref
  156.2 1.7 near_gradient.1
  157.9 3.6 %all-to-all-start.1 = ((bf16[4,512,256]{2,1,0:T(8,128)(2,1)}), bf16[4,512,256]{2,1,0:T(8,128)(2,1)S(1)}, u32[]{:S(2)}, u32[]{:S(2)}) async-start(bf16[4,512,256]{2,1,0:T(8,128)(2,1)} %get-tuple-element.18), calls=%async_computation.1 | async-start | bytes 2097152 | tf_op jit(solution)/shard_map/gradient/all_to_all | solution.py:29
  161.5 6.8 %collective-permute-start.9 = (f32[8,128]{1,0:T(8,128)S(1)}, f32[8,128]{1,0:T(8,128)S(1)}, u32[]{:S(2)}, u32[]{:S(2)}) collective-permute-start(f32[8,128]{1,0:T(8,128)S(1)} %get-tuple-element.17), channel_id=1, source_target_pairs={{0,1},{1,0},{2,3},{3,2},{4,5},{5,4},{6,7},{7,6},{8,9},{9,8},{10,11... | collective-permute-start | bytes 12296 | tf_op jit(solution)/shard_map/gradient/ppermute | solution.py:33
  168.4 2.6 %collective-permute-done.9 = f32[8,128]{1,0:T(8,128)S(1)} collective-permute-done((f32[8,128]{1,0:T(8,128)S(1)}, f32[8,128]{1,0:T(8,128)S(1)}, u32[]{:S(2)}, u32[]{:S(2)}) %collective-permute-start.9) | collective-permute-done | bytes 4128 | tf_op jit(solution)/shard_map/gradient/ppermute | solution.py:33
  171.0 5.1 %collective-permute-start.12 = (f32[8,128]{1,0:T(8,128)S(1)}, f32[8,128]{1,0:T(8,128)S(1)}, u32[]{:S(2)}, u32[]{:S(2)}) collective-permute-start(f32[8,128]{1,0:T(8,128)S(1)} %add.18), channel_id=1, source_target_pairs={{0,6},{1,7},{2,0},{3,1},{4,2},{5,3},{6,4},{7,5},{8,14},{9,15},{10,... | collective-permute-start | bytes 12296 | tf_op jit(solution)/shard_map/gradient/ppermute | solution.py:38
  176.1 2.8 %collective-permute-start.11 = (f32[8,128]{1,0:T(8,128)S(1)}, f32[8,128]{1,0:T(8,128)S(1)}, u32[]{:S(2)}, u32[]{:S(2)}) collective-permute-start(f32[8,128]{1,0:T(8,128)S(1)} %add.18), channel_id=1, source_target_pairs={{0,4},{1,5},{2,6},{3,7},{4,0},{5,1},{6,2},{7,3},{8,12},{9,13},{10,... | collective-permute-start | bytes 12296 | tf_op jit(solution)/shard_map/gradient/ppermute | solution.py:38
  178.8 2.8 %collective-permute-start.10 = (f32[8,128]{1,0:T(8,128)S(1)}, f32[8,128]{1,0:T(8,128)S(1)}, u32[]{:S(2)}, u32[]{:S(2)}) collective-permute-start(f32[8,128]{1,0:T(8,128)S(1)} %add.18), channel_id=1, source_target_pairs={{0,2},{1,3},{2,4},{3,5},{4,6},{5,7},{6,0},{7,1},{8,10},{9,11},{10,... | collective-permute-start | bytes 12296 | tf_op jit(solution)/shard_map/gradient/ppermute | solution.py:38
  181.6 1.5 collective-permute-done.11
  183.1 2.5 %collective-permute-done.10 = f32[8,128]{1,0:T(8,128)S(1)} collective-permute-done((f32[8,128]{1,0:T(8,128)S(1)}, f32[8,128]{1,0:T(8,128)S(1)}, u32[]{:S(2)}, u32[]{:S(2)}) %collective-permute-start.10) | collective-permute-done | bytes 4128 | tf_op jit(solution)/shard_map/gradient/ppermute | solution.py:38
  185.5 1.9 convert_reduce_fusion
  187.5 0.9 subtract_convert_fusion
  188.5 2.8 %step.1 = bf16[1,512,1024]{2,1,0:T(8,128)(2,1)} custom-call(s32[8]{0:T(128)S(1)} %copy-done.6, f32[8,128]{1,0:T(8,128)S(1)} %add_add_fusion.squares_ref, bf16[4,512,256]{2,1,0:T(8,128)(2,1)S(1)} %all-to-all-done.1.rows_ref, bf16[1,512,1024]{2,1,0:T(8,128)(2,1)S(1)} %copy-done, bf16[512,256]{1,0:T(8,128)(2,1)S(1)} %get-tuple-element.19.global_ref), custom_call_target="tpu_custom_call" | custom-call | tf_op jit(solution)/shard_map/step/step/pallas_call | solution.py:133
  (20 shorter events, 0.0 us)
Async XLA Ops:
  7.2 53.4 %copy-start = (bf16[1,512,1024]{2,1,0:T(8,128)(2,1)S(1)}, bf16[1,512,1024]{2,1,0:T(8,128)(2,1)}, u32[]{:S(2)}) copy-start(bf16[1,512,1024]{2,1,0:T(8,128)(2,1)} %weight_ref.3) | copy-start | bytes 3145732
  7.2 53.4 %copy-start.5 = (bf16[128,1024]{1,0:T(8,128)(2,1)S(1)}, bf16[128,1024]{1,0:T(8,128)(2,1)}, u32[]{:S(2)}) copy-start(bf16[128,1024]{1,0:T(8,128)(2,1)} %targets_ref.1) | copy-start | bytes 786436
  7.2 50.7 %all-gather.4.cloned.1.call-start = ((), (), s32[]{:S(2)}) async-start(), calls=%async_computation.2 | async-start | bytes 2359296 | tf_op jit(solution)/shard_map/outer_sum/all_gather | solution.py:195
  7.9 177.6 %all-gather.6.cloned.1.call-start = ((), (), s32[]{:S(2)}) async-start(), calls=%async_computation.3 | async-start | bytes 2359296 | tf_op jit(solution)/shard_map/outer_sum/all_gather | solution.py:198
  60.6 5.4 %copy-start.3 = (bf16[128,4096]{1,0:T(8,128)(2,1)S(1)}, bf16[128,4096]{1,0:T(8,128)(2,1)}, u32[]{:S(2)}) copy-start(bf16[128,4096]{1,0:T(8,128)(2,1)} %tokens_ref.1) | copy-start | bytes 3145732
  61.8 55.6 %all-to-all-start = ((bf16[4,640,256]{2,1,0:T(8,128)(2,1)}), bf16[4,640,256]{2,1,0:T(8,128)(2,1)S(1)}, u32[]{:S(2)}, u32[]{:S(2)}) async-start(bf16[4,640,256]{2,1,0:T(8,128)(2,1)} %pack.1), calls=%async_computation | async-start | bytes 2621440 | tf_op jit(solution)/shard_map/weight_columns/all_to_all | solution.py:29
  67.9 36.7 %collective-permute-start.3 = (bf16[128,2048]{1,0:T(8,128)(2,1)S(1)}, bf16[128,2048]{1,0:T(8,128)(2,1)S(1)}, u32[]{:S(2)}, u32[]{:S(2)}) collective-permute-start(bf16[128,2048]{1,0:T(8,128)(2,1)S(1)} %get-tuple-element.13), channel_id=1, source_target_pairs={{0,1},{1,0},{2,3},{3,2},{4,5},{5,4},{6,7},{7,6},{8,9},{9,8},{10,11... | collective-permute-start | bytes 1572872 | tf_op jit(solution)/shard_map/activations/ppermute | solution.py:33
  75.2 38.0 %collective-permute-start = (bf16[128,2048]{1,0:T(8,128)(2,1)}, bf16[128,2048]{1,0:T(8,128)(2,1)S(1)}, u32[]{:S(2)}, u32[]{:S(2)}) collective-permute-start(bf16[128,2048]{1,0:T(8,128)(2,1)} %get-tuple-element.11.b0), channel_id=1, source_target_pairs={{0,2},{1,3},{2,4},{3,5},{4,6},{5,7},{6,0},{7,1},{8,10},{9,11},{10,... | collective-permute-start | bytes 1572872 | tf_op jit(solution)/shard_map/activations/ppermute | solution.py:38
  79.2 38.2 %collective-permute-start.1 = (bf16[128,2048]{1,0:T(8,128)(2,1)}, bf16[128,2048]{1,0:T(8,128)(2,1)}, u32[]{:S(2)}, u32[]{:S(2)}) collective-permute-start(bf16[128,2048]{1,0:T(8,128)(2,1)} %get-tuple-element.11.b0), channel_id=1, source_target_pairs={{0,4},{1,5},{2,6},{3,7},{4,0},{5,1},{6,2},{7,3},{8,12},{9,13},{10,... | collective-permute-start | bytes 1572872 | tf_op jit(solution)/shard_map/activations/ppermute | solution.py:38
  83.8 33.6 %collective-permute-start.2 = (bf16[128,2048]{1,0:T(8,128)(2,1)}, bf16[128,2048]{1,0:T(8,128)(2,1)}, u32[]{:S(2)}, u32[]{:S(2)}) collective-permute-start(bf16[128,2048]{1,0:T(8,128)(2,1)} %get-tuple-element.11.b0), channel_id=1, source_target_pairs={{0,6},{1,7},{2,0},{3,1},{4,2},{5,3},{6,4},{7,5},{8,14},{9,15},{10,... | collective-permute-start | bytes 1572872 | tf_op jit(solution)/shard_map/activations/ppermute | solution.py:38
  104.6 24.6 %collective-permute-start.4 = (bf16[128,2048]{1,0:T(8,128)(2,1)S(1)}, bf16[128,2048]{1,0:T(8,128)(2,1)S(1)}, u32[]{:S(2)}, u32[]{:S(2)}) collective-permute-start(bf16[128,2048]{1,0:T(8,128)(2,1)S(1)} %collective-permute-done.3.b0), channel_id=1, source_target_pairs={{0,2},{1,3},{2,4},{3,5},{4,6},{5,7},{6,0},{7,1},{8,10},{9,11},{10,... | collective-permute-start | bytes 1572872 | tf_op jit(solution)/shard_map/far_activations/ppermute | solution.py:38
  108.6 20.6 %collective-permute-start.5 = (bf16[128,2048]{1,0:T(8,128)(2,1)S(1)}, bf16[128,2048]{1,0:T(8,128)(2,1)}, u32[]{:S(2)}, u32[]{:S(2)}) collective-permute-start(bf16[128,2048]{1,0:T(8,128)(2,1)S(1)} %collective-permute-done.3.b0), channel_id=1, source_target_pairs={{0,4},{1,5},{2,6},{3,7},{4,0},{5,1},{6,2},{7,3},{8,12},{9,13},{10,... | collective-permute-start | bytes 1572872 | tf_op jit(solution)/shard_map/far_activations/ppermute | solution.py:38
  113.2 0.8 copy-start.1
  114.0 15.2 %collective-permute-start.6 = (bf16[128,2048]{1,0:T(8,128)(2,1)S(1)}, bf16[128,2048]{1,0:T(8,128)(2,1)}, u32[]{:S(2)}, u32[]{:S(2)}) collective-permute-start(bf16[128,2048]{1,0:T(8,128)(2,1)S(1)} %collective-permute-done.3.b0), channel_id=1, source_target_pairs={{0,6},{1,7},{2,0},{3,1},{4,2},{5,3},{6,4},{7,5},{8,14},{9,15},{10,... | collective-permute-start | bytes 1572872 | tf_op jit(solution)/shard_map/far_activations/ppermute | solution.py:38
  117.4 1.0 copy-start.2
  120.5 16.9 %collective-permute-start.7 = (bf16[512,256]{1,0:T(8,128)(2,1)S(1)}, bf16[512,256]{1,0:T(8,128)(2,1)S(1)}, u32[]{:S(2)}, u32[]{:S(2)}) collective-permute-start(bf16[512,256]{1,0:T(8,128)(2,1)S(1)} %get-tuple-element.14), channel_id=1, source_target_pairs={{0,1},{1,0},{2,3},{3,2},{4,5},{5,4},{6,7},{7,6},{8,9},{9,8},{10,11... | collective-permute-start | bytes 786440 | tf_op jit(solution)/shard_map/keys/ppermute | solution.py:33
  139.3 16.9 %collective-permute-start.8 = (bf16[512,256]{1,0:T(8,128)(2,1)S(1)}, bf16[512,256]{1,0:T(8,128)(2,1)S(1)}, u32[]{:S(2)}, u32[]{:S(2)}) collective-permute-start(bf16[512,256]{1,0:T(8,128)(2,1)S(1)} %get-tuple-element.15), channel_id=1, source_target_pairs={{0,1},{1,0},{2,3},{3,2},{4,5},{5,4},{6,7},{7,6},{8,9},{9,8},{10,11... | collective-permute-start | bytes 786440 | tf_op jit(solution)/shard_map/keys/ppermute | solution.py:33
  157.9 29.6 %copy-start.7 = (f32[512,256]{1,0:T(8,128)S(1)}, f32[512,256]{1,0:T(8,128)}, u32[]{:S(2)}) copy-start(f32[512,256]{1,0:T(8,128)} %param.13) | copy-start | bytes 1572868
  157.9 29.6 %copy-start.8 = (bf16[512,256]{1,0:T(8,128)(2,1)S(1)}, bf16[512,256]{1,0:T(8,128)(2,1)}, u32[]{:S(2)}) copy-start(bf16[512,256]{1,0:T(8,128)(2,1)} %param.12) | copy-start | bytes 786436
  157.9 30.6 %all-to-all-start.1 = ((bf16[4,512,256]{2,1,0:T(8,128)(2,1)}), bf16[4,512,256]{2,1,0:T(8,128)(2,1)S(1)}, u32[]{:S(2)}, u32[]{:S(2)}) async-start(bf16[4,512,256]{2,1,0:T(8,128)(2,1)} %get-tuple-element.18), calls=%async_computation.1 | async-start | bytes 2097152 | tf_op jit(solution)/shard_map/gradient/all_to_all | solution.py:29
  161.5 9.4 %collective-permute-start.9 = (f32[8,128]{1,0:T(8,128)S(1)}, f32[8,128]{1,0:T(8,128)S(1)}, u32[]{:S(2)}, u32[]{:S(2)}) collective-permute-start(f32[8,128]{1,0:T(8,128)S(1)} %get-tuple-element.17), channel_id=1, source_target_pairs={{0,1},{1,0},{2,3},{3,2},{4,5},{5,4},{6,7},{7,6},{8,9},{9,8},{10,11... | collective-permute-start | bytes 12296 | tf_op jit(solution)/shard_map/gradient/ppermute | solution.py:33
  171.0 10.6 %collective-permute-start.12 = (f32[8,128]{1,0:T(8,128)S(1)}, f32[8,128]{1,0:T(8,128)S(1)}, u32[]{:S(2)}, u32[]{:S(2)}) collective-permute-start(f32[8,128]{1,0:T(8,128)S(1)} %add.18), channel_id=1, source_target_pairs={{0,6},{1,7},{2,0},{3,1},{4,2},{5,3},{6,4},{7,5},{8,14},{9,15},{10,... | collective-permute-start | bytes 12296 | tf_op jit(solution)/shard_map/gradient/ppermute | solution.py:38
  176.1 7.0 %collective-permute-start.11 = (f32[8,128]{1,0:T(8,128)S(1)}, f32[8,128]{1,0:T(8,128)S(1)}, u32[]{:S(2)}, u32[]{:S(2)}) collective-permute-start(f32[8,128]{1,0:T(8,128)S(1)} %add.18), channel_id=1, source_target_pairs={{0,4},{1,5},{2,6},{3,7},{4,0},{5,1},{6,2},{7,3},{8,12},{9,13},{10,... | collective-permute-start | bytes 12296 | tf_op jit(solution)/shard_map/gradient/ppermute | solution.py:38
  178.8 6.7 %collective-permute-start.10 = (f32[8,128]{1,0:T(8,128)S(1)}, f32[8,128]{1,0:T(8,128)S(1)}, u32[]{:S(2)}, u32[]{:S(2)}) collective-permute-start(f32[8,128]{1,0:T(8,128)S(1)} %add.18), channel_id=1, source_target_pairs={{0,2},{1,3},{2,4},{3,5},{4,6},{5,7},{6,0},{7,1},{8,10},{9,11},{10,... | collective-permute-start | bytes 12296 | tf_op jit(solution)/shard_map/gradient/ppermute | solution.py:38
  185.5 2.9 %copy-start.6 = (s32[8]{0:T(128)S(1)}, s32[8]{0:T(128)}, u32[]{:S(2)}) copy-start(s32[8]{0:T(128)} %order_ref.1) | copy-start | bytes 100
  188.4 2.8 %copy-start.4 = (bf16[512,256]{1,0:T(8,128)(2,1)}, bf16[512,256]{1,0:T(8,128)(2,1)S(1)}, u32[]{:S(2)}) copy-start(bf16[512,256]{1,0:T(8,128)(2,1)S(1)} %get-tuple-element.19.global_ref) | copy-start | bytes 786436
Sparse Core Ops, SparseCore 0:
  10.1 47.7 all-gather.3
  60.7 55.2 all-gather.5

commit v4 on v3

v4 whole, which is shorter than its diff:
```python
import math

import jax
import jax.numpy as jnp
from jax import lax
from jax.experimental import pallas as pl
from jax.experimental.pallas import tpu as pltpu
from jax.sharding import PartitionSpec as P

D = 4096
HEAD = 128
FRAG_HEADS = 2
KV = 1024
NX = 4
COLS = KV // NX
FACTOR = 1.0 / math.sqrt(D)
F32 = jnp.float32
BF16 = jnp.bfloat16
SDS = jax.ShapeDtypeStruct
SMEM = pl.BlockSpec(memory_space=pltpu.SMEM)
PARAMS = pltpu.CompilerParams(vmem_limit_bytes=16 * 1024 * 1024)

X_GROUPS = [[x * 2 + h for x in range(NX)] for h in range(2)]
Z_GROUPS = [[z * 8 + l for z in range(8)] for l in range(8)]
Y_GROUPS = [[z * 8 + y * 2 + core for y in range(4)] for z in range(8) for core in range(2)]


def exchange(blocks, axis, groups):
    return lax.all_to_all(blocks, axis, 0, 0, axis_index_groups=groups, tiled=True)


def flip(block, mask):
    return lax.ppermute(block, "fsdp", [(i, i ^ mask) for i in range(8)])


def rotate(blocks):
    moves = [[(x * 2 + h, (x + d) % NX * 2 + h) for x in range(NX) for h in range(2)] for d in range(NX)]
    return [blocks[0]] + [lax.ppermute(blocks[d], "fsdp", moves[d]) for d in (1, 2, 3)]


def gather(block):
    return rotate([block] * NX)


def pack_kernel(place_ref, tokens_ref, weight_ref, targets_ref, other_ref, *message_refs):
    half, x = place_ref[0], place_ref[1]
    floated = tokens_ref[...].astype(F32)
    scale = lax.rsqrt(jnp.mean(floated * floated, axis=-1, keepdims=True) + 1e-06)
    for block in range(NX):
        lanes = slice(block * 512, (block + 1) * 512)
        for refs, side in ((message_refs, half), ((other_ref,), 1 - half)):
            start = pl.multiple_of((2 * block + side) * 512, 512)
            piece = (tokens_ref[:, pl.ds(start, 512)].astype(F32) * scale).astype(BF16)
            for ref in refs:
                ref[:128, lanes] = piece
    for d, ref in enumerate(message_refs):
        columns = pl.ds(pl.multiple_of(lax.rem(x + d, NX) * COLS, COLS), COLS)
        for j in range(8):
            lanes = slice(j * COLS, (j + 1) * COLS)
            ref[128:192, lanes] = weight_ref[0, j * 64 : (j + 1) * 64, columns]
            ref[192:, lanes] = targets_ref[j * 16 : (j + 1) * 16, columns]


def raw_keys(blocks, weight):
    lhs = jnp.concatenate([b[:128] for b in blocks], axis=0)
    return jnp.dot(lhs, weight, preferred_element_type=F32) * FACTOR


def near_kernel(place_ref, m0, m1, m2, m3, part_ref, sent_ref, weight_ref, turned_ref):
    messages = (m0, m1, m2, m3)
    for d, m in enumerate(messages):
        source = lax.rem(place_ref[1] - d + NX, NX)
        for j in range(8):
            rows = pl.ds(pl.multiple_of(source * 512 + j * 64, 64), 64)
            weight_ref[rows, :] = m[128:192, j * COLS : (j + 1) * COLS]
    keys = raw_keys(messages, weight_ref[...])
    for d, m in enumerate(messages):
        for j in range(8):
            rows = slice(d * 128 + j * 16, d * 128 + (j + 1) * 16)
            part = keys[rows] - m[192:, j * COLS : (j + 1) * COLS].astype(F32)
            part_ref[rows] = part
            sent_ref[rows] = part.astype(BF16)
        turned_ref[:, d * 128 : (d + 1) * 128] = m[:128].T


def far_kernel(*refs):
    sources, (sent_ref, residual_ref, delta_sum_ref), held, done = refs[:7], refs[7:10], refs[10:17], refs[17]
    fetches = [pltpu.make_async_copy(s, h, done.at[i]) for i, (s, h) in enumerate(zip(sources, held))]
    for fetch in fetches:
        fetch.start()
    for fetch in fetches[:6]:
        fetch.wait()
    keys = raw_keys(held[:4], held[4][...])
    sent_ref[...] = keys.astype(BF16)
    residual_ref[...] = (keys + held[5][...].astype(F32)).astype(BF16)
    fetches[6].wait()
    for rows in (slice(0, 256), slice(256, 512)):
        delta_sum_ref[rows] = jnp.sum(held[6][:, rows].astype(F32), axis=0).astype(BF16)


def turn_kernel(b0, b1, b2, b3, out_ref):
    for d, b in enumerate((b0, b1, b2, b3)):
        out_ref[:, d * 128 : (d + 1) * 128] = b[:128].T


def far_gradient_kernel(turned_ref, residual_ref, out_ref):
    out_ref[...] = jnp.dot(turned_ref[...], residual_ref[...], preferred_element_type=F32)


def near_gradient_kernel(turned_ref, part_ref, rest_ref, far_ref, out_ref, squares_ref):
    residual = (part_ref[...] + rest_ref[...].astype(F32)).astype(BF16)
    squares = jnp.zeros((8, COLS), F32)
    for x in range(NX):
        rows = slice(x * 512, (x + 1) * 512)
        near = jnp.dot(turned_ref[rows], residual, preferred_element_type=F32)
        gradient = (near + far_ref[rows]) * FACTOR
        out_ref[x, :512] = gradient.astype(BF16)
        out_ref[x, 512:] = jnp.zeros((16, COLS), BF16)
        squares += jnp.sum((gradient * gradient).reshape(64, 8, COLS), axis=0)
    squares_ref[...] = squares[:, :128] + squares[:, 128:]


def embed_kernel(squares_ref, _, out_ref):
    squares = squares_ref[...]
    high = squares.astype(BF16).astype(F32)
    middle = (squares - high).astype(BF16).astype(F32)
    low = squares - high - middle
    upper = jnp.concatenate([high, middle], axis=1)
    lower = jnp.concatenate([low, jnp.zeros((8, 128), F32)], axis=1)
    rows = jnp.concatenate([upper, lower], axis=0).astype(BF16)
    for x in range(NX):
        out_ref[x] = rows


def embed(squares, gradient):
    return pl.pallas_call(
        embed_kernel,
        grid=(1,),
        in_specs=[pl.BlockSpec((8, 128), lambda i: (0, 0)), pl.BlockSpec(memory_space=pl.ANY)],
        out_specs=pl.BlockSpec((NX, 16, COLS), lambda i: (0, 32, 0)),
        out_shape=SDS((NX, 528, COLS), BF16),
        input_output_aliases={1: 0},
        compiler_params=PARAMS,
        name="embed",
    )(squares, gradient)


def sum_kernel(blocks_ref, _, out_ref):
    out_ref[...] = jnp.sum(blocks_ref[...].astype(F32), axis=0)


def sum_blocks(blocks, later_than):
    return pl.pallas_call(
        sum_kernel,
        in_specs=[pl.BlockSpec(memory_space=pltpu.VMEM), pl.BlockSpec(memory_space=pl.ANY)],
        out_specs=pl.BlockSpec(memory_space=pltpu.VMEM),
        out_shape=SDS((512, 256), F32),
        compiler_params=PARAMS,
        name="sum_blocks",
    )(blocks, later_than)


def step_kernel(order_ref, squares_ref, rows_ref, weight_ref, global_ref, out_ref, new_ref):
    total = jnp.sum(squares_ref[...].astype(F32), axis=0)
    total = jnp.sum(total, axis=(0, 1), keepdims=True)
    rate = 0.25 * lax.rsqrt(total / (D * KV) + 1e-06)
    for x in range(NX):
        columns = slice(x * COLS, (x + 1) * COLS)
        weight = weight_ref[0, :, columns].astype(F32)
        new_ref[:, columns] = weight - rows_ref[x].astype(F32) * rate
    for slot in range(FRAG_HEADS):
        at = pl.ds(pl.multiple_of(order_ref[slot] * HEAD, HEAD), HEAD)
        incoming = global_ref[:, slot * HEAD : (slot + 1) * HEAD].astype(F32)
        new_ref[:, at] = 0.5 * new_ref[:, at] + 0.5 * incoming
    out_ref[0] = new_ref[...].astype(BF16)


def step(order, rows, weight, new_global):
    return pl.pallas_call(
        step_kernel,
        grid=(4,),
        in_specs=[
            SMEM,
            pl.BlockSpec((NX, 16, COLS), lambda i: (0, 32, 0)),
            pl.BlockSpec((NX, 128, COLS), lambda i: (0, i, 0)),
            pl.BlockSpec((1, 128, KV), lambda i: (0, i, 0)),
            pl.BlockSpec((128, COLS), lambda i: (i, 0)),
        ],
        out_specs=pl.BlockSpec((1, 128, KV), lambda i: (0, i, 0)),
        out_shape=SDS((1, 512, KV), BF16),
        scratch_shapes=[pltpu.VMEM((128, KV), F32)],
        compiler_params=PARAMS,
        name="step",
    )(order, rows, rows, weight, new_global)


def call(kernel, outs, *args, scalars=0, hbm=0, scratch=(), vmem_mib=16, flops=0):
    vmem = len(args) - scalars - hbm
    return pl.pallas_call(
        kernel,
        in_specs=[SMEM] * scalars
        + [pl.BlockSpec(memory_space=pltpu.VMEM)] * vmem
        + [pl.BlockSpec(memory_space=pltpu.HBM)] * hbm,
        scratch_shapes=scratch,
        out_specs=jax.tree.map(lambda _: pl.BlockSpec(memory_space=pltpu.VMEM), outs),
        out_shape=outs,
        compiler_params=pltpu.CompilerParams(vmem_limit_bytes=vmem_mib << 20),
        cost_estimate=pl.CostEstimate(flops=flops, bytes_accessed=4 << 20, transcendentals=0),
        name=kernel.__name__.removesuffix("_kernel"),
    )(*args)


def body(tokens, targets, local_weights, pending_delta, frag_order, global_frag, outer_momentum):
    index = lax.axis_index("fsdp")
    place = jnp.stack([lax.rem(index, 2), lax.div(index, 2)]).astype(jnp.int32)
    dot_flops = 2 * 512 * 2048 * COLS
    tall = (512, COLS)

    with jax.named_scope("activations"):
        other, *messages = call(
            pack_kernel,
            (SDS((128, 2048), BF16),) + (SDS((208, 2048), BF16),) * NX,
            place, tokens, local_weights, targets, scalars=1,
        )
        arrived = flip(other, 1)
        near = rotate(messages)
        far = gather(arrived)

    with jax.named_scope("near_keys"):
        near_part, near_sent, columns, near_turned = call(
            near_kernel,
            (SDS(tall, F32), SDS(tall, BF16), SDS((2048, COLS), BF16), SDS((2048, 512), BF16)),
            place, *near, scalars=1, flops=dot_flops,
        )
        far_rest = flip(near_sent, 1)

    with jax.named_scope("far_keys"):
        by_z = lax.all_gather(pending_delta[0], "rep", axis_index_groups=Z_GROUPS)
        far_sent, far_residual, delta_sum = call(
            far_kernel,
            (SDS(tall, BF16), SDS(tall, BF16), SDS((512, 256), BF16)),
            *far, columns, far_rest, by_z, flops=dot_flops, hbm=7, vmem_mib=58,
            scratch=[pltpu.VMEM((128, 2048), BF16)] * NX
            + [pltpu.VMEM((2048, COLS), BF16), pltpu.VMEM(tall, BF16), pltpu.VMEM((8, 512, 256), BF16)]
            + [pltpu.SemaphoreType.DMA((7,))],
        )
        by_y = lax.all_gather(delta_sum, "rep", axis_index_groups=Y_GROUPS)
        near_rest = flip(far_sent, 1)
        far_turned = call(turn_kernel, SDS((2048, 512), BF16), *far)

    with jax.named_scope("gradient"):
        far_gradient = call(
            far_gradient_kernel, SDS((2048, COLS), F32), far_turned, far_residual, flops=dot_flops
        )
        gradient, squares = call(
            near_gradient_kernel,
            (SDS((NX, 528, COLS), BF16), SDS((8, 128), F32)),
            near_turned, near_part, near_rest, far_gradient, flops=dot_flops,
        )
        squares = squares + flip(squares, 1)
        embedded = embed(squares, gradient)
        by_rows = exchange(embedded, "fsdp", X_GROUPS)

    with jax.named_scope("outer_sum"):
        core_sum = sum_blocks(by_y, embedded)
        total = core_sum + lax.ppermute(core_sum, "rep", [(i, i ^ 1) for i in range(64)])
        mean = total / lax.axis_size("rep")
        new_momentum = 0.9 * outer_momentum + mean
        new_global = (global_frag.astype(F32) - 0.7 * (mean + 0.9 * new_momentum)).astype(BF16)

    with jax.named_scope("step"):
        new_weights = step(frag_order, by_rows, local_weights, new_global)
    return (new_weights, new_global, new_momentum)


def solution(mesh):
    placed = (
        P(("rep", "fsdp"), None),
        P(("rep", "fsdp"), None),
        P("rep", "fsdp", None),
        P("rep", "fsdp", None),
        P(),
        P("fsdp", None),
        P("fsdp", None),
    )
    return jax.shard_map(
        body,
        mesh=mesh,
        in_specs=placed,
        out_specs=(P("rep", "fsdp", None), P("fsdp", None), P("fsdp", None)),
        check_vma=False,
    )
```

time: 199 us -> 163 us (0.82)
  the two profiles are of different devices: /device:TPU:64 before, /device:TPU:6 now
where the time goes in v4:
time: 163 us; the launch traced here: 160 us
  waiting for transfers between devices  66.1 us (41%)
  starting transfers between devices  52 us (32%)
  between operations  14.3 us (9%)
  Pallas kernels  12.8 us (8%)
  local copies, waits for them, and re-layouts  12.4 us (8%)
  other arithmetic  2.17 us (1%)
    ppermute x4, waiting for transfers between devices, flip(): return lax.ppermute(block, 'fsdp', [(i, i ^ mask) for i in range(8)])  29.9 us
    ppermute x6, starting transfers between devices, rotate(): lax.ppermute(blocks[d], 'fsdp', moves[d])  22.6 us
    ppermute x4, starting transfers between devices, flip(): return lax.ppermute(block, 'fsdp', [(i, i ^ mask) for i in range(8)])  22.4 us
    all_gather x1, waiting for transfers between devices, body(): by_y = lax.all_gather(delta_sum, 'rep', axis_index_groups=Y_GROUPS)  16 us
    unnamed x42, local copies, waits for them, and re-layouts  12.4 us
    all_to_all x1, waiting for transfers between devices, exchange(): lax.all_to_all(blocks, axis, 0, 0, axis_index_groups=groups, tiled=True)  11.9 us
    pallas_call x6, Pallas kernels, call(): pl.pallas_call(kernel, in_specs=[SMEM] * scalars + [pl.BlockSpec(memory_s...  9.29 us
    ppermute x6, waiting for transfers between devices, rotate(): lax.ppermute(blocks[d], 'fsdp', moves[d])  7.6 us
  transfers between devices with their start and end apart: 14, of which 9 were waited for; matrix products, arithmetic and copies ran while one was open for 1% of the time, Pallas kernels for 4%

profile of v4, /device:TPU:6, one launch (start us, length us, event | category | flops | bytes accessed | tf_op | source)
XLA Modules:
  0.0 159.8 jit_solution(653792421131226254)
XLA Ops:
  7.2 0.0 all-gather.4.cloned.1.call-start
  7.2 0.7 all-gather.4.cloned.1.call-update
  7.9 0.0 all-gather.6.cloned.1.call-start
  7.9 0.1 pad_add_fusion.place_ref
  8.0 1.2 copy-done
  9.3 1.2 copy-done.11
  10.5 0.9 copy-done.16
  11.4 1.2 pack.1
  12.6 7.8 %collective-permute-start = (bf16[208,2048]{1,0:T(8,128)(2,1)S(1)}, bf16[208,2048]{1,0:T(8,128)(2,1)S(1)}, u32[]{:S(2)}, u32[]{:S(2)}) collective-permute-start(bf16[208,2048]{1,0:T(8,128)(2,1)S(1)} %get-tuple-element.18), channel_id=1, source_target_pairs={{0,2},{1,3},{2,4},{3,5},{4,6},{5,7},{6,0},{7,1},{8,10},{9,11},{10,... | collective-permute-start | bytes 2555912 | tf_op jit(solution)/shard_map/activations/ppermute | solution.py:38
  20.4 1.9 %collective-permute-start.1 = (bf16[208,2048]{1,0:T(8,128)(2,1)S(1)}, bf16[208,2048]{1,0:T(8,128)(2,1)S(1)}, u32[]{:S(2)}, u32[]{:S(2)}) collective-permute-start(bf16[208,2048]{1,0:T(8,128)(2,1)S(1)} %get-tuple-element.19), channel_id=1, source_target_pairs={{0,4},{1,5},{2,6},{3,7},{4,0},{5,1},{6,2},{7,3},{8,12},{9,13},{10,... | collective-permute-start | bytes 2555912 | tf_op jit(solution)/shard_map/activations/ppermute | solution.py:38
  22.3 2.8 %collective-permute-start.2 = (bf16[208,2048]{1,0:T(8,128)(2,1)S(1)}, bf16[208,2048]{1,0:T(8,128)(2,1)S(1)}, u32[]{:S(2)}, u32[]{:S(2)}) collective-permute-start(bf16[208,2048]{1,0:T(8,128)(2,1)S(1)} %get-tuple-element.20), channel_id=1, source_target_pairs={{0,6},{1,7},{2,0},{3,1},{4,2},{5,3},{6,4},{7,5},{8,14},{9,15},{10,... | collective-permute-start | bytes 2555912 | tf_op jit(solution)/shard_map/activations/ppermute | solution.py:38
  25.1 3.9 %collective-permute-start.3 = (bf16[128,2048]{1,0:T(8,128)(2,1)S(1)}, bf16[128,2048]{1,0:T(8,128)(2,1)S(1)}, u32[]{:S(2)}, u32[]{:S(2)}) collective-permute-start(bf16[128,2048]{1,0:T(8,128)(2,1)S(1)} %get-tuple-element.23), channel_id=1, source_target_pairs={{0,1},{1,0},{2,3},{3,2},{4,5},{5,4},{6,7},{7,6},{8,9},{9,8},{10,11... | collective-permute-start | bytes 1572872 | tf_op jit(solution)/shard_map/activations/ppermute | solution.py:33
  29.0 21.9 %collective-permute-done.3.refs_0_.b0 = bf16[128,2048]{1,0:T(8,128)(2,1)S(1)} collective-permute-done((bf16[128,2048]{1,0:T(8,128)(2,1)S(1)}, bf16[128,2048]{1,0:T(8,128)(2,1)S(1)}, u32[]{:S(2)}, u32[]{:S(2)}) %collective-permute-start.3) | collective-permute-done | bytes 524320 | tf_op jit(solution)/shard_map/activations/ppermute | solution.py:33
  50.9 4.8 %collective-permute-start.4 = (bf16[128,2048]{1,0:T(8,128)(2,1)S(1)}, bf16[128,2048]{1,0:T(8,128)(2,1)S(1)}, u32[]{:S(2)}, u32[]{:S(2)}) collective-permute-start(bf16[128,2048]{1,0:T(8,128)(2,1)S(1)} %collective-permute-done.3.refs_0_.b0), channel_id=1, source_target_pairs={{0,2},{1,3},{2,4},{3,5},{4,6},{5,7},{6,0},{7,1},{8,10},{9,11},{10,... | collective-permute-start | bytes 1572872 | tf_op jit(solution)/shard_map/activations/ppermute | solution.py:38
  55.7 1.9 %collective-permute-start.5 = (bf16[128,2048]{1,0:T(8,128)(2,1)S(1)}, bf16[128,2048]{1,0:T(8,128)(2,1)S(1)}, u32[]{:S(2)}, u32[]{:S(2)}) collective-permute-start(bf16[128,2048]{1,0:T(8,128)(2,1)S(1)} %collective-permute-done.3.refs_0_.b0), channel_id=1, source_target_pairs={{0,4},{1,5},{2,6},{3,7},{4,0},{5,1},{6,2},{7,3},{8,12},{9,13},{10,... | collective-permute-start | bytes 1572872 | tf_op jit(solution)/shard_map/activations/ppermute | solution.py:38
  57.7 3.3 %collective-permute-start.6 = (bf16[128,2048]{1,0:T(8,128)(2,1)S(1)}, bf16[128,2048]{1,0:T(8,128)(2,1)S(1)}, u32[]{:S(2)}, u32[]{:S(2)}) collective-permute-start(bf16[128,2048]{1,0:T(8,128)(2,1)S(1)} %collective-permute-done.3.refs_0_.b0), channel_id=1, source_target_pairs={{0,6},{1,7},{2,0},{3,1},{4,2},{5,3},{6,4},{7,5},{8,14},{9,15},{10,... | collective-permute-start | bytes 1572872 | tf_op jit(solution)/shard_map/activations/ppermute | solution.py:38
  61.0 0.8 collective-permute-done.2.m3
  61.8 1.4 near.1
  63.2 1.0 copy-done.13
  64.2 0.8 copy-done.14
  65.0 7.5 %collective-permute-start.7 = (bf16[512,256]{1,0:T(8,128)(2,1)S(1)}, bf16[512,256]{1,0:T(8,128)(2,1)S(1)}, u32[]{:S(2)}, u32[]{:S(2)}) collective-permute-start(bf16[512,256]{1,0:T(8,128)(2,1)S(1)} %get-tuple-element.25), channel_id=1, source_target_pairs={{0,1},{1,0},{2,3},{3,2},{4,5},{5,4},{6,7},{7,6},{8,9},{9,8},{10,11... | collective-permute-start | bytes 786440 | tf_op jit(solution)/shard_map/near_keys/ppermute | solution.py:33
  72.5 1.2 collective-permute-done.5.refs_2_.b2
  73.8 5.5 %collective-permute-done.6.refs_3_.b3 = bf16[128,2048]{1,0:T(8,128)(2,1)S(1)} collective-permute-done((bf16[128,2048]{1,0:T(8,128)(2,1)S(1)}, bf16[128,2048]{1,0:T(8,128)(2,1)S(1)}, u32[]{:S(2)}, u32[]{:S(2)}) %collective-permute-start.6) | collective-permute-done | bytes 524320 | tf_op jit(solution)/shard_map/activations/ppermute | solution.py:38
  79.4 0.8 copy-done.8
  80.2 2.3 %collective-permute-done.7.refs_5_ = bf16[512,256]{1,0:T(8,128)(2,1)S(1)} collective-permute-done((bf16[512,256]{1,0:T(8,128)(2,1)S(1)}, bf16[512,256]{1,0:T(8,128)(2,1)S(1)}, u32[]{:S(2)}, u32[]{:S(2)}) %collective-permute-start.7) | collective-permute-done | bytes 262176 | tf_op jit(solution)/shard_map/near_keys/ppermute | solution.py:33
  82.5 0.7 copy-done.20
  83.2 3.7 %far.1 = (bf16[512,256]{1,0:T(8,128)(2,1)}, bf16[512,256]{1,0:T(8,128)(2,1)}, bf16[512,256]{1,0:T(8,128)(2,1)}) custom-call(bf16[128,2048]{1,0:T(8,128)(2,1)} %copy-done.2, bf16[128,2048]{1,0:T(8,128)(2,1)} %copy-done.4, bf16[128,2048]{1,0:T(8,128)(2,1)} %copy-done.6, bf16[128,2048]{1,0:T(8,128)(2,1)} %copy-done.8, bf16[2048,256]{1,0:T(8,128)(2,1)} %copy-done.13, ...), custom_call_target="tpu_custom_call" | custom-call | flops 536870912 | bytes 4194304 | tf_op jit(solution)/shard_map/far_keys/far/pallas_call | solution.py:199
  86.9 5.6 %collective-permute-start.8 = (bf16[512,256]{1,0:T(8,128)(2,1)}, bf16[512,256]{1,0:T(8,128)(2,1)S(1)}, u32[]{:S(2)}, u32[]{:S(2)}) collective-permute-start(bf16[512,256]{1,0:T(8,128)(2,1)} %get-tuple-element.26), channel_id=1, source_target_pairs={{0,1},{1,0},{2,3},{3,2},{4,5},{5,4},{6,7},{7,6},{8,9},{9,8},{10,11... | collective-permute-start | bytes 786440 | tf_op jit(solution)/shard_map/far_keys/ppermute | solution.py:33
  92.5 1.0 copy-done.3
  93.6 1.0 copy-done.5
  94.6 1.0 copy-done.7
  95.6 1.0 copy-done.9
  96.7 0.6 turn.1.turned_ref
  97.3 0.4 copy-done.17
  97.6 0.7 far_gradient.1.far_ref
  98.3 1.7 %collective-permute-done.8.rest_ref = bf16[512,256]{1,0:T(8,128)(2,1)S(1)} collective-permute-done((bf16[512,256]{1,0:T(8,128)(2,1)}, bf16[512,256]{1,0:T(8,128)(2,1)S(1)}, u32[]{:S(2)}, u32[]{:S(2)}) %collective-permute-start.8) | collective-permute-done | bytes 262176 | tf_op jit(solution)/shard_map/far_keys/ppermute | solution.py:33
  100.0 1.8 %near_gradient.1 = (bf16[4,528,256]{2,1,0:T(8,128)(2,1)}, f32[8,128]{1,0:T(8,128)S(1)}) custom-call(bf16[2048,512]{1,0:T(8,128)(2,1)S(1)} %get-tuple-element.21.turned_ref, f32[512,256]{1,0:T(8,128)S(1)} %copy-done.15, bf16[512,256]{1,0:T(8,128)(2,1)S(1)} %collective-permute-done.8.rest_ref, f32[2048,256]{1,0:T(8,128)S(1)} %far_gradient.1.far_ref), custom_call_target="tpu_custom_call" | custom-call | flops 536870912 | bytes 4194304 | tf_op jit(solution)/shard_map/gradient/near_gradient/pallas_call | solution.py:199
  101.8 5.4 %collective-permute-start.9 = (f32[8,128]{1,0:T(8,128)S(1)}, f32[8,128]{1,0:T(8,128)S(1)}, u32[]{:S(2)}, u32[]{:S(2)}) collective-permute-start(f32[8,128]{1,0:T(8,128)S(1)} %get-tuple-element.28), channel_id=1, source_target_pairs={{0,1},{1,0},{2,3},{3,2},{4,5},{5,4},{6,7},{7,6},{8,9},{9,8},{10,11... | collective-permute-start | bytes 12296 | tf_op jit(solution)/shard_map/gradient/ppermute | solution.py:33
  107.2 4.0 %collective-permute-done.9 = f32[8,128]{1,0:T(8,128)S(1)} collective-permute-done((f32[8,128]{1,0:T(8,128)S(1)}, f32[8,128]{1,0:T(8,128)S(1)}, u32[]{:S(2)}, u32[]{:S(2)}) %collective-permute-start.9) | collective-permute-done | bytes 4128 | tf_op jit(solution)/shard_map/gradient/ppermute | solution.py:33
  111.2 0.6 embed.1._
  111.8 16.0 %all-gather.6.cloned.1.call-done = bf16[2048,256]{1,0:T(8,128)(2,1)} async-done(((bf16[512,256]{1,0:T(8,128)(2,1)}), bf16[2048,256]{1,0:T(8,128)(2,1)}) %all-gather.6.cloned.1.call-update) | async-done | bytes 1048592 | tf_op jit(solution)/shard_map/far_keys/all_gather | solution.py:247
  127.8 1.2 copy-done.12
  129.0 0.1 sum_blocks.1
  129.2 2.1 %collective-permute-start.10 = (f32[512,256]{1,0:T(8,128)S(1)}, f32[512,256]{1,0:T(8,128)}, u32[]{:S(2)}, u32[]{:S(2)}) collective-permute-start(f32[512,256]{1,0:T(8,128)S(1)} %sum_blocks.1), channel_id=1, source_target_pairs={{0,8},{8,0},{16,24},{24,16},{32,40},{40,32},{48,56},{56,48},{64,72... | collective-permute-start | bytes 1572872 | tf_op jit(solution)/shard_map/outer_sum/ppermute | solution.py:266
  131.2 4.8 %all-to-all-start = ((bf16[4,528,256]{2,1,0:T(8,128)(2,1)}), bf16[4,528,256]{2,1,0:T(8,128)(2,1)S(1)}, u32[]{:S(2)}, u32[]{:S(2)}) async-start(bf16[4,528,256]{2,1,0:T(8,128)(2,1)} %embed.1._), calls=%async_computation | async-start | bytes 2162688 | tf_op jit(solution)/shard_map/gradient/all_to_all | solution.py:29
  136.1 2.1 %subtract_convert_fusion = (bf16[512,256]{1,0:T(8,128)(2,1)S(1)}, f32[512,256]{1,0:T(8,128)}) fusion(bf16[512,256]{1,0:T(8,128)(2,1)} %param.12, f32[512,256]{1,0:T(8,128)S(1)} %sum_blocks.1, f32[512,256]{1,0:T(8,128)} %collective-permute-done.10, f32[512,256]{1,0:T(8,128)S(1)} %copy-done.19), kind=kLoop, calls=%fused_computation | loop fusion | flops 1310720 | bytes 2621440 | tf_op jit(solution)/shard_map/outer_sum/convert_element_type | solution.py:269
  138.2 11.9 %all-to-all-done.squares_ref.rows_ref = bf16[4,528,256]{2,1,0:T(8,128)(2,1)S(1)} async-done(((bf16[4,528,256]{2,1,0:T(8,128)(2,1)}), bf16[4,528,256]{2,1,0:T(8,128)(2,1)S(1)}, u32[]{:S(2)}, u32[]{:S(2)}) %all-to-all-start) | async-done | bytes 1081376 | tf_op jit(solution)/shard_map/gradient/all_to_all | solution.py:29
  150.1 2.8 %step.1 = bf16[1,512,1024]{2,1,0:T(8,128)(2,1)} custom-call(s32[8]{0:T(128)S(1)} %copy-done.18, bf16[4,528,256]{2,1,0:T(8,128)(2,1)S(1)} %all-to-all-done.squares_ref.rows_ref, bf16[4,528,256]{2,1,0:T(8,128)(2,1)S(1)} %all-to-all-done.squares_ref.rows_ref, bf16[1,512,1024]{2,1,0:T(8,128)(2,1)S(1)} %copy-done.1, bf16[512,256]{1,0:T(8,128)(2,1)S(1)} %get-tuple-element.31.global_ref), custom_call_target="tpu_custom_call" | custom-call | tf_op jit(solution)/shard_map/step/step/pallas_call | solution.py:179
  (36 shorter events, 0.1 us)
Async XLA Ops:
  7.2 75.3 %all-gather.4.cloned.1.call-start = ((), (), s32[]{:S(2)}) async-start(), calls=%async_computation.1 | async-start | bytes 2359296 | tf_op jit(solution)/shard_map/far_keys/all_gather | solution.py:238
  7.9 119.9 %all-gather.6.cloned.1.call-start = ((), (), s32[]{:S(2)}) async-start(), calls=%async_computation.2 | async-start | bytes 1310720 | tf_op jit(solution)/shard_map/far_keys/all_gather | solution.py:247
  8.0 1.2 copy-start
  9.2 1.2 copy-start.11
  10.5 0.9 copy-start.16
  12.6 45.1 %collective-permute-start = (bf16[208,2048]{1,0:T(8,128)(2,1)S(1)}, bf16[208,2048]{1,0:T(8,128)(2,1)S(1)}, u32[]{:S(2)}, u32[]{:S(2)}) collective-permute-start(bf16[208,2048]{1,0:T(8,128)(2,1)S(1)} %get-tuple-element.18), channel_id=1, source_target_pairs={{0,2},{1,3},{2,4},{3,5},{4,6},{5,7},{6,0},{7,1},{8,10},{9,11},{10,... | collective-permute-start | bytes 2555912 | tf_op jit(solution)/shard_map/activations/ppermute | solution.py:38
  20.4 40.6 %collective-permute-start.1 = (bf16[208,2048]{1,0:T(8,128)(2,1)S(1)}, bf16[208,2048]{1,0:T(8,128)(2,1)S(1)}, u32[]{:S(2)}, u32[]{:S(2)}) collective-permute-start(bf16[208,2048]{1,0:T(8,128)(2,1)S(1)} %get-tuple-element.19), channel_id=1, source_target_pairs={{0,4},{1,5},{2,6},{3,7},{4,0},{5,1},{6,2},{7,3},{8,12},{9,13},{10,... | collective-permute-start | bytes 2555912 | tf_op jit(solution)/shard_map/activations/ppermute | solution.py:38
  22.3 39.5 %collective-permute-start.2 = (bf16[208,2048]{1,0:T(8,128)(2,1)S(1)}, bf16[208,2048]{1,0:T(8,128)(2,1)S(1)}, u32[]{:S(2)}, u32[]{:S(2)}) collective-permute-start(bf16[208,2048]{1,0:T(8,128)(2,1)S(1)} %get-tuple-element.20), channel_id=1, source_target_pairs={{0,6},{1,7},{2,0},{3,1},{4,2},{5,3},{6,4},{7,5},{8,14},{9,15},{10,... | collective-permute-start | bytes 2555912 | tf_op jit(solution)/shard_map/activations/ppermute | solution.py:38
  25.1 25.8 %collective-permute-start.3 = (bf16[128,2048]{1,0:T(8,128)(2,1)S(1)}, bf16[128,2048]{1,0:T(8,128)(2,1)S(1)}, u32[]{:S(2)}, u32[]{:S(2)}) collective-permute-start(bf16[128,2048]{1,0:T(8,128)(2,1)S(1)} %get-tuple-element.23), channel_id=1, source_target_pairs={{0,1},{1,0},{2,3},{3,2},{4,5},{5,4},{6,7},{7,6},{8,9},{9,8},{10,11... | collective-permute-start | bytes 1572872 | tf_op jit(solution)/shard_map/activations/ppermute | solution.py:33
  50.9 31.6 %copy-start.2 = (bf16[128,2048]{1,0:T(8,128)(2,1)}, bf16[128,2048]{1,0:T(8,128)(2,1)S(1)}, u32[]{:S(2)}) copy-start(bf16[128,2048]{1,0:T(8,128)(2,1)S(1)} %collective-permute-done.3.refs_0_.b0) | copy-start | bytes 1572868
  50.9 21.6 %collective-permute-start.4 = (bf16[128,2048]{1,0:T(8,128)(2,1)S(1)}, bf16[128,2048]{1,0:T(8,128)(2,1)S(1)}, u32[]{:S(2)}, u32[]{:S(2)}) collective-permute-start(bf16[128,2048]{1,0:T(8,128)(2,1)S(1)} %collective-permute-done.3.refs_0_.b0), channel_id=1, source_target_pairs={{0,2},{1,3},{2,4},{3,5},{4,6},{5,7},{6,0},{7,1},{8,10},{9,11},{10,... | collective-permute-start | bytes 1572872 | tf_op jit(solution)/shard_map/activations/ppermute | solution.py:38
  55.7 18.1 %collective-permute-start.5 = (bf16[128,2048]{1,0:T(8,128)(2,1)S(1)}, bf16[128,2048]{1,0:T(8,128)(2,1)S(1)}, u32[]{:S(2)}, u32[]{:S(2)}) collective-permute-start(bf16[128,2048]{1,0:T(8,128)(2,1)S(1)} %collective-permute-done.3.refs_0_.b0), channel_id=1, source_target_pairs={{0,4},{1,5},{2,6},{3,7},{4,0},{5,1},{6,2},{7,3},{8,12},{9,13},{10,... | collective-permute-start | bytes 1572872 | tf_op jit(solution)/shard_map/activations/ppermute | solution.py:38
  57.7 21.6 %collective-permute-start.6 = (bf16[128,2048]{1,0:T(8,128)(2,1)S(1)}, bf16[128,2048]{1,0:T(8,128)(2,1)S(1)}, u32[]{:S(2)}, u32[]{:S(2)}) collective-permute-start(bf16[128,2048]{1,0:T(8,128)(2,1)S(1)} %collective-permute-done.3.refs_0_.b0), channel_id=1, source_target_pairs={{0,6},{1,7},{2,0},{3,1},{4,2},{5,3},{6,4},{7,5},{8,14},{9,15},{10,... | collective-permute-start | bytes 1572872 | tf_op jit(solution)/shard_map/activations/ppermute | solution.py:38
  63.2 1.0 copy-start.13
  64.2 0.8 copy-start.14
  65.0 17.5 %collective-permute-start.7 = (bf16[512,256]{1,0:T(8,128)(2,1)S(1)}, bf16[512,256]{1,0:T(8,128)(2,1)S(1)}, u32[]{:S(2)}, u32[]{:S(2)}) collective-permute-start(bf16[512,256]{1,0:T(8,128)(2,1)S(1)} %get-tuple-element.25), channel_id=1, source_target_pairs={{0,1},{1,0},{2,3},{3,2},{4,5},{5,4},{6,7},{7,6},{8,9},{9,8},{10,11... | collective-permute-start | bytes 786440 | tf_op jit(solution)/shard_map/near_keys/ppermute | solution.py:33
  72.5 9.9 %copy-start.4 = (bf16[128,2048]{1,0:T(8,128)(2,1)}, bf16[128,2048]{1,0:T(8,128)(2,1)S(1)}, u32[]{:S(2)}) copy-start(bf16[128,2048]{1,0:T(8,128)(2,1)S(1)} %collective-permute-done.4.refs_1_.b1) | copy-start | bytes 1572868
  73.8 5.6 %copy-start.6 = (bf16[128,2048]{1,0:T(8,128)(2,1)}, bf16[128,2048]{1,0:T(8,128)(2,1)S(1)}, u32[]{:S(2)}) copy-start(bf16[128,2048]{1,0:T(8,128)(2,1)S(1)} %collective-permute-done.5.refs_2_.b2) | copy-start | bytes 1572868
  79.3 0.8 copy-start.8
  82.5 0.7 copy-start.20
  86.9 13.1 %collective-permute-start.8 = (bf16[512,256]{1,0:T(8,128)(2,1)}, bf16[512,256]{1,0:T(8,128)(2,1)S(1)}, u32[]{:S(2)}, u32[]{:S(2)}) collective-permute-start(bf16[512,256]{1,0:T(8,128)(2,1)} %get-tuple-element.26), channel_id=1, source_target_pairs={{0,1},{1,0},{2,3},{3,2},{4,5},{5,4},{6,7},{7,6},{8,9},{9,8},{10,11... | collective-permute-start | bytes 786440 | tf_op jit(solution)/shard_map/far_keys/ppermute | solution.py:33
  92.5 1.0 copy-start.3
  93.6 1.0 copy-start.5
  94.6 1.0 copy-start.7
  95.6 1.0 copy-start.9
  96.7 0.9 copy-start.17
  97.6 2.4 %copy-start.15 = (f32[512,256]{1,0:T(8,128)S(1)}, f32[512,256]{1,0:T(8,128)}, u32[]{:S(2)}) copy-start(f32[512,256]{1,0:T(8,128)} %copy-done.14) | copy-start | bytes 1572868
  101.8 9.4 %collective-permute-start.9 = (f32[8,128]{1,0:T(8,128)S(1)}, f32[8,128]{1,0:T(8,128)S(1)}, u32[]{:S(2)}, u32[]{:S(2)}) collective-permute-start(f32[8,128]{1,0:T(8,128)S(1)} %get-tuple-element.28), channel_id=1, source_target_pairs={{0,1},{1,0},{2,3},{3,2},{4,5},{5,4},{6,7},{7,6},{8,9},{9,8},{10,11... | collective-permute-start | bytes 12296 | tf_op jit(solution)/shard_map/gradient/ppermute | solution.py:33
  127.8 1.2 copy-start.12
  129.0 7.1 %copy-start.19 = (f32[512,256]{1,0:T(8,128)S(1)}, f32[512,256]{1,0:T(8,128)}, u32[]{:S(2)}) copy-start(f32[512,256]{1,0:T(8,128)} %param.13) | copy-start | bytes 1572868
  129.2 21.0 %copy-start.1 = (bf16[1,512,1024]{2,1,0:T(8,128)(2,1)S(1)}, bf16[1,512,1024]{2,1,0:T(8,128)(2,1)}, u32[]{:S(2)}) copy-start(bf16[1,512,1024]{2,1,0:T(8,128)(2,1)} %weight_ref.3) | copy-start | bytes 3145732
  129.2 21.0 %copy-start.18 = (s32[8]{0:T(128)S(1)}, s32[8]{0:T(128)}, u32[]{:S(2)}) copy-start(s32[8]{0:T(128)} %order_ref.1) | copy-start | bytes 100
  129.2 6.9 %collective-permute-start.10 = (f32[512,256]{1,0:T(8,128)S(1)}, f32[512,256]{1,0:T(8,128)}, u32[]{:S(2)}, u32[]{:S(2)}) collective-permute-start(f32[512,256]{1,0:T(8,128)S(1)} %sum_blocks.1), channel_id=1, source_target_pairs={{0,8},{8,0},{16,24},{24,16},{32,40},{40,32},{48,56},{56,48},{64,72... | collective-permute-start | bytes 1572872 | tf_op jit(solution)/shard_map/outer_sum/ppermute | solution.py:266
  131.2 18.9 %all-to-all-start = ((bf16[4,528,256]{2,1,0:T(8,128)(2,1)}), bf16[4,528,256]{2,1,0:T(8,128)(2,1)S(1)}, u32[]{:S(2)}, u32[]{:S(2)}) async-start(bf16[4,528,256]{2,1,0:T(8,128)(2,1)} %embed.1._), calls=%async_computation | async-start | bytes 2162688 | tf_op jit(solution)/shard_map/gradient/all_to_all | solution.py:29
  138.2 14.8 %copy-start.10 = (bf16[512,256]{1,0:T(8,128)(2,1)}, bf16[512,256]{1,0:T(8,128)(2,1)S(1)}, u32[]{:S(2)}) copy-start(bf16[512,256]{1,0:T(8,128)(2,1)S(1)} %get-tuple-element.31.global_ref) | copy-start | bytes 786436
Sparse Core Ops, SparseCore 0:
  10.1 49.2 all-gather.3
  87.0 40.7 all-gather.5

commit v5 on v4

--- a/solution.py
+++ b/solution.py
@@ -22,7 +22,6 @@
 
 X_GROUPS = [[x * 2 + h for x in range(NX)] for h in range(2)]
 Z_GROUPS = [[z * 8 + l for z in range(8)] for l in range(8)]
-Y_GROUPS = [[z * 8 + y * 2 + core for y in range(4)] for z in range(8) for core in range(2)]
 
 
 def exchange(blocks, axis, groups):
@@ -42,8 +41,14 @@
     return rotate([block] * NX)
 
 
-def pack_kernel(place_ref, tokens_ref, weight_ref, targets_ref, other_ref, *message_refs):
+def pack_kernel(place_ref, *refs):
+    sources, other_ref, message_refs, held, done = refs[:3], refs[3], refs[4:8], refs[8:11], refs[11]
+    fetches = [pltpu.make_async_copy(s, h, done.at[i]) for i, (s, h) in enumerate(zip(sources, held))]
+    for fetch in fetches:
+        fetch.start()
     half, x = place_ref[0], place_ref[1]
+    tokens_ref, weight_ref, targets_ref = held
+    fetches[0].wait()
     floated = tokens_ref[...].astype(F32)
     scale = lax.rsqrt(jnp.mean(floated * floated, axis=-1, keepdims=True) + 1e-06)
     for block in range(NX):
@@ -53,6 +58,8 @@
             piece = (tokens_ref[:, pl.ds(start, 512)].astype(F32) * scale).astype(BF16)
             for ref in refs:
                 ref[:128, lanes] = piece
+    fetches[1].wait()
+    fetches[2].wait()
     for d, ref in enumerate(message_refs):
         columns = pl.ds(pl.multiple_of(lax.rem(x + d, NX) * COLS, COLS), COLS)
         for j in range(8):
@@ -83,19 +90,10 @@
         turned_ref[:, d * 128 : (d + 1) * 128] = m[:128].T
 
 
-def far_kernel(*refs):
-    sources, (sent_ref, residual_ref, delta_sum_ref), held, done = refs[:7], refs[7:10], refs[10:17], refs[17]
-    fetches = [pltpu.make_async_copy(s, h, done.at[i]) for i, (s, h) in enumerate(zip(sources, held))]
-    for fetch in fetches:
-        fetch.start()
-    for fetch in fetches[:6]:
-        fetch.wait()
-    keys = raw_keys(held[:4], held[4][...])
+def far_kernel(b0, b1, b2, b3, weight_ref, rest_ref, sent_ref, residual_ref):
+    keys = raw_keys((b0, b1, b2, b3), weight_ref[...])
     sent_ref[...] = keys.astype(BF16)
-    residual_ref[...] = (keys + held[5][...].astype(F32)).astype(BF16)
-    fetches[6].wait()
-    for rows in (slice(0, 256), slice(256, 512)):
-        delta_sum_ref[rows] = jnp.sum(held[6][:, rows].astype(F32), axis=0).astype(BF16)
+    residual_ref[...] = (keys + rest_ref[...].astype(F32)).astype(BF16)
 
 
 def turn_kernel(b0, b1, b2, b3, out_ref):
@@ -143,21 +141,6 @@
         compiler_params=PARAMS,
         name="embed",
     )(squares, gradient)
-
-
-def sum_kernel(blocks_ref, _, out_ref):
-    out_ref[...] = jnp.sum(blocks_ref[...].astype(F32), axis=0)
-
-
-def sum_blocks(blocks, later_than):
-    return pl.pallas_call(
-        sum_kernel,
-        in_specs=[pl.BlockSpec(memory_space=pltpu.VMEM), pl.BlockSpec(memory_space=pl.ANY)],
-        out_specs=pl.BlockSpec(memory_space=pltpu.VMEM),
-        out_shape=SDS((512, 256), F32),
-        compiler_params=PARAMS,
-        name="sum_blocks",
-    )(blocks, later_than)
 
 
 def step_kernel(order_ref, squares_ref, rows_ref, weight_ref, global_ref, out_ref, new_ref):
@@ -220,7 +203,9 @@
         other, *messages = call(
             pack_kernel,
             (SDS((128, 2048), BF16),) + (SDS((208, 2048), BF16),) * NX,
-            place, tokens, local_weights, targets, scalars=1,
+            place, tokens, local_weights, targets, scalars=1, hbm=3, vmem_mib=58,
+            scratch=[pltpu.VMEM(a.shape, BF16) for a in (tokens, local_weights, targets)]
+            + [pltpu.SemaphoreType.DMA((3,))],
         )
         arrived = flip(other, 1)
         near = rotate(messages)
@@ -235,16 +220,9 @@
         far_rest = flip(near_sent, 1)
 
     with jax.named_scope("far_keys"):
-        by_z = lax.all_gather(pending_delta[0], "rep", axis_index_groups=Z_GROUPS)
-        far_sent, far_residual, delta_sum = call(
-            far_kernel,
-            (SDS(tall, BF16), SDS(tall, BF16), SDS((512, 256), BF16)),
-            *far, columns, far_rest, by_z, flops=dot_flops, hbm=7, vmem_mib=58,
-            scratch=[pltpu.VMEM((128, 2048), BF16)] * NX
-            + [pltpu.VMEM((2048, COLS), BF16), pltpu.VMEM(tall, BF16), pltpu.VMEM((8, 512, 256), BF16)]
-            + [pltpu.SemaphoreType.DMA((7,))],
-        )
-        by_y = lax.all_gather(delta_sum, "rep", axis_index_groups=Y_GROUPS)
+        far_sent, far_residual = call(
+            far_kernel, (SDS(tall, BF16), SDS(tall, BF16)), *far, columns, far_rest, flops=dot_flops
+        )
         near_rest = flip(far_sent, 1)
         far_turned = call(turn_kernel, SDS((2048, 512), BF16), *far)
 
@@ -262,9 +240,12 @@
         by_rows = exchange(embedded, "fsdp", X_GROUPS)
 
     with jax.named_scope("outer_sum"):
-        core_sum = sum_blocks(by_y, embedded)
-        total = core_sum + lax.ppermute(core_sum, "rep", [(i, i ^ 1) for i in range(64)])
-        mean = total / lax.axis_size("rep")
+        by_z = exchange(pending_delta[0].reshape(8, 64, 256), "rep", Z_GROUPS)
+        total = jnp.sum(by_z.astype(F32), axis=0)
+        for mask in (1, 2, 4):
+            total += lax.ppermute(total, "rep", [(i, i ^ mask) for i in range(64)])
+        by_rows_z = exchange(jnp.broadcast_to(total[None], (8, 64, 256)), "rep", Z_GROUPS)
+        mean = by_rows_z.reshape(512, 256) / lax.axis_size("rep")
         new_momentum = 0.9 * outer_momentum + mean
         new_global = (global_frag.astype(F32) - 0.7 * (mean + 0.9 * new_momentum)).astype(BF16)
 

time: 163 us -> 156 us (0.957)
  the two profiles are of different devices: /device:TPU:6 before, /device:TPU:16 now
where the time goes in v5:
time: 156 us; the launch traced here: 155 us
  waiting for transfers between devices  70.4 us (45%)
  starting transfers between devices  66 us (42%)
  Pallas kernels  13.7 us (9%)
  other arithmetic  2.83 us (2%)
    all_to_all x3, starting transfers between devices, exchange(): lax.all_to_all(blocks, axis, 0, 0, axis_index_groups=groups, tiled=True)  22.4 us
    ppermute x3, waiting for transfers between devices, body(): total += lax.ppermute(total, 'rep', [(i, i ^ mask) for i in range(64)])  22.4 us
    ppermute x4, waiting for transfers between devices, flip(): return lax.ppermute(block, 'fsdp', [(i, i ^ mask) for i in range(8)])  20.6 us
    ppermute x6, starting transfers between devices, rotate(): lax.ppermute(blocks[d], 'fsdp', moves[d])  20.5 us
    ppermute x6, waiting for transfers between devices, rotate(): lax.ppermute(blocks[d], 'fsdp', moves[d])  15.1 us
    ppermute x4, starting transfers between devices, flip(): return lax.ppermute(block, 'fsdp', [(i, i ^ mask) for i in range(8)])  14.5 us
    all_to_all x3, waiting for transfers between devices, exchange(): lax.all_to_all(blocks, axis, 0, 0, axis_index_groups=groups, tiled=True)  12.3 us
    pallas_call x6, Pallas kernels, call(): pl.pallas_call(kernel, in_specs=[SMEM] * scalars + [pl.BlockSpec(memory_s...  10.3 us
  transfers between devices with their start and end apart: 16, of which 8 were waited for; matrix products, arithmetic and copies ran while one was open for 2% of the time, Pallas kernels for 4%

profile of v5, /device:TPU:16, one launch (start us, length us, event | category | flops | bytes accessed | tf_op | source)
XLA Modules:
  0.0 154.8 jit_solution(1227807817623836910)
XLA Ops:
  0.6 0.7 pad_add_fusion.place_ref
  1.3 4.5 %pack.1 = (bf16[128,2048]{1,0:T(8,128)(2,1)}, bf16[208,2048]{1,0:T(8,128)(2,1)}, bf16[208,2048]{1,0:T(8,128)(2,1)}, bf16[208,2048]{1,0:T(8,128)(2,1)}, bf16[208,2048]{1,0:T(8,128)(2,1)}) custom-call(s32[2]{0:T(128)} %pad_add_fusion.place_ref, bf16[128,4096]{1,0:T(8,128)(2,1)} %refs_0_.1, bf16[1,512,1024]{2,1,0:T(8,128)(2,1)} %weight_ref.1, ...), custom_call_target="tpu_custom_call" | custom-call | bytes 4194304 | tf_op jit(solution)/shard_map/activations/pack/pallas_call | solution.py:182
  5.8 0.0 copy-start.2
  5.9 0.0 copy-start.3
  5.9 3.5 %collective-permute-start = (bf16[208,2048]{1,0:T(8,128)(2,1)}, bf16[208,2048]{1,0:T(8,128)(2,1)S(1)}, u32[]{:S(2)}, u32[]{:S(2)}) collective-permute-start(bf16[208,2048]{1,0:T(8,128)(2,1)} %get-tuple-element.17), channel_id=1, source_target_pairs={{0,2},{1,3},{2,4},{3,5},{4,6},{5,7},{6,0},{7,1},{8,10},{9,11},{10,... | collective-permute-start | bytes 2555912 | tf_op jit(solution)/shard_map/activations/ppermute | solution.py:37
  9.4 10.3 %all-to-all-start.1 = ((bf16[8,64,256]{2,1,0:T(8,128)(2,1)}), bf16[8,64,256]{2,1,0:T(8,128)(2,1)S(1)}, u32[]{:S(2)}, u32[]{:S(2)}) async-start(bf16[8,64,256]{2,1,0:T(8,128)(2,1)} %bitcast.2), calls=%async_computation.1 | async-start | bytes 524288 | tf_op jit(solution)/shard_map/outer_sum/all_to_all | solution.py:28
  19.7 4.6 %collective-permute-start.1 = (bf16[208,2048]{1,0:T(8,128)(2,1)}, bf16[208,2048]{1,0:T(8,128)(2,1)S(1)}, u32[]{:S(2)}, u32[]{:S(2)}) collective-permute-start(bf16[208,2048]{1,0:T(8,128)(2,1)} %get-tuple-element.18), channel_id=1, source_target_pairs={{0,4},{1,5},{2,6},{3,7},{4,0},{5,1},{6,2},{7,3},{8,12},{9,13},{10,... | collective-permute-start | bytes 2555912 | tf_op jit(solution)/shard_map/activations/ppermute | solution.py:37
  24.4 3.3 %collective-permute-start.2 = (bf16[208,2048]{1,0:T(8,128)(2,1)}, bf16[208,2048]{1,0:T(8,128)(2,1)}, u32[]{:S(2)}, u32[]{:S(2)}) collective-permute-start(bf16[208,2048]{1,0:T(8,128)(2,1)} %get-tuple-element.19), channel_id=1, source_target_pairs={{0,6},{1,7},{2,0},{3,1},{4,2},{5,3},{6,4},{7,5},{8,14},{9,15},{10,... | collective-permute-start | bytes 2555912 | tf_op jit(solution)/shard_map/activations/ppermute | solution.py:37
  27.7 5.9 %collective-permute-start.3 = (bf16[128,2048]{1,0:T(8,128)(2,1)}, bf16[128,2048]{1,0:T(8,128)(2,1)S(1)}, u32[]{:S(2)}, u32[]{:S(2)}) collective-permute-start(bf16[128,2048]{1,0:T(8,128)(2,1)} %get-tuple-element.22), channel_id=1, source_target_pairs={{0,1},{1,0},{2,3},{3,2},{4,5},{5,4},{6,7},{7,6},{8,9},{9,8},{10,11... | collective-permute-start | bytes 1572872 | tf_op jit(solution)/shard_map/activations/ppermute | solution.py:32
  33.7 0.0 all-to-all-done.1
  33.7 1.9 %collective-permute-start.10 = (f32[64,256]{1,0:T(8,128)S(1)}, f32[64,256]{1,0:T(8,128)S(1)}, u32[]{:S(2)}, u32[]{:S(2)}) collective-permute-start(f32[64,256]{1,0:T(8,128)S(1)} %convert_reduce_fusion), channel_id=1, source_target_pairs={{0,8},{8,0},{16,24},{24,16},{32,40},{40,32},{48,56},{56,48},{64,72... | collective-permute-start | bytes 196616 | tf_op jit(solution)/shard_map/outer_sum/ppermute | solution.py:246
  35.6 1.2 collective-permute-done.10
  36.9 2.6 %collective-permute-start.11 = (f32[64,256]{1,0:T(8,128)S(1)}, f32[64,256]{1,0:T(8,128)S(1)}, u32[]{:S(2)}, u32[]{:S(2)}) collective-permute-start(f32[64,256]{1,0:T(8,128)S(1)} %add.19), channel_id=1, source_target_pairs={{0,16},{8,24},{16,0},{24,8},{32,48},{40,56},{48,32},{56,40},{64,80... | collective-permute-start | bytes 196616 | tf_op jit(solution)/shard_map/outer_sum/ppermute | solution.py:246
  39.5 18.2 %collective-permute-done.11 = f32[64,256]{1,0:T(8,128)S(1)} collective-permute-done((f32[64,256]{1,0:T(8,128)S(1)}, f32[64,256]{1,0:T(8,128)S(1)}, u32[]{:S(2)}, u32[]{:S(2)}) %collective-permute-start.11) | collective-permute-done | bytes 65568 | tf_op jit(solution)/shard_map/outer_sum/ppermute | solution.py:246
  57.7 4.0 %collective-permute-start.12 = (f32[64,256]{1,0:T(8,128)S(1)}, f32[64,256]{1,0:T(8,128)S(1)}, u32[]{:S(2)}, u32[]{:S(2)}) collective-permute-start(f32[64,256]{1,0:T(8,128)S(1)} %add.20), channel_id=1, source_target_pairs={{0,32},{8,40},{16,48},{24,56},{32,0},{40,8},{48,16},{56,24},{64,96... | collective-permute-start | bytes 196616 | tf_op jit(solution)/shard_map/outer_sum/ppermute | solution.py:246
  61.7 3.0 %collective-permute-done.12 = f32[64,256]{1,0:T(8,128)S(1)} collective-permute-done((f32[64,256]{1,0:T(8,128)S(1)}, f32[64,256]{1,0:T(8,128)S(1)}, u32[]{:S(2)}, u32[]{:S(2)}) %collective-permute-start.12) | collective-permute-done | bytes 65568 | tf_op jit(solution)/shard_map/outer_sum/ppermute | solution.py:246
  64.8 0.8 broadcast_in_dim.2
  65.6 7.0 %all-to-all-start.2 = ((f32[8,64,256]{2,1,0:T(8,128)}), f32[8,64,256]{2,1,0:T(8,128)}, u32[]{:S(2)}, u32[]{:S(2)}) async-start(f32[8,64,256]{2,1,0:T(8,128)} %broadcast_in_dim.2), calls=%async_computation.2 | async-start | bytes 1048576 | tf_op jit(solution)/shard_map/outer_sum/all_to_all | solution.py:28
  72.6 0.0 collective-permute-done.3.b0
  72.6 2.5 %collective-permute-start.4 = (bf16[128,2048]{1,0:T(8,128)(2,1)S(1)}, bf16[128,2048]{1,0:T(8,128)(2,1)S(1)}, u32[]{:S(2)}, u32[]{:S(2)}) collective-permute-start(bf16[128,2048]{1,0:T(8,128)(2,1)S(1)} %collective-permute-done.3.b0), channel_id=1, source_target_pairs={{0,2},{1,3},{2,4},{3,5},{4,6},{5,7},{6,0},{7,1},{8,10},{9,11},{10,... | collective-permute-start | bytes 1572872 | tf_op jit(solution)/shard_map/activations/ppermute | solution.py:37
  75.1 3.0 %collective-permute-start.5 = (bf16[128,2048]{1,0:T(8,128)(2,1)S(1)}, bf16[128,2048]{1,0:T(8,128)(2,1)S(1)}, u32[]{:S(2)}, u32[]{:S(2)}) collective-permute-start(bf16[128,2048]{1,0:T(8,128)(2,1)S(1)} %collective-permute-done.3.b0), channel_id=1, source_target_pairs={{0,4},{1,5},{2,6},{3,7},{4,0},{5,1},{6,2},{7,3},{8,12},{9,13},{10,... | collective-permute-start | bytes 1572872 | tf_op jit(solution)/shard_map/activations/ppermute | solution.py:37
  78.1 0.0 collective-permute-done.m1
  78.1 3.5 %collective-permute-start.6 = (bf16[128,2048]{1,0:T(8,128)(2,1)S(1)}, bf16[128,2048]{1,0:T(8,128)(2,1)S(1)}, u32[]{:S(2)}, u32[]{:S(2)}) collective-permute-start(bf16[128,2048]{1,0:T(8,128)(2,1)S(1)} %collective-permute-done.3.b0), channel_id=1, source_target_pairs={{0,6},{1,7},{2,0},{3,1},{4,2},{5,3},{6,4},{7,5},{8,14},{9,15},{10,... | collective-permute-start | bytes 1572872 | tf_op jit(solution)/shard_map/activations/ppermute | solution.py:37
  81.7 0.0 collective-permute-done.1.m2
  81.7 0.0 collective-permute-done.2.m3
  81.7 2.0 %near.1 = (f32[512,256]{1,0:T(8,128)S(1)}, bf16[512,256]{1,0:T(8,128)(2,1)S(1)}, bf16[2048,256]{1,0:T(8,128)(2,1)S(1)}, bf16[2048,512]{1,0:T(8,128)(2,1)S(1)}) custom-call(s32[2]{0:T(128)S(1)} %copy-done.3, bf16[208,2048]{1,0:T(8,128)(2,1)S(1)} %copy-done.2, bf16[208,2048]{1,0:T(8,128)(2,1)S(1)} %collective-permute-done.m1, ...), custom_call_target="tpu_custom_call" | custom-call | flops 536870912 | bytes 4194304 | tf_op jit(solution)/shard_map/near_keys/near/pallas_call | solution.py:182
  83.7 2.8 %collective-permute-start.7 = (bf16[512,256]{1,0:T(8,128)(2,1)S(1)}, bf16[512,256]{1,0:T(8,128)(2,1)S(1)}, u32[]{:S(2)}, u32[]{:S(2)}) collective-permute-start(bf16[512,256]{1,0:T(8,128)(2,1)S(1)} %get-tuple-element.24), channel_id=1, source_target_pairs={{0,1},{1,0},{2,3},{3,2},{4,5},{5,4},{6,7},{7,6},{8,9},{9,8},{10,11... | collective-permute-start | bytes 786440 | tf_op jit(solution)/shard_map/near_keys/ppermute | solution.py:32
  86.5 12.5 %collective-permute-done.4.b1 = bf16[128,2048]{1,0:T(8,128)(2,1)S(1)} collective-permute-done((bf16[128,2048]{1,0:T(8,128)(2,1)S(1)}, bf16[128,2048]{1,0:T(8,128)(2,1)S(1)}, u32[]{:S(2)}, u32[]{:S(2)}) %collective-permute-start.4) | collective-permute-done | bytes 524320 | tf_op jit(solution)/shard_map/activations/ppermute | solution.py:37
  99.1 0.0 collective-permute-done.5.b2
  99.1 2.5 %collective-permute-done.6.b3 = bf16[128,2048]{1,0:T(8,128)(2,1)S(1)} collective-permute-done((bf16[128,2048]{1,0:T(8,128)(2,1)S(1)}, bf16[128,2048]{1,0:T(8,128)(2,1)S(1)}, u32[]{:S(2)}, u32[]{:S(2)}) %collective-permute-start.6) | collective-permute-done | bytes 524320 | tf_op jit(solution)/shard_map/activations/ppermute | solution.py:37
  101.6 0.0 collective-permute-done.7.rest_ref
  101.6 0.7 far.1
  102.3 2.9 %collective-permute-start.8 = (bf16[512,256]{1,0:T(8,128)(2,1)S(1)}, bf16[512,256]{1,0:T(8,128)(2,1)S(1)}, u32[]{:S(2)}, u32[]{:S(2)}) collective-permute-start(bf16[512,256]{1,0:T(8,128)(2,1)S(1)} %get-tuple-element.25), channel_id=1, source_target_pairs={{0,1},{1,0},{2,3},{3,2},{4,5},{5,4},{6,7},{7,6},{8,9},{9,8},{10,11... | collective-permute-start | bytes 786440 | tf_op jit(solution)/shard_map/far_keys/ppermute | solution.py:32
  105.2 0.6 turn.1.turned_ref
  105.8 0.7 far_gradient.1.far_ref
  106.5 14.1 %collective-permute-done.8.rest_ref = bf16[512,256]{1,0:T(8,128)(2,1)S(1)} collective-permute-done((bf16[512,256]{1,0:T(8,128)(2,1)S(1)}, bf16[512,256]{1,0:T(8,128)(2,1)S(1)}, u32[]{:S(2)}, u32[]{:S(2)}) %collective-permute-start.8) | collective-permute-done | bytes 262176 | tf_op jit(solution)/shard_map/far_keys/ppermute | solution.py:32
  120.6 1.8 %near_gradient.1 = (bf16[4,528,256]{2,1,0:T(8,128)(2,1)}, f32[8,128]{1,0:T(8,128)S(1)}) custom-call(bf16[2048,512]{1,0:T(8,128)(2,1)S(1)} %get-tuple-element.20.turned_ref, f32[512,256]{1,0:T(8,128)S(1)} %get-tuple-element.21.part_ref, bf16[512,256]{1,0:T(8,128)(2,1)S(1)} %collective-permute-done.8.rest_ref, f32[2048,256]{1,0:T(8,128)S(1)} %far_gradient.1.far_ref), custom_call_target="tpu_custom_call" | custom-call | flops 536870912 | bytes 4194304 | tf_op jit(solution)/shard_map/gradient/near_gradient/pallas_call | solution.py:182
  122.4 2.9 %collective-permute-start.9 = (f32[8,128]{1,0:T(8,128)S(1)}, f32[8,128]{1,0:T(8,128)S(1)}, u32[]{:S(2)}, u32[]{:S(2)}) collective-permute-start(f32[8,128]{1,0:T(8,128)S(1)} %get-tuple-element.27), channel_id=1, source_target_pairs={{0,1},{1,0},{2,3},{3,2},{4,5},{5,4},{6,7},{7,6},{8,9},{9,8},{10,11... | collective-permute-start | bytes 12296 | tf_op jit(solution)/shard_map/gradient/ppermute | solution.py:32
  125.3 6.5 %collective-permute-done.9 = f32[8,128]{1,0:T(8,128)S(1)} collective-permute-done((f32[8,128]{1,0:T(8,128)S(1)}, f32[8,128]{1,0:T(8,128)S(1)}, u32[]{:S(2)}, u32[]{:S(2)}) %collective-permute-start.9) | collective-permute-done | bytes 4128 | tf_op jit(solution)/shard_map/gradient/ppermute | solution.py:32
  131.8 0.6 embed.1
  132.4 0.0 all-to-all-done.2
  132.4 5.1 %all-to-all-start = ((bf16[4,528,256]{2,1,0:T(8,128)(2,1)}), bf16[4,528,256]{2,1,0:T(8,128)(2,1)S(1)}, u32[]{:S(2)}, u32[]{:S(2)}) async-start(bf16[4,528,256]{2,1,0:T(8,128)(2,1)} %embed.1), calls=%async_computation | async-start | bytes 2162688 | tf_op jit(solution)/shard_map/gradient/all_to_all | solution.py:28
  137.5 1.2 broadcast_multiply_fusion
  138.7 0.0 copy-done.5
  138.7 0.0 copy-done.6
  138.7 0.9 fusion.2
  139.6 12.3 %all-to-all-done.squares_ref.rows_ref = bf16[4,528,256]{2,1,0:T(8,128)(2,1)S(1)} async-done(((bf16[4,528,256]{2,1,0:T(8,128)(2,1)}), bf16[4,528,256]{2,1,0:T(8,128)(2,1)S(1)}, u32[]{:S(2)}, u32[]{:S(2)}) %all-to-all-start) | async-done | bytes 1081376 | tf_op jit(solution)/shard_map/gradient/all_to_all | solution.py:28
  152.0 2.8 %step.1 = bf16[1,512,1024]{2,1,0:T(8,128)(2,1)} custom-call(s32[8]{0:T(128)S(1)} %copy-done.4, bf16[4,528,256]{2,1,0:T(8,128)(2,1)S(1)} %all-to-all-done.squares_ref.rows_ref, bf16[4,528,256]{2,1,0:T(8,128)(2,1)S(1)} %all-to-all-done.squares_ref.rows_ref, bf16[1,512,1024]{2,1,0:T(8,128)(2,1)S(1)} %copy-done, bf16[512,256]{1,0:T(8,128)(2,1)S(1)} %get-tuple-element.29.global_ref), custom_call_target="tpu_custom_call" | custom-call | tf_op jit(solution)/shard_map/step/step/pallas_call | solution.py:162
  (15 shorter events, 0.1 us)
Async XLA Ops:
  5.8 75.9 %copy-start.2 = (bf16[208,2048]{1,0:T(8,128)(2,1)S(1)}, bf16[208,2048]{1,0:T(8,128)(2,1)}, u32[]{:S(2)}) copy-start(bf16[208,2048]{1,0:T(8,128)(2,1)} %get-tuple-element.16.m0) | copy-start | bytes 2555908
  5.9 75.9 %copy-start.3 = (s32[2]{0:T(128)S(1)}, s32[2]{0:T(128)}, u32[]{:S(2)}) copy-start(s32[2]{0:T(128)} %pad_add_fusion.place_ref) | copy-start | bytes 28
  5.9 72.3 %collective-permute-start = (bf16[208,2048]{1,0:T(8,128)(2,1)}, bf16[208,2048]{1,0:T(8,128)(2,1)S(1)}, u32[]{:S(2)}, u32[]{:S(2)}) collective-permute-start(bf16[208,2048]{1,0:T(8,128)(2,1)} %get-tuple-element.17), channel_id=1, source_target_pairs={{0,2},{1,3},{2,4},{3,5},{4,6},{5,7},{6,0},{7,1},{8,10},{9,11},{10,... | collective-permute-start | bytes 2555912 | tf_op jit(solution)/shard_map/activations/ppermute | solution.py:37
  9.4 24.3 %all-to-all-start.1 = ((bf16[8,64,256]{2,1,0:T(8,128)(2,1)}), bf16[8,64,256]{2,1,0:T(8,128)(2,1)S(1)}, u32[]{:S(2)}, u32[]{:S(2)}) async-start(bf16[8,64,256]{2,1,0:T(8,128)(2,1)} %bitcast.2), calls=%async_computation.1 | async-start | bytes 524288 | tf_op jit(solution)/shard_map/outer_sum/all_to_all | solution.py:28
  19.7 61.9 %collective-permute-start.1 = (bf16[208,2048]{1,0:T(8,128)(2,1)}, bf16[208,2048]{1,0:T(8,128)(2,1)S(1)}, u32[]{:S(2)}, u32[]{:S(2)}) collective-permute-start(bf16[208,2048]{1,0:T(8,128)(2,1)} %get-tuple-element.18), channel_id=1, source_target_pairs={{0,4},{1,5},{2,6},{3,7},{4,0},{5,1},{6,2},{7,3},{8,12},{9,13},{10,... | collective-permute-start | bytes 2555912 | tf_op jit(solution)/shard_map/activations/ppermute | solution.py:37
  24.4 57.3 %collective-permute-start.2 = (bf16[208,2048]{1,0:T(8,128)(2,1)}, bf16[208,2048]{1,0:T(8,128)(2,1)}, u32[]{:S(2)}, u32[]{:S(2)}) collective-permute-start(bf16[208,2048]{1,0:T(8,128)(2,1)} %get-tuple-element.19), channel_id=1, source_target_pairs={{0,6},{1,7},{2,0},{3,1},{4,2},{5,3},{6,4},{7,5},{8,14},{9,15},{10,... | collective-permute-start | bytes 2555912 | tf_op jit(solution)/shard_map/activations/ppermute | solution.py:37
  27.7 44.9 %collective-permute-start.3 = (bf16[128,2048]{1,0:T(8,128)(2,1)}, bf16[128,2048]{1,0:T(8,128)(2,1)S(1)}, u32[]{:S(2)}, u32[]{:S(2)}) collective-permute-start(bf16[128,2048]{1,0:T(8,128)(2,1)} %get-tuple-element.22), channel_id=1, source_target_pairs={{0,1},{1,0},{2,3},{3,2},{4,5},{5,4},{6,7},{7,6},{8,9},{9,8},{10,11... | collective-permute-start | bytes 1572872 | tf_op jit(solution)/shard_map/activations/ppermute | solution.py:32
  33.7 3.1 %collective-permute-start.10 = (f32[64,256]{1,0:T(8,128)S(1)}, f32[64,256]{1,0:T(8,128)S(1)}, u32[]{:S(2)}, u32[]{:S(2)}) collective-permute-start(f32[64,256]{1,0:T(8,128)S(1)} %convert_reduce_fusion), channel_id=1, source_target_pairs={{0,8},{8,0},{16,24},{24,16},{32,40},{40,32},{48,56},{56,48},{64,72... | collective-permute-start | bytes 196616 | tf_op jit(solution)/shard_map/outer_sum/ppermute | solution.py:246
  36.9 20.8 %collective-permute-start.11 = (f32[64,256]{1,0:T(8,128)S(1)}, f32[64,256]{1,0:T(8,128)S(1)}, u32[]{:S(2)}, u32[]{:S(2)}) collective-permute-start(f32[64,256]{1,0:T(8,128)S(1)} %add.19), channel_id=1, source_target_pairs={{0,16},{8,24},{16,0},{24,8},{32,48},{40,56},{48,32},{56,40},{64,80... | collective-permute-start | bytes 196616 | tf_op jit(solution)/shard_map/outer_sum/ppermute | solution.py:246
  57.7 7.1 %collective-permute-start.12 = (f32[64,256]{1,0:T(8,128)S(1)}, f32[64,256]{1,0:T(8,128)S(1)}, u32[]{:S(2)}, u32[]{:S(2)}) collective-permute-start(f32[64,256]{1,0:T(8,128)S(1)} %add.20), channel_id=1, source_target_pairs={{0,32},{8,40},{16,48},{24,56},{32,0},{40,8},{48,16},{56,24},{64,96... | collective-permute-start | bytes 196616 | tf_op jit(solution)/shard_map/outer_sum/ppermute | solution.py:246
  65.6 66.8 %all-to-all-start.2 = ((f32[8,64,256]{2,1,0:T(8,128)}), f32[8,64,256]{2,1,0:T(8,128)}, u32[]{:S(2)}, u32[]{:S(2)}) async-start(f32[8,64,256]{2,1,0:T(8,128)} %broadcast_in_dim.2), calls=%async_computation.2 | async-start | bytes 1048576 | tf_op jit(solution)/shard_map/outer_sum/all_to_all | solution.py:28
  72.6 26.4 %collective-permute-start.4 = (bf16[128,2048]{1,0:T(8,128)(2,1)S(1)}, bf16[128,2048]{1,0:T(8,128)(2,1)S(1)}, u32[]{:S(2)}, u32[]{:S(2)}) collective-permute-start(bf16[128,2048]{1,0:T(8,128)(2,1)S(1)} %collective-permute-done.3.b0), channel_id=1, source_target_pairs={{0,2},{1,3},{2,4},{3,5},{4,6},{5,7},{6,0},{7,1},{8,10},{9,11},{10,... | collective-permute-start | bytes 1572872 | tf_op jit(solution)/shard_map/activations/ppermute | solution.py:37
  75.1 23.9 %collective-permute-start.5 = (bf16[128,2048]{1,0:T(8,128)(2,1)S(1)}, bf16[128,2048]{1,0:T(8,128)(2,1)S(1)}, u32[]{:S(2)}, u32[]{:S(2)}) collective-permute-start(bf16[128,2048]{1,0:T(8,128)(2,1)S(1)} %collective-permute-done.3.b0), channel_id=1, source_target_pairs={{0,4},{1,5},{2,6},{3,7},{4,0},{5,1},{6,2},{7,3},{8,12},{9,13},{10,... | collective-permute-start | bytes 1572872 | tf_op jit(solution)/shard_map/activations/ppermute | solution.py:37
  78.1 23.5 %collective-permute-start.6 = (bf16[128,2048]{1,0:T(8,128)(2,1)S(1)}, bf16[128,2048]{1,0:T(8,128)(2,1)S(1)}, u32[]{:S(2)}, u32[]{:S(2)}) collective-permute-start(bf16[128,2048]{1,0:T(8,128)(2,1)S(1)} %collective-permute-done.3.b0), channel_id=1, source_target_pairs={{0,6},{1,7},{2,0},{3,1},{4,2},{5,3},{6,4},{7,5},{8,14},{9,15},{10,... | collective-permute-start | bytes 1572872 | tf_op jit(solution)/shard_map/activations/ppermute | solution.py:37
  83.7 17.9 %collective-permute-start.7 = (bf16[512,256]{1,0:T(8,128)(2,1)S(1)}, bf16[512,256]{1,0:T(8,128)(2,1)S(1)}, u32[]{:S(2)}, u32[]{:S(2)}) collective-permute-start(bf16[512,256]{1,0:T(8,128)(2,1)S(1)} %get-tuple-element.24), channel_id=1, source_target_pairs={{0,1},{1,0},{2,3},{3,2},{4,5},{5,4},{6,7},{7,6},{8,9},{9,8},{10,11... | collective-permute-start | bytes 786440 | tf_op jit(solution)/shard_map/near_keys/ppermute | solution.py:32
  102.3 18.3 %collective-permute-start.8 = (bf16[512,256]{1,0:T(8,128)(2,1)S(1)}, bf16[512,256]{1,0:T(8,128)(2,1)S(1)}, u32[]{:S(2)}, u32[]{:S(2)}) collective-permute-start(bf16[512,256]{1,0:T(8,128)(2,1)S(1)} %get-tuple-element.25), channel_id=1, source_target_pairs={{0,1},{1,0},{2,3},{3,2},{4,5},{5,4},{6,7},{7,6},{8,9},{9,8},{10,11... | collective-permute-start | bytes 786440 | tf_op jit(solution)/shard_map/far_keys/ppermute | solution.py:32
  122.4 9.4 %collective-permute-start.9 = (f32[8,128]{1,0:T(8,128)S(1)}, f32[8,128]{1,0:T(8,128)S(1)}, u32[]{:S(2)}, u32[]{:S(2)}) collective-permute-start(f32[8,128]{1,0:T(8,128)S(1)} %get-tuple-element.27), channel_id=1, source_target_pairs={{0,1},{1,0},{2,3},{3,2},{4,5},{5,4},{6,7},{7,6},{8,9},{9,8},{10,11... | collective-permute-start | bytes 12296 | tf_op jit(solution)/shard_map/gradient/ppermute | solution.py:32
  132.4 6.3 %copy-start.5 = (f32[512,256]{1,0:T(8,128)S(1)}, f32[512,256]{1,0:T(8,128)}, u32[]{:S(2)}) copy-start(f32[512,256]{1,0:T(8,128)} %param.13) | copy-start | bytes 1572868
  132.4 6.3 %copy-start.6 = (bf16[512,256]{1,0:T(8,128)(2,1)S(1)}, bf16[512,256]{1,0:T(8,128)(2,1)}, u32[]{:S(2)}) copy-start(bf16[512,256]{1,0:T(8,128)(2,1)} %param.12) | copy-start | bytes 786436
  132.4 19.5 %all-to-all-start = ((bf16[4,528,256]{2,1,0:T(8,128)(2,1)}), bf16[4,528,256]{2,1,0:T(8,128)(2,1)S(1)}, u32[]{:S(2)}, u32[]{:S(2)}) async-start(bf16[4,528,256]{2,1,0:T(8,128)(2,1)} %embed.1), calls=%async_computation | async-start | bytes 2162688 | tf_op jit(solution)/shard_map/gradient/all_to_all | solution.py:28
  137.5 14.4 %copy-start = (bf16[1,512,1024]{2,1,0:T(8,128)(2,1)S(1)}, bf16[1,512,1024]{2,1,0:T(8,128)(2,1)}, u32[]{:S(2)}) copy-start(bf16[1,512,1024]{2,1,0:T(8,128)(2,1)} %weight_ref.1) | copy-start | bytes 3145732
  137.5 14.4 %copy-start.4 = (s32[8]{0:T(128)S(1)}, s32[8]{0:T(128)}, u32[]{:S(2)}) copy-start(s32[8]{0:T(128)} %order_ref.1) | copy-start | bytes 100
  139.6 15.1 %copy-start.1 = (bf16[512,256]{1,0:T(8,128)(2,1)}, bf16[512,256]{1,0:T(8,128)(2,1)S(1)}, u32[]{:S(2)}) copy-start(bf16[512,256]{1,0:T(8,128)(2,1)S(1)} %get-tuple-element.29.global_ref) | copy-start | bytes 786436

commit v6 on v5

--- a/solution.py
+++ b/solution.py
@@ -73,14 +73,16 @@
     return jnp.dot(lhs, weight, preferred_element_type=F32) * FACTOR
 
 
-def near_kernel(place_ref, m0, m1, m2, m3, part_ref, sent_ref, weight_ref, turned_ref):
+def near_kernel(place_ref, m0, m1, m2, m3, arrived_ref, part_ref, sent_ref, weight_ref, turned_ref, first_ref):
     messages = (m0, m1, m2, m3)
     for d, m in enumerate(messages):
         source = lax.rem(place_ref[1] - d + NX, NX)
         for j in range(8):
             rows = pl.ds(pl.multiple_of(source * 512 + j * 64, 64), 64)
             weight_ref[rows, :] = m[128:192, j * COLS : (j + 1) * COLS]
-    keys = raw_keys(messages, weight_ref[...])
+    keys = raw_keys((*messages, arrived_ref), weight_ref[...])
+    first_ref[...] = keys[512:]
+    sent_ref[512:] = keys[512:].astype(BF16)
     for d, m in enumerate(messages):
         for j in range(8):
             rows = slice(d * 128 + j * 16, d * 128 + (j + 1) * 16)
@@ -90,23 +92,28 @@
         turned_ref[:, d * 128 : (d + 1) * 128] = m[:128].T
 
 
-def far_kernel(b0, b1, b2, b3, weight_ref, rest_ref, sent_ref, residual_ref):
-    keys = raw_keys((b0, b1, b2, b3), weight_ref[...])
-    sent_ref[...] = keys.astype(BF16)
-    residual_ref[...] = (keys + rest_ref[...].astype(F32)).astype(BF16)
-
-
-def turn_kernel(b0, b1, b2, b3, out_ref):
-    for d, b in enumerate((b0, b1, b2, b3)):
-        out_ref[:, d * 128 : (d + 1) * 128] = b[:128].T
-
-
-def far_gradient_kernel(turned_ref, residual_ref, out_ref):
-    out_ref[...] = jnp.dot(turned_ref[...], residual_ref[...], preferred_element_type=F32)
-
-
-def near_gradient_kernel(turned_ref, part_ref, rest_ref, far_ref, out_ref, squares_ref):
-    residual = (part_ref[...] + rest_ref[...].astype(F32)).astype(BF16)
+def far_kernel(*refs):
+    *blocks, weight_ref, keys_ref, sent_ref = refs
+    keys_ref[...] = raw_keys(blocks, weight_ref[...])
+    sent_ref[...] = keys_ref[...].astype(BF16)
+
+
+def turn_kernel(b0, b1, b3, b2, out_ref):
+    for i, b in enumerate((b0, b1, b3, b2)):
+        out_ref[:, i * 128 : (i + 1) * 128] = b[...].T
+
+
+def far_gradient_kernel(turned_ref, first_ref, sides_ref, last_ref, rest_ref, out_ref):
+    keys = (first_ref[...], sides_ref[:128], sides_ref[128:], last_ref[...])
+    rests = (rest_ref[:128], rest_ref[128:256], rest_ref[384:512], rest_ref[256:384])
+    residual = jnp.concatenate([(k + r.astype(F32)).astype(BF16) for k, r in zip(keys, rests)], axis=0)
+    out_ref[...] = jnp.dot(turned_ref[...], residual, preferred_element_type=F32)
+
+
+def near_gradient_kernel(turned_ref, part_ref, rest_ref, sides_ref, last_ref, far_ref, out_ref, squares_ref):
+    rests = (rest_ref[512:], sides_ref[:128], last_ref[...], sides_ref[128:])
+    rest = jnp.concatenate([r.astype(F32) for r in rests], axis=0)
+    residual = (part_ref[...] + rest).astype(BF16)
     squares = jnp.zeros((8, COLS), F32)
     for x in range(NX):
         rows = slice(x * 512, (x + 1) * 512)
@@ -141,6 +148,10 @@
         compiler_params=PARAMS,
         name="embed",
     )(squares, gradient)
+
+
+def sum_kernel(blocks_ref, _, out_ref):
+    out_ref[...] = jnp.sum(blocks_ref[...].astype(F32), axis=0)
 
 
 def step_kernel(order_ref, squares_ref, rows_ref, weight_ref, global_ref, out_ref, new_ref):
@@ -212,28 +223,33 @@
         far = gather(arrived)
 
     with jax.named_scope("near_keys"):
-        near_part, near_sent, columns, near_turned = call(
+        near_part, near_sent, columns, near_turned, first_keys = call(
             near_kernel,
-            (SDS(tall, F32), SDS(tall, BF16), SDS((2048, COLS), BF16), SDS((2048, 512), BF16)),
-            place, *near, scalars=1, flops=dot_flops,
-        )
-        far_rest = flip(near_sent, 1)
+            (SDS(tall, F32), SDS((640, COLS), BF16), SDS((2048, COLS), BF16), SDS((2048, 512), BF16), SDS((128, COLS), F32)),
+            place, *near, arrived, scalars=1, flops=dot_flops,
+        )
+        rest = flip(near_sent, 1)
 
     with jax.named_scope("far_keys"):
-        far_sent, far_residual = call(
-            far_kernel, (SDS(tall, BF16), SDS(tall, BF16)), *far, columns, far_rest, flops=dot_flops
-        )
-        near_rest = flip(far_sent, 1)
-        far_turned = call(turn_kernel, SDS((2048, 512), BF16), *far)
+        sides_keys, sides_sent = call(
+            far_kernel, (SDS((256, COLS), F32), SDS((256, COLS), BF16)), far[1], far[3], columns, flops=dot_flops // 2
+        )
+        sides_rest = flip(sides_sent, 1)
+        last_keys, last_sent = call(
+            far_kernel, (SDS((128, COLS), F32), SDS((128, COLS), BF16)), far[2], columns, flops=dot_flops // 4
+        )
+        last_rest = flip(last_sent, 1)
+        far_turned = call(turn_kernel, SDS((2048, 512), BF16), far[0], far[1], far[3], far[2])
 
     with jax.named_scope("gradient"):
         far_gradient = call(
-            far_gradient_kernel, SDS((2048, COLS), F32), far_turned, far_residual, flops=dot_flops
+            far_gradient_kernel, SDS((2048, COLS), F32),
+            far_turned, first_keys, sides_keys, last_keys, rest, flops=dot_flops,
         )
         gradient, squares = call(
             near_gradient_kernel,
             (SDS((NX, 528, COLS), BF16), SDS((8, 128), F32)),
-            near_turned, near_part, near_rest, far_gradient, flops=dot_flops,
+            near_turned, near_part, rest, sides_rest, last_rest, far_gradient, flops=dot_flops,
         )
         squares = squares + flip(squares, 1)
         embedded = embed(squares, gradient)
@@ -241,7 +257,7 @@
 
     with jax.named_scope("outer_sum"):
         by_z = exchange(pending_delta[0].reshape(8, 64, 256), "rep", Z_GROUPS)
-        total = jnp.sum(by_z.astype(F32), axis=0)
+        total = call(sum_kernel, SDS((64, 256), F32), by_z, arrived, hbm=1)
         for mask in (1, 2, 4):
             total += lax.ppermute(total, "rep", [(i, i ^ mask) for i in range(64)])
         by_rows_z = exchange(jnp.broadcast_to(total[None], (8, 64, 256)), "rep", Z_GROUPS)

time: 156 us -> 143 us (0.917)
  the two profiles are of different devices: /device:TPU:16 before, /device:TPU:6 now
where the time goes in v6:
time: 143 us; the launch traced here: 141 us
  starting transfers between devices  80.9 us (57%)
  waiting for transfers between devices  42 us (29%)
  Pallas kernels  13.9 us (10%)
  other arithmetic  2.79 us (2%)
    ppermute x5, starting transfers between devices, flip(): return lax.ppermute(block, 'fsdp', [(i, i ^ mask) for i in range(8)])  27.7 us
    all_to_all x3, starting transfers between devices, exchange(): lax.all_to_all(blocks, axis, 0, 0, axis_index_groups=groups, tiled=True)  25.4 us
    ppermute x6, starting transfers between devices, rotate(): lax.ppermute(blocks[d], 'fsdp', moves[d])  17.8 us
    ppermute x5, waiting for transfers between devices, flip(): return lax.ppermute(block, 'fsdp', [(i, i ^ mask) for i in range(8)])  15.1 us
    pallas_call x8, Pallas kernels, call(): pl.pallas_call(kernel, in_specs=[SMEM] * scalars + [pl.BlockSpec(memory_s...  10.5 us
    ppermute x3, starting transfers between devices, body(): total += lax.ppermute(total, 'rep', [(i, i ^ mask) for i in range(64)])  10 us
    all_to_all x3, waiting for transfers between devices, exchange(): lax.all_to_all(blocks, axis, 0, 0, axis_index_groups=groups, tiled=True)  9.83 us
    ppermute x6, waiting for transfers between devices, rotate(): lax.ppermute(blocks[d], 'fsdp', moves[d])  9.73 us
  transfers between devices with their start and end apart: 17, of which 9 were waited for; matrix products, arithmetic and copies ran while one was open for 2% of the time, Pallas kernels for 5%

profile of v6, /device:TPU:6, one launch (start us, length us, event | category | flops | bytes accessed | tf_op | source)
XLA Modules:
  0.0 141.3 jit_solution(3449945366985290251)
XLA Ops:
  0.6 0.7 pad_add_fusion.place_ref
  1.3 4.5 %pack.1 = (bf16[128,2048]{1,0:T(8,128)(2,1)}, bf16[208,2048]{1,0:T(8,128)(2,1)}, bf16[208,2048]{1,0:T(8,128)(2,1)}, bf16[208,2048]{1,0:T(8,128)(2,1)}, bf16[208,2048]{1,0:T(8,128)(2,1)}) custom-call(s32[2]{0:T(128)} %pad_add_fusion.place_ref, bf16[128,4096]{1,0:T(8,128)(2,1)} %refs_0_.1, bf16[1,512,1024]{2,1,0:T(8,128)(2,1)} %weight_ref.1, ...), custom_call_target="tpu_custom_call" | custom-call | bytes 4194304 | tf_op jit(solution)/shard_map/activations/pack/pallas_call | solution.py:193
  5.8 0.0 copy-start.2
  5.9 7.9 %collective-permute-start.3 = (bf16[128,2048]{1,0:T(8,128)(2,1)}, bf16[128,2048]{1,0:T(8,128)(2,1)S(1)}, u32[]{:S(2)}, u32[]{:S(2)}) collective-permute-start(bf16[128,2048]{1,0:T(8,128)(2,1)} %get-tuple-element.23), channel_id=1, source_target_pairs={{0,1},{1,0},{2,3},{3,2},{4,5},{5,4},{6,7},{7,6},{8,9},{9,8},{10,11... | collective-permute-start | bytes 1572872 | tf_op jit(solution)/shard_map/activations/ppermute | solution.py:32
  13.7 10.3 %all-to-all-start.1 = ((bf16[8,64,256]{2,1,0:T(8,128)(2,1)}), bf16[8,64,256]{2,1,0:T(8,128)(2,1)S(1)}, u32[]{:S(2)}, u32[]{:S(2)}) async-start(bf16[8,64,256]{2,1,0:T(8,128)(2,1)} %bitcast.2), calls=%async_computation.1 | async-start | bytes 524288 | tf_op jit(solution)/shard_map/outer_sum/all_to_all | solution.py:28
  24.1 2.4 %collective-permute-start = (bf16[208,2048]{1,0:T(8,128)(2,1)}, bf16[208,2048]{1,0:T(8,128)(2,1)S(1)}, u32[]{:S(2)}, u32[]{:S(2)}) collective-permute-start(bf16[208,2048]{1,0:T(8,128)(2,1)} %get-tuple-element.20), channel_id=1, source_target_pairs={{0,2},{1,3},{2,4},{3,5},{4,6},{5,7},{6,0},{7,1},{8,10},{9,11},{10,... | collective-permute-start | bytes 2555912 | tf_op jit(solution)/shard_map/activations/ppermute | solution.py:37
  26.4 4.3 %collective-permute-start.1 = (bf16[208,2048]{1,0:T(8,128)(2,1)}, bf16[208,2048]{1,0:T(8,128)(2,1)S(1)}, u32[]{:S(2)}, u32[]{:S(2)}) collective-permute-start(bf16[208,2048]{1,0:T(8,128)(2,1)} %get-tuple-element.21), channel_id=1, source_target_pairs={{0,4},{1,5},{2,6},{3,7},{4,0},{5,1},{6,2},{7,3},{8,12},{9,13},{10,... | collective-permute-start | bytes 2555912 | tf_op jit(solution)/shard_map/activations/ppermute | solution.py:37
  30.8 1.9 %collective-permute-start.2 = (bf16[208,2048]{1,0:T(8,128)(2,1)}, bf16[208,2048]{1,0:T(8,128)(2,1)}, u32[]{:S(2)}, u32[]{:S(2)}) collective-permute-start(bf16[208,2048]{1,0:T(8,128)(2,1)} %get-tuple-element.22), channel_id=1, source_target_pairs={{0,6},{1,7},{2,0},{3,1},{4,2},{5,3},{6,4},{7,5},{8,14},{9,15},{10,... | collective-permute-start | bytes 2555912 | tf_op jit(solution)/shard_map/activations/ppermute | solution.py:37
  32.7 3.0 %all-to-all-done.1.blocks_ref = bf16[8,64,256]{2,1,0:T(8,128)(2,1)S(1)} async-done(((bf16[8,64,256]{2,1,0:T(8,128)(2,1)}), bf16[8,64,256]{2,1,0:T(8,128)(2,1)S(1)}, u32[]{:S(2)}, u32[]{:S(2)}) %all-to-all-start.1) | async-done | bytes 262176 | tf_op jit(solution)/shard_map/outer_sum/all_to_all | solution.py:28
  35.7 0.8 collective-permute-done.3.arrived_ref.b0._
  36.5 1.9 %collective-permute-start.11 = (f32[64,256]{1,0:T(8,128)S(1)}, f32[64,256]{1,0:T(8,128)S(1)}, u32[]{:S(2)}, u32[]{:S(2)}) collective-permute-start(f32[64,256]{1,0:T(8,128)S(1)} %sum.1), channel_id=1, source_target_pairs={{0,8},{8,0},{16,24},{24,16},{32,40},{40,32},{48,56},{56,48},{64,72... | collective-permute-start | bytes 196616 | tf_op jit(solution)/shard_map/outer_sum/ppermute | solution.py:262
  38.5 1.2 collective-permute-done.11
  39.7 3.1 %collective-permute-start.12 = (f32[64,256]{1,0:T(8,128)S(1)}, f32[64,256]{1,0:T(8,128)S(1)}, u32[]{:S(2)}, u32[]{:S(2)}) collective-permute-start(f32[64,256]{1,0:T(8,128)S(1)} %add.19), channel_id=1, source_target_pairs={{0,16},{8,24},{16,0},{24,8},{32,48},{40,56},{48,32},{56,40},{64,80... | collective-permute-start | bytes 196616 | tf_op jit(solution)/shard_map/outer_sum/ppermute | solution.py:262
  42.8 3.1 %collective-permute-done.12 = f32[64,256]{1,0:T(8,128)S(1)} collective-permute-done((f32[64,256]{1,0:T(8,128)S(1)}, f32[64,256]{1,0:T(8,128)S(1)}, u32[]{:S(2)}, u32[]{:S(2)}) %collective-permute-start.12) | collective-permute-done | bytes 65568 | tf_op jit(solution)/shard_map/outer_sum/ppermute | solution.py:262
  45.9 5.0 %collective-permute-start.13 = (f32[64,256]{1,0:T(8,128)S(1)}, f32[64,256]{1,0:T(8,128)S(1)}, u32[]{:S(2)}, u32[]{:S(2)}) collective-permute-start(f32[64,256]{1,0:T(8,128)S(1)} %add.20), channel_id=1, source_target_pairs={{0,32},{8,40},{16,48},{24,56},{32,0},{40,8},{48,16},{56,24},{64,96... | collective-permute-start | bytes 196616 | tf_op jit(solution)/shard_map/outer_sum/ppermute | solution.py:262
  50.9 2.9 %collective-permute-done.13 = f32[64,256]{1,0:T(8,128)S(1)} collective-permute-done((f32[64,256]{1,0:T(8,128)S(1)}, f32[64,256]{1,0:T(8,128)S(1)}, u32[]{:S(2)}, u32[]{:S(2)}) %collective-permute-start.13) | collective-permute-done | bytes 65568 | tf_op jit(solution)/shard_map/outer_sum/ppermute | solution.py:262
  53.9 0.8 broadcast_in_dim.2
  54.7 10.4 %all-to-all-start.2 = ((f32[8,64,256]{2,1,0:T(8,128)}), f32[8,64,256]{2,1,0:T(8,128)}, u32[]{:S(2)}, u32[]{:S(2)}) async-start(f32[8,64,256]{2,1,0:T(8,128)} %broadcast_in_dim.2), calls=%async_computation.2 | async-start | bytes 1048576 | tf_op jit(solution)/shard_map/outer_sum/all_to_all | solution.py:28
  65.1 2.4 %collective-permute-start.5 = (bf16[128,2048]{1,0:T(8,128)(2,1)S(1)}, bf16[128,2048]{1,0:T(8,128)(2,1)S(1)}, u32[]{:S(2)}, u32[]{:S(2)}) collective-permute-start(bf16[128,2048]{1,0:T(8,128)(2,1)S(1)} %collective-permute-done.3.arrived_ref.b0._), channel_id=1, source_target_pairs={{0,2},{1,3},{2,4},{3,5},{4,6},{5,7},{6,0},{7,1},{8,10},{9,11},{10,... | collective-permute-start | bytes 1572872 | tf_op jit(solution)/shard_map/activations/ppermute | solution.py:37
  67.5 3.5 %collective-permute-start.6 = (bf16[128,2048]{1,0:T(8,128)(2,1)S(1)}, bf16[128,2048]{1,0:T(8,128)(2,1)S(1)}, u32[]{:S(2)}, u32[]{:S(2)}) collective-permute-start(bf16[128,2048]{1,0:T(8,128)(2,1)S(1)} %collective-permute-done.3.arrived_ref.b0._), channel_id=1, source_target_pairs={{0,6},{1,7},{2,0},{3,1},{4,2},{5,3},{6,4},{7,5},{8,14},{9,15},{10,... | collective-permute-start | bytes 1572872 | tf_op jit(solution)/shard_map/activations/ppermute | solution.py:37
  71.0 0.0 collective-permute-done.m1
  71.0 3.3 %collective-permute-start.8 = (bf16[128,2048]{1,0:T(8,128)(2,1)S(1)}, bf16[128,2048]{1,0:T(8,128)(2,1)S(1)}, u32[]{:S(2)}, u32[]{:S(2)}) collective-permute-start(bf16[128,2048]{1,0:T(8,128)(2,1)S(1)} %collective-permute-done.3.arrived_ref.b0._), channel_id=1, source_target_pairs={{0,4},{1,5},{2,6},{3,7},{4,0},{5,1},{6,2},{7,3},{8,12},{9,13},{10,... | collective-permute-start | bytes 1572872 | tf_op jit(solution)/shard_map/activations/ppermute | solution.py:37
  74.3 0.0 collective-permute-done.1.m2
  74.3 0.0 collective-permute-done.2.m3
  74.3 2.1 %near.1 = (f32[512,256]{1,0:T(8,128)S(1)}, bf16[640,256]{1,0:T(8,128)(2,1)S(1)}, bf16[2048,256]{1,0:T(8,128)(2,1)S(1)}, bf16[2048,512]{1,0:T(8,128)(2,1)S(1)}, f32[128,256]{1,0:T(8,128)S(1)}) custom-call(s32[2]{0:T(128)S(1)} %copy-done.3, bf16[208,2048]{1,0:T(8,128)(2,1)S(1)} %copy-done.2, bf16[208,2048]{1,0:T(8,128)(2,1)S(1)} %collective-permute-done.m1, ...), custom_call_target="tpu_custom_call" | custom-call | flops 536870912 | bytes 4194304 | tf_op jit(solution)/shard_map/near_keys/near/pallas_call | solution.py:193
  76.5 7.7 %collective-permute-start.4 = (bf16[640,256]{1,0:T(8,128)(2,1)S(1)}, bf16[640,256]{1,0:T(8,128)(2,1)S(1)}, u32[]{:S(2)}, u32[]{:S(2)}) collective-permute-start(bf16[640,256]{1,0:T(8,128)(2,1)S(1)} %get-tuple-element.26), channel_id=1, source_target_pairs={{0,1},{1,0},{2,3},{3,2},{4,5},{5,4},{6,7},{7,6},{8,9},{9,8},{10,11... | collective-permute-start | bytes 983048 | tf_op jit(solution)/shard_map/near_keys/ppermute | solution.py:32
  84.2 0.0 collective-permute-done.5.refs_0_.b1
  84.2 9.7 %collective-permute-done.6.refs_1_.b3 = bf16[128,2048]{1,0:T(8,128)(2,1)S(1)} collective-permute-done((bf16[128,2048]{1,0:T(8,128)(2,1)S(1)}, bf16[128,2048]{1,0:T(8,128)(2,1)S(1)}, u32[]{:S(2)}, u32[]{:S(2)}) %collective-permute-start.6) | collective-permute-done | bytes 524320 | tf_op jit(solution)/shard_map/activations/ppermute | solution.py:37
  93.9 0.4 far.2
  94.3 8.3 %collective-permute-start.7 = (bf16[256,256]{1,0:T(8,128)(2,1)S(1)}, bf16[256,256]{1,0:T(8,128)(2,1)S(1)}, u32[]{:S(2)}, u32[]{:S(2)}) collective-permute-start(bf16[256,256]{1,0:T(8,128)(2,1)S(1)} %get-tuple-element.28), channel_id=1, source_target_pairs={{0,1},{1,0},{2,3},{3,2},{4,5},{5,4},{6,7},{7,6},{8,9},{9,8},{10,11... | collective-permute-start | bytes 393224 | tf_op jit(solution)/shard_map/far_keys/ppermute | solution.py:32
  102.7 0.0 collective-permute-done.8.refs_0_.b2
  102.7 0.3 far.3
  103.0 1.9 %collective-permute-start.9 = (bf16[128,256]{1,0:T(8,128)(2,1)S(1)}, bf16[128,256]{1,0:T(8,128)(2,1)S(1)}, u32[]{:S(2)}, u32[]{:S(2)}) collective-permute-start(bf16[128,256]{1,0:T(8,128)(2,1)S(1)} %get-tuple-element.29), channel_id=1, source_target_pairs={{0,1},{1,0},{2,3},{3,2},{4,5},{5,4},{6,7},{7,6},{8,9},{9,8},{10,11... | collective-permute-start | bytes 196616 | tf_op jit(solution)/shard_map/far_keys/ppermute | solution.py:32
  104.9 0.6 turn.1.turned_ref
  105.5 0.0 collective-permute-done.4.rest_ref
  105.6 0.7 far_gradient.1.far_ref
  106.3 6.8 %collective-permute-done.9.last_ref = bf16[128,256]{1,0:T(8,128)(2,1)S(1)} collective-permute-done((bf16[128,256]{1,0:T(8,128)(2,1)S(1)}, bf16[128,256]{1,0:T(8,128)(2,1)S(1)}, u32[]{:S(2)}, u32[]{:S(2)}) %collective-permute-start.9) | collective-permute-done | bytes 65568 | tf_op jit(solution)/shard_map/far_keys/ppermute | solution.py:32
  113.1 0.0 collective-permute-done.7.sides_ref
  113.1 1.7 %near_gradient.1 = (bf16[4,528,256]{2,1,0:T(8,128)(2,1)}, f32[8,128]{1,0:T(8,128)S(1)}) custom-call(bf16[2048,512]{1,0:T(8,128)(2,1)S(1)} %get-tuple-element.24.turned_ref, f32[512,256]{1,0:T(8,128)S(1)} %get-tuple-element.25.part_ref, bf16[640,256]{1,0:T(8,128)(2,1)S(1)} %collective-permute-done.4.rest_ref, ...), custom_call_target="tpu_custom_call" | custom-call | flops 536870912 | bytes 4194304 | tf_op jit(solution)/shard_map/gradient/near_gradient/pallas_call | solution.py:193
  114.8 1.9 %collective-permute-start.10 = (f32[8,128]{1,0:T(8,128)S(1)}, f32[8,128]{1,0:T(8,128)S(1)}, u32[]{:S(2)}, u32[]{:S(2)}) collective-permute-start(f32[8,128]{1,0:T(8,128)S(1)} %get-tuple-element.33), channel_id=1, source_target_pairs={{0,1},{1,0},{2,3},{3,2},{4,5},{5,4},{6,7},{7,6},{8,9},{9,8},{10,11... | collective-permute-start | bytes 12296 | tf_op jit(solution)/shard_map/gradient/ppermute | solution.py:32
  116.8 7.5 %collective-permute-done.10 = f32[8,128]{1,0:T(8,128)S(1)} collective-permute-done((f32[8,128]{1,0:T(8,128)S(1)}, f32[8,128]{1,0:T(8,128)S(1)}, u32[]{:S(2)}, u32[]{:S(2)}) %collective-permute-start.10) | collective-permute-done | bytes 4128 | tf_op jit(solution)/shard_map/gradient/ppermute | solution.py:32
  124.2 0.6 embed.1
  124.9 0.0 all-to-all-done.2
  124.9 4.6 %all-to-all-start = ((bf16[4,528,256]{2,1,0:T(8,128)(2,1)}), bf16[4,528,256]{2,1,0:T(8,128)(2,1)S(1)}, u32[]{:S(2)}, u32[]{:S(2)}) async-start(bf16[4,528,256]{2,1,0:T(8,128)(2,1)} %embed.1), calls=%async_computation | async-start | bytes 2162688 | tf_op jit(solution)/shard_map/gradient/all_to_all | solution.py:28
  129.5 1.2 broadcast_multiply_fusion
  130.7 0.9 fusion.2
  131.6 6.9 %all-to-all-done.squares_ref.rows_ref = bf16[4,528,256]{2,1,0:T(8,128)(2,1)S(1)} async-done(((bf16[4,528,256]{2,1,0:T(8,128)(2,1)}), bf16[4,528,256]{2,1,0:T(8,128)(2,1)S(1)}, u32[]{:S(2)}, u32[]{:S(2)}) %all-to-all-start) | async-done | bytes 1081376 | tf_op jit(solution)/shard_map/gradient/all_to_all | solution.py:28
  138.5 2.8 %step.1 = bf16[1,512,1024]{2,1,0:T(8,128)(2,1)} custom-call(s32[8]{0:T(128)S(1)} %copy-done.4, bf16[4,528,256]{2,1,0:T(8,128)(2,1)S(1)} %all-to-all-done.squares_ref.rows_ref, bf16[4,528,256]{2,1,0:T(8,128)(2,1)S(1)} %all-to-all-done.squares_ref.rows_ref, bf16[1,512,1024]{2,1,0:T(8,128)(2,1)S(1)} %copy-done, bf16[512,256]{1,0:T(8,128)(2,1)S(1)} %get-tuple-element.35.global_ref), custom_call_target="tpu_custom_call" | custom-call | tf_op jit(solution)/shard_map/step/step/pallas_call | solution.py:173
  (18 shorter events, 0.1 us)
Async XLA Ops:
  5.8 68.5 %copy-start.2 = (bf16[208,2048]{1,0:T(8,128)(2,1)S(1)}, bf16[208,2048]{1,0:T(8,128)(2,1)}, u32[]{:S(2)}) copy-start(bf16[208,2048]{1,0:T(8,128)(2,1)} %get-tuple-element.19.m0) | copy-start | bytes 2555908
  5.9 68.5 %copy-start.3 = (s32[2]{0:T(128)S(1)}, s32[2]{0:T(128)}, u32[]{:S(2)}) copy-start(s32[2]{0:T(128)} %pad_add_fusion.place_ref) | copy-start | bytes 28
  5.9 30.6 %collective-permute-start.3 = (bf16[128,2048]{1,0:T(8,128)(2,1)}, bf16[128,2048]{1,0:T(8,128)(2,1)S(1)}, u32[]{:S(2)}, u32[]{:S(2)}) collective-permute-start(bf16[128,2048]{1,0:T(8,128)(2,1)} %get-tuple-element.23), channel_id=1, source_target_pairs={{0,1},{1,0},{2,3},{3,2},{4,5},{5,4},{6,7},{7,6},{8,9},{9,8},{10,11... | collective-permute-start | bytes 1572872 | tf_op jit(solution)/shard_map/activations/ppermute | solution.py:32
  13.7 21.9 %all-to-all-start.1 = ((bf16[8,64,256]{2,1,0:T(8,128)(2,1)}), bf16[8,64,256]{2,1,0:T(8,128)(2,1)S(1)}, u32[]{:S(2)}, u32[]{:S(2)}) async-start(bf16[8,64,256]{2,1,0:T(8,128)(2,1)} %bitcast.2), calls=%async_computation.1 | async-start | bytes 524288 | tf_op jit(solution)/shard_map/outer_sum/all_to_all | solution.py:28
  24.1 46.9 %collective-permute-start = (bf16[208,2048]{1,0:T(8,128)(2,1)}, bf16[208,2048]{1,0:T(8,128)(2,1)S(1)}, u32[]{:S(2)}, u32[]{:S(2)}) collective-permute-start(bf16[208,2048]{1,0:T(8,128)(2,1)} %get-tuple-element.20), channel_id=1, source_target_pairs={{0,2},{1,3},{2,4},{3,5},{4,6},{5,7},{6,0},{7,1},{8,10},{9,11},{10,... | collective-permute-start | bytes 2555912 | tf_op jit(solution)/shard_map/activations/ppermute | solution.py:37
  26.4 47.9 %collective-permute-start.1 = (bf16[208,2048]{1,0:T(8,128)(2,1)}, bf16[208,2048]{1,0:T(8,128)(2,1)S(1)}, u32[]{:S(2)}, u32[]{:S(2)}) collective-permute-start(bf16[208,2048]{1,0:T(8,128)(2,1)} %get-tuple-element.21), channel_id=1, source_target_pairs={{0,4},{1,5},{2,6},{3,7},{4,0},{5,1},{6,2},{7,3},{8,12},{9,13},{10,... | collective-permute-start | bytes 2555912 | tf_op jit(solution)/shard_map/activations/ppermute | solution.py:37
  30.8 43.5 %collective-permute-start.2 = (bf16[208,2048]{1,0:T(8,128)(2,1)}, bf16[208,2048]{1,0:T(8,128)(2,1)}, u32[]{:S(2)}, u32[]{:S(2)}) collective-permute-start(bf16[208,2048]{1,0:T(8,128)(2,1)} %get-tuple-element.22), channel_id=1, source_target_pairs={{0,6},{1,7},{2,0},{3,1},{4,2},{5,3},{6,4},{7,5},{8,14},{9,15},{10,... | collective-permute-start | bytes 2555912 | tf_op jit(solution)/shard_map/activations/ppermute | solution.py:37
  36.5 3.1 %collective-permute-start.11 = (f32[64,256]{1,0:T(8,128)S(1)}, f32[64,256]{1,0:T(8,128)S(1)}, u32[]{:S(2)}, u32[]{:S(2)}) collective-permute-start(f32[64,256]{1,0:T(8,128)S(1)} %sum.1), channel_id=1, source_target_pairs={{0,8},{8,0},{16,24},{24,16},{32,40},{40,32},{48,56},{56,48},{64,72... | collective-permute-start | bytes 196616 | tf_op jit(solution)/shard_map/outer_sum/ppermute | solution.py:262
  39.7 6.2 %collective-permute-start.12 = (f32[64,256]{1,0:T(8,128)S(1)}, f32[64,256]{1,0:T(8,128)S(1)}, u32[]{:S(2)}, u32[]{:S(2)}) collective-permute-start(f32[64,256]{1,0:T(8,128)S(1)} %add.19), channel_id=1, source_target_pairs={{0,16},{8,24},{16,0},{24,8},{32,48},{40,56},{48,32},{56,40},{64,80... | collective-permute-start | bytes 196616 | tf_op jit(solution)/shard_map/outer_sum/ppermute | solution.py:262
  45.9 8.0 %collective-permute-start.13 = (f32[64,256]{1,0:T(8,128)S(1)}, f32[64,256]{1,0:T(8,128)S(1)}, u32[]{:S(2)}, u32[]{:S(2)}) collective-permute-start(f32[64,256]{1,0:T(8,128)S(1)} %add.20), channel_id=1, source_target_pairs={{0,32},{8,40},{16,48},{24,56},{32,0},{40,8},{48,16},{56,24},{64,96... | collective-permute-start | bytes 196616 | tf_op jit(solution)/shard_map/outer_sum/ppermute | solution.py:262
  54.7 70.2 %all-to-all-start.2 = ((f32[8,64,256]{2,1,0:T(8,128)}), f32[8,64,256]{2,1,0:T(8,128)}, u32[]{:S(2)}, u32[]{:S(2)}) async-start(f32[8,64,256]{2,1,0:T(8,128)} %broadcast_in_dim.2), calls=%async_computation.2 | async-start | bytes 1048576 | tf_op jit(solution)/shard_map/outer_sum/all_to_all | solution.py:28
  65.1 19.1 %collective-permute-start.5 = (bf16[128,2048]{1,0:T(8,128)(2,1)S(1)}, bf16[128,2048]{1,0:T(8,128)(2,1)S(1)}, u32[]{:S(2)}, u32[]{:S(2)}) collective-permute-start(bf16[128,2048]{1,0:T(8,128)(2,1)S(1)} %collective-permute-done.3.arrived_ref.b0._), channel_id=1, source_target_pairs={{0,2},{1,3},{2,4},{3,5},{4,6},{5,7},{6,0},{7,1},{8,10},{9,11},{10,... | collective-permute-start | bytes 1572872 | tf_op jit(solution)/shard_map/activations/ppermute | solution.py:37
  67.5 26.4 %collective-permute-start.6 = (bf16[128,2048]{1,0:T(8,128)(2,1)S(1)}, bf16[128,2048]{1,0:T(8,128)(2,1)S(1)}, u32[]{:S(2)}, u32[]{:S(2)}) collective-permute-start(bf16[128,2048]{1,0:T(8,128)(2,1)S(1)} %collective-permute-done.3.arrived_ref.b0._), channel_id=1, source_target_pairs={{0,6},{1,7},{2,0},{3,1},{4,2},{5,3},{6,4},{7,5},{8,14},{9,15},{10,... | collective-permute-start | bytes 1572872 | tf_op jit(solution)/shard_map/activations/ppermute | solution.py:37
  71.0 31.7 %collective-permute-start.8 = (bf16[128,2048]{1,0:T(8,128)(2,1)S(1)}, bf16[128,2048]{1,0:T(8,128)(2,1)S(1)}, u32[]{:S(2)}, u32[]{:S(2)}) collective-permute-start(bf16[128,2048]{1,0:T(8,128)(2,1)S(1)} %collective-permute-done.3.arrived_ref.b0._), channel_id=1, source_target_pairs={{0,4},{1,5},{2,6},{3,7},{4,0},{5,1},{6,2},{7,3},{8,12},{9,13},{10,... | collective-permute-start | bytes 1572872 | tf_op jit(solution)/shard_map/activations/ppermute | solution.py:37
  76.5 29.1 %collective-permute-start.4 = (bf16[640,256]{1,0:T(8,128)(2,1)S(1)}, bf16[640,256]{1,0:T(8,128)(2,1)S(1)}, u32[]{:S(2)}, u32[]{:S(2)}) collective-permute-start(bf16[640,256]{1,0:T(8,128)(2,1)S(1)} %get-tuple-element.26), channel_id=1, source_target_pairs={{0,1},{1,0},{2,3},{3,2},{4,5},{5,4},{6,7},{7,6},{8,9},{9,8},{10,11... | collective-permute-start | bytes 983048 | tf_op jit(solution)/shard_map/near_keys/ppermute | solution.py:32
  94.3 18.8 %collective-permute-start.7 = (bf16[256,256]{1,0:T(8,128)(2,1)S(1)}, bf16[256,256]{1,0:T(8,128)(2,1)S(1)}, u32[]{:S(2)}, u32[]{:S(2)}) collective-permute-start(bf16[256,256]{1,0:T(8,128)(2,1)S(1)} %get-tuple-element.28), channel_id=1, source_target_pairs={{0,1},{1,0},{2,3},{3,2},{4,5},{5,4},{6,7},{7,6},{8,9},{9,8},{10,11... | collective-permute-start | bytes 393224 | tf_op jit(solution)/shard_map/far_keys/ppermute | solution.py:32
  103.0 10.1 %collective-permute-start.9 = (bf16[128,256]{1,0:T(8,128)(2,1)S(1)}, bf16[128,256]{1,0:T(8,128)(2,1)S(1)}, u32[]{:S(2)}, u32[]{:S(2)}) collective-permute-start(bf16[128,256]{1,0:T(8,128)(2,1)S(1)} %get-tuple-element.29), channel_id=1, source_target_pairs={{0,1},{1,0},{2,3},{3,2},{4,5},{5,4},{6,7},{7,6},{8,9},{9,8},{10,11... | collective-permute-start | bytes 196616 | tf_op jit(solution)/shard_map/far_keys/ppermute | solution.py:32
  114.8 9.4 %collective-permute-start.10 = (f32[8,128]{1,0:T(8,128)S(1)}, f32[8,128]{1,0:T(8,128)S(1)}, u32[]{:S(2)}, u32[]{:S(2)}) collective-permute-start(f32[8,128]{1,0:T(8,128)S(1)} %get-tuple-element.33), channel_id=1, source_target_pairs={{0,1},{1,0},{2,3},{3,2},{4,5},{5,4},{6,7},{7,6},{8,9},{9,8},{10,11... | collective-permute-start | bytes 12296 | tf_op jit(solution)/shard_map/gradient/ppermute | solution.py:32
  124.9 5.8 %copy-start.5 = (f32[512,256]{1,0:T(8,128)S(1)}, f32[512,256]{1,0:T(8,128)}, u32[]{:S(2)}) copy-start(f32[512,256]{1,0:T(8,128)} %param.13) | copy-start | bytes 1572868
  124.9 5.8 %copy-start.6 = (bf16[512,256]{1,0:T(8,128)(2,1)S(1)}, bf16[512,256]{1,0:T(8,128)(2,1)}, u32[]{:S(2)}) copy-start(bf16[512,256]{1,0:T(8,128)(2,1)} %param.12) | copy-start | bytes 786436
  124.9 13.6 %all-to-all-start = ((bf16[4,528,256]{2,1,0:T(8,128)(2,1)}), bf16[4,528,256]{2,1,0:T(8,128)(2,1)S(1)}, u32[]{:S(2)}, u32[]{:S(2)}) async-start(bf16[4,528,256]{2,1,0:T(8,128)(2,1)} %embed.1), calls=%async_computation | async-start | bytes 2162688 | tf_op jit(solution)/shard_map/gradient/all_to_all | solution.py:28
  129.5 9.0 %copy-start = (bf16[1,512,1024]{2,1,0:T(8,128)(2,1)S(1)}, bf16[1,512,1024]{2,1,0:T(8,128)(2,1)}, u32[]{:S(2)}) copy-start(bf16[1,512,1024]{2,1,0:T(8,128)(2,1)} %weight_ref.1) | copy-start | bytes 3145732
  129.5 9.0 %copy-start.4 = (s32[8]{0:T(128)S(1)}, s32[8]{0:T(128)}, u32[]{:S(2)}) copy-start(s32[8]{0:T(128)} %order_ref.1) | copy-start | bytes 100
  131.6 9.7 %copy-start.1 = (bf16[512,256]{1,0:T(8,128)(2,1)}, bf16[512,256]{1,0:T(8,128)(2,1)S(1)}, u32[]{:S(2)}) copy-start(bf16[512,256]{1,0:T(8,128)(2,1)S(1)} %get-tuple-element.35.global_ref) | copy-start | bytes 786436

commit v7 on v6

--- a/solution.py
+++ b/solution.py
@@ -41,31 +41,38 @@
     return rotate([block] * NX)
 
 
-def pack_kernel(place_ref, *refs):
-    sources, other_ref, message_refs, held, done = refs[:3], refs[3], refs[4:8], refs[8:11], refs[11]
-    fetches = [pltpu.make_async_copy(s, h, done.at[i]) for i, (s, h) in enumerate(zip(sources, held))]
+def pack_kernel(index_ref, *refs):
+    sources, outs, held, (mine_ref, away_ref, columns_ref), (fetched, stored) = refs[:3], refs[3:8], refs[8:11], refs[11:14], refs[14:]
+    fetches = [pltpu.make_async_copy(s, h, fetched.at[i]) for i, (s, h) in enumerate(zip(sources, held))]
     for fetch in fetches:
         fetch.start()
-    half, x = place_ref[0], place_ref[1]
+    half, x = lax.rem(index_ref[0], 2), lax.div(index_ref[0], 2)
     tokens_ref, weight_ref, targets_ref = held
     fetches[0].wait()
     floated = tokens_ref[...].astype(F32)
     scale = lax.rsqrt(jnp.mean(floated * floated, axis=-1, keepdims=True) + 1e-06)
-    for block in range(NX):
-        lanes = slice(block * 512, (block + 1) * 512)
-        for refs, side in ((message_refs, half), ((other_ref,), 1 - half)):
+    for ref, side in ((away_ref, 1 - half), (mine_ref, half)):
+        for block in range(NX):
             start = pl.multiple_of((2 * block + side) * 512, 512)
-            piece = (tokens_ref[:, pl.ds(start, 512)].astype(F32) * scale).astype(BF16)
-            for ref in refs:
-                ref[:128, lanes] = piece
+            piece = tokens_ref[:, pl.ds(start, 512)].astype(F32) * scale
+            ref[:, block * 512 : (block + 1) * 512] = piece.astype(BF16)
+    stores = [pltpu.make_async_copy(away_ref, outs[0], stored.at[0])]
+    stores += [pltpu.make_async_copy(mine_ref, out.at[:128], stored.at[1 + d]) for d, out in enumerate(outs[1:])]
+    for store in stores:
+        store.start()
     fetches[1].wait()
     fetches[2].wait()
-    for d, ref in enumerate(message_refs):
+    for d, out in enumerate(outs[1:]):
         columns = pl.ds(pl.multiple_of(lax.rem(x + d, NX) * COLS, COLS), COLS)
         for j in range(8):
             lanes = slice(j * COLS, (j + 1) * COLS)
-            ref[128:192, lanes] = weight_ref[0, j * 64 : (j + 1) * 64, columns]
-            ref[192:, lanes] = targets_ref[j * 16 : (j + 1) * 16, columns]
+            columns_ref[d, :64, lanes] = weight_ref[0, j * 64 : (j + 1) * 64, columns]
+            columns_ref[d, 64:, lanes] = targets_ref[j * 16 : (j + 1) * 16, columns]
+        store = pltpu.make_async_copy(columns_ref.at[d], out.at[128:], stored.at[5 + d])
+        store.start()
+        stores.append(store)
+    for store in stores:
+        store.wait()
 
 
 def raw_keys(blocks, weight):
@@ -73,10 +80,10 @@
     return jnp.dot(lhs, weight, preferred_element_type=F32) * FACTOR
 
 
-def near_kernel(place_ref, m0, m1, m2, m3, arrived_ref, part_ref, sent_ref, weight_ref, turned_ref, first_ref):
+def near_kernel(index_ref, m0, m1, m2, m3, arrived_ref, part_ref, sent_ref, weight_ref, turned_ref, first_ref):
     messages = (m0, m1, m2, m3)
     for d, m in enumerate(messages):
-        source = lax.rem(place_ref[1] - d + NX, NX)
+        source = lax.rem(lax.div(index_ref[0], 2) - d + NX, NX)
         for j in range(8):
             rows = pl.ds(pl.multiple_of(source * 512 + j * 64, 64), 64)
             weight_ref[rows, :] = m[128:192, j * COLS : (j + 1) * COLS]
@@ -188,7 +195,7 @@
     )(order, rows, rows, weight, new_global)
 
 
-def call(kernel, outs, *args, scalars=0, hbm=0, scratch=(), vmem_mib=16, flops=0):
+def call(kernel, outs, *args, scalars=0, hbm=0, scratch=(), vmem_mib=16, out_space=pltpu.VMEM, flops=0):
     vmem = len(args) - scalars - hbm
     return pl.pallas_call(
         kernel,
@@ -196,7 +203,7 @@
         + [pl.BlockSpec(memory_space=pltpu.VMEM)] * vmem
         + [pl.BlockSpec(memory_space=pltpu.HBM)] * hbm,
         scratch_shapes=scratch,
-        out_specs=jax.tree.map(lambda _: pl.BlockSpec(memory_space=pltpu.VMEM), outs),
+        out_specs=jax.tree.map(lambda _: pl.BlockSpec(memory_space=out_space), outs),
         out_shape=outs,
         compiler_params=pltpu.CompilerParams(vmem_limit_bytes=vmem_mib << 20),
         cost_estimate=pl.CostEstimate(flops=flops, bytes_accessed=4 << 20, transcendentals=0),
@@ -205,8 +212,7 @@
 
 
 def body(tokens, targets, local_weights, pending_delta, frag_order, global_frag, outer_momentum):
-    index = lax.axis_index("fsdp")
-    place = jnp.stack([lax.rem(index, 2), lax.div(index, 2)]).astype(jnp.int32)
+    index = lax.axis_index("fsdp").astype(jnp.int32).reshape(1)
     dot_flops = 2 * 512 * 2048 * COLS
     tall = (512, COLS)
 
@@ -214,9 +220,10 @@
         other, *messages = call(
             pack_kernel,
             (SDS((128, 2048), BF16),) + (SDS((208, 2048), BF16),) * NX,
-            place, tokens, local_weights, targets, scalars=1, hbm=3, vmem_mib=58,
+            index, tokens, local_weights, targets, scalars=1, hbm=3, out_space=pltpu.HBM, vmem_mib=58,
             scratch=[pltpu.VMEM(a.shape, BF16) for a in (tokens, local_weights, targets)]
-            + [pltpu.SemaphoreType.DMA((3,))],
+            + [pltpu.VMEM((128, 2048), BF16)] * 2
+            + [pltpu.VMEM((NX, 80, 2048), BF16), pltpu.SemaphoreType.DMA((3,)), pltpu.SemaphoreType.DMA((9,))],
         )
         arrived = flip(other, 1)
         near = rotate(messages)
@@ -226,7 +233,7 @@
         near_part, near_sent, columns, near_turned, first_keys = call(
             near_kernel,
             (SDS(tall, F32), SDS((640, COLS), BF16), SDS((2048, COLS), BF16), SDS((2048, 512), BF16), SDS((128, COLS), F32)),
-            place, *near, arrived, scalars=1, flops=dot_flops,
+            index, *near, arrived, scalars=1, flops=dot_flops,
         )
         rest = flip(near_sent, 1)
 
@@ -260,8 +267,8 @@
         total = call(sum_kernel, SDS((64, 256), F32), by_z, arrived, hbm=1)
         for mask in (1, 2, 4):
             total += lax.ppermute(total, "rep", [(i, i ^ mask) for i in range(64)])
-        by_rows_z = exchange(jnp.broadcast_to(total[None], (8, 64, 256)), "rep", Z_GROUPS)
-        mean = by_rows_z.reshape(512, 256) / lax.axis_size("rep")
+        by_rows_z = exchange(jnp.broadcast_to(total.astype(BF16)[None], (8, 64, 256)), "rep", Z_GROUPS)
+        mean = by_rows_z.astype(F32).reshape(512, 256) / lax.axis_size("rep")
         new_momentum = 0.9 * outer_momentum + mean
         new_global = (global_frag.astype(F32) - 0.7 * (mean + 0.9 * new_momentum)).astype(BF16)
 

time: 143 us -> 137 us (0.958)
  waiting for transfers between devices: 42 us -> 30.4 us
  starting transfers between devices: 80.9 us -> 88.1 us
  other arithmetic: 2.79 us -> 1.01 us
    ppermute x6, starting transfers between devices: 17.8 us -> 24.3 us  [rotate(): lax.ppermute(blocks[d], 'fsdp', moves[d])]
    ppermute x5, waiting for transfers between devices: 15.1 us -> 8.8 us  [flip(): return lax.ppermute(block, 'fsdp', [(i, i ^ mask) for i in range(8)])]
    ppermute x6, waiting for transfers between devices: 9.73 us -> 3.5 us  [rotate(): lax.ppermute(blocks[d], 'fsdp', moves[d])]
    all_to_all x3, waiting for transfers between devices: 9.83 us -> 13.8 us  [exchange(): lax.all_to_all(blocks, axis, 0, 0, axis_index_groups=groups, tiled=True)]
    ppermute x3, waiting for transfers between devices: 7.26 us -> 4.34 us  [body(): total += lax.ppermute(total, 'rep', [(i, i ^ mask) for i in range(64)])]
    all_to_all x3, starting transfers between devices: 25.4 us -> 28.1 us  [exchange(): lax.all_to_all(blocks, axis, 0, 0, axis_index_groups=groups, tiled=True)]
    ppermute x5, starting transfers between devices: 27.7 us -> 25.7 us  [flip(): return lax.ppermute(block, 'fsdp', [(i, i ^ mask) for i in range(8)])]
  transfers between devices with their start and end apart: 17 -> 17, of which waited for: 9 -> 9; matrix products, arithmetic and copies ran while one was open for 2% -> 1% of each run, Pallas kernels for 5% -> 5%
where the time goes in v7:
time: 137 us; the launch traced here: 135 us
  starting transfers between devices  88.1 us (64%)
  waiting for transfers between devices  30.4 us (22%)
  Pallas kernels  13.5 us (10%)
    all_to_all x3, starting transfers between devices, exchange(): lax.all_to_all(blocks, axis, 0, 0, axis_index_groups=groups, tiled=True)  28.1 us
    ppermute x5, starting transfers between devices, flip(): return lax.ppermute(block, 'fsdp', [(i, i ^ mask) for i in range(8)])  25.7 us
    ppermute x6, starting transfers between devices, rotate(): lax.ppermute(blocks[d], 'fsdp', moves[d])  24.3 us
    all_to_all x3, waiting for transfers between devices, exchange(): lax.all_to_all(blocks, axis, 0, 0, axis_index_groups=groups, tiled=True)  13.8 us
    pallas_call x8, Pallas kernels, call(): pl.pallas_call(kernel, in_specs=[SMEM] * scalars + [pl.BlockSpec(memory_s...  10.1 us
    ppermute x3, starting transfers between devices, body(): total += lax.ppermute(total, 'rep', [(i, i ^ mask) for i in range(64)])  9.98 us
    ppermute x5, waiting for transfers between devices, flip(): return lax.ppermute(block, 'fsdp', [(i, i ^ mask) for i in range(8)])  8.8 us
    ppermute x3, waiting for transfers between devices, body(): total += lax.ppermute(total, 'rep', [(i, i ^ mask) for i in range(64)])  4.34 us
  transfers between devices with their start and end apart: 17, of which 9 were waited for; matrix products, arithmetic and copies ran while one was open for 1% of the time, Pallas kernels for 5%

profile of v7, /device:TPU:6, one launch (start us, length us, event | category | flops | bytes accessed | tf_op | source)
XLA Modules:
  0.0 134.6 jit_solution(14705275923530226485)
XLA Ops:
  0.6 3.6 %pack.1 = (bf16[128,2048]{1,0:T(8,128)(2,1)}, bf16[208,2048]{1,0:T(8,128)(2,1)}, bf16[208,2048]{1,0:T(8,128)(2,1)}, bf16[208,2048]{1,0:T(8,128)(2,1)}, bf16[208,2048]{1,0:T(8,128)(2,1)}) custom-call(s32[1]{0:T(128)} %bitcast.index_ref, bf16[128,4096]{1,0:T(8,128)(2,1)} %refs_0_.1, bf16[1,512,1024]{2,1,0:T(8,128)(2,1)} %weight_ref.1, bf16[128,1024]{1,0:T(8,128)(2,1)} %refs_2_.1), custom_call_target="tpu_custom_call" | custom-call | bytes 4194304 | tf_op jit(solution)/shard_map/activations/pack/pallas_call | solution.py:200
  4.2 0.0 copy-start.2
  4.2 7.9 %collective-permute-start = (bf16[208,2048]{1,0:T(8,128)(2,1)}, bf16[208,2048]{1,0:T(8,128)(2,1)}, u32[]{:S(2)}, u32[]{:S(2)}) collective-permute-start(bf16[208,2048]{1,0:T(8,128)(2,1)} %get-tuple-element.20), channel_id=1, source_target_pairs={{0,2},{1,3},{2,4},{3,5},{4,6},{5,7},{6,0},{7,1},{8,10},{9,11},{10,... | collective-permute-start | bytes 2555912 | tf_op jit(solution)/shard_map/activations/ppermute | solution.py:37
  12.1 2.4 %collective-permute-start.3 = (bf16[128,2048]{1,0:T(8,128)(2,1)}, bf16[128,2048]{1,0:T(8,128)(2,1)S(1)}, u32[]{:S(2)}, u32[]{:S(2)}) collective-permute-start(bf16[128,2048]{1,0:T(8,128)(2,1)} %get-tuple-element.23), channel_id=1, source_target_pairs={{0,1},{1,0},{2,3},{3,2},{4,5},{5,4},{6,7},{7,6},{8,9},{9,8},{10,11... | collective-permute-start | bytes 1572872 | tf_op jit(solution)/shard_map/activations/ppermute | solution.py:32
  14.5 10.3 %all-to-all-start.1 = ((bf16[8,64,256]{2,1,0:T(8,128)(2,1)}), bf16[8,64,256]{2,1,0:T(8,128)(2,1)S(1)}, u32[]{:S(2)}, u32[]{:S(2)}) async-start(bf16[8,64,256]{2,1,0:T(8,128)(2,1)} %bitcast.1), calls=%async_computation.1 | async-start | bytes 524288 | tf_op jit(solution)/shard_map/outer_sum/all_to_all | solution.py:28
  24.8 4.3 %collective-permute-start.1 = (bf16[208,2048]{1,0:T(8,128)(2,1)}, bf16[208,2048]{1,0:T(8,128)(2,1)}, u32[]{:S(2)}, u32[]{:S(2)}) collective-permute-start(bf16[208,2048]{1,0:T(8,128)(2,1)} %get-tuple-element.21), channel_id=1, source_target_pairs={{0,4},{1,5},{2,6},{3,7},{4,0},{5,1},{6,2},{7,3},{8,12},{9,13},{10,... | collective-permute-start | bytes 2555912 | tf_op jit(solution)/shard_map/activations/ppermute | solution.py:37
  29.1 1.9 %collective-permute-start.2 = (bf16[208,2048]{1,0:T(8,128)(2,1)}, bf16[208,2048]{1,0:T(8,128)(2,1)}, u32[]{:S(2)}, u32[]{:S(2)}) collective-permute-start(bf16[208,2048]{1,0:T(8,128)(2,1)} %get-tuple-element.22), channel_id=1, source_target_pairs={{0,6},{1,7},{2,0},{3,1},{4,2},{5,3},{6,4},{7,5},{8,14},{9,15},{10,... | collective-permute-start | bytes 2555912 | tf_op jit(solution)/shard_map/activations/ppermute | solution.py:37
  31.1 5.1 %all-to-all-done.1.blocks_ref = bf16[8,64,256]{2,1,0:T(8,128)(2,1)S(1)} async-done(((bf16[8,64,256]{2,1,0:T(8,128)(2,1)}), bf16[8,64,256]{2,1,0:T(8,128)(2,1)S(1)}, u32[]{:S(2)}, u32[]{:S(2)}) %all-to-all-start.1) | async-done | bytes 262176 | tf_op jit(solution)/shard_map/outer_sum/all_to_all | solution.py:28
  36.1 0.8 collective-permute-done.3.arrived_ref.b0._
  37.0 1.9 %collective-permute-start.11 = (f32[64,256]{1,0:T(8,128)S(1)}, f32[64,256]{1,0:T(8,128)S(1)}, u32[]{:S(2)}, u32[]{:S(2)}) collective-permute-start(f32[64,256]{1,0:T(8,128)S(1)} %sum.1), channel_id=1, source_target_pairs={{0,8},{8,0},{16,24},{24,16},{32,40},{40,32},{48,56},{56,48},{64,72... | collective-permute-start | bytes 196616 | tf_op jit(solution)/shard_map/outer_sum/ppermute | solution.py:269
  38.9 1.2 collective-permute-done.11
  40.2 3.0 %collective-permute-start.12 = (f32[64,256]{1,0:T(8,128)S(1)}, f32[64,256]{1,0:T(8,128)S(1)}, u32[]{:S(2)}, u32[]{:S(2)}) collective-permute-start(f32[64,256]{1,0:T(8,128)S(1)} %add.19), channel_id=1, source_target_pairs={{0,16},{8,24},{16,0},{24,8},{32,48},{40,56},{48,32},{56,40},{64,80... | collective-permute-start | bytes 196616 | tf_op jit(solution)/shard_map/outer_sum/ppermute | solution.py:269
  43.2 3.1 %collective-permute-done.12 = f32[64,256]{1,0:T(8,128)S(1)} collective-permute-done((f32[64,256]{1,0:T(8,128)S(1)}, f32[64,256]{1,0:T(8,128)S(1)}, u32[]{:S(2)}, u32[]{:S(2)}) %collective-permute-start.12) | collective-permute-done | bytes 65568 | tf_op jit(solution)/shard_map/outer_sum/ppermute | solution.py:269
  46.3 5.0 %collective-permute-start.13 = (f32[64,256]{1,0:T(8,128)S(1)}, f32[64,256]{1,0:T(8,128)S(1)}, u32[]{:S(2)}, u32[]{:S(2)}) collective-permute-start(f32[64,256]{1,0:T(8,128)S(1)} %add.20), channel_id=1, source_target_pairs={{0,32},{8,40},{16,48},{24,56},{32,0},{40,8},{48,16},{56,24},{64,96... | collective-permute-start | bytes 196616 | tf_op jit(solution)/shard_map/outer_sum/ppermute | solution.py:269
  51.4 3.4 %collective-permute-start.5 = (bf16[128,2048]{1,0:T(8,128)(2,1)S(1)}, bf16[128,2048]{1,0:T(8,128)(2,1)S(1)}, u32[]{:S(2)}, u32[]{:S(2)}) collective-permute-start(bf16[128,2048]{1,0:T(8,128)(2,1)S(1)} %collective-permute-done.3.arrived_ref.b0._), channel_id=1, source_target_pairs={{0,2},{1,3},{2,4},{3,5},{4,6},{5,7},{6,0},{7,1},{8,10},{9,11},{10,... | collective-permute-start | bytes 1572872 | tf_op jit(solution)/shard_map/activations/ppermute | solution.py:37
  54.8 0.0 collective-permute-done.13
  54.8 3.1 %collective-permute-start.6 = (bf16[128,2048]{1,0:T(8,128)(2,1)S(1)}, bf16[128,2048]{1,0:T(8,128)(2,1)S(1)}, u32[]{:S(2)}, u32[]{:S(2)}) collective-permute-start(bf16[128,2048]{1,0:T(8,128)(2,1)S(1)} %collective-permute-done.3.arrived_ref.b0._), channel_id=1, source_target_pairs={{0,6},{1,7},{2,0},{3,1},{4,2},{5,3},{6,4},{7,5},{8,14},{9,15},{10,... | collective-permute-start | bytes 1572872 | tf_op jit(solution)/shard_map/activations/ppermute | solution.py:37
  57.9 0.0 collective-permute-done.m1
  57.9 3.7 %collective-permute-start.8 = (bf16[128,2048]{1,0:T(8,128)(2,1)S(1)}, bf16[128,2048]{1,0:T(8,128)(2,1)S(1)}, u32[]{:S(2)}, u32[]{:S(2)}) collective-permute-start(bf16[128,2048]{1,0:T(8,128)(2,1)S(1)} %collective-permute-done.3.arrived_ref.b0._), channel_id=1, source_target_pairs={{0,4},{1,5},{2,6},{3,7},{4,0},{5,1},{6,2},{7,3},{8,12},{9,13},{10,... | collective-permute-start | bytes 1572872 | tf_op jit(solution)/shard_map/activations/ppermute | solution.py:37
  61.6 0.7 broadcast_in_dim.2
  62.3 10.3 %all-to-all-start.2 = ((bf16[8,64,256]{2,1,0:T(8,128)(2,1)}), bf16[8,64,256]{2,1,0:T(8,128)(2,1)S(1)}, u32[]{:S(2)}, u32[]{:S(2)}) async-start(bf16[8,64,256]{2,1,0:T(8,128)(2,1)} %broadcast_in_dim.2), calls=%async_computation.2 | async-start | bytes 524288 | tf_op jit(solution)/shard_map/outer_sum/all_to_all | solution.py:28
  72.6 0.0 collective-permute-done.1.m2
  72.6 0.0 collective-permute-done.2.m3
  72.7 0.0 copy-done.2
  72.7 2.6 %near.1 = (f32[512,256]{1,0:T(8,128)S(1)}, bf16[640,256]{1,0:T(8,128)(2,1)S(1)}, bf16[2048,256]{1,0:T(8,128)(2,1)S(1)}, bf16[2048,512]{1,0:T(8,128)(2,1)S(1)}, f32[128,256]{1,0:T(8,128)S(1)}) custom-call(s32[1]{0:T(128)} %bitcast.index_ref, bf16[208,2048]{1,0:T(8,128)(2,1)S(1)} %copy-done.2, bf16[208,2048]{1,0:T(8,128)(2,1)} %collective-permute-done.m1, ...), custom_call_target="tpu_custom_call" | custom-call | flops 536870912 | bytes 4194304 | tf_op jit(solution)/shard_map/near_keys/near/pallas_call | solution.py:200
  75.3 7.3 %collective-permute-start.4 = (bf16[640,256]{1,0:T(8,128)(2,1)S(1)}, bf16[640,256]{1,0:T(8,128)(2,1)S(1)}, u32[]{:S(2)}, u32[]{:S(2)}) collective-permute-start(bf16[640,256]{1,0:T(8,128)(2,1)S(1)} %get-tuple-element.26), channel_id=1, source_target_pairs={{0,1},{1,0},{2,3},{3,2},{4,5},{5,4},{6,7},{7,6},{8,9},{9,8},{10,11... | collective-permute-start | bytes 983048 | tf_op jit(solution)/shard_map/near_keys/ppermute | solution.py:32
  82.6 0.0 collective-permute-done.5.refs_0_.b1
  82.6 0.0 collective-permute-done.6.refs_1_.b3
  82.6 0.5 far.2
  83.1 2.4 %collective-permute-start.7 = (bf16[256,256]{1,0:T(8,128)(2,1)S(1)}, bf16[256,256]{1,0:T(8,128)(2,1)S(1)}, u32[]{:S(2)}, u32[]{:S(2)}) collective-permute-start(bf16[256,256]{1,0:T(8,128)(2,1)S(1)} %get-tuple-element.28), channel_id=1, source_target_pairs={{0,1},{1,0},{2,3},{3,2},{4,5},{5,4},{6,7},{7,6},{8,9},{9,8},{10,11... | collective-permute-start | bytes 393224 | tf_op jit(solution)/shard_map/far_keys/ppermute | solution.py:32
  85.5 3.5 %collective-permute-done.8.refs_0_.b2 = bf16[128,2048]{1,0:T(8,128)(2,1)S(1)} collective-permute-done((bf16[128,2048]{1,0:T(8,128)(2,1)S(1)}, bf16[128,2048]{1,0:T(8,128)(2,1)S(1)}, u32[]{:S(2)}, u32[]{:S(2)}) %collective-permute-start.8) | collective-permute-done | bytes 524320 | tf_op jit(solution)/shard_map/activations/ppermute | solution.py:37
  89.0 0.3 far.3
  89.3 3.8 %collective-permute-start.9 = (bf16[128,256]{1,0:T(8,128)(2,1)S(1)}, bf16[128,256]{1,0:T(8,128)(2,1)S(1)}, u32[]{:S(2)}, u32[]{:S(2)}) collective-permute-start(bf16[128,256]{1,0:T(8,128)(2,1)S(1)} %get-tuple-element.29), channel_id=1, source_target_pairs={{0,1},{1,0},{2,3},{3,2},{4,5},{5,4},{6,7},{7,6},{8,9},{9,8},{10,11... | collective-permute-start | bytes 196616 | tf_op jit(solution)/shard_map/far_keys/ppermute | solution.py:32
  93.2 0.6 turn.1.turned_ref
  93.8 4.2 %collective-permute-done.4.rest_ref = bf16[640,256]{1,0:T(8,128)(2,1)S(1)} collective-permute-done((bf16[640,256]{1,0:T(8,128)(2,1)S(1)}, bf16[640,256]{1,0:T(8,128)(2,1)S(1)}, u32[]{:S(2)}, u32[]{:S(2)}) %collective-permute-start.4) | collective-permute-done | bytes 327712 | tf_op jit(solution)/shard_map/near_keys/ppermute | solution.py:32
  98.0 0.7 far_gradient.1.far_ref
  98.7 2.2 %collective-permute-done.9.last_ref = bf16[128,256]{1,0:T(8,128)(2,1)S(1)} collective-permute-done((bf16[128,256]{1,0:T(8,128)(2,1)S(1)}, bf16[128,256]{1,0:T(8,128)(2,1)S(1)}, u32[]{:S(2)}, u32[]{:S(2)}) %collective-permute-start.9) | collective-permute-done | bytes 65568 | tf_op jit(solution)/shard_map/far_keys/ppermute | solution.py:32
  100.9 0.0 collective-permute-done.7.sides_ref
  100.9 1.8 %near_gradient.1 = (bf16[4,528,256]{2,1,0:T(8,128)(2,1)}, f32[8,128]{1,0:T(8,128)S(1)}) custom-call(bf16[2048,512]{1,0:T(8,128)(2,1)S(1)} %get-tuple-element.24.turned_ref, f32[512,256]{1,0:T(8,128)S(1)} %get-tuple-element.25.part_ref, bf16[640,256]{1,0:T(8,128)(2,1)S(1)} %collective-permute-done.4.rest_ref, ...), custom_call_target="tpu_custom_call" | custom-call | flops 536870912 | bytes 4194304 | tf_op jit(solution)/shard_map/gradient/near_gradient/pallas_call | solution.py:200
  102.7 9.8 %collective-permute-start.10 = (f32[8,128]{1,0:T(8,128)S(1)}, f32[8,128]{1,0:T(8,128)S(1)}, u32[]{:S(2)}, u32[]{:S(2)}) collective-permute-start(f32[8,128]{1,0:T(8,128)S(1)} %get-tuple-element.33), channel_id=1, source_target_pairs={{0,1},{1,0},{2,3},{3,2},{4,5},{5,4},{6,7},{7,6},{8,9},{9,8},{10,11... | collective-permute-start | bytes 12296 | tf_op jit(solution)/shard_map/gradient/ppermute | solution.py:32
  112.4 1.6 %collective-permute-done.10 = f32[8,128]{1,0:T(8,128)S(1)} collective-permute-done((f32[8,128]{1,0:T(8,128)S(1)}, f32[8,128]{1,0:T(8,128)S(1)}, u32[]{:S(2)}, u32[]{:S(2)}) %collective-permute-start.10) | collective-permute-done | bytes 4128 | tf_op jit(solution)/shard_map/gradient/ppermute | solution.py:32
  114.0 0.6 embed.1
  114.6 0.0 all-to-all-done.2
  114.6 7.4 %all-to-all-start = ((bf16[4,528,256]{2,1,0:T(8,128)(2,1)}), bf16[4,528,256]{2,1,0:T(8,128)(2,1)S(1)}, u32[]{:S(2)}, u32[]{:S(2)}) async-start(bf16[4,528,256]{2,1,0:T(8,128)(2,1)} %embed.1), calls=%async_computation | async-start | bytes 2162688 | tf_op jit(solution)/shard_map/gradient/all_to_all | solution.py:28
  122.1 0.0 copy-done.4
  122.1 0.9 fusion.2
  123.1 8.7 %all-to-all-done.squares_ref.rows_ref = bf16[4,528,256]{2,1,0:T(8,128)(2,1)S(1)} async-done(((bf16[4,528,256]{2,1,0:T(8,128)(2,1)}), bf16[4,528,256]{2,1,0:T(8,128)(2,1)S(1)}, u32[]{:S(2)}, u32[]{:S(2)}) %all-to-all-start) | async-done | bytes 1081376 | tf_op jit(solution)/shard_map/gradient/all_to_all | solution.py:28
  131.8 2.8 %step.1 = bf16[1,512,1024]{2,1,0:T(8,128)(2,1)} custom-call(s32[8]{0:T(128)S(1)} %copy-done.3, bf16[4,528,256]{2,1,0:T(8,128)(2,1)S(1)} %all-to-all-done.squares_ref.rows_ref, bf16[4,528,256]{2,1,0:T(8,128)(2,1)S(1)} %all-to-all-done.squares_ref.rows_ref, bf16[1,512,1024]{2,1,0:T(8,128)(2,1)S(1)} %copy-done, bf16[512,256]{1,0:T(8,128)(2,1)S(1)} %get-tuple-element.35.global_ref), custom_call_target="tpu_custom_call" | custom-call | tf_op jit(solution)/shard_map/step/step/pallas_call | solution.py:180
  (15 shorter events, 0.1 us)
Async XLA Ops:
  4.2 68.5 %copy-start.2 = (bf16[208,2048]{1,0:T(8,128)(2,1)S(1)}, bf16[208,2048]{1,0:T(8,128)(2,1)}, u32[]{:S(2)}) copy-start(bf16[208,2048]{1,0:T(8,128)(2,1)} %get-tuple-element.19.m0) | copy-start | bytes 2555908
  4.2 53.7 %collective-permute-start = (bf16[208,2048]{1,0:T(8,128)(2,1)}, bf16[208,2048]{1,0:T(8,128)(2,1)}, u32[]{:S(2)}, u32[]{:S(2)}) collective-permute-start(bf16[208,2048]{1,0:T(8,128)(2,1)} %get-tuple-element.20), channel_id=1, source_target_pairs={{0,2},{1,3},{2,4},{3,5},{4,6},{5,7},{6,0},{7,1},{8,10},{9,11},{10,... | collective-permute-start | bytes 2555912 | tf_op jit(solution)/shard_map/activations/ppermute | solution.py:37
  12.1 24.8 %collective-permute-start.3 = (bf16[128,2048]{1,0:T(8,128)(2,1)}, bf16[128,2048]{1,0:T(8,128)(2,1)S(1)}, u32[]{:S(2)}, u32[]{:S(2)}) collective-permute-start(bf16[128,2048]{1,0:T(8,128)(2,1)} %get-tuple-element.23), channel_id=1, source_target_pairs={{0,1},{1,0},{2,3},{3,2},{4,5},{5,4},{6,7},{7,6},{8,9},{9,8},{10,11... | collective-permute-start | bytes 1572872 | tf_op jit(solution)/shard_map/activations/ppermute | solution.py:32
  14.5 21.6 %all-to-all-start.1 = ((bf16[8,64,256]{2,1,0:T(8,128)(2,1)}), bf16[8,64,256]{2,1,0:T(8,128)(2,1)S(1)}, u32[]{:S(2)}, u32[]{:S(2)}) async-start(bf16[8,64,256]{2,1,0:T(8,128)(2,1)} %bitcast.1), calls=%async_computation.1 | async-start | bytes 524288 | tf_op jit(solution)/shard_map/outer_sum/all_to_all | solution.py:28
  24.8 47.8 %collective-permute-start.1 = (bf16[208,2048]{1,0:T(8,128)(2,1)}, bf16[208,2048]{1,0:T(8,128)(2,1)}, u32[]{:S(2)}, u32[]{:S(2)}) collective-permute-start(bf16[208,2048]{1,0:T(8,128)(2,1)} %get-tuple-element.21), channel_id=1, source_target_pairs={{0,4},{1,5},{2,6},{3,7},{4,0},{5,1},{6,2},{7,3},{8,12},{9,13},{10,... | collective-permute-start | bytes 2555912 | tf_op jit(solution)/shard_map/activations/ppermute | solution.py:37
  29.1 43.5 %collective-permute-start.2 = (bf16[208,2048]{1,0:T(8,128)(2,1)}, bf16[208,2048]{1,0:T(8,128)(2,1)}, u32[]{:S(2)}, u32[]{:S(2)}) collective-permute-start(bf16[208,2048]{1,0:T(8,128)(2,1)} %get-tuple-element.22), channel_id=1, source_target_pairs={{0,6},{1,7},{2,0},{3,1},{4,2},{5,3},{6,4},{7,5},{8,14},{9,15},{10,... | collective-permute-start | bytes 2555912 | tf_op jit(solution)/shard_map/activations/ppermute | solution.py:37
  37.0 3.1 %collective-permute-start.11 = (f32[64,256]{1,0:T(8,128)S(1)}, f32[64,256]{1,0:T(8,128)S(1)}, u32[]{:S(2)}, u32[]{:S(2)}) collective-permute-start(f32[64,256]{1,0:T(8,128)S(1)} %sum.1), channel_id=1, source_target_pairs={{0,8},{8,0},{16,24},{24,16},{32,40},{40,32},{48,56},{56,48},{64,72... | collective-permute-start | bytes 196616 | tf_op jit(solution)/shard_map/outer_sum/ppermute | solution.py:269
  40.2 6.2 %collective-permute-start.12 = (f32[64,256]{1,0:T(8,128)S(1)}, f32[64,256]{1,0:T(8,128)S(1)}, u32[]{:S(2)}, u32[]{:S(2)}) collective-permute-start(f32[64,256]{1,0:T(8,128)S(1)} %add.19), channel_id=1, source_target_pairs={{0,16},{8,24},{16,0},{24,8},{32,48},{40,56},{48,32},{56,40},{64,80... | collective-permute-start | bytes 196616 | tf_op jit(solution)/shard_map/outer_sum/ppermute | solution.py:269
  46.3 8.4 %collective-permute-start.13 = (f32[64,256]{1,0:T(8,128)S(1)}, f32[64,256]{1,0:T(8,128)S(1)}, u32[]{:S(2)}, u32[]{:S(2)}) collective-permute-start(f32[64,256]{1,0:T(8,128)S(1)} %add.20), channel_id=1, source_target_pairs={{0,32},{8,40},{16,48},{24,56},{32,0},{40,8},{48,16},{56,24},{64,96... | collective-permute-start | bytes 196616 | tf_op jit(solution)/shard_map/outer_sum/ppermute | solution.py:269
  51.4 31.3 %collective-permute-start.5 = (bf16[128,2048]{1,0:T(8,128)(2,1)S(1)}, bf16[128,2048]{1,0:T(8,128)(2,1)S(1)}, u32[]{:S(2)}, u32[]{:S(2)}) collective-permute-start(bf16[128,2048]{1,0:T(8,128)(2,1)S(1)} %collective-permute-done.3.arrived_ref.b0._), channel_id=1, source_target_pairs={{0,2},{1,3},{2,4},{3,5},{4,6},{5,7},{6,0},{7,1},{8,10},{9,11},{10,... | collective-permute-start | bytes 1572872 | tf_op jit(solution)/shard_map/activations/ppermute | solution.py:37
  54.8 27.8 %collective-permute-start.6 = (bf16[128,2048]{1,0:T(8,128)(2,1)S(1)}, bf16[128,2048]{1,0:T(8,128)(2,1)S(1)}, u32[]{:S(2)}, u32[]{:S(2)}) collective-permute-start(bf16[128,2048]{1,0:T(8,128)(2,1)S(1)} %collective-permute-done.3.arrived_ref.b0._), channel_id=1, source_target_pairs={{0,6},{1,7},{2,0},{3,1},{4,2},{5,3},{6,4},{7,5},{8,14},{9,15},{10,... | collective-permute-start | bytes 1572872 | tf_op jit(solution)/shard_map/activations/ppermute | solution.py:37
  57.9 31.1 %collective-permute-start.8 = (bf16[128,2048]{1,0:T(8,128)(2,1)S(1)}, bf16[128,2048]{1,0:T(8,128)(2,1)S(1)}, u32[]{:S(2)}, u32[]{:S(2)}) collective-permute-start(bf16[128,2048]{1,0:T(8,128)(2,1)S(1)} %collective-permute-done.3.arrived_ref.b0._), channel_id=1, source_target_pairs={{0,4},{1,5},{2,6},{3,7},{4,0},{5,1},{6,2},{7,3},{8,12},{9,13},{10,... | collective-permute-start | bytes 1572872 | tf_op jit(solution)/shard_map/activations/ppermute | solution.py:37
  62.3 52.3 %all-to-all-start.2 = ((bf16[8,64,256]{2,1,0:T(8,128)(2,1)}), bf16[8,64,256]{2,1,0:T(8,128)(2,1)S(1)}, u32[]{:S(2)}, u32[]{:S(2)}) async-start(bf16[8,64,256]{2,1,0:T(8,128)(2,1)} %broadcast_in_dim.2), calls=%async_computation.2 | async-start | bytes 524288 | tf_op jit(solution)/shard_map/outer_sum/all_to_all | solution.py:28
  75.3 22.7 %collective-permute-start.4 = (bf16[640,256]{1,0:T(8,128)(2,1)S(1)}, bf16[640,256]{1,0:T(8,128)(2,1)S(1)}, u32[]{:S(2)}, u32[]{:S(2)}) collective-permute-start(bf16[640,256]{1,0:T(8,128)(2,1)S(1)} %get-tuple-element.26), channel_id=1, source_target_pairs={{0,1},{1,0},{2,3},{3,2},{4,5},{5,4},{6,7},{7,6},{8,9},{9,8},{10,11... | collective-permute-start | bytes 983048 | tf_op jit(solution)/shard_map/near_keys/ppermute | solution.py:32
  83.1 17.8 %collective-permute-start.7 = (bf16[256,256]{1,0:T(8,128)(2,1)S(1)}, bf16[256,256]{1,0:T(8,128)(2,1)S(1)}, u32[]{:S(2)}, u32[]{:S(2)}) collective-permute-start(bf16[256,256]{1,0:T(8,128)(2,1)S(1)} %get-tuple-element.28), channel_id=1, source_target_pairs={{0,1},{1,0},{2,3},{3,2},{4,5},{5,4},{6,7},{7,6},{8,9},{9,8},{10,11... | collective-permute-start | bytes 393224 | tf_op jit(solution)/shard_map/far_keys/ppermute | solution.py:32
  89.3 11.6 %collective-permute-start.9 = (bf16[128,256]{1,0:T(8,128)(2,1)S(1)}, bf16[128,256]{1,0:T(8,128)(2,1)S(1)}, u32[]{:S(2)}, u32[]{:S(2)}) collective-permute-start(bf16[128,256]{1,0:T(8,128)(2,1)S(1)} %get-tuple-element.29), channel_id=1, source_target_pairs={{0,1},{1,0},{2,3},{3,2},{4,5},{5,4},{6,7},{7,6},{8,9},{9,8},{10,11... | collective-permute-start | bytes 196616 | tf_op jit(solution)/shard_map/far_keys/ppermute | solution.py:32
  102.7 11.3 %collective-permute-start.10 = (f32[8,128]{1,0:T(8,128)S(1)}, f32[8,128]{1,0:T(8,128)S(1)}, u32[]{:S(2)}, u32[]{:S(2)}) collective-permute-start(f32[8,128]{1,0:T(8,128)S(1)} %get-tuple-element.33), channel_id=1, source_target_pairs={{0,1},{1,0},{2,3},{3,2},{4,5},{5,4},{6,7},{7,6},{8,9},{9,8},{10,11... | collective-permute-start | bytes 12296 | tf_op jit(solution)/shard_map/gradient/ppermute | solution.py:32
  114.0 8.1 %copy-start.4 = (f32[512,256]{1,0:T(8,128)S(1)}, f32[512,256]{1,0:T(8,128)}, u32[]{:S(2)}) copy-start(f32[512,256]{1,0:T(8,128)} %param.13) | copy-start | bytes 1572868
  114.0 8.1 %copy-start.5 = (bf16[512,256]{1,0:T(8,128)(2,1)S(1)}, bf16[512,256]{1,0:T(8,128)(2,1)}, u32[]{:S(2)}) copy-start(bf16[512,256]{1,0:T(8,128)(2,1)} %param.12) | copy-start | bytes 786436
  114.6 17.1 %copy-start = (bf16[1,512,1024]{2,1,0:T(8,128)(2,1)S(1)}, bf16[1,512,1024]{2,1,0:T(8,128)(2,1)}, u32[]{:S(2)}) copy-start(bf16[1,512,1024]{2,1,0:T(8,128)(2,1)} %weight_ref.1) | copy-start | bytes 3145732
  114.6 17.1 %copy-start.3 = (s32[8]{0:T(128)S(1)}, s32[8]{0:T(128)}, u32[]{:S(2)}) copy-start(s32[8]{0:T(128)} %order_ref.1) | copy-start | bytes 100
  114.6 17.1 %all-to-all-start = ((bf16[4,528,256]{2,1,0:T(8,128)(2,1)}), bf16[4,528,256]{2,1,0:T(8,128)(2,1)S(1)}, u32[]{:S(2)}, u32[]{:S(2)}) async-start(bf16[4,528,256]{2,1,0:T(8,128)(2,1)} %embed.1), calls=%async_computation | async-start | bytes 2162688 | tf_op jit(solution)/shard_map/gradient/all_to_all | solution.py:28
  123.1 11.5 %copy-start.1 = (bf16[512,256]{1,0:T(8,128)(2,1)}, bf16[512,256]{1,0:T(8,128)(2,1)S(1)}, u32[]{:S(2)}) copy-start(bf16[512,256]{1,0:T(8,128)(2,1)S(1)} %get-tuple-element.35.global_ref) | copy-start | bytes 786436

commit v8 on v7

--- a/solution.py
+++ b/solution.py
@@ -21,6 +21,7 @@
 PARAMS = pltpu.CompilerParams(vmem_limit_bytes=16 * 1024 * 1024)
 
 X_GROUPS = [[x * 2 + h for x in range(NX)] for h in range(2)]
+L_GROUPS = [[z * 8 + l for l in range(8)] for z in range(8)]
 Z_GROUPS = [[z * 8 + l for z in range(8)] for l in range(8)]
 
 
@@ -100,7 +101,7 @@
 
 
 def far_kernel(*refs):
-    *blocks, weight_ref, keys_ref, sent_ref = refs
+    *blocks, weight_ref, _, keys_ref, sent_ref = refs
     keys_ref[...] = raw_keys(blocks, weight_ref[...])
     sent_ref[...] = keys_ref[...].astype(BF16)
 
@@ -157,8 +158,10 @@
     )(squares, gradient)
 
 
-def sum_kernel(blocks_ref, _, out_ref):
-    out_ref[...] = jnp.sum(blocks_ref[...].astype(F32), axis=0)
+def sum_kernel(blocks_ref, *refs):
+    total = jnp.sum(blocks_ref[...].astype(F32), axis=0).astype(refs[-1].dtype)
+    for i in range(8):
+        refs[-1][i] = total
 
 
 def step_kernel(order_ref, squares_ref, rows_ref, weight_ref, global_ref, out_ref, new_ref):
@@ -239,11 +242,11 @@
 
     with jax.named_scope("far_keys"):
         sides_keys, sides_sent = call(
-            far_kernel, (SDS((256, COLS), F32), SDS((256, COLS), BF16)), far[1], far[3], columns, flops=dot_flops // 2
+            far_kernel, (SDS((256, COLS), F32), SDS((256, COLS), BF16)), far[1], far[3], columns, rest, flops=dot_flops // 2, hbm=1
         )
         sides_rest = flip(sides_sent, 1)
         last_keys, last_sent = call(
-            far_kernel, (SDS((128, COLS), F32), SDS((128, COLS), BF16)), far[2], columns, flops=dot_flops // 4
+            far_kernel, (SDS((128, COLS), F32), SDS((128, COLS), BF16)), far[2], columns, rest, flops=dot_flops // 4, hbm=1
         )
         last_rest = flip(last_sent, 1)
         far_turned = call(turn_kernel, SDS((2048, 512), BF16), far[0], far[1], far[3], far[2])
@@ -263,12 +266,10 @@
         by_rows = exchange(embedded, "fsdp", X_GROUPS)
 
     with jax.named_scope("outer_sum"):
-        by_z = exchange(pending_delta[0].reshape(8, 64, 256), "rep", Z_GROUPS)
-        total = call(sum_kernel, SDS((64, 256), F32), by_z, arrived, hbm=1)
-        for mask in (1, 2, 4):
-            total += lax.ppermute(total, "rep", [(i, i ^ mask) for i in range(64)])
-        by_rows_z = exchange(jnp.broadcast_to(total.astype(BF16)[None], (8, 64, 256)), "rep", Z_GROUPS)
-        mean = by_rows_z.astype(F32).reshape(512, 256) / lax.axis_size("rep")
+        by_l = exchange(pending_delta[0].reshape(8, 64, 256), "rep", L_GROUPS)
+        by_z = exchange(call(sum_kernel, SDS((8, 64, 256), BF16), by_l, arrived, hbm=1), "rep", Z_GROUPS)
+        rows = exchange(call(sum_kernel, SDS((8, 64, 256), BF16), by_z), "rep", L_GROUPS)
+        mean = rows.reshape(512, 256).astype(F32) / lax.axis_size("rep")
         new_momentum = 0.9 * outer_momentum + mean
         new_global = (global_frag.astype(F32) - 0.7 * (mean + 0.9 * new_momentum)).astype(BF16)
 

time: 137 us -> 144 us (1.051)
  blocking collectives: 0 us -> 23.1 us
  starting transfers between devices: 88.1 us -> 65.4 us
  local copies, waits for them, and re-layouts: 0.75 us -> 6.76 us
  Pallas kernels: 13.5 us -> 15.6 us
  waiting for transfers between devices: 30.4 us -> 28.5 us
    all_to_all x0 -> x1, blocking collectives: none -> 23.1 us  [exchange(): lax.all_to_all(blocks, axis, 0, 0, axis_index_groups=groups, tiled=True)]
    ppermute x5, waiting for transfers between devices: 8.8 us -> 19.3 us  [flip(): return lax.ppermute(block, 'fsdp', [(i, i ^ mask) for i in range(8)])]
    ppermute x3 -> x0, starting transfers between devices: 9.98 us -> none  [body(): total += lax.ppermute(total, 'rep', [(i, i ^ mask) for i in range(64)])]
    all_to_all x3, starting transfers between devices: 28.1 us -> 20.2 us  [exchange(): lax.all_to_all(blocks, axis, 0, 0, axis_index_groups=groups, tiled=True)]
    unnamed x12 -> x32, local copies, waits for them, and re-layouts: 0.02 us -> 6.76 us
    all_to_all x3, waiting for transfers between devices: 13.8 us -> 7.9 us  [exchange(): lax.all_to_all(blocks, axis, 0, 0, axis_index_groups=groups, tiled=True)]
    ppermute x5, starting transfers between devices: 25.7 us -> 21 us  [flip(): return lax.ppermute(block, 'fsdp', [(i, i ^ mask) for i in range(8)])]
    ppermute x3 -> x0, waiting for transfers between devices: 4.34 us -> none  [body(): total += lax.ppermute(total, 'rep', [(i, i ^ mask) for i in range(64)])]
  transfers between devices with their start and end apart: 17 -> 14, of which waited for: 9 -> 5; matrix products, arithmetic and copies ran while one was open for 1% -> 1% of each run, Pallas kernels for 5% -> 6%
where the time goes in v8:
time: 144 us; the launch traced here: 142 us
  starting transfers between devices  65.4 us (45%)
  waiting for transfers between devices  28.5 us (20%)
  blocking collectives  23.1 us (16%)
  Pallas kernels  15.6 us (11%)
  local copies, waits for them, and re-layouts  6.76 us (5%)
  other arithmetic  1.93 us (1%)
    ppermute x6, starting transfers between devices, rotate(): lax.ppermute(blocks[d], 'fsdp', moves[d])  24.1 us
    all_to_all x1, blocking collectives, exchange(): lax.all_to_all(blocks, axis, 0, 0, axis_index_groups=groups, tiled=True)  23.1 us
    ppermute x5, starting transfers between devices, flip(): return lax.ppermute(block, 'fsdp', [(i, i ^ mask) for i in range(8)])  21 us
    all_to_all x3, starting transfers between devices, exchange(): lax.all_to_all(blocks, axis, 0, 0, axis_index_groups=groups, tiled=True)  20.2 us
    ppermute x5, waiting for transfers between devices, flip(): return lax.ppermute(block, 'fsdp', [(i, i ^ mask) for i in range(8)])  19.3 us
    pallas_call x9, Pallas kernels, call(): pl.pallas_call(kernel, in_specs=[SMEM] * scalars + [pl.BlockSpec(memory_s...  12.2 us
    all_to_all x3, waiting for transfers between devices, exchange(): lax.all_to_all(blocks, axis, 0, 0, axis_index_groups=groups, tiled=True)  7.9 us
    unnamed x32, local copies, waits for them, and re-layouts  6.76 us
  transfers between devices with their start and end apart: 14, of which 5 were waited for; matrix products, arithmetic and copies ran while one was open for 1% of the time, Pallas kernels for 6%

profile of v8, /device:TPU:6, one launch (start us, length us, event | category | flops | bytes accessed | tf_op | source)
XLA Modules:
  0.0 142.2 jit_solution(1749899983550571328)
XLA Ops:
  0.6 3.6 %pack.1 = (bf16[128,2048]{1,0:T(8,128)(2,1)}, bf16[208,2048]{1,0:T(8,128)(2,1)}, bf16[208,2048]{1,0:T(8,128)(2,1)}, bf16[208,2048]{1,0:T(8,128)(2,1)}, bf16[208,2048]{1,0:T(8,128)(2,1)}) custom-call(s32[1]{0:T(128)} %bitcast.index_ref, bf16[128,4096]{1,0:T(8,128)(2,1)} %refs_0_.1, bf16[1,512,1024]{2,1,0:T(8,128)(2,1)} %weight_ref.1, bf16[128,1024]{1,0:T(8,128)(2,1)} %refs_2_.1), custom_call_target="tpu_custom_call" | custom-call | bytes 4194304 | tf_op jit(solution)/shard_map/activations/pack/pallas_call | solution.py:203
  4.2 7.8 %collective-permute-start = (bf16[208,2048]{1,0:T(8,128)(2,1)}, bf16[208,2048]{1,0:T(8,128)(2,1)S(1)}, u32[]{:S(2)}, u32[]{:S(2)}) collective-permute-start(bf16[208,2048]{1,0:T(8,128)(2,1)} %get-tuple-element.20), channel_id=1, source_target_pairs={{0,2},{1,3},{2,4},{3,5},{4,6},{5,7},{6,0},{7,1},{8,10},{9,11},{10,... | collective-permute-start | bytes 2555912 | tf_op jit(solution)/shard_map/activations/ppermute | solution.py:38
  12.0 2.4 %collective-permute-start.3 = (bf16[128,2048]{1,0:T(8,128)(2,1)}, bf16[128,2048]{1,0:T(8,128)(2,1)S(1)}, u32[]{:S(2)}, u32[]{:S(2)}) collective-permute-start(bf16[128,2048]{1,0:T(8,128)(2,1)} %get-tuple-element.23), channel_id=1, source_target_pairs={{0,1},{1,0},{2,3},{3,2},{4,5},{5,4},{6,7},{7,6},{8,9},{9,8},{10,11... | collective-permute-start | bytes 1572872 | tf_op jit(solution)/shard_map/activations/ppermute | solution.py:33
  14.4 4.3 %collective-permute-start.1 = (bf16[208,2048]{1,0:T(8,128)(2,1)}, bf16[208,2048]{1,0:T(8,128)(2,1)}, u32[]{:S(2)}, u32[]{:S(2)}) collective-permute-start(bf16[208,2048]{1,0:T(8,128)(2,1)} %get-tuple-element.21), channel_id=1, source_target_pairs={{0,4},{1,5},{2,6},{3,7},{4,0},{5,1},{6,2},{7,3},{8,12},{9,13},{10,... | collective-permute-start | bytes 2555912 | tf_op jit(solution)/shard_map/activations/ppermute | solution.py:38
  18.7 1.9 %collective-permute-start.2 = (bf16[208,2048]{1,0:T(8,128)(2,1)}, bf16[208,2048]{1,0:T(8,128)(2,1)}, u32[]{:S(2)}, u32[]{:S(2)}) collective-permute-start(bf16[208,2048]{1,0:T(8,128)(2,1)} %get-tuple-element.22), channel_id=1, source_target_pairs={{0,6},{1,7},{2,0},{3,1},{4,2},{5,3},{6,4},{7,5},{8,14},{9,15},{10,... | collective-permute-start | bytes 2555912 | tf_op jit(solution)/shard_map/activations/ppermute | solution.py:38
  20.7 23.1 %all_to_all.20.blocks_ref = bf16[8,64,256]{2,1,0:T(8,128)(2,1)S(1)} all-to-all(bf16[8,64,256]{2,1,0:T(8,128)(2,1)S(1)} %bitcast.12), channel_id=1, replica_groups={{0,8,16,24,32,40,48,56},{64,72,80,88,96,104,112,120},{128,136,144,152,1..., dimensions={0} | all-to-all | bytes 524288 | tf_op jit(solution)/shard_map/outer_sum/all_to_all | solution.py:29
  43.7 0.0 collective-permute-done.3.arrived_ref.b0.refs_0_
  43.7 0.7 sum.2
  44.5 10.4 %all-to-all-start.2 = ((bf16[8,64,256]{2,1,0:T(8,128)(2,1)}), bf16[8,64,256]{2,1,0:T(8,128)(2,1)}, u32[]{:S(2)}, u32[]{:S(2)}) async-start(bf16[8,64,256]{2,1,0:T(8,128)(2,1)} %sum.2), calls=%async_computation.2 | async-start | bytes 524288 | tf_op jit(solution)/shard_map/outer_sum/all_to_all | solution.py:29
  54.8 3.3 %collective-permute-start.5 = (bf16[128,2048]{1,0:T(8,128)(2,1)S(1)}, bf16[128,2048]{1,0:T(8,128)(2,1)S(1)}, u32[]{:S(2)}, u32[]{:S(2)}) collective-permute-start(bf16[128,2048]{1,0:T(8,128)(2,1)S(1)} %collective-permute-done.3.arrived_ref.b0.refs_0_), channel_id=1, source_target_pairs={{0,2},{1,3},{2,4},{3,5},{4,6},{5,7},{6,0},{7,1},{8,10},{9,11},{10,... | collective-permute-start | bytes 1572872 | tf_op jit(solution)/shard_map/activations/ppermute | solution.py:38
  58.2 2.5 %collective-permute-start.6 = (bf16[128,2048]{1,0:T(8,128)(2,1)S(1)}, bf16[128,2048]{1,0:T(8,128)(2,1)S(1)}, u32[]{:S(2)}, u32[]{:S(2)}) collective-permute-start(bf16[128,2048]{1,0:T(8,128)(2,1)S(1)} %collective-permute-done.3.arrived_ref.b0.refs_0_), channel_id=1, source_target_pairs={{0,6},{1,7},{2,0},{3,1},{4,2},{5,3},{6,4},{7,5},{8,14},{9,15},{10,... | collective-permute-start | bytes 1572872 | tf_op jit(solution)/shard_map/activations/ppermute | solution.py:38
  60.7 0.0 collective-permute-done.m1
  60.7 0.9 copy-done.6
  61.6 4.3 %collective-permute-start.8 = (bf16[128,2048]{1,0:T(8,128)(2,1)S(1)}, bf16[128,2048]{1,0:T(8,128)(2,1)S(1)}, u32[]{:S(2)}, u32[]{:S(2)}) collective-permute-start(bf16[128,2048]{1,0:T(8,128)(2,1)S(1)} %collective-permute-done.3.arrived_ref.b0.refs_0_), channel_id=1, source_target_pairs={{0,4},{1,5},{2,6},{3,7},{4,0},{5,1},{6,2},{7,3},{8,12},{9,13},{10,... | collective-permute-start | bytes 1572872 | tf_op jit(solution)/shard_map/activations/ppermute | solution.py:38
  65.9 0.0 collective-permute-done.1.m2
  65.9 0.0 collective-permute-done.2.m3
  65.9 0.0 copy-start.5
  65.9 1.1 copy-done.5
  67.1 1.2 copy-done.7
  68.2 3.1 %near.1 = (f32[512,256]{1,0:T(8,128)S(1)}, bf16[640,256]{1,0:T(8,128)(2,1)}, bf16[2048,256]{1,0:T(8,128)(2,1)S(1)}, bf16[2048,512]{1,0:T(8,128)(2,1)S(1)}, f32[128,256]{1,0:T(8,128)S(1)}) custom-call(s32[1]{0:T(128)} %bitcast.index_ref, bf16[208,2048]{1,0:T(8,128)(2,1)S(1)} %copy-done.5, bf16[208,2048]{1,0:T(8,128)(2,1)S(1)} %copy-done.7, ...), custom_call_target="tpu_custom_call" | custom-call | flops 536870912 | bytes 4194304 | tf_op jit(solution)/shard_map/near_keys/near/pallas_call | solution.py:203
  71.3 1.4 copy-done.1
  72.7 0.8 copy-done.8
  73.5 0.7 copy-done.10
  74.1 4.7 %collective-permute-start.4 = (bf16[640,256]{1,0:T(8,128)(2,1)}, bf16[640,256]{1,0:T(8,128)(2,1)S(1)}, u32[]{:S(2)}, u32[]{:S(2)}) collective-permute-start(bf16[640,256]{1,0:T(8,128)(2,1)} %get-tuple-element.26), channel_id=1, source_target_pairs={{0,1},{1,0},{2,3},{3,2},{4,5},{5,4},{6,7},{7,6},{8,9},{9,8},{10,11... | collective-permute-start | bytes 983048 | tf_op jit(solution)/shard_map/near_keys/ppermute | solution.py:33
  78.8 0.0 all-to-all-done.2.blocks_ref
  78.9 1.0 sum.3
  79.9 0.0 copy-start.3
  79.9 0.7 copy-done.3
  80.6 4.1 %all-to-all-start.3 = ((bf16[8,64,256]{2,1,0:T(8,128)(2,1)}), bf16[8,64,256]{2,1,0:T(8,128)(2,1)}, u32[]{:S(2)}, u32[]{:S(2)}) async-start(bf16[8,64,256]{2,1,0:T(8,128)(2,1)} %copy-done.3), calls=%async_computation.3 | async-start | bytes 524288 | tf_op jit(solution)/shard_map/outer_sum/all_to_all | solution.py:29
  84.6 1.3 collective-permute-done.6.refs_1_.b3
  86.0 9.4 %collective-permute-done.4.refs_3_.refs_2_.rest_ref = bf16[640,256]{1,0:T(8,128)(2,1)S(1)} collective-permute-done((bf16[640,256]{1,0:T(8,128)(2,1)}, bf16[640,256]{1,0:T(8,128)(2,1)S(1)}, u32[]{:S(2)}, u32[]{:S(2)}) %collective-permute-start.4) | collective-permute-done | bytes 327712 | tf_op jit(solution)/shard_map/near_keys/ppermute | solution.py:33
  95.4 0.4 far.2
  95.8 5.6 %collective-permute-start.7 = (bf16[256,256]{1,0:T(8,128)(2,1)S(1)}, bf16[256,256]{1,0:T(8,128)(2,1)S(1)}, u32[]{:S(2)}, u32[]{:S(2)}) collective-permute-start(bf16[256,256]{1,0:T(8,128)(2,1)S(1)} %get-tuple-element.28), channel_id=1, source_target_pairs={{0,1},{1,0},{2,3},{3,2},{4,5},{5,4},{6,7},{7,6},{8,9},{9,8},{10,11... | collective-permute-start | bytes 393224 | tf_op jit(solution)/shard_map/far_keys/ppermute | solution.py:33
  101.5 0.3 far.3
  101.8 4.2 %collective-permute-start.9 = (bf16[128,256]{1,0:T(8,128)(2,1)S(1)}, bf16[128,256]{1,0:T(8,128)(2,1)S(1)}, u32[]{:S(2)}, u32[]{:S(2)}) collective-permute-start(bf16[128,256]{1,0:T(8,128)(2,1)S(1)} %get-tuple-element.29), channel_id=1, source_target_pairs={{0,1},{1,0},{2,3},{3,2},{4,5},{5,4},{6,7},{7,6},{8,9},{9,8},{10,11... | collective-permute-start | bytes 196616 | tf_op jit(solution)/shard_map/far_keys/ppermute | solution.py:33
  106.0 0.6 turn.1.turned_ref
  106.7 0.0 copy-start.9
  106.7 0.7 far_gradient.1.far_ref
  107.4 4.6 %collective-permute-done.9.last_ref = bf16[128,256]{1,0:T(8,128)(2,1)S(1)} collective-permute-done((bf16[128,256]{1,0:T(8,128)(2,1)S(1)}, bf16[128,256]{1,0:T(8,128)(2,1)S(1)}, u32[]{:S(2)}, u32[]{:S(2)}) %collective-permute-start.9) | collective-permute-done | bytes 65568 | tf_op jit(solution)/shard_map/far_keys/ppermute | solution.py:33
  112.0 1.7 %near_gradient.1 = (bf16[4,528,256]{2,1,0:T(8,128)(2,1)}, f32[8,128]{1,0:T(8,128)S(1)}) custom-call(bf16[2048,512]{1,0:T(8,128)(2,1)S(1)} %copy-done.2, f32[512,256]{1,0:T(8,128)S(1)} %copy-done.9, bf16[640,256]{1,0:T(8,128)(2,1)S(1)} %collective-permute-done.4.refs_3_.refs_2_.rest_ref, bf16[256,256]{1,0:T(8,128)(2,1)S(1)} %collective-permute-done.7.sides_ref, ...), custom_call_target="tpu_custom_call" | custom-call | flops 536870912 | bytes 4194304 | tf_op jit(solution)/shard_map/gradient/near_gradient/pallas_call | solution.py:203
  113.7 4.1 %collective-permute-start.10 = (f32[8,128]{1,0:T(8,128)S(1)}, f32[8,128]{1,0:T(8,128)S(1)}, u32[]{:S(2)}, u32[]{:S(2)}) collective-permute-start(f32[8,128]{1,0:T(8,128)S(1)} %get-tuple-element.33), channel_id=1, source_target_pairs={{0,1},{1,0},{2,3},{3,2},{4,5},{5,4},{6,7},{7,6},{8,9},{9,8},{10,11... | collective-permute-start | bytes 12296 | tf_op jit(solution)/shard_map/gradient/ppermute | solution.py:33
  117.8 5.3 %collective-permute-done.10 = f32[8,128]{1,0:T(8,128)S(1)} collective-permute-done((f32[8,128]{1,0:T(8,128)S(1)}, f32[8,128]{1,0:T(8,128)S(1)}, u32[]{:S(2)}, u32[]{:S(2)}) %collective-permute-start.10) | collective-permute-done | bytes 4128 | tf_op jit(solution)/shard_map/gradient/ppermute | solution.py:33
  123.1 0.6 embed.1
  123.8 5.8 %all-to-all-start = ((bf16[4,528,256]{2,1,0:T(8,128)(2,1)}), bf16[4,528,256]{2,1,0:T(8,128)(2,1)S(1)}, u32[]{:S(2)}, u32[]{:S(2)}) async-start(bf16[4,528,256]{2,1,0:T(8,128)(2,1)} %embed.1), calls=%async_computation | async-start | bytes 2162688 | tf_op jit(solution)/shard_map/gradient/all_to_all | solution.py:29
  129.5 1.0 convert_multiply_fusion
  130.6 0.9 fusion.2
  131.5 7.9 %all-to-all-done.squares_ref.rows_ref = bf16[4,528,256]{2,1,0:T(8,128)(2,1)S(1)} async-done(((bf16[4,528,256]{2,1,0:T(8,128)(2,1)}), bf16[4,528,256]{2,1,0:T(8,128)(2,1)S(1)}, u32[]{:S(2)}, u32[]{:S(2)}) %all-to-all-start) | async-done | bytes 1081376 | tf_op jit(solution)/shard_map/gradient/all_to_all | solution.py:29
  139.4 2.8 %step.1 = bf16[1,512,1024]{2,1,0:T(8,128)(2,1)} custom-call(s32[8]{0:T(128)S(1)} %copy-done.12, bf16[4,528,256]{2,1,0:T(8,128)(2,1)S(1)} %all-to-all-done.squares_ref.rows_ref, bf16[4,528,256]{2,1,0:T(8,128)(2,1)S(1)} %all-to-all-done.squares_ref.rows_ref, bf16[1,512,1024]{2,1,0:T(8,128)(2,1)S(1)} %copy-done, bf16[512,256]{1,0:T(8,128)(2,1)S(1)} %get-tuple-element.35.global_ref), custom_call_target="tpu_custom_call" | custom-call | tf_op jit(solution)/shard_map/step/step/pallas_call | solution.py:183
  (27 shorter events, 0.1 us)
Async XLA Ops:
  0.6 20.0 %copy-start.14 = (bf16[1,512,256]{2,1,0:T(8,128)(2,1)S(1)}, bf16[1,512,256]{2,1,0:T(8,128)(2,1)}, u32[]{:S(2)}) copy-start(bf16[1,512,256]{2,1,0:T(8,128)(2,1)} %param.10) | copy-start | bytes 786436
  4.2 56.4 %collective-permute-start = (bf16[208,2048]{1,0:T(8,128)(2,1)}, bf16[208,2048]{1,0:T(8,128)(2,1)S(1)}, u32[]{:S(2)}, u32[]{:S(2)}) collective-permute-start(bf16[208,2048]{1,0:T(8,128)(2,1)} %get-tuple-element.20), channel_id=1, source_target_pairs={{0,2},{1,3},{2,4},{3,5},{4,6},{5,7},{6,0},{7,1},{8,10},{9,11},{10,... | collective-permute-start | bytes 2555912 | tf_op jit(solution)/shard_map/activations/ppermute | solution.py:38
  12.0 31.7 %collective-permute-start.3 = (bf16[128,2048]{1,0:T(8,128)(2,1)}, bf16[128,2048]{1,0:T(8,128)(2,1)S(1)}, u32[]{:S(2)}, u32[]{:S(2)}) collective-permute-start(bf16[128,2048]{1,0:T(8,128)(2,1)} %get-tuple-element.23), channel_id=1, source_target_pairs={{0,1},{1,0},{2,3},{3,2},{4,5},{5,4},{6,7},{7,6},{8,9},{9,8},{10,11... | collective-permute-start | bytes 1572872 | tf_op jit(solution)/shard_map/activations/ppermute | solution.py:33
  14.4 51.5 %collective-permute-start.1 = (bf16[208,2048]{1,0:T(8,128)(2,1)}, bf16[208,2048]{1,0:T(8,128)(2,1)}, u32[]{:S(2)}, u32[]{:S(2)}) collective-permute-start(bf16[208,2048]{1,0:T(8,128)(2,1)} %get-tuple-element.21), channel_id=1, source_target_pairs={{0,4},{1,5},{2,6},{3,7},{4,0},{5,1},{6,2},{7,3},{8,12},{9,13},{10,... | collective-permute-start | bytes 2555912 | tf_op jit(solution)/shard_map/activations/ppermute | solution.py:38
  18.7 47.2 %collective-permute-start.2 = (bf16[208,2048]{1,0:T(8,128)(2,1)}, bf16[208,2048]{1,0:T(8,128)(2,1)}, u32[]{:S(2)}, u32[]{:S(2)}) collective-permute-start(bf16[208,2048]{1,0:T(8,128)(2,1)} %get-tuple-element.22), channel_id=1, source_target_pairs={{0,6},{1,7},{2,0},{3,1},{4,2},{5,3},{6,4},{7,5},{8,14},{9,15},{10,... | collective-permute-start | bytes 2555912 | tf_op jit(solution)/shard_map/activations/ppermute | solution.py:38
  44.5 34.4 %all-to-all-start.2 = ((bf16[8,64,256]{2,1,0:T(8,128)(2,1)}), bf16[8,64,256]{2,1,0:T(8,128)(2,1)}, u32[]{:S(2)}, u32[]{:S(2)}) async-start(bf16[8,64,256]{2,1,0:T(8,128)(2,1)} %sum.2), calls=%async_computation.2 | async-start | bytes 524288 | tf_op jit(solution)/shard_map/outer_sum/all_to_all | solution.py:29
  54.8 29.8 %collective-permute-start.5 = (bf16[128,2048]{1,0:T(8,128)(2,1)S(1)}, bf16[128,2048]{1,0:T(8,128)(2,1)S(1)}, u32[]{:S(2)}, u32[]{:S(2)}) collective-permute-start(bf16[128,2048]{1,0:T(8,128)(2,1)S(1)} %collective-permute-done.3.arrived_ref.b0.refs_0_), channel_id=1, source_target_pairs={{0,2},{1,3},{2,4},{3,5},{4,6},{5,7},{6,0},{7,1},{8,10},{9,11},{10,... | collective-permute-start | bytes 1572872 | tf_op jit(solution)/shard_map/activations/ppermute | solution.py:38
  58.2 27.8 %collective-permute-start.6 = (bf16[128,2048]{1,0:T(8,128)(2,1)S(1)}, bf16[128,2048]{1,0:T(8,128)(2,1)S(1)}, u32[]{:S(2)}, u32[]{:S(2)}) collective-permute-start(bf16[128,2048]{1,0:T(8,128)(2,1)S(1)} %collective-permute-done.3.arrived_ref.b0.refs_0_), channel_id=1, source_target_pairs={{0,6},{1,7},{2,0},{3,1},{4,2},{5,3},{6,4},{7,5},{8,14},{9,15},{10,... | collective-permute-start | bytes 1572872 | tf_op jit(solution)/shard_map/activations/ppermute | solution.py:38
  60.7 0.9 copy-start.6
  61.6 39.8 %collective-permute-start.8 = (bf16[128,2048]{1,0:T(8,128)(2,1)S(1)}, bf16[128,2048]{1,0:T(8,128)(2,1)S(1)}, u32[]{:S(2)}, u32[]{:S(2)}) collective-permute-start(bf16[128,2048]{1,0:T(8,128)(2,1)S(1)} %collective-permute-done.3.arrived_ref.b0.refs_0_), channel_id=1, source_target_pairs={{0,4},{1,5},{2,6},{3,7},{4,0},{5,1},{6,2},{7,3},{8,12},{9,13},{10,... | collective-permute-start | bytes 1572872 | tf_op jit(solution)/shard_map/activations/ppermute | solution.py:38
  65.9 1.2 copy-start.5
  67.1 1.2 copy-start.7
  71.3 1.4 copy-start.1
  72.7 0.8 copy-start.8
  73.5 0.7 copy-start.10
  74.1 21.2 %collective-permute-start.4 = (bf16[640,256]{1,0:T(8,128)(2,1)}, bf16[640,256]{1,0:T(8,128)(2,1)S(1)}, u32[]{:S(2)}, u32[]{:S(2)}) collective-permute-start(bf16[640,256]{1,0:T(8,128)(2,1)} %get-tuple-element.26), channel_id=1, source_target_pairs={{0,1},{1,0},{2,3},{3,2},{4,5},{5,4},{6,7},{7,6},{8,9},{9,8},{10,11... | collective-permute-start | bytes 983048 | tf_op jit(solution)/shard_map/near_keys/ppermute | solution.py:33
  79.9 0.7 copy-start.3
  80.6 43.2 %all-to-all-start.3 = ((bf16[8,64,256]{2,1,0:T(8,128)(2,1)}), bf16[8,64,256]{2,1,0:T(8,128)(2,1)}, u32[]{:S(2)}, u32[]{:S(2)}) async-start(bf16[8,64,256]{2,1,0:T(8,128)(2,1)} %copy-done.3), calls=%async_computation.3 | async-start | bytes 524288 | tf_op jit(solution)/shard_map/outer_sum/all_to_all | solution.py:29
  95.8 16.2 %collective-permute-start.7 = (bf16[256,256]{1,0:T(8,128)(2,1)S(1)}, bf16[256,256]{1,0:T(8,128)(2,1)S(1)}, u32[]{:S(2)}, u32[]{:S(2)}) collective-permute-start(bf16[256,256]{1,0:T(8,128)(2,1)S(1)} %get-tuple-element.28), channel_id=1, source_target_pairs={{0,1},{1,0},{2,3},{3,2},{4,5},{5,4},{6,7},{7,6},{8,9},{9,8},{10,11... | collective-permute-start | bytes 393224 | tf_op jit(solution)/shard_map/far_keys/ppermute | solution.py:33
  101.8 4.9 %copy-start.11 = (f32[128,256]{1,0:T(8,128)S(1)}, f32[128,256]{1,0:T(8,128)}, u32[]{:S(2)}) copy-start(f32[128,256]{1,0:T(8,128)} %copy-done.10) | copy-start | bytes 393220
  101.8 10.2 %collective-permute-start.9 = (bf16[128,256]{1,0:T(8,128)(2,1)S(1)}, bf16[128,256]{1,0:T(8,128)(2,1)S(1)}, u32[]{:S(2)}, u32[]{:S(2)}) collective-permute-start(bf16[128,256]{1,0:T(8,128)(2,1)S(1)} %get-tuple-element.29), channel_id=1, source_target_pairs={{0,1},{1,0},{2,3},{3,2},{4,5},{5,4},{6,7},{7,6},{8,9},{9,8},{10,11... | collective-permute-start | bytes 196616 | tf_op jit(solution)/shard_map/far_keys/ppermute | solution.py:33
  106.6 5.3 %copy-start.2 = (bf16[2048,512]{1,0:T(8,128)(2,1)S(1)}, bf16[2048,512]{1,0:T(8,128)(2,1)}, u32[]{:S(2)}) copy-start(bf16[2048,512]{1,0:T(8,128)(2,1)} %copy-done.1) | copy-start | bytes 6291460
  106.7 5.3 %copy-start.9 = (f32[512,256]{1,0:T(8,128)S(1)}, f32[512,256]{1,0:T(8,128)}, u32[]{:S(2)}) copy-start(f32[512,256]{1,0:T(8,128)} %copy-done.8) | copy-start | bytes 1572868
  113.7 9.4 %collective-permute-start.10 = (f32[8,128]{1,0:T(8,128)S(1)}, f32[8,128]{1,0:T(8,128)S(1)}, u32[]{:S(2)}, u32[]{:S(2)}) collective-permute-start(f32[8,128]{1,0:T(8,128)S(1)} %get-tuple-element.33), channel_id=1, source_target_pairs={{0,1},{1,0},{2,3},{3,2},{4,5},{5,4},{6,7},{7,6},{8,9},{9,8},{10,11... | collective-permute-start | bytes 12296 | tf_op jit(solution)/shard_map/gradient/ppermute | solution.py:33
  123.1 7.4 %copy-start.13 = (f32[512,256]{1,0:T(8,128)S(1)}, f32[512,256]{1,0:T(8,128)}, u32[]{:S(2)}) copy-start(f32[512,256]{1,0:T(8,128)} %param.13) | copy-start | bytes 1572868
  123.1 7.4 %copy-start.15 = (bf16[512,256]{1,0:T(8,128)(2,1)S(1)}, bf16[512,256]{1,0:T(8,128)(2,1)}, u32[]{:S(2)}) copy-start(bf16[512,256]{1,0:T(8,128)(2,1)} %param.12) | copy-start | bytes 786436
  123.8 15.6 %copy-start = (bf16[1,512,1024]{2,1,0:T(8,128)(2,1)S(1)}, bf16[1,512,1024]{2,1,0:T(8,128)(2,1)}, u32[]{:S(2)}) copy-start(bf16[1,512,1024]{2,1,0:T(8,128)(2,1)} %weight_ref.1) | copy-start | bytes 3145732
  123.8 15.6 %copy-start.12 = (s32[8]{0:T(128)S(1)}, s32[8]{0:T(128)}, u32[]{:S(2)}) copy-start(s32[8]{0:T(128)} %order_ref.1) | copy-start | bytes 100
  123.8 15.6 %all-to-all-start = ((bf16[4,528,256]{2,1,0:T(8,128)(2,1)}), bf16[4,528,256]{2,1,0:T(8,128)(2,1)S(1)}, u32[]{:S(2)}, u32[]{:S(2)}) async-start(bf16[4,528,256]{2,1,0:T(8,128)(2,1)} %embed.1), calls=%async_computation | async-start | bytes 2162688 | tf_op jit(solution)/shard_map/gradient/all_to_all | solution.py:29
  131.5 10.7 %copy-start.4 = (bf16[512,256]{1,0:T(8,128)(2,1)}, bf16[512,256]{1,0:T(8,128)(2,1)S(1)}, u32[]{:S(2)}) copy-start(bf16[512,256]{1,0:T(8,128)(2,1)S(1)} %get-tuple-element.35.global_ref) | copy-start | bytes 786436

commit v9 on v7

--- a/solution.py
+++ b/solution.py
@@ -21,7 +21,6 @@
 PARAMS = pltpu.CompilerParams(vmem_limit_bytes=16 * 1024 * 1024)
 
 X_GROUPS = [[x * 2 + h for x in range(NX)] for h in range(2)]
-Z_GROUPS = [[z * 8 + l for z in range(8)] for l in range(8)]
 
 
 def exchange(blocks, axis, groups):
@@ -263,12 +262,10 @@
         by_rows = exchange(embedded, "fsdp", X_GROUPS)
 
     with jax.named_scope("outer_sum"):
-        by_z = exchange(pending_delta[0].reshape(8, 64, 256), "rep", Z_GROUPS)
-        total = call(sum_kernel, SDS((64, 256), F32), by_z, arrived, hbm=1)
-        for mask in (1, 2, 4):
-            total += lax.ppermute(total, "rep", [(i, i ^ mask) for i in range(64)])
-        by_rows_z = exchange(jnp.broadcast_to(total.astype(BF16)[None], (8, 64, 256)), "rep", Z_GROUPS)
-        mean = by_rows_z.astype(F32).reshape(512, 256) / lax.axis_size("rep")
+        parts = exchange(pending_delta[0].reshape(64, 8, 256), "rep", None)
+        total = call(sum_kernel, SDS((8, 256), F32), parts, arrived, hbm=1)
+        rows = exchange(jnp.broadcast_to(total.astype(BF16)[None], (64, 8, 256)), "rep", None)
+        mean = rows.astype(F32).reshape(512, 256) / lax.axis_size("rep")
         new_momentum = 0.9 * outer_momentum + mean
         new_global = (global_frag.astype(F32) - 0.7 * (mean + 0.9 * new_momentum)).astype(BF16)
 

time: 137 us -> 140 us (1.022)
  the two profiles are of different devices: /device:TPU:6 before, /device:TPU:56 now
where the time goes in v9:
time: 140 us; the launch traced here: 139 us
  starting transfers between devices  75.5 us (54%)
  waiting for transfers between devices  47.3 us (34%)
  Pallas kernels  13.5 us (10%)
    all_to_all x3, starting transfers between devices, exchange(): lax.all_to_all(blocks, axis, 0, 0, axis_index_groups=groups, tiled=True)  32.6 us
    ppermute x5, waiting for transfers between devices, flip(): return lax.ppermute(block, 'fsdp', [(i, i ^ mask) for i in range(8)])  31.9 us
    ppermute x5, starting transfers between devices, flip(): return lax.ppermute(block, 'fsdp', [(i, i ^ mask) for i in range(8)])  22.4 us
    ppermute x6, starting transfers between devices, rotate(): lax.ppermute(blocks[d], 'fsdp', moves[d])  20.5 us
    all_to_all x3, waiting for transfers between devices, exchange(): lax.all_to_all(blocks, axis, 0, 0, axis_index_groups=groups, tiled=True)  15.4 us
    pallas_call x8, Pallas kernels, call(): pl.pallas_call(kernel, in_specs=[SMEM] * scalars + [pl.BlockSpec(memory_s...  10.1 us
  transfers between devices with their start and end apart: 14, of which 6 were waited for; matrix products, arithmetic and copies ran while one was open for 1% of the time, Pallas kernels for 5%

profile of v9, /device:TPU:56, one launch (start us, length us, event | category | flops | bytes accessed | tf_op | source)
XLA Modules:
  0.0 138.9 jit_solution(643116387936656066)
XLA Ops:
  0.6 3.6 %pack.1 = (bf16[128,2048]{1,0:T(8,128)(2,1)}, bf16[208,2048]{1,0:T(8,128)(2,1)}, bf16[208,2048]{1,0:T(8,128)(2,1)}, bf16[208,2048]{1,0:T(8,128)(2,1)}, bf16[208,2048]{1,0:T(8,128)(2,1)}) custom-call(s32[1]{0:T(128)} %bitcast.index_ref, bf16[128,4096]{1,0:T(8,128)(2,1)} %refs_0_.1, bf16[1,512,1024]{2,1,0:T(8,128)(2,1)} %weight_ref.1, bf16[128,1024]{1,0:T(8,128)(2,1)} %refs_2_.1), custom_call_target="tpu_custom_call" | custom-call | bytes 4194304 | tf_op jit(solution)/shard_map/activations/pack/pallas_call | solution.py:199
  4.2 0.0 copy-start.2
  4.2 3.5 %collective-permute-start = (bf16[208,2048]{1,0:T(8,128)(2,1)}, bf16[208,2048]{1,0:T(8,128)(2,1)}, u32[]{:S(2)}, u32[]{:S(2)}) collective-permute-start(bf16[208,2048]{1,0:T(8,128)(2,1)} %get-tuple-element.20), channel_id=1, source_target_pairs={{0,2},{1,3},{2,4},{3,5},{4,6},{5,7},{6,0},{7,1},{8,10},{9,11},{10,... | collective-permute-start | bytes 2555912 | tf_op jit(solution)/shard_map/activations/ppermute | solution.py:36
  7.8 4.6 %collective-permute-start.1 = (bf16[208,2048]{1,0:T(8,128)(2,1)}, bf16[208,2048]{1,0:T(8,128)(2,1)}, u32[]{:S(2)}, u32[]{:S(2)}) collective-permute-start(bf16[208,2048]{1,0:T(8,128)(2,1)} %get-tuple-element.21), channel_id=1, source_target_pairs={{0,4},{1,5},{2,6},{3,7},{4,0},{5,1},{6,2},{7,3},{8,12},{9,13},{10,... | collective-permute-start | bytes 2555912 | tf_op jit(solution)/shard_map/activations/ppermute | solution.py:36
  12.4 3.3 %collective-permute-start.2 = (bf16[208,2048]{1,0:T(8,128)(2,1)}, bf16[208,2048]{1,0:T(8,128)(2,1)}, u32[]{:S(2)}, u32[]{:S(2)}) collective-permute-start(bf16[208,2048]{1,0:T(8,128)(2,1)} %get-tuple-element.22), channel_id=1, source_target_pairs={{0,6},{1,7},{2,0},{3,1},{4,2},{5,3},{6,4},{7,5},{8,14},{9,15},{10,... | collective-permute-start | bytes 2555912 | tf_op jit(solution)/shard_map/activations/ppermute | solution.py:36
  15.8 4.7 %collective-permute-start.3 = (bf16[128,2048]{1,0:T(8,128)(2,1)}, bf16[128,2048]{1,0:T(8,128)(2,1)S(1)}, u32[]{:S(2)}, u32[]{:S(2)}) collective-permute-start(bf16[128,2048]{1,0:T(8,128)(2,1)} %get-tuple-element.23), channel_id=1, source_target_pairs={{0,1},{1,0},{2,3},{3,2},{4,5},{5,4},{6,7},{7,6},{8,9},{9,8},{10,11... | collective-permute-start | bytes 1572872 | tf_op jit(solution)/shard_map/activations/ppermute | solution.py:31
  20.5 14.1 %all-to-all-start.1 = ((bf16[64,8,256]{2,1,0:T(8,128)(2,1)}), bf16[64,8,256]{2,1,0:T(8,128)(2,1)S(1)}, u32[]{:S(2)}, u32[]{:S(2)}) async-start(bf16[64,8,256]{2,1,0:T(8,128)(2,1)} %bitcast.1), calls=%async_computation.1 | async-start | bytes 524288 | tf_op jit(solution)/shard_map/outer_sum/all_to_all | solution.py:27
  34.6 11.6 %collective-permute-done.3.arrived_ref.b0._ = bf16[128,2048]{1,0:T(8,128)(2,1)S(1)} collective-permute-done((bf16[128,2048]{1,0:T(8,128)(2,1)}, bf16[128,2048]{1,0:T(8,128)(2,1)S(1)}, u32[]{:S(2)}, u32[]{:S(2)}) %collective-permute-start.3) | collective-permute-done | bytes 524320 | tf_op jit(solution)/shard_map/activations/ppermute | solution.py:31
  46.2 2.5 %collective-permute-start.5 = (bf16[128,2048]{1,0:T(8,128)(2,1)S(1)}, bf16[128,2048]{1,0:T(8,128)(2,1)S(1)}, u32[]{:S(2)}, u32[]{:S(2)}) collective-permute-start(bf16[128,2048]{1,0:T(8,128)(2,1)S(1)} %collective-permute-done.3.arrived_ref.b0._), channel_id=1, source_target_pairs={{0,2},{1,3},{2,4},{3,5},{4,6},{5,7},{6,0},{7,1},{8,10},{9,11},{10,... | collective-permute-start | bytes 1572872 | tf_op jit(solution)/shard_map/activations/ppermute | solution.py:36
  48.7 4.6 %collective-permute-start.6 = (bf16[128,2048]{1,0:T(8,128)(2,1)S(1)}, bf16[128,2048]{1,0:T(8,128)(2,1)S(1)}, u32[]{:S(2)}, u32[]{:S(2)}) collective-permute-start(bf16[128,2048]{1,0:T(8,128)(2,1)S(1)} %collective-permute-done.3.arrived_ref.b0._), channel_id=1, source_target_pairs={{0,6},{1,7},{2,0},{3,1},{4,2},{5,3},{6,4},{7,5},{8,14},{9,15},{10,... | collective-permute-start | bytes 1572872 | tf_op jit(solution)/shard_map/activations/ppermute | solution.py:36
  53.3 0.0 collective-permute-done.m1
  53.3 1.9 %collective-permute-start.8 = (bf16[128,2048]{1,0:T(8,128)(2,1)S(1)}, bf16[128,2048]{1,0:T(8,128)(2,1)S(1)}, u32[]{:S(2)}, u32[]{:S(2)}) collective-permute-start(bf16[128,2048]{1,0:T(8,128)(2,1)S(1)} %collective-permute-done.3.arrived_ref.b0._), channel_id=1, source_target_pairs={{0,4},{1,5},{2,6},{3,7},{4,0},{5,1},{6,2},{7,3},{8,12},{9,13},{10,... | collective-permute-start | bytes 1572872 | tf_op jit(solution)/shard_map/activations/ppermute | solution.py:36
  55.2 1.9 %all-to-all-done.1.blocks_ref = bf16[64,8,256]{2,1,0:T(8,128)(2,1)S(1)} async-done(((bf16[64,8,256]{2,1,0:T(8,128)(2,1)}), bf16[64,8,256]{2,1,0:T(8,128)(2,1)S(1)}, u32[]{:S(2)}, u32[]{:S(2)}) %all-to-all-start.1) | async-done | bytes 262176 | tf_op jit(solution)/shard_map/outer_sum/all_to_all | solution.py:27
  57.1 0.1 sum.1
  57.2 0.7 broadcast_in_dim.2
  58.0 13.6 %all-to-all-start.2 = ((bf16[64,8,256]{2,1,0:T(8,128)(2,1)}), bf16[64,8,256]{2,1,0:T(8,128)(2,1)S(1)}, u32[]{:S(2)}, u32[]{:S(2)}) async-start(bf16[64,8,256]{2,1,0:T(8,128)(2,1)} %broadcast_in_dim.2), calls=%async_computation.2 | async-start | bytes 524288 | tf_op jit(solution)/shard_map/outer_sum/all_to_all | solution.py:27
  71.5 0.0 collective-permute-done.1.m2
  71.5 0.0 collective-permute-done.2.m3
  71.5 0.0 copy-done.2
  71.5 2.6 %near.1 = (f32[512,256]{1,0:T(8,128)S(1)}, bf16[640,256]{1,0:T(8,128)(2,1)S(1)}, bf16[2048,256]{1,0:T(8,128)(2,1)S(1)}, bf16[2048,512]{1,0:T(8,128)(2,1)S(1)}, f32[128,256]{1,0:T(8,128)S(1)}) custom-call(s32[1]{0:T(128)} %bitcast.index_ref, bf16[208,2048]{1,0:T(8,128)(2,1)S(1)} %copy-done.2, bf16[208,2048]{1,0:T(8,128)(2,1)} %collective-permute-done.m1, ...), custom_call_target="tpu_custom_call" | custom-call | flops 536870912 | bytes 4194304 | tf_op jit(solution)/shard_map/near_keys/near/pallas_call | solution.py:199
  74.2 3.8 %collective-permute-start.4 = (bf16[640,256]{1,0:T(8,128)(2,1)S(1)}, bf16[640,256]{1,0:T(8,128)(2,1)S(1)}, u32[]{:S(2)}, u32[]{:S(2)}) collective-permute-start(bf16[640,256]{1,0:T(8,128)(2,1)S(1)} %get-tuple-element.26), channel_id=1, source_target_pairs={{0,1},{1,0},{2,3},{3,2},{4,5},{5,4},{6,7},{7,6},{8,9},{9,8},{10,11... | collective-permute-start | bytes 983048 | tf_op jit(solution)/shard_map/near_keys/ppermute | solution.py:31
  77.9 0.0 collective-permute-done.5.refs_0_.b1
  77.9 0.0 collective-permute-done.6.refs_1_.b3
  78.0 0.5 far.2
  78.4 6.0 %collective-permute-start.7 = (bf16[256,256]{1,0:T(8,128)(2,1)S(1)}, bf16[256,256]{1,0:T(8,128)(2,1)S(1)}, u32[]{:S(2)}, u32[]{:S(2)}) collective-permute-start(bf16[256,256]{1,0:T(8,128)(2,1)S(1)} %get-tuple-element.28), channel_id=1, source_target_pairs={{0,1},{1,0},{2,3},{3,2},{4,5},{5,4},{6,7},{7,6},{8,9},{9,8},{10,11... | collective-permute-start | bytes 393224 | tf_op jit(solution)/shard_map/far_keys/ppermute | solution.py:31
  84.4 0.0 collective-permute-done.8.refs_0_.b2
  84.4 0.3 far.3
  84.7 3.8 %collective-permute-start.9 = (bf16[128,256]{1,0:T(8,128)(2,1)S(1)}, bf16[128,256]{1,0:T(8,128)(2,1)S(1)}, u32[]{:S(2)}, u32[]{:S(2)}) collective-permute-start(bf16[128,256]{1,0:T(8,128)(2,1)S(1)} %get-tuple-element.29), channel_id=1, source_target_pairs={{0,1},{1,0},{2,3},{3,2},{4,5},{5,4},{6,7},{7,6},{8,9},{9,8},{10,11... | collective-permute-start | bytes 196616 | tf_op jit(solution)/shard_map/far_keys/ppermute | solution.py:31
  88.5 0.6 turn.1.turned_ref
  89.1 11.6 %collective-permute-done.4.rest_ref = bf16[640,256]{1,0:T(8,128)(2,1)S(1)} collective-permute-done((bf16[640,256]{1,0:T(8,128)(2,1)S(1)}, bf16[640,256]{1,0:T(8,128)(2,1)S(1)}, u32[]{:S(2)}, u32[]{:S(2)}) %collective-permute-start.4) | collective-permute-done | bytes 327712 | tf_op jit(solution)/shard_map/near_keys/ppermute | solution.py:31
  100.7 0.7 far_gradient.1.far_ref
  101.5 3.4 %collective-permute-done.9.last_ref = bf16[128,256]{1,0:T(8,128)(2,1)S(1)} collective-permute-done((bf16[128,256]{1,0:T(8,128)(2,1)S(1)}, bf16[128,256]{1,0:T(8,128)(2,1)S(1)}, u32[]{:S(2)}, u32[]{:S(2)}) %collective-permute-start.9) | collective-permute-done | bytes 65568 | tf_op jit(solution)/shard_map/far_keys/ppermute | solution.py:31
  104.9 0.0 collective-permute-done.7.sides_ref
  104.9 1.8 %near_gradient.1 = (bf16[4,528,256]{2,1,0:T(8,128)(2,1)}, f32[8,128]{1,0:T(8,128)S(1)}) custom-call(bf16[2048,512]{1,0:T(8,128)(2,1)S(1)} %get-tuple-element.24.turned_ref, f32[512,256]{1,0:T(8,128)S(1)} %get-tuple-element.25.part_ref, bf16[640,256]{1,0:T(8,128)(2,1)S(1)} %collective-permute-done.4.rest_ref, ...), custom_call_target="tpu_custom_call" | custom-call | flops 536870912 | bytes 4194304 | tf_op jit(solution)/shard_map/gradient/near_gradient/pallas_call | solution.py:199
  106.7 4.2 %collective-permute-start.10 = (f32[8,128]{1,0:T(8,128)S(1)}, f32[8,128]{1,0:T(8,128)S(1)}, u32[]{:S(2)}, u32[]{:S(2)}) collective-permute-start(f32[8,128]{1,0:T(8,128)S(1)} %get-tuple-element.33), channel_id=1, source_target_pairs={{0,1},{1,0},{2,3},{3,2},{4,5},{5,4},{6,7},{7,6},{8,9},{9,8},{10,11... | collective-permute-start | bytes 12296 | tf_op jit(solution)/shard_map/gradient/ppermute | solution.py:31
  110.8 5.2 %collective-permute-done.10 = f32[8,128]{1,0:T(8,128)S(1)} collective-permute-done((f32[8,128]{1,0:T(8,128)S(1)}, f32[8,128]{1,0:T(8,128)S(1)}, u32[]{:S(2)}, u32[]{:S(2)}) %collective-permute-start.10) | collective-permute-done | bytes 4128 | tf_op jit(solution)/shard_map/gradient/ppermute | solution.py:31
  116.1 0.0 copy-start.4
  116.1 0.6 embed.1
  116.7 0.0 all-to-all-done.2
  116.7 4.9 %all-to-all-start = ((bf16[4,528,256]{2,1,0:T(8,128)(2,1)}), bf16[4,528,256]{2,1,0:T(8,128)(2,1)S(1)}, u32[]{:S(2)}, u32[]{:S(2)}) async-start(bf16[4,528,256]{2,1,0:T(8,128)(2,1)} %embed.1), calls=%async_computation | async-start | bytes 2162688 | tf_op jit(solution)/shard_map/gradient/all_to_all | solution.py:27
  121.6 0.0 copy-done.4
  121.6 0.0 copy-done.5
  121.6 1.0 fusion.2
  122.6 13.5 %all-to-all-done.squares_ref.rows_ref = bf16[4,528,256]{2,1,0:T(8,128)(2,1)S(1)} async-done(((bf16[4,528,256]{2,1,0:T(8,128)(2,1)}), bf16[4,528,256]{2,1,0:T(8,128)(2,1)S(1)}, u32[]{:S(2)}, u32[]{:S(2)}) %all-to-all-start) | async-done | bytes 1081376 | tf_op jit(solution)/shard_map/gradient/all_to_all | solution.py:27
  136.1 0.0 copy-done
  136.1 0.0 copy-done.3
  136.1 2.8 %step.1 = bf16[1,512,1024]{2,1,0:T(8,128)(2,1)} custom-call(s32[8]{0:T(128)S(1)} %copy-done.3, bf16[4,528,256]{2,1,0:T(8,128)(2,1)S(1)} %all-to-all-done.squares_ref.rows_ref, bf16[4,528,256]{2,1,0:T(8,128)(2,1)S(1)} %all-to-all-done.squares_ref.rows_ref, bf16[1,512,1024]{2,1,0:T(8,128)(2,1)S(1)} %copy-done, bf16[512,256]{1,0:T(8,128)(2,1)S(1)} %get-tuple-element.35.global_ref), custom_call_target="tpu_custom_call" | custom-call | tf_op jit(solution)/shard_map/step/step/pallas_call | solution.py:179
  138.9 0.0 copy-done.1
  (6 shorter events, 0.0 us)
Async XLA Ops:
  4.2 67.3 %copy-start.2 = (bf16[208,2048]{1,0:T(8,128)(2,1)S(1)}, bf16[208,2048]{1,0:T(8,128)(2,1)}, u32[]{:S(2)}) copy-start(bf16[208,2048]{1,0:T(8,128)(2,1)} %get-tuple-element.19.m0) | copy-start | bytes 2555908
  4.2 49.1 %collective-permute-start = (bf16[208,2048]{1,0:T(8,128)(2,1)}, bf16[208,2048]{1,0:T(8,128)(2,1)}, u32[]{:S(2)}, u32[]{:S(2)}) collective-permute-start(bf16[208,2048]{1,0:T(8,128)(2,1)} %get-tuple-element.20), channel_id=1, source_target_pairs={{0,2},{1,3},{2,4},{3,5},{4,6},{5,7},{6,0},{7,1},{8,10},{9,11},{10,... | collective-permute-start | bytes 2555912 | tf_op jit(solution)/shard_map/activations/ppermute | solution.py:36
  7.8 63.8 %collective-permute-start.1 = (bf16[208,2048]{1,0:T(8,128)(2,1)}, bf16[208,2048]{1,0:T(8,128)(2,1)}, u32[]{:S(2)}, u32[]{:S(2)}) collective-permute-start(bf16[208,2048]{1,0:T(8,128)(2,1)} %get-tuple-element.21), channel_id=1, source_target_pairs={{0,4},{1,5},{2,6},{3,7},{4,0},{5,1},{6,2},{7,3},{8,12},{9,13},{10,... | collective-permute-start | bytes 2555912 | tf_op jit(solution)/shard_map/activations/ppermute | solution.py:36
  12.4 59.1 %collective-permute-start.2 = (bf16[208,2048]{1,0:T(8,128)(2,1)}, bf16[208,2048]{1,0:T(8,128)(2,1)}, u32[]{:S(2)}, u32[]{:S(2)}) collective-permute-start(bf16[208,2048]{1,0:T(8,128)(2,1)} %get-tuple-element.22), channel_id=1, source_target_pairs={{0,6},{1,7},{2,0},{3,1},{4,2},{5,3},{6,4},{7,5},{8,14},{9,15},{10,... | collective-permute-start | bytes 2555912 | tf_op jit(solution)/shard_map/activations/ppermute | solution.py:36
  15.8 30.5 %collective-permute-start.3 = (bf16[128,2048]{1,0:T(8,128)(2,1)}, bf16[128,2048]{1,0:T(8,128)(2,1)S(1)}, u32[]{:S(2)}, u32[]{:S(2)}) collective-permute-start(bf16[128,2048]{1,0:T(8,128)(2,1)} %get-tuple-element.23), channel_id=1, source_target_pairs={{0,1},{1,0},{2,3},{3,2},{4,5},{5,4},{6,7},{7,6},{8,9},{9,8},{10,11... | collective-permute-start | bytes 1572872 | tf_op jit(solution)/shard_map/activations/ppermute | solution.py:31
  20.5 36.7 %all-to-all-start.1 = ((bf16[64,8,256]{2,1,0:T(8,128)(2,1)}), bf16[64,8,256]{2,1,0:T(8,128)(2,1)S(1)}, u32[]{:S(2)}, u32[]{:S(2)}) async-start(bf16[64,8,256]{2,1,0:T(8,128)(2,1)} %bitcast.1), calls=%async_computation.1 | async-start | bytes 524288 | tf_op jit(solution)/shard_map/outer_sum/all_to_all | solution.py:27
  46.2 31.7 %collective-permute-start.5 = (bf16[128,2048]{1,0:T(8,128)(2,1)S(1)}, bf16[128,2048]{1,0:T(8,128)(2,1)S(1)}, u32[]{:S(2)}, u32[]{:S(2)}) collective-permute-start(bf16[128,2048]{1,0:T(8,128)(2,1)S(1)} %collective-permute-done.3.arrived_ref.b0._), channel_id=1, source_target_pairs={{0,2},{1,3},{2,4},{3,5},{4,6},{5,7},{6,0},{7,1},{8,10},{9,11},{10,... | collective-permute-start | bytes 1572872 | tf_op jit(solution)/shard_map/activations/ppermute | solution.py:36
  48.7 29.2 %collective-permute-start.6 = (bf16[128,2048]{1,0:T(8,128)(2,1)S(1)}, bf16[128,2048]{1,0:T(8,128)(2,1)S(1)}, u32[]{:S(2)}, u32[]{:S(2)}) collective-permute-start(bf16[128,2048]{1,0:T(8,128)(2,1)S(1)} %collective-permute-done.3.arrived_ref.b0._), channel_id=1, source_target_pairs={{0,6},{1,7},{2,0},{3,1},{4,2},{5,3},{6,4},{7,5},{8,14},{9,15},{10,... | collective-permute-start | bytes 1572872 | tf_op jit(solution)/shard_map/activations/ppermute | solution.py:36
  53.3 31.1 %collective-permute-start.8 = (bf16[128,2048]{1,0:T(8,128)(2,1)S(1)}, bf16[128,2048]{1,0:T(8,128)(2,1)S(1)}, u32[]{:S(2)}, u32[]{:S(2)}) collective-permute-start(bf16[128,2048]{1,0:T(8,128)(2,1)S(1)} %collective-permute-done.3.arrived_ref.b0._), channel_id=1, source_target_pairs={{0,4},{1,5},{2,6},{3,7},{4,0},{5,1},{6,2},{7,3},{8,12},{9,13},{10,... | collective-permute-start | bytes 1572872 | tf_op jit(solution)/shard_map/activations/ppermute | solution.py:36
  58.0 58.7 %all-to-all-start.2 = ((bf16[64,8,256]{2,1,0:T(8,128)(2,1)}), bf16[64,8,256]{2,1,0:T(8,128)(2,1)S(1)}, u32[]{:S(2)}, u32[]{:S(2)}) async-start(bf16[64,8,256]{2,1,0:T(8,128)(2,1)} %broadcast_in_dim.2), calls=%async_computation.2 | async-start | bytes 524288 | tf_op jit(solution)/shard_map/outer_sum/all_to_all | solution.py:27
  74.2 26.6 %collective-permute-start.4 = (bf16[640,256]{1,0:T(8,128)(2,1)S(1)}, bf16[640,256]{1,0:T(8,128)(2,1)S(1)}, u32[]{:S(2)}, u32[]{:S(2)}) collective-permute-start(bf16[640,256]{1,0:T(8,128)(2,1)S(1)} %get-tuple-element.26), channel_id=1, source_target_pairs={{0,1},{1,0},{2,3},{3,2},{4,5},{5,4},{6,7},{7,6},{8,9},{9,8},{10,11... | collective-permute-start | bytes 983048 | tf_op jit(solution)/shard_map/near_keys/ppermute | solution.py:31
  78.4 26.5 %collective-permute-start.7 = (bf16[256,256]{1,0:T(8,128)(2,1)S(1)}, bf16[256,256]{1,0:T(8,128)(2,1)S(1)}, u32[]{:S(2)}, u32[]{:S(2)}) collective-permute-start(bf16[256,256]{1,0:T(8,128)(2,1)S(1)} %get-tuple-element.28), channel_id=1, source_target_pairs={{0,1},{1,0},{2,3},{3,2},{4,5},{5,4},{6,7},{7,6},{8,9},{9,8},{10,11... | collective-permute-start | bytes 393224 | tf_op jit(solution)/shard_map/far_keys/ppermute | solution.py:31
  84.7 20.1 %collective-permute-start.9 = (bf16[128,256]{1,0:T(8,128)(2,1)S(1)}, bf16[128,256]{1,0:T(8,128)(2,1)S(1)}, u32[]{:S(2)}, u32[]{:S(2)}) collective-permute-start(bf16[128,256]{1,0:T(8,128)(2,1)S(1)} %get-tuple-element.29), channel_id=1, source_target_pairs={{0,1},{1,0},{2,3},{3,2},{4,5},{5,4},{6,7},{7,6},{8,9},{9,8},{10,11... | collective-permute-start | bytes 196616 | tf_op jit(solution)/shard_map/far_keys/ppermute | solution.py:31
  106.7 9.4 %collective-permute-start.10 = (f32[8,128]{1,0:T(8,128)S(1)}, f32[8,128]{1,0:T(8,128)S(1)}, u32[]{:S(2)}, u32[]{:S(2)}) collective-permute-start(f32[8,128]{1,0:T(8,128)S(1)} %get-tuple-element.33), channel_id=1, source_target_pairs={{0,1},{1,0},{2,3},{3,2},{4,5},{5,4},{6,7},{7,6},{8,9},{9,8},{10,11... | collective-permute-start | bytes 12296 | tf_op jit(solution)/shard_map/gradient/ppermute | solution.py:31
  116.1 5.6 %copy-start.4 = (f32[512,256]{1,0:T(8,128)S(1)}, f32[512,256]{1,0:T(8,128)}, u32[]{:S(2)}) copy-start(f32[512,256]{1,0:T(8,128)} %param.13) | copy-start | bytes 1572868
  116.1 5.6 %copy-start.5 = (bf16[512,256]{1,0:T(8,128)(2,1)S(1)}, bf16[512,256]{1,0:T(8,128)(2,1)}, u32[]{:S(2)}) copy-start(bf16[512,256]{1,0:T(8,128)(2,1)} %param.12) | copy-start | bytes 786436
  116.7 19.4 %copy-start = (bf16[1,512,1024]{2,1,0:T(8,128)(2,1)S(1)}, bf16[1,512,1024]{2,1,0:T(8,128)(2,1)}, u32[]{:S(2)}) copy-start(bf16[1,512,1024]{2,1,0:T(8,128)(2,1)} %weight_ref.1) | copy-start | bytes 3145732
  116.7 19.4 %copy-start.3 = (s32[8]{0:T(128)S(1)}, s32[8]{0:T(128)}, u32[]{:S(2)}) copy-start(s32[8]{0:T(128)} %order_ref.1) | copy-start | bytes 100
  116.7 19.4 %all-to-all-start = ((bf16[4,528,256]{2,1,0:T(8,128)(2,1)}), bf16[4,528,256]{2,1,0:T(8,128)(2,1)S(1)}, u32[]{:S(2)}, u32[]{:S(2)}) async-start(bf16[4,528,256]{2,1,0:T(8,128)(2,1)} %embed.1), calls=%async_computation | async-start | bytes 2162688 | tf_op jit(solution)/shard_map/gradient/all_to_all | solution.py:27
  122.6 16.3 %copy-start.1 = (bf16[512,256]{1,0:T(8,128)(2,1)}, bf16[512,256]{1,0:T(8,128)(2,1)S(1)}, u32[]{:S(2)}) copy-start(bf16[512,256]{1,0:T(8,128)(2,1)S(1)} %get-tuple-element.35.global_ref) | copy-start | bytes 786436

commit v10 on v9

--- a/solution.py
+++ b/solution.py
@@ -126,13 +126,9 @@
         near = jnp.dot(turned_ref[rows], residual, preferred_element_type=F32)
         gradient = (near + far_ref[rows]) * FACTOR
         out_ref[x, :512] = gradient.astype(BF16)
-        out_ref[x, 512:] = jnp.zeros((16, COLS), BF16)
         squares += jnp.sum((gradient * gradient).reshape(64, 8, COLS), axis=0)
-    squares_ref[...] = squares[:, :128] + squares[:, 128:]
-
-
-def embed_kernel(squares_ref, _, out_ref):
-    squares = squares_ref[...]
+    squares = squares[:, :128] + squares[:, 128:]
+    squares_ref[...] = squares
     high = squares.astype(BF16).astype(F32)
     middle = (squares - high).astype(BF16).astype(F32)
     low = squares - high - middle
@@ -140,42 +136,33 @@
     lower = jnp.concatenate([low, jnp.zeros((8, 128), F32)], axis=1)
     rows = jnp.concatenate([upper, lower], axis=0).astype(BF16)
     for x in range(NX):
-        out_ref[x] = rows
-
-
-def embed(squares, gradient):
-    return pl.pallas_call(
-        embed_kernel,
-        grid=(1,),
-        in_specs=[pl.BlockSpec((8, 128), lambda i: (0, 0)), pl.BlockSpec(memory_space=pl.ANY)],
-        out_specs=pl.BlockSpec((NX, 16, COLS), lambda i: (0, 32, 0)),
-        out_shape=SDS((NX, 528, COLS), BF16),
-        input_output_aliases={1: 0},
-        compiler_params=PARAMS,
-        name="embed",
-    )(squares, gradient)
+        out_ref[x, 512:] = rows
 
 
 def sum_kernel(blocks_ref, _, out_ref):
     out_ref[...] = jnp.sum(blocks_ref[...].astype(F32), axis=0)
 
 
-def step_kernel(order_ref, squares_ref, rows_ref, weight_ref, global_ref, out_ref, new_ref):
+def step_kernel(order_ref, squares_ref, rows_ref, weight_ref, global_ref, s0, s1, s2, s3, out_ref):
     total = jnp.sum(squares_ref[...].astype(F32), axis=0)
     total = jnp.sum(total, axis=(0, 1), keepdims=True)
+    total += jnp.sum(s0[...] + s1[...] + s2[...] + s3[...], axis=(0, 1), keepdims=True)
     rate = 0.25 * lax.rsqrt(total / (D * KV) + 1e-06)
     for x in range(NX):
         columns = slice(x * COLS, (x + 1) * COLS)
-        weight = weight_ref[0, :, columns].astype(F32)
-        new_ref[:, columns] = weight - rows_ref[x].astype(F32) * rate
+        stepped = weight_ref[0, :, columns].astype(F32) - rows_ref[x].astype(F32) * rate
+        out_ref[0, :, columns] = stepped.astype(BF16)
     for slot in range(FRAG_HEADS):
-        at = pl.ds(pl.multiple_of(order_ref[slot] * HEAD, HEAD), HEAD)
+        head = order_ref[slot]
+        at = pl.ds(pl.multiple_of(head * HEAD, HEAD), HEAD)
+        inner = pl.ds(pl.multiple_of(lax.rem(head, 2) * HEAD, HEAD), HEAD)
+        gradient = rows_ref[lax.div(head, 2), :, inner].astype(F32)
+        stepped = weight_ref[0, :, at].astype(F32) - gradient * rate
         incoming = global_ref[:, slot * HEAD : (slot + 1) * HEAD].astype(F32)
-        new_ref[:, at] = 0.5 * new_ref[:, at] + 0.5 * incoming
-    out_ref[0] = new_ref[...].astype(BF16)
-
-
-def step(order, rows, weight, new_global):
+        out_ref[0, :, at] = (0.5 * stepped + 0.5 * incoming).astype(BF16)
+
+
+def step(order, rows, weight, new_global, others):
     return pl.pallas_call(
         step_kernel,
         grid=(4,),
@@ -185,13 +172,13 @@
             pl.BlockSpec((NX, 128, COLS), lambda i: (0, i, 0)),
             pl.BlockSpec((1, 128, KV), lambda i: (0, i, 0)),
             pl.BlockSpec((128, COLS), lambda i: (i, 0)),
-        ],
+        ]
+        + [pl.BlockSpec((8, 128), lambda i: (0, 0))] * NX,
         out_specs=pl.BlockSpec((1, 128, KV), lambda i: (0, i, 0)),
         out_shape=SDS((1, 512, KV), BF16),
-        scratch_shapes=[pltpu.VMEM((128, KV), F32)],
         compiler_params=PARAMS,
         name="step",
-    )(order, rows, rows, weight, new_global)
+    )(order, rows, rows, weight, new_global, *others)
 
 
 def call(kernel, outs, *args, scalars=0, hbm=0, scratch=(), vmem_mib=16, out_space=pltpu.VMEM, flops=0):
@@ -257,9 +244,9 @@
             (SDS((NX, 528, COLS), BF16), SDS((8, 128), F32)),
             near_turned, near_part, rest, sides_rest, last_rest, far_gradient, flops=dot_flops,
         )
-        squares = squares + flip(squares, 1)
-        embedded = embed(squares, gradient)
-        by_rows = exchange(embedded, "fsdp", X_GROUPS)
+        by_rows = exchange(gradient, "fsdp", X_GROUPS)
+        crossings = [[(x * 2 + h, (x + d) % NX * 2 + 1 - h) for x in range(NX) for h in range(2)] for d in range(NX)]
+        others = [lax.ppermute(squares, "fsdp", crossing) for crossing in crossings]
 
     with jax.named_scope("outer_sum"):
         parts = exchange(pending_delta[0].reshape(64, 8, 256), "rep", None)
@@ -270,7 +257,7 @@
         new_global = (global_frag.astype(F32) - 0.7 * (mean + 0.9 * new_momentum)).astype(BF16)
 
     with jax.named_scope("step"):
-        new_weights = step(frag_order, by_rows, local_weights, new_global)
+        new_weights = step(frag_order, by_rows, local_weights, new_global, others)
     return (new_weights, new_global, new_momentum)
 
 

time: 140 us -> 144 us (1.029)
  the two profiles are of different devices: /device:TPU:56 before, /device:TPU:16 now
where the time goes in v10:
time: 144 us; the launch traced here: 143 us
  starting transfers between devices  94.2 us (65%)
  waiting for transfers between devices  33.6 us (23%)
  Pallas kernels  13 us (9%)
    all_to_all x3, starting transfers between devices, exchange(): lax.all_to_all(blocks, axis, 0, 0, axis_index_groups=groups, tiled=True)  28.1 us
    ppermute x4, waiting for transfers between devices, flip(): return lax.ppermute(block, 'fsdp', [(i, i ^ mask) for i in range(8)])  25.5 us
    ppermute x4, starting transfers between devices, body(): others = [lax.ppermute(squares, 'fsdp', crossing) for crossing in crossings]  24 us
    ppermute x4, starting transfers between devices, flip(): return lax.ppermute(block, 'fsdp', [(i, i ^ mask) for i in range(8)])  21.7 us
    ppermute x6, starting transfers between devices, rotate(): lax.ppermute(blocks[d], 'fsdp', moves[d])  20.5 us
    pallas_call x8, Pallas kernels, call(): pl.pallas_call(kernel, in_specs=[SMEM] * scalars + [pl.BlockSpec(memory_s...  10.1 us
    ppermute x4, waiting for transfers between devices, body(): others = [lax.ppermute(squares, 'fsdp', crossing) for crossing in crossings]  4.67 us
    all_to_all x3, waiting for transfers between devices, exchange(): lax.all_to_all(blocks, axis, 0, 0, axis_index_groups=groups, tiled=True)  3.43 us
  transfers between devices with their start and end apart: 17, of which 5 were waited for; matrix products, arithmetic and copies ran while one was open for 1% of the time, Pallas kernels for 5%

profile of v10, /device:TPU:16, one launch (start us, length us, event | category | flops | bytes accessed | tf_op | source)
XLA Modules:
  0.0 143.5 jit_solution(9288794832361442796)
XLA Ops:
  0.6 3.6 %pack.1 = (bf16[128,2048]{1,0:T(8,128)(2,1)}, bf16[208,2048]{1,0:T(8,128)(2,1)}, bf16[208,2048]{1,0:T(8,128)(2,1)}, bf16[208,2048]{1,0:T(8,128)(2,1)}, bf16[208,2048]{1,0:T(8,128)(2,1)}) custom-call(s32[1]{0:T(128)} %bitcast.index_ref, bf16[128,4096]{1,0:T(8,128)(2,1)} %refs_0_.1, bf16[1,512,1024]{2,1,0:T(8,128)(2,1)} %weight_ref.1, bf16[128,1024]{1,0:T(8,128)(2,1)} %refs_2_.1), custom_call_target="tpu_custom_call" | custom-call | bytes 4194304 | tf_op jit(solution)/shard_map/activations/pack/pallas_call | solution.py:186
  4.2 0.0 copy-start.2
  4.2 3.5 %collective-permute-start = (bf16[208,2048]{1,0:T(8,128)(2,1)}, bf16[208,2048]{1,0:T(8,128)(2,1)}, u32[]{:S(2)}, u32[]{:S(2)}) collective-permute-start(bf16[208,2048]{1,0:T(8,128)(2,1)} %get-tuple-element.20), channel_id=1, source_target_pairs={{0,2},{1,3},{2,4},{3,5},{4,6},{5,7},{6,0},{7,1},{8,10},{9,11},{10,... | collective-permute-start | bytes 2555912 | tf_op jit(solution)/shard_map/activations/ppermute | solution.py:36
  7.7 4.6 %collective-permute-start.1 = (bf16[208,2048]{1,0:T(8,128)(2,1)}, bf16[208,2048]{1,0:T(8,128)(2,1)}, u32[]{:S(2)}, u32[]{:S(2)}) collective-permute-start(bf16[208,2048]{1,0:T(8,128)(2,1)} %get-tuple-element.21), channel_id=1, source_target_pairs={{0,4},{1,5},{2,6},{3,7},{4,0},{5,1},{6,2},{7,3},{8,12},{9,13},{10,... | collective-permute-start | bytes 2555912 | tf_op jit(solution)/shard_map/activations/ppermute | solution.py:36
  12.4 3.3 %collective-permute-start.2 = (bf16[208,2048]{1,0:T(8,128)(2,1)}, bf16[208,2048]{1,0:T(8,128)(2,1)}, u32[]{:S(2)}, u32[]{:S(2)}) collective-permute-start(bf16[208,2048]{1,0:T(8,128)(2,1)} %get-tuple-element.22), channel_id=1, source_target_pairs={{0,6},{1,7},{2,0},{3,1},{4,2},{5,3},{6,4},{7,5},{8,14},{9,15},{10,... | collective-permute-start | bytes 2555912 | tf_op jit(solution)/shard_map/activations/ppermute | solution.py:36
  15.7 5.9 %collective-permute-start.3 = (bf16[128,2048]{1,0:T(8,128)(2,1)}, bf16[128,2048]{1,0:T(8,128)(2,1)S(1)}, u32[]{:S(2)}, u32[]{:S(2)}) collective-permute-start(bf16[128,2048]{1,0:T(8,128)(2,1)} %get-tuple-element.23), channel_id=1, source_target_pairs={{0,1},{1,0},{2,3},{3,2},{4,5},{5,4},{6,7},{7,6},{8,9},{9,8},{10,11... | collective-permute-start | bytes 1572872 | tf_op jit(solution)/shard_map/activations/ppermute | solution.py:31
  21.7 13.4 %all-to-all-start.1 = ((bf16[64,8,256]{2,1,0:T(8,128)(2,1)}), bf16[64,8,256]{2,1,0:T(8,128)(2,1)S(1)}, u32[]{:S(2)}, u32[]{:S(2)}) async-start(bf16[64,8,256]{2,1,0:T(8,128)(2,1)} %bitcast.1), calls=%async_computation.1 | async-start | bytes 524288 | tf_op jit(solution)/shard_map/outer_sum/all_to_all | solution.py:27
  35.1 12.6 %collective-permute-done.3.arrived_ref.b0._ = bf16[128,2048]{1,0:T(8,128)(2,1)S(1)} collective-permute-done((bf16[128,2048]{1,0:T(8,128)(2,1)}, bf16[128,2048]{1,0:T(8,128)(2,1)S(1)}, u32[]{:S(2)}, u32[]{:S(2)}) %collective-permute-start.3) | collective-permute-done | bytes 524320 | tf_op jit(solution)/shard_map/activations/ppermute | solution.py:31
  47.6 2.5 %collective-permute-start.5 = (bf16[128,2048]{1,0:T(8,128)(2,1)S(1)}, bf16[128,2048]{1,0:T(8,128)(2,1)S(1)}, u32[]{:S(2)}, u32[]{:S(2)}) collective-permute-start(bf16[128,2048]{1,0:T(8,128)(2,1)S(1)} %collective-permute-done.3.arrived_ref.b0._), channel_id=1, source_target_pairs={{0,2},{1,3},{2,4},{3,5},{4,6},{5,7},{6,0},{7,1},{8,10},{9,11},{10,... | collective-permute-start | bytes 1572872 | tf_op jit(solution)/shard_map/activations/ppermute | solution.py:36
  50.1 4.6 %collective-permute-start.6 = (bf16[128,2048]{1,0:T(8,128)(2,1)S(1)}, bf16[128,2048]{1,0:T(8,128)(2,1)S(1)}, u32[]{:S(2)}, u32[]{:S(2)}) collective-permute-start(bf16[128,2048]{1,0:T(8,128)(2,1)S(1)} %collective-permute-done.3.arrived_ref.b0._), channel_id=1, source_target_pairs={{0,6},{1,7},{2,0},{3,1},{4,2},{5,3},{6,4},{7,5},{8,14},{9,15},{10,... | collective-permute-start | bytes 1572872 | tf_op jit(solution)/shard_map/activations/ppermute | solution.py:36
  54.7 0.0 collective-permute-done.m1
  54.7 1.9 %collective-permute-start.8 = (bf16[128,2048]{1,0:T(8,128)(2,1)S(1)}, bf16[128,2048]{1,0:T(8,128)(2,1)S(1)}, u32[]{:S(2)}, u32[]{:S(2)}) collective-permute-start(bf16[128,2048]{1,0:T(8,128)(2,1)S(1)} %collective-permute-done.3.arrived_ref.b0._), channel_id=1, source_target_pairs={{0,4},{1,5},{2,6},{3,7},{4,0},{5,1},{6,2},{7,3},{8,12},{9,13},{10,... | collective-permute-start | bytes 1572872 | tf_op jit(solution)/shard_map/activations/ppermute | solution.py:36
  56.6 3.4 %all-to-all-done.1.blocks_ref = bf16[64,8,256]{2,1,0:T(8,128)(2,1)S(1)} async-done(((bf16[64,8,256]{2,1,0:T(8,128)(2,1)}), bf16[64,8,256]{2,1,0:T(8,128)(2,1)S(1)}, u32[]{:S(2)}, u32[]{:S(2)}) %all-to-all-start.1) | async-done | bytes 262176 | tf_op jit(solution)/shard_map/outer_sum/all_to_all | solution.py:27
  60.1 0.1 sum.1
  60.2 0.7 broadcast_in_dim.2
  60.9 9.8 %all-to-all-start.2 = ((bf16[64,8,256]{2,1,0:T(8,128)(2,1)}), bf16[64,8,256]{2,1,0:T(8,128)(2,1)S(1)}, u32[]{:S(2)}, u32[]{:S(2)}) async-start(bf16[64,8,256]{2,1,0:T(8,128)(2,1)} %broadcast_in_dim.2), calls=%async_computation.2 | async-start | bytes 524288 | tf_op jit(solution)/shard_map/outer_sum/all_to_all | solution.py:27
  70.7 0.0 collective-permute-done.1.m2
  70.7 0.0 collective-permute-done.2.m3
  70.7 0.0 copy-done.2
  70.7 2.6 %near.1 = (f32[512,256]{1,0:T(8,128)S(1)}, bf16[640,256]{1,0:T(8,128)(2,1)S(1)}, bf16[2048,256]{1,0:T(8,128)(2,1)S(1)}, bf16[2048,512]{1,0:T(8,128)(2,1)S(1)}, f32[128,256]{1,0:T(8,128)S(1)}) custom-call(s32[1]{0:T(128)} %bitcast.index_ref, bf16[208,2048]{1,0:T(8,128)(2,1)S(1)} %copy-done.2, bf16[208,2048]{1,0:T(8,128)(2,1)} %collective-permute-done.m1, ...), custom_call_target="tpu_custom_call" | custom-call | flops 536870912 | bytes 4194304 | tf_op jit(solution)/shard_map/near_keys/near/pallas_call | solution.py:186
  73.3 6.0 %collective-permute-start.4 = (bf16[640,256]{1,0:T(8,128)(2,1)S(1)}, bf16[640,256]{1,0:T(8,128)(2,1)S(1)}, u32[]{:S(2)}, u32[]{:S(2)}) collective-permute-start(bf16[640,256]{1,0:T(8,128)(2,1)S(1)} %get-tuple-element.26), channel_id=1, source_target_pairs={{0,1},{1,0},{2,3},{3,2},{4,5},{5,4},{6,7},{7,6},{8,9},{9,8},{10,11... | collective-permute-start | bytes 983048 | tf_op jit(solution)/shard_map/near_keys/ppermute | solution.py:31
  79.3 0.0 collective-permute-done.5.refs_0_.b1
  79.3 0.0 collective-permute-done.6.refs_1_.b3
  79.3 0.5 far.2
  79.8 3.8 %collective-permute-start.7 = (bf16[256,256]{1,0:T(8,128)(2,1)S(1)}, bf16[256,256]{1,0:T(8,128)(2,1)S(1)}, u32[]{:S(2)}, u32[]{:S(2)}) collective-permute-start(bf16[256,256]{1,0:T(8,128)(2,1)S(1)} %get-tuple-element.28), channel_id=1, source_target_pairs={{0,1},{1,0},{2,3},{3,2},{4,5},{5,4},{6,7},{7,6},{8,9},{9,8},{10,11... | collective-permute-start | bytes 393224 | tf_op jit(solution)/shard_map/far_keys/ppermute | solution.py:31
  83.6 0.0 collective-permute-done.8.refs_0_.b2
  83.6 0.3 far.3
  83.9 6.0 %collective-permute-start.9 = (bf16[128,256]{1,0:T(8,128)(2,1)S(1)}, bf16[128,256]{1,0:T(8,128)(2,1)S(1)}, u32[]{:S(2)}, u32[]{:S(2)}) collective-permute-start(bf16[128,256]{1,0:T(8,128)(2,1)S(1)} %get-tuple-element.29), channel_id=1, source_target_pairs={{0,1},{1,0},{2,3},{3,2},{4,5},{5,4},{6,7},{7,6},{8,9},{9,8},{10,11... | collective-permute-start | bytes 196616 | tf_op jit(solution)/shard_map/far_keys/ppermute | solution.py:31
  89.9 0.6 turn.1.turned_ref
  90.5 9.5 %collective-permute-done.4.rest_ref = bf16[640,256]{1,0:T(8,128)(2,1)S(1)} collective-permute-done((bf16[640,256]{1,0:T(8,128)(2,1)S(1)}, bf16[640,256]{1,0:T(8,128)(2,1)S(1)}, u32[]{:S(2)}, u32[]{:S(2)}) %collective-permute-start.4) | collective-permute-done | bytes 327712 | tf_op jit(solution)/shard_map/near_keys/ppermute | solution.py:31
  100.0 0.7 far_gradient.1.far_ref
  100.7 3.4 %collective-permute-done.9.last_ref = bf16[128,256]{1,0:T(8,128)(2,1)S(1)} collective-permute-done((bf16[128,256]{1,0:T(8,128)(2,1)S(1)}, bf16[128,256]{1,0:T(8,128)(2,1)S(1)}, u32[]{:S(2)}, u32[]{:S(2)}) %collective-permute-start.9) | collective-permute-done | bytes 65568 | tf_op jit(solution)/shard_map/far_keys/ppermute | solution.py:31
  104.1 0.0 collective-permute-done.7.sides_ref
  104.1 1.8 %near_gradient.1 = (bf16[4,528,256]{2,1,0:T(8,128)(2,1)}, f32[8,128]{1,0:T(8,128)S(1)}) custom-call(bf16[2048,512]{1,0:T(8,128)(2,1)S(1)} %get-tuple-element.24.turned_ref, f32[512,256]{1,0:T(8,128)S(1)} %get-tuple-element.25.part_ref, bf16[640,256]{1,0:T(8,128)(2,1)S(1)} %collective-permute-done.4.rest_ref, ...), custom_call_target="tpu_custom_call" | custom-call | flops 536870912 | bytes 4194304 | tf_op jit(solution)/shard_map/gradient/near_gradient/pallas_call | solution.py:186
  105.9 0.0 all-to-all-done.2
  105.9 4.9 %all-to-all-start = ((bf16[4,528,256]{2,1,0:T(8,128)(2,1)}), bf16[4,528,256]{2,1,0:T(8,128)(2,1)S(1)}, u32[]{:S(2)}, u32[]{:S(2)}) async-start(bf16[4,528,256]{2,1,0:T(8,128)(2,1)} %get-tuple-element.33), calls=%async_computation | async-start | bytes 2162688 | tf_op jit(solution)/shard_map/gradient/all_to_all | solution.py:27
  110.9 6.0 %collective-permute-start.10 = (f32[8,128]{1,0:T(8,128)S(1)}, f32[8,128]{1,0:T(8,128)S(1)}, u32[]{:S(2)}, u32[]{:S(2)}) collective-permute-start(f32[8,128]{1,0:T(8,128)S(1)} %get-tuple-element.34), channel_id=1, source_target_pairs={{0,1},{1,0},{2,3},{3,2},{4,5},{5,4},{6,7},{7,6},{8,9},{9,8},{10,11... | collective-permute-start | bytes 12296 | tf_op jit(solution)/shard_map/gradient/ppermute | solution.py:249
  116.9 5.2 %collective-permute-start.11 = (f32[8,128]{1,0:T(8,128)S(1)}, f32[8,128]{1,0:T(8,128)S(1)}, u32[]{:S(2)}, u32[]{:S(2)}) collective-permute-start(f32[8,128]{1,0:T(8,128)S(1)} %get-tuple-element.34), channel_id=1, source_target_pairs={{0,3},{1,2},{2,5},{3,4},{4,7},{5,6},{6,1},{7,0},{8,11},{9,10},{10,... | collective-permute-start | bytes 12296 | tf_op jit(solution)/shard_map/gradient/ppermute | solution.py:249
  122.1 8.1 %collective-permute-start.12 = (f32[8,128]{1,0:T(8,128)S(1)}, f32[8,128]{1,0:T(8,128)S(1)}, u32[]{:S(2)}, u32[]{:S(2)}) collective-permute-start(f32[8,128]{1,0:T(8,128)S(1)} %get-tuple-element.34), channel_id=1, source_target_pairs={{0,5},{1,4},{2,7},{3,6},{4,1},{5,0},{6,3},{7,2},{8,13},{9,12},{10,... | collective-permute-start | bytes 12296 | tf_op jit(solution)/shard_map/gradient/ppermute | solution.py:249
  130.2 4.6 %collective-permute-start.13 = (f32[8,128]{1,0:T(8,128)S(1)}, f32[8,128]{1,0:T(8,128)S(1)}, u32[]{:S(2)}, u32[]{:S(2)}) collective-permute-start(f32[8,128]{1,0:T(8,128)S(1)} %get-tuple-element.34), channel_id=1, source_target_pairs={{0,7},{1,6},{2,1},{3,0},{4,3},{5,2},{6,5},{7,4},{8,15},{9,14},{10,... | collective-permute-start | bytes 12296 | tf_op jit(solution)/shard_map/gradient/ppermute | solution.py:249
  134.9 0.0 copy-done.4
  134.9 1.0 fusion.2
  135.9 0.0 collective-permute-done.10.s0
  135.9 0.0 collective-permute-done.11.s1
  135.9 0.0 collective-permute-done.12.s2
  135.9 4.7 %collective-permute-done.13.s3 = f32[8,128]{1,0:T(8,128)S(1)} collective-permute-done((f32[8,128]{1,0:T(8,128)S(1)}, f32[8,128]{1,0:T(8,128)S(1)}, u32[]{:S(2)}, u32[]{:S(2)}) %collective-permute-start.13) | collective-permute-done | bytes 4128 | tf_op jit(solution)/shard_map/gradient/ppermute | solution.py:249
  140.5 0.0 all-to-all-done.squares_ref.rows_ref
  140.6 2.9 %step.1 = bf16[1,512,1024]{2,1,0:T(8,128)(2,1)} custom-call(s32[8]{0:T(128)S(1)} %copy-done.3, bf16[4,528,256]{2,1,0:T(8,128)(2,1)S(1)} %all-to-all-done.squares_ref.rows_ref, bf16[4,528,256]{2,1,0:T(8,128)(2,1)S(1)} %all-to-all-done.squares_ref.rows_ref, bf16[1,512,1024]{2,1,0:T(8,128)(2,1)S(1)} %copy-done, ...), custom_call_target="tpu_custom_call" | custom-call | tf_op jit(solution)/shard_map/step/step/pallas_call | solution.py:166
  (10 shorter events, 0.0 us)
Async XLA Ops:
  4.2 66.5 %copy-start.2 = (bf16[208,2048]{1,0:T(8,128)(2,1)S(1)}, bf16[208,2048]{1,0:T(8,128)(2,1)}, u32[]{:S(2)}) copy-start(bf16[208,2048]{1,0:T(8,128)(2,1)} %get-tuple-element.19.m0) | copy-start | bytes 2555908
  4.2 50.5 %collective-permute-start = (bf16[208,2048]{1,0:T(8,128)(2,1)}, bf16[208,2048]{1,0:T(8,128)(2,1)}, u32[]{:S(2)}, u32[]{:S(2)}) collective-permute-start(bf16[208,2048]{1,0:T(8,128)(2,1)} %get-tuple-element.20), channel_id=1, source_target_pairs={{0,2},{1,3},{2,4},{3,5},{4,6},{5,7},{6,0},{7,1},{8,10},{9,11},{10,... | collective-permute-start | bytes 2555912 | tf_op jit(solution)/shard_map/activations/ppermute | solution.py:36
  7.7 62.9 %collective-permute-start.1 = (bf16[208,2048]{1,0:T(8,128)(2,1)}, bf16[208,2048]{1,0:T(8,128)(2,1)}, u32[]{:S(2)}, u32[]{:S(2)}) collective-permute-start(bf16[208,2048]{1,0:T(8,128)(2,1)} %get-tuple-element.21), channel_id=1, source_target_pairs={{0,4},{1,5},{2,6},{3,7},{4,0},{5,1},{6,2},{7,3},{8,12},{9,13},{10,... | collective-permute-start | bytes 2555912 | tf_op jit(solution)/shard_map/activations/ppermute | solution.py:36
  12.4 58.3 %collective-permute-start.2 = (bf16[208,2048]{1,0:T(8,128)(2,1)}, bf16[208,2048]{1,0:T(8,128)(2,1)}, u32[]{:S(2)}, u32[]{:S(2)}) collective-permute-start(bf16[208,2048]{1,0:T(8,128)(2,1)} %get-tuple-element.22), channel_id=1, source_target_pairs={{0,6},{1,7},{2,0},{3,1},{4,2},{5,3},{6,4},{7,5},{8,14},{9,15},{10,... | collective-permute-start | bytes 2555912 | tf_op jit(solution)/shard_map/activations/ppermute | solution.py:36
  15.7 31.9 %collective-permute-start.3 = (bf16[128,2048]{1,0:T(8,128)(2,1)}, bf16[128,2048]{1,0:T(8,128)(2,1)S(1)}, u32[]{:S(2)}, u32[]{:S(2)}) collective-permute-start(bf16[128,2048]{1,0:T(8,128)(2,1)} %get-tuple-element.23), channel_id=1, source_target_pairs={{0,1},{1,0},{2,3},{3,2},{4,5},{5,4},{6,7},{7,6},{8,9},{9,8},{10,11... | collective-permute-start | bytes 1572872 | tf_op jit(solution)/shard_map/activations/ppermute | solution.py:31
  21.7 38.4 %all-to-all-start.1 = ((bf16[64,8,256]{2,1,0:T(8,128)(2,1)}), bf16[64,8,256]{2,1,0:T(8,128)(2,1)S(1)}, u32[]{:S(2)}, u32[]{:S(2)}) async-start(bf16[64,8,256]{2,1,0:T(8,128)(2,1)} %bitcast.1), calls=%async_computation.1 | async-start | bytes 524288 | tf_op jit(solution)/shard_map/outer_sum/all_to_all | solution.py:27
  47.6 31.7 %collective-permute-start.5 = (bf16[128,2048]{1,0:T(8,128)(2,1)S(1)}, bf16[128,2048]{1,0:T(8,128)(2,1)S(1)}, u32[]{:S(2)}, u32[]{:S(2)}) collective-permute-start(bf16[128,2048]{1,0:T(8,128)(2,1)S(1)} %collective-permute-done.3.arrived_ref.b0._), channel_id=1, source_target_pairs={{0,2},{1,3},{2,4},{3,5},{4,6},{5,7},{6,0},{7,1},{8,10},{9,11},{10,... | collective-permute-start | bytes 1572872 | tf_op jit(solution)/shard_map/activations/ppermute | solution.py:36
  50.1 29.2 %collective-permute-start.6 = (bf16[128,2048]{1,0:T(8,128)(2,1)S(1)}, bf16[128,2048]{1,0:T(8,128)(2,1)S(1)}, u32[]{:S(2)}, u32[]{:S(2)}) collective-permute-start(bf16[128,2048]{1,0:T(8,128)(2,1)S(1)} %collective-permute-done.3.arrived_ref.b0._), channel_id=1, source_target_pairs={{0,6},{1,7},{2,0},{3,1},{4,2},{5,3},{6,4},{7,5},{8,14},{9,15},{10,... | collective-permute-start | bytes 1572872 | tf_op jit(solution)/shard_map/activations/ppermute | solution.py:36
  54.7 28.9 %collective-permute-start.8 = (bf16[128,2048]{1,0:T(8,128)(2,1)S(1)}, bf16[128,2048]{1,0:T(8,128)(2,1)S(1)}, u32[]{:S(2)}, u32[]{:S(2)}) collective-permute-start(bf16[128,2048]{1,0:T(8,128)(2,1)S(1)} %collective-permute-done.3.arrived_ref.b0._), channel_id=1, source_target_pairs={{0,4},{1,5},{2,6},{3,7},{4,0},{5,1},{6,2},{7,3},{8,12},{9,13},{10,... | collective-permute-start | bytes 1572872 | tf_op jit(solution)/shard_map/activations/ppermute | solution.py:36
  60.9 45.1 %all-to-all-start.2 = ((bf16[64,8,256]{2,1,0:T(8,128)(2,1)}), bf16[64,8,256]{2,1,0:T(8,128)(2,1)S(1)}, u32[]{:S(2)}, u32[]{:S(2)}) async-start(bf16[64,8,256]{2,1,0:T(8,128)(2,1)} %broadcast_in_dim.2), calls=%async_computation.2 | async-start | bytes 524288 | tf_op jit(solution)/shard_map/outer_sum/all_to_all | solution.py:27
  73.3 26.7 %collective-permute-start.4 = (bf16[640,256]{1,0:T(8,128)(2,1)S(1)}, bf16[640,256]{1,0:T(8,128)(2,1)S(1)}, u32[]{:S(2)}, u32[]{:S(2)}) collective-permute-start(bf16[640,256]{1,0:T(8,128)(2,1)S(1)} %get-tuple-element.26), channel_id=1, source_target_pairs={{0,1},{1,0},{2,3},{3,2},{4,5},{5,4},{6,7},{7,6},{8,9},{9,8},{10,11... | collective-permute-start | bytes 983048 | tf_op jit(solution)/shard_map/near_keys/ppermute | solution.py:31
  79.8 24.3 %collective-permute-start.7 = (bf16[256,256]{1,0:T(8,128)(2,1)S(1)}, bf16[256,256]{1,0:T(8,128)(2,1)S(1)}, u32[]{:S(2)}, u32[]{:S(2)}) collective-permute-start(bf16[256,256]{1,0:T(8,128)(2,1)S(1)} %get-tuple-element.28), channel_id=1, source_target_pairs={{0,1},{1,0},{2,3},{3,2},{4,5},{5,4},{6,7},{7,6},{8,9},{9,8},{10,11... | collective-permute-start | bytes 393224 | tf_op jit(solution)/shard_map/far_keys/ppermute | solution.py:31
  83.9 20.2 %collective-permute-start.9 = (bf16[128,256]{1,0:T(8,128)(2,1)S(1)}, bf16[128,256]{1,0:T(8,128)(2,1)S(1)}, u32[]{:S(2)}, u32[]{:S(2)}) collective-permute-start(bf16[128,256]{1,0:T(8,128)(2,1)S(1)} %get-tuple-element.29), channel_id=1, source_target_pairs={{0,1},{1,0},{2,3},{3,2},{4,5},{5,4},{6,7},{7,6},{8,9},{9,8},{10,11... | collective-permute-start | bytes 196616 | tf_op jit(solution)/shard_map/far_keys/ppermute | solution.py:31
  105.9 28.9 %copy-start.4 = (f32[512,256]{1,0:T(8,128)S(1)}, f32[512,256]{1,0:T(8,128)}, u32[]{:S(2)}) copy-start(f32[512,256]{1,0:T(8,128)} %param.13) | copy-start | bytes 1572868
  105.9 29.0 %copy-start.5 = (bf16[512,256]{1,0:T(8,128)(2,1)S(1)}, bf16[512,256]{1,0:T(8,128)(2,1)}, u32[]{:S(2)}) copy-start(bf16[512,256]{1,0:T(8,128)(2,1)} %param.12) | copy-start | bytes 786436
  105.9 34.6 %copy-start = (bf16[1,512,1024]{2,1,0:T(8,128)(2,1)S(1)}, bf16[1,512,1024]{2,1,0:T(8,128)(2,1)}, u32[]{:S(2)}) copy-start(bf16[1,512,1024]{2,1,0:T(8,128)(2,1)} %weight_ref.1) | copy-start | bytes 3145732
  105.9 34.6 %copy-start.3 = (s32[8]{0:T(128)S(1)}, s32[8]{0:T(128)}, u32[]{:S(2)}) copy-start(s32[8]{0:T(128)} %order_ref.1) | copy-start | bytes 100
  105.9 34.6 %all-to-all-start = ((bf16[4,528,256]{2,1,0:T(8,128)(2,1)}), bf16[4,528,256]{2,1,0:T(8,128)(2,1)S(1)}, u32[]{:S(2)}, u32[]{:S(2)}) async-start(bf16[4,528,256]{2,1,0:T(8,128)(2,1)} %get-tuple-element.33), calls=%async_computation | async-start | bytes 2162688 | tf_op jit(solution)/shard_map/gradient/all_to_all | solution.py:27
  110.9 25.0 %collective-permute-start.10 = (f32[8,128]{1,0:T(8,128)S(1)}, f32[8,128]{1,0:T(8,128)S(1)}, u32[]{:S(2)}, u32[]{:S(2)}) collective-permute-start(f32[8,128]{1,0:T(8,128)S(1)} %get-tuple-element.34), channel_id=1, source_target_pairs={{0,1},{1,0},{2,3},{3,2},{4,5},{5,4},{6,7},{7,6},{8,9},{9,8},{10,11... | collective-permute-start | bytes 12296 | tf_op jit(solution)/shard_map/gradient/ppermute | solution.py:249
  116.9 19.0 %collective-permute-start.11 = (f32[8,128]{1,0:T(8,128)S(1)}, f32[8,128]{1,0:T(8,128)S(1)}, u32[]{:S(2)}, u32[]{:S(2)}) collective-permute-start(f32[8,128]{1,0:T(8,128)S(1)} %get-tuple-element.34), channel_id=1, source_target_pairs={{0,3},{1,2},{2,5},{3,4},{4,7},{5,6},{6,1},{7,0},{8,11},{9,10},{10,... | collective-permute-start | bytes 12296 | tf_op jit(solution)/shard_map/gradient/ppermute | solution.py:249
  122.1 13.8 %collective-permute-start.12 = (f32[8,128]{1,0:T(8,128)S(1)}, f32[8,128]{1,0:T(8,128)S(1)}, u32[]{:S(2)}, u32[]{:S(2)}) collective-permute-start(f32[8,128]{1,0:T(8,128)S(1)} %get-tuple-element.34), channel_id=1, source_target_pairs={{0,5},{1,4},{2,7},{3,6},{4,1},{5,0},{6,3},{7,2},{8,13},{9,12},{10,... | collective-permute-start | bytes 12296 | tf_op jit(solution)/shard_map/gradient/ppermute | solution.py:249
  130.2 10.3 %collective-permute-start.13 = (f32[8,128]{1,0:T(8,128)S(1)}, f32[8,128]{1,0:T(8,128)S(1)}, u32[]{:S(2)}, u32[]{:S(2)}) collective-permute-start(f32[8,128]{1,0:T(8,128)S(1)} %get-tuple-element.34), channel_id=1, source_target_pairs={{0,7},{1,6},{2,1},{3,0},{4,3},{5,2},{6,5},{7,4},{8,15},{9,14},{10,... | collective-permute-start | bytes 12296 | tf_op jit(solution)/shard_map/gradient/ppermute | solution.py:249
  135.9 7.6 %copy-start.1 = (bf16[512,256]{1,0:T(8,128)(2,1)}, bf16[512,256]{1,0:T(8,128)(2,1)S(1)}, u32[]{:S(2)}) copy-start(bf16[512,256]{1,0:T(8,128)(2,1)S(1)} %get-tuple-element.35.global_ref) | copy-start | bytes 786436

commit v11 on v9

--- a/solution.py
+++ b/solution.py
@@ -263,7 +263,7 @@
 
     with jax.named_scope("outer_sum"):
         parts = exchange(pending_delta[0].reshape(64, 8, 256), "rep", None)
-        total = call(sum_kernel, SDS((8, 256), F32), parts, arrived, hbm=1)
+        total = call(sum_kernel, SDS((8, 256), F32), parts, arrived, hbm=1, flops=6 * 10**9)
         rows = exchange(jnp.broadcast_to(total.astype(BF16)[None], (64, 8, 256)), "rep", None)
         mean = rows.astype(F32).reshape(512, 256) / lax.axis_size("rep")
         new_momentum = 0.9 * outer_momentum + mean

time: 140 us -> 138 us (0.986)
  the two profiles are of different devices: /device:TPU:56 before, /device:TPU:16 now
where the time goes in v11:
time: 138 us
  starting transfers between devices  80 us (58%)
  waiting for transfers between devices  41.7 us (30%)
  Pallas kernels  13.5 us (10%)
    all_to_all x3, starting transfers between devices, exchange(): lax.all_to_all(blocks, axis, 0, 0, axis_index_groups=groups, tiled=True)  32.6 us
    ppermute x5, starting transfers between devices, flip(): return lax.ppermute(block, 'fsdp', [(i, i ^ mask) for i in range(8)])  25.4 us
    ppermute x6, starting transfers between devices, rotate(): lax.ppermute(blocks[d], 'fsdp', moves[d])  22 us
    ppermute x5, waiting for transfers between devices, flip(): return lax.ppermute(block, 'fsdp', [(i, i ^ mask) for i in range(8)])  17.5 us
    all_to_all x3, waiting for transfers between devices, exchange(): lax.all_to_all(blocks, axis, 0, 0, axis_index_groups=groups, tiled=True)  15.4 us
    pallas_call x8, Pallas kernels, call(): pl.pallas_call(kernel, in_specs=[SMEM] * scalars + [pl.BlockSpec(memory_s...  10.1 us
    ppermute x6, waiting for transfers between devices, rotate(): lax.ppermute(blocks[d], 'fsdp', moves[d])  8.84 us
    pallas_call x1, Pallas kernels, step(): pl.pallas_call(step_kernel, grid=(4,), in_specs=[SMEM, pl.BlockSpec((NX,...  2.8 us
  transfers between devices with their start and end apart: 14, of which 8 were waited for; matrix products, arithmetic and copies ran while one was open for 1% of the time, Pallas kernels for 5%

profile of v11, /device:TPU:16, one launch (start us, length us, event | category | flops | bytes accessed | tf_op | source)
XLA Modules:
  0.0 137.7 jit_solution(5217893819978768967)
XLA Ops:
  0.6 3.6 %pack.1 = (bf16[128,2048]{1,0:T(8,128)(2,1)}, bf16[208,2048]{1,0:T(8,128)(2,1)}, bf16[208,2048]{1,0:T(8,128)(2,1)}, bf16[208,2048]{1,0:T(8,128)(2,1)}, bf16[208,2048]{1,0:T(8,128)(2,1)}) custom-call(s32[1]{0:T(128)} %bitcast.index_ref, bf16[128,4096]{1,0:T(8,128)(2,1)} %refs_0_.1, bf16[1,512,1024]{2,1,0:T(8,128)(2,1)} %weight_ref.1, bf16[128,1024]{1,0:T(8,128)(2,1)} %refs_2_.1), custom_call_target="tpu_custom_call" | custom-call | bytes 4194304 | tf_op jit(solution)/shard_map/activations/pack/pallas_call | solution.py:199
  4.2 3.4 %collective-permute-start = (bf16[208,2048]{1,0:T(8,128)(2,1)}, bf16[208,2048]{1,0:T(8,128)(2,1)}, u32[]{:S(2)}, u32[]{:S(2)}) collective-permute-start(bf16[208,2048]{1,0:T(8,128)(2,1)} %get-tuple-element.20), channel_id=1, source_target_pairs={{0,2},{1,3},{2,4},{3,5},{4,6},{5,7},{6,0},{7,1},{8,10},{9,11},{10,... | collective-permute-start | bytes 2555912 | tf_op jit(solution)/shard_map/activations/ppermute | solution.py:36
  7.6 5.9 %collective-permute-start.3 = (bf16[128,2048]{1,0:T(8,128)(2,1)}, bf16[128,2048]{1,0:T(8,128)(2,1)S(1)}, u32[]{:S(2)}, u32[]{:S(2)}) collective-permute-start(bf16[128,2048]{1,0:T(8,128)(2,1)} %get-tuple-element.23), channel_id=1, source_target_pairs={{0,1},{1,0},{2,3},{3,2},{4,5},{5,4},{6,7},{7,6},{8,9},{9,8},{10,11... | collective-permute-start | bytes 1572872 | tf_op jit(solution)/shard_map/activations/ppermute | solution.py:31
  13.6 13.4 %all-to-all-start.1 = ((bf16[64,8,256]{2,1,0:T(8,128)(2,1)}), bf16[64,8,256]{2,1,0:T(8,128)(2,1)S(1)}, u32[]{:S(2)}, u32[]{:S(2)}) async-start(bf16[64,8,256]{2,1,0:T(8,128)(2,1)} %bitcast.1), calls=%async_computation.1 | async-start | bytes 524288 | tf_op jit(solution)/shard_map/outer_sum/all_to_all | solution.py:27
  26.9 4.6 %collective-permute-start.1 = (bf16[208,2048]{1,0:T(8,128)(2,1)}, bf16[208,2048]{1,0:T(8,128)(2,1)}, u32[]{:S(2)}, u32[]{:S(2)}) collective-permute-start(bf16[208,2048]{1,0:T(8,128)(2,1)} %get-tuple-element.21), channel_id=1, source_target_pairs={{0,4},{1,5},{2,6},{3,7},{4,0},{5,1},{6,2},{7,3},{8,12},{9,13},{10,... | collective-permute-start | bytes 2555912 | tf_op jit(solution)/shard_map/activations/ppermute | solution.py:36
  31.6 0.0 copy-start.2
  31.6 3.5 %collective-permute-start.2 = (bf16[208,2048]{1,0:T(8,128)(2,1)}, bf16[208,2048]{1,0:T(8,128)(2,1)}, u32[]{:S(2)}, u32[]{:S(2)}) collective-permute-start(bf16[208,2048]{1,0:T(8,128)(2,1)} %get-tuple-element.22), channel_id=1, source_target_pairs={{0,6},{1,7},{2,0},{3,1},{4,2},{5,3},{6,4},{7,5},{8,14},{9,15},{10,... | collective-permute-start | bytes 2555912 | tf_op jit(solution)/shard_map/activations/ppermute | solution.py:36
  35.1 5.1 %collective-permute-done.3.arrived_ref.b0._ = bf16[128,2048]{1,0:T(8,128)(2,1)S(1)} collective-permute-done((bf16[128,2048]{1,0:T(8,128)(2,1)}, bf16[128,2048]{1,0:T(8,128)(2,1)S(1)}, u32[]{:S(2)}, u32[]{:S(2)}) %collective-permute-start.3) | collective-permute-done | bytes 524320 | tf_op jit(solution)/shard_map/activations/ppermute | solution.py:31
  40.1 3.4 %collective-permute-start.5 = (bf16[128,2048]{1,0:T(8,128)(2,1)S(1)}, bf16[128,2048]{1,0:T(8,128)(2,1)S(1)}, u32[]{:S(2)}, u32[]{:S(2)}) collective-permute-start(bf16[128,2048]{1,0:T(8,128)(2,1)S(1)} %collective-permute-done.3.arrived_ref.b0._), channel_id=1, source_target_pairs={{0,2},{1,3},{2,4},{3,5},{4,6},{5,7},{6,0},{7,1},{8,10},{9,11},{10,... | collective-permute-start | bytes 1572872 | tf_op jit(solution)/shard_map/activations/ppermute | solution.py:36
  43.5 3.7 %collective-permute-start.6 = (bf16[128,2048]{1,0:T(8,128)(2,1)S(1)}, bf16[128,2048]{1,0:T(8,128)(2,1)S(1)}, u32[]{:S(2)}, u32[]{:S(2)}) collective-permute-start(bf16[128,2048]{1,0:T(8,128)(2,1)S(1)} %collective-permute-done.3.arrived_ref.b0._), channel_id=1, source_target_pairs={{0,6},{1,7},{2,0},{3,1},{4,2},{5,3},{6,4},{7,5},{8,14},{9,15},{10,... | collective-permute-start | bytes 1572872 | tf_op jit(solution)/shard_map/activations/ppermute | solution.py:36
  47.2 0.0 collective-permute-done.m1
  47.2 3.4 %collective-permute-start.8 = (bf16[128,2048]{1,0:T(8,128)(2,1)S(1)}, bf16[128,2048]{1,0:T(8,128)(2,1)S(1)}, u32[]{:S(2)}, u32[]{:S(2)}) collective-permute-start(bf16[128,2048]{1,0:T(8,128)(2,1)S(1)} %collective-permute-done.3.arrived_ref.b0._), channel_id=1, source_target_pairs={{0,4},{1,5},{2,6},{3,7},{4,0},{5,1},{6,2},{7,3},{8,12},{9,13},{10,... | collective-permute-start | bytes 1572872 | tf_op jit(solution)/shard_map/activations/ppermute | solution.py:36
  50.6 1.9 %all-to-all-done.1.blocks_ref = bf16[64,8,256]{2,1,0:T(8,128)(2,1)S(1)} async-done(((bf16[64,8,256]{2,1,0:T(8,128)(2,1)}), bf16[64,8,256]{2,1,0:T(8,128)(2,1)S(1)}, u32[]{:S(2)}, u32[]{:S(2)}) %all-to-all-start.1) | async-done | bytes 262176 | tf_op jit(solution)/shard_map/outer_sum/all_to_all | solution.py:27
  52.5 0.1 sum.1
  52.6 0.7 broadcast_in_dim.2
  53.3 11.4 %all-to-all-start.2 = ((bf16[64,8,256]{2,1,0:T(8,128)(2,1)}), bf16[64,8,256]{2,1,0:T(8,128)(2,1)S(1)}, u32[]{:S(2)}, u32[]{:S(2)}) async-start(bf16[64,8,256]{2,1,0:T(8,128)(2,1)} %broadcast_in_dim.2), calls=%async_computation.2 | async-start | bytes 524288 | tf_op jit(solution)/shard_map/outer_sum/all_to_all | solution.py:27
  64.7 0.0 collective-permute-done.1.m2
  64.7 5.0 %collective-permute-done.2.m3 = bf16[208,2048]{1,0:T(8,128)(2,1)} collective-permute-done((bf16[208,2048]{1,0:T(8,128)(2,1)}, bf16[208,2048]{1,0:T(8,128)(2,1)}, u32[]{:S(2)}, u32[]{:S(2)}) %collective-permute-start.2) | collective-permute-done | bytes 852000 | tf_op jit(solution)/shard_map/activations/ppermute | solution.py:36
  69.8 0.0 copy-done.2
  69.8 2.6 %near.1 = (f32[512,256]{1,0:T(8,128)S(1)}, bf16[640,256]{1,0:T(8,128)(2,1)S(1)}, bf16[2048,256]{1,0:T(8,128)(2,1)S(1)}, bf16[2048,512]{1,0:T(8,128)(2,1)S(1)}, f32[128,256]{1,0:T(8,128)S(1)}) custom-call(s32[1]{0:T(128)} %bitcast.index_ref, bf16[208,2048]{1,0:T(8,128)(2,1)S(1)} %copy-done.2, bf16[208,2048]{1,0:T(8,128)(2,1)} %collective-permute-done.m1, ...), custom_call_target="tpu_custom_call" | custom-call | flops 536870912 | bytes 4194304 | tf_op jit(solution)/shard_map/near_keys/near/pallas_call | solution.py:199
  72.4 4.7 %collective-permute-start.4 = (bf16[640,256]{1,0:T(8,128)(2,1)S(1)}, bf16[640,256]{1,0:T(8,128)(2,1)S(1)}, u32[]{:S(2)}, u32[]{:S(2)}) collective-permute-start(bf16[640,256]{1,0:T(8,128)(2,1)S(1)} %get-tuple-element.26), channel_id=1, source_target_pairs={{0,1},{1,0},{2,3},{3,2},{4,5},{5,4},{6,7},{7,6},{8,9},{9,8},{10,11... | collective-permute-start | bytes 983048 | tf_op jit(solution)/shard_map/near_keys/ppermute | solution.py:31
  77.1 0.0 collective-permute-done.5.refs_0_.b1
  77.1 3.8 %collective-permute-done.6.refs_1_.b3 = bf16[128,2048]{1,0:T(8,128)(2,1)S(1)} collective-permute-done((bf16[128,2048]{1,0:T(8,128)(2,1)S(1)}, bf16[128,2048]{1,0:T(8,128)(2,1)S(1)}, u32[]{:S(2)}, u32[]{:S(2)}) %collective-permute-start.6) | collective-permute-done | bytes 524320 | tf_op jit(solution)/shard_map/activations/ppermute | solution.py:36
  80.9 0.5 far.2
  81.4 4.7 %collective-permute-start.7 = (bf16[256,256]{1,0:T(8,128)(2,1)S(1)}, bf16[256,256]{1,0:T(8,128)(2,1)S(1)}, u32[]{:S(2)}, u32[]{:S(2)}) collective-permute-start(bf16[256,256]{1,0:T(8,128)(2,1)S(1)} %get-tuple-element.28), channel_id=1, source_target_pairs={{0,1},{1,0},{2,3},{3,2},{4,5},{5,4},{6,7},{7,6},{8,9},{9,8},{10,11... | collective-permute-start | bytes 393224 | tf_op jit(solution)/shard_map/far_keys/ppermute | solution.py:31
  86.1 0.0 collective-permute-done.8.refs_0_.b2
  86.1 0.3 far.3
  86.4 5.0 %collective-permute-start.9 = (bf16[128,256]{1,0:T(8,128)(2,1)S(1)}, bf16[128,256]{1,0:T(8,128)(2,1)S(1)}, u32[]{:S(2)}, u32[]{:S(2)}) collective-permute-start(bf16[128,256]{1,0:T(8,128)(2,1)S(1)} %get-tuple-element.29), channel_id=1, source_target_pairs={{0,1},{1,0},{2,3},{3,2},{4,5},{5,4},{6,7},{7,6},{8,9},{9,8},{10,11... | collective-permute-start | bytes 196616 | tf_op jit(solution)/shard_map/far_keys/ppermute | solution.py:31
  91.5 0.6 turn.1.turned_ref
  92.1 3.2 %collective-permute-done.4.rest_ref = bf16[640,256]{1,0:T(8,128)(2,1)S(1)} collective-permute-done((bf16[640,256]{1,0:T(8,128)(2,1)S(1)}, bf16[640,256]{1,0:T(8,128)(2,1)S(1)}, u32[]{:S(2)}, u32[]{:S(2)}) %collective-permute-start.4) | collective-permute-done | bytes 327712 | tf_op jit(solution)/shard_map/near_keys/ppermute | solution.py:31
  95.3 0.7 far_gradient.1.far_ref
  96.0 4.8 %collective-permute-done.9.last_ref = bf16[128,256]{1,0:T(8,128)(2,1)S(1)} collective-permute-done((bf16[128,256]{1,0:T(8,128)(2,1)S(1)}, bf16[128,256]{1,0:T(8,128)(2,1)S(1)}, u32[]{:S(2)}, u32[]{:S(2)}) %collective-permute-start.9) | collective-permute-done | bytes 65568 | tf_op jit(solution)/shard_map/far_keys/ppermute | solution.py:31
  100.8 0.0 collective-permute-done.7.sides_ref
  100.8 1.8 %near_gradient.1 = (bf16[4,528,256]{2,1,0:T(8,128)(2,1)}, f32[8,128]{1,0:T(8,128)S(1)}) custom-call(bf16[2048,512]{1,0:T(8,128)(2,1)S(1)} %get-tuple-element.24.turned_ref, f32[512,256]{1,0:T(8,128)S(1)} %get-tuple-element.25.part_ref, bf16[640,256]{1,0:T(8,128)(2,1)S(1)} %collective-permute-done.4.rest_ref, ...), custom_call_target="tpu_custom_call" | custom-call | flops 536870912 | bytes 4194304 | tf_op jit(solution)/shard_map/gradient/near_gradient/pallas_call | solution.py:199
  102.6 5.0 %collective-permute-start.10 = (f32[8,128]{1,0:T(8,128)S(1)}, f32[8,128]{1,0:T(8,128)S(1)}, u32[]{:S(2)}, u32[]{:S(2)}) collective-permute-start(f32[8,128]{1,0:T(8,128)S(1)} %get-tuple-element.33), channel_id=1, source_target_pairs={{0,1},{1,0},{2,3},{3,2},{4,5},{5,4},{6,7},{7,6},{8,9},{9,8},{10,11... | collective-permute-start | bytes 12296 | tf_op jit(solution)/shard_map/gradient/ppermute | solution.py:31
  107.6 4.4 %collective-permute-done.10 = f32[8,128]{1,0:T(8,128)S(1)} collective-permute-done((f32[8,128]{1,0:T(8,128)S(1)}, f32[8,128]{1,0:T(8,128)S(1)}, u32[]{:S(2)}, u32[]{:S(2)}) %collective-permute-start.10) | collective-permute-done | bytes 4128 | tf_op jit(solution)/shard_map/gradient/ppermute | solution.py:31
  112.0 0.0 copy-start.4
  112.0 0.6 embed.1
  112.6 0.0 all-to-all-done.2
  112.6 7.8 %all-to-all-start = ((bf16[4,528,256]{2,1,0:T(8,128)(2,1)}), bf16[4,528,256]{2,1,0:T(8,128)(2,1)S(1)}, u32[]{:S(2)}, u32[]{:S(2)}) async-start(bf16[4,528,256]{2,1,0:T(8,128)(2,1)} %embed.1), calls=%async_computation | async-start | bytes 2162688 | tf_op jit(solution)/shard_map/gradient/all_to_all | solution.py:27
  120.4 0.0 copy-done.4
  120.4 0.0 copy-done.5
  120.4 1.0 fusion.2
  121.4 13.5 %all-to-all-done.squares_ref.rows_ref = bf16[4,528,256]{2,1,0:T(8,128)(2,1)S(1)} async-done(((bf16[4,528,256]{2,1,0:T(8,128)(2,1)}), bf16[4,528,256]{2,1,0:T(8,128)(2,1)S(1)}, u32[]{:S(2)}, u32[]{:S(2)}) %all-to-all-start) | async-done | bytes 1081376 | tf_op jit(solution)/shard_map/gradient/all_to_all | solution.py:27
  134.9 0.0 copy-done
  134.9 0.0 copy-done.3
  134.9 2.8 %step.1 = bf16[1,512,1024]{2,1,0:T(8,128)(2,1)} custom-call(s32[8]{0:T(128)S(1)} %copy-done.3, bf16[4,528,256]{2,1,0:T(8,128)(2,1)S(1)} %all-to-all-done.squares_ref.rows_ref, bf16[4,528,256]{2,1,0:T(8,128)(2,1)S(1)} %all-to-all-done.squares_ref.rows_ref, bf16[1,512,1024]{2,1,0:T(8,128)(2,1)S(1)} %copy-done, bf16[512,256]{1,0:T(8,128)(2,1)S(1)} %get-tuple-element.35.global_ref), custom_call_target="tpu_custom_call" | custom-call | tf_op jit(solution)/shard_map/step/step/pallas_call | solution.py:179
  137.7 0.0 copy-done.1
  (6 shorter events, 0.0 us)
Async XLA Ops:
  4.2 43.0 %collective-permute-start = (bf16[208,2048]{1,0:T(8,128)(2,1)}, bf16[208,2048]{1,0:T(8,128)(2,1)}, u32[]{:S(2)}, u32[]{:S(2)}) collective-permute-start(bf16[208,2048]{1,0:T(8,128)(2,1)} %get-tuple-element.20), channel_id=1, source_target_pairs={{0,2},{1,3},{2,4},{3,5},{4,6},{5,7},{6,0},{7,1},{8,10},{9,11},{10,... | collective-permute-start | bytes 2555912 | tf_op jit(solution)/shard_map/activations/ppermute | solution.py:36
  7.6 32.5 %collective-permute-start.3 = (bf16[128,2048]{1,0:T(8,128)(2,1)}, bf16[128,2048]{1,0:T(8,128)(2,1)S(1)}, u32[]{:S(2)}, u32[]{:S(2)}) collective-permute-start(bf16[128,2048]{1,0:T(8,128)(2,1)} %get-tuple-element.23), channel_id=1, source_target_pairs={{0,1},{1,0},{2,3},{3,2},{4,5},{5,4},{6,7},{7,6},{8,9},{9,8},{10,11... | collective-permute-start | bytes 1572872 | tf_op jit(solution)/shard_map/activations/ppermute | solution.py:31
  13.6 38.9 %all-to-all-start.1 = ((bf16[64,8,256]{2,1,0:T(8,128)(2,1)}), bf16[64,8,256]{2,1,0:T(8,128)(2,1)S(1)}, u32[]{:S(2)}, u32[]{:S(2)}) async-start(bf16[64,8,256]{2,1,0:T(8,128)(2,1)} %bitcast.1), calls=%async_computation.1 | async-start | bytes 524288 | tf_op jit(solution)/shard_map/outer_sum/all_to_all | solution.py:27
  26.9 37.8 %collective-permute-start.1 = (bf16[208,2048]{1,0:T(8,128)(2,1)}, bf16[208,2048]{1,0:T(8,128)(2,1)}, u32[]{:S(2)}, u32[]{:S(2)}) collective-permute-start(bf16[208,2048]{1,0:T(8,128)(2,1)} %get-tuple-element.21), channel_id=1, source_target_pairs={{0,4},{1,5},{2,6},{3,7},{4,0},{5,1},{6,2},{7,3},{8,12},{9,13},{10,... | collective-permute-start | bytes 2555912 | tf_op jit(solution)/shard_map/activations/ppermute | solution.py:36
  31.6 38.2 %copy-start.2 = (bf16[208,2048]{1,0:T(8,128)(2,1)S(1)}, bf16[208,2048]{1,0:T(8,128)(2,1)}, u32[]{:S(2)}) copy-start(bf16[208,2048]{1,0:T(8,128)(2,1)} %get-tuple-element.19.m0) | copy-start | bytes 2555908
  31.6 38.2 %collective-permute-start.2 = (bf16[208,2048]{1,0:T(8,128)(2,1)}, bf16[208,2048]{1,0:T(8,128)(2,1)}, u32[]{:S(2)}, u32[]{:S(2)}) collective-permute-start(bf16[208,2048]{1,0:T(8,128)(2,1)} %get-tuple-element.22), channel_id=1, source_target_pairs={{0,6},{1,7},{2,0},{3,1},{4,2},{5,3},{6,4},{7,5},{8,14},{9,15},{10,... | collective-permute-start | bytes 2555912 | tf_op jit(solution)/shard_map/activations/ppermute | solution.py:36
  40.1 37.0 %collective-permute-start.5 = (bf16[128,2048]{1,0:T(8,128)(2,1)S(1)}, bf16[128,2048]{1,0:T(8,128)(2,1)S(1)}, u32[]{:S(2)}, u32[]{:S(2)}) collective-permute-start(bf16[128,2048]{1,0:T(8,128)(2,1)S(1)} %collective-permute-done.3.arrived_ref.b0._), channel_id=1, source_target_pairs={{0,2},{1,3},{2,4},{3,5},{4,6},{5,7},{6,0},{7,1},{8,10},{9,11},{10,... | collective-permute-start | bytes 1572872 | tf_op jit(solution)/shard_map/activations/ppermute | solution.py:36
  43.5 37.4 %collective-permute-start.6 = (bf16[128,2048]{1,0:T(8,128)(2,1)S(1)}, bf16[128,2048]{1,0:T(8,128)(2,1)S(1)}, u32[]{:S(2)}, u32[]{:S(2)}) collective-permute-start(bf16[128,2048]{1,0:T(8,128)(2,1)S(1)} %collective-permute-done.3.arrived_ref.b0._), channel_id=1, source_target_pairs={{0,6},{1,7},{2,0},{3,1},{4,2},{5,3},{6,4},{7,5},{8,14},{9,15},{10,... | collective-permute-start | bytes 1572872 | tf_op jit(solution)/shard_map/activations/ppermute | solution.py:36
  47.2 38.9 %collective-permute-start.8 = (bf16[128,2048]{1,0:T(8,128)(2,1)S(1)}, bf16[128,2048]{1,0:T(8,128)(2,1)S(1)}, u32[]{:S(2)}, u32[]{:S(2)}) collective-permute-start(bf16[128,2048]{1,0:T(8,128)(2,1)S(1)} %collective-permute-done.3.arrived_ref.b0._), channel_id=1, source_target_pairs={{0,4},{1,5},{2,6},{3,7},{4,0},{5,1},{6,2},{7,3},{8,12},{9,13},{10,... | collective-permute-start | bytes 1572872 | tf_op jit(solution)/shard_map/activations/ppermute | solution.py:36
  53.3 59.4 %all-to-all-start.2 = ((bf16[64,8,256]{2,1,0:T(8,128)(2,1)}), bf16[64,8,256]{2,1,0:T(8,128)(2,1)S(1)}, u32[]{:S(2)}, u32[]{:S(2)}) async-start(bf16[64,8,256]{2,1,0:T(8,128)(2,1)} %broadcast_in_dim.2), calls=%async_computation.2 | async-start | bytes 524288 | tf_op jit(solution)/shard_map/outer_sum/all_to_all | solution.py:27
  72.4 22.9 %collective-permute-start.4 = (bf16[640,256]{1,0:T(8,128)(2,1)S(1)}, bf16[640,256]{1,0:T(8,128)(2,1)S(1)}, u32[]{:S(2)}, u32[]{:S(2)}) collective-permute-start(bf16[640,256]{1,0:T(8,128)(2,1)S(1)} %get-tuple-element.26), channel_id=1, source_target_pairs={{0,1},{1,0},{2,3},{3,2},{4,5},{5,4},{6,7},{7,6},{8,9},{9,8},{10,11... | collective-permute-start | bytes 983048 | tf_op jit(solution)/shard_map/near_keys/ppermute | solution.py:31
  81.4 19.4 %collective-permute-start.7 = (bf16[256,256]{1,0:T(8,128)(2,1)S(1)}, bf16[256,256]{1,0:T(8,128)(2,1)S(1)}, u32[]{:S(2)}, u32[]{:S(2)}) collective-permute-start(bf16[256,256]{1,0:T(8,128)(2,1)S(1)} %get-tuple-element.28), channel_id=1, source_target_pairs={{0,1},{1,0},{2,3},{3,2},{4,5},{5,4},{6,7},{7,6},{8,9},{9,8},{10,11... | collective-permute-start | bytes 393224 | tf_op jit(solution)/shard_map/far_keys/ppermute | solution.py:31
  86.4 14.4 %collective-permute-start.9 = (bf16[128,256]{1,0:T(8,128)(2,1)S(1)}, bf16[128,256]{1,0:T(8,128)(2,1)S(1)}, u32[]{:S(2)}, u32[]{:S(2)}) collective-permute-start(bf16[128,256]{1,0:T(8,128)(2,1)S(1)} %get-tuple-element.29), channel_id=1, source_target_pairs={{0,1},{1,0},{2,3},{3,2},{4,5},{5,4},{6,7},{7,6},{8,9},{9,8},{10,11... | collective-permute-start | bytes 196616 | tf_op jit(solution)/shard_map/far_keys/ppermute | solution.py:31
  102.6 9.4 %collective-permute-start.10 = (f32[8,128]{1,0:T(8,128)S(1)}, f32[8,128]{1,0:T(8,128)S(1)}, u32[]{:S(2)}, u32[]{:S(2)}) collective-permute-start(f32[8,128]{1,0:T(8,128)S(1)} %get-tuple-element.33), channel_id=1, source_target_pairs={{0,1},{1,0},{2,3},{3,2},{4,5},{5,4},{6,7},{7,6},{8,9},{9,8},{10,11... | collective-permute-start | bytes 12296 | tf_op jit(solution)/shard_map/gradient/ppermute | solution.py:31
  112.0 8.4 %copy-start.4 = (f32[512,256]{1,0:T(8,128)S(1)}, f32[512,256]{1,0:T(8,128)}, u32[]{:S(2)}) copy-start(f32[512,256]{1,0:T(8,128)} %param.13) | copy-start | bytes 1572868
  112.0 8.4 %copy-start.5 = (bf16[512,256]{1,0:T(8,128)(2,1)S(1)}, bf16[512,256]{1,0:T(8,128)(2,1)}, u32[]{:S(2)}) copy-start(bf16[512,256]{1,0:T(8,128)(2,1)} %param.12) | copy-start | bytes 786436
  112.6 22.2 %copy-start = (bf16[1,512,1024]{2,1,0:T(8,128)(2,1)S(1)}, bf16[1,512,1024]{2,1,0:T(8,128)(2,1)}, u32[]{:S(2)}) copy-start(bf16[1,512,1024]{2,1,0:T(8,128)(2,1)} %weight_ref.1) | copy-start | bytes 3145732
  112.6 22.2 %copy-start.3 = (s32[8]{0:T(128)S(1)}, s32[8]{0:T(128)}, u32[]{:S(2)}) copy-start(s32[8]{0:T(128)} %order_ref.1) | copy-start | bytes 100
  112.6 22.2 %all-to-all-start = ((bf16[4,528,256]{2,1,0:T(8,128)(2,1)}), bf16[4,528,256]{2,1,0:T(8,128)(2,1)S(1)}, u32[]{:S(2)}, u32[]{:S(2)}) async-start(bf16[4,528,256]{2,1,0:T(8,128)(2,1)} %embed.1), calls=%async_computation | async-start | bytes 2162688 | tf_op jit(solution)/shard_map/gradient/all_to_all | solution.py:27
  121.4 16.3 %copy-start.1 = (bf16[512,256]{1,0:T(8,128)(2,1)}, bf16[512,256]{1,0:T(8,128)(2,1)S(1)}, u32[]{:S(2)}) copy-start(bf16[512,256]{1,0:T(8,128)(2,1)S(1)} %get-tuple-element.35.global_ref) | copy-start | bytes 786436
